TPU v7x, 768 devices: a whole 4x8x12 slice. The times are simulated.
768 devices in a mesh: wide: 192 (over y, x_hi, z), narrow: 4 (over x_lo, core).
Axes of the slice: x: 4 (x_hi: 2, x_lo: 2; x = x_hi * 2 + x_lo), y: 8, z: 12, core: 2. Of those that a mesh axis runs over, the one named last changes fastest.
Arguments:
- load: float32 [49152, 512], P(('wide', 'narrow')), may hold values from -48 to 48
- geom: bfloat16 [7, 49152, 512], P(None, ('wide', 'narrow')), may hold values from -0.15 to 3, as said below
- element_order: int32 [192, 4, 64], P('wide', 'narrow'), may hold values from 0 to 63, each once within a row
Outputs:
- solution: float32 [49152, 512], P(('wide', 'narrow'))
- residual: float32 [49152, 512], P(('wide', 'narrow'))
Inputs may be any that keep to these rules, and one draw needn't show every extreme that they name: `geom`: at every point G0, G1, G2 and G6 are positive and |G3|, |G4|, |G5| stay below 0.15. `element_order`: each device's list names each of its 64 block positions exactly once.
All inputs are finite; a program needn't handle non-finite values.
Results may differ from a plain program's by a relative error of at most 0.02.
Values sent between devices are 32-bit elements; how exact they have to be, the bound alone decides.
No kernel may reach another device: no remote copies, remote signals or barrier semaphores. Data moves between devices by JAX's collectives and lax.ppermute only.
A program may use at most 64 MiB of HBM per device.

v0:
```python
import jax
import jax.numpy as jnp
import numpy as np
from jax import lax
from jax.sharding import PartitionSpec as P

EZ = 1
EA = 4
ER = 16
CHEB = 3
ITERS = 2
E_DEV = 64


interval_low = 0.03
interval_high = 1.0


def with_halo(cells, sides, width):
    for axis, dim in sides:
        count = lax.axis_size(axis)
        head = lax.slice_in_dim(cells, 0, width, axis=dim)
        tail = lax.slice_in_dim(cells, cells.shape[dim] - width, cells.shape[dim], axis=dim)
        cells = jnp.concatenate(
            [
                lax.ppermute(tail, axis, [(i, (i + 1) % count) for i in range(count)]),
                cells,
                lax.ppermute(head, axis, [((i + 1) % count, i) for i in range(count)]),
            ],
            axis=dim,
        )
    return cells


def legendre_seven(point):
    before = 1.0
    current = point
    for degree in range(1, 7):
        after = ((2.0 * degree + 1.0) * point * current - degree * before) / (degree + 1.0)
        before = current
        current = after
    return current


def gll_derivative():
    points = 8
    inner_nodes = [
        -0.8717401485096066,
        -0.5917001814331423,
        -0.2092992179024789,
        0.2092992179024789,
        0.5917001814331423,
        0.8717401485096066,
    ]
    nodes = [-1.0] + inner_nodes + [1.0]
    values_at = [legendre_seven(node) for node in nodes]
    matrix = np.zeros((points, points))
    for source in range(points):
        for target in range(points):
            if source != target:
                matrix[source, target] = values_at[source] / (
                    values_at[target] * (nodes[source] - nodes[target])
                )
    matrix[0, 0] = -(points - 1) * points / 4.0
    matrix[points - 1, points - 1] = (points - 1) * points / 4.0
    return matrix


def radial_apply(field, radial_matrix):
    flat = field.reshape(-1, field.shape[-1])
    result = jnp.dot(
        flat, radial_matrix, precision=lax.Precision.HIGHEST, preferred_element_type=jnp.float32
    )
    return result.reshape(field.shape)


def gradients(field, derivative, radial_matrix):
    pipe_len, cycle_len, radial_len = field.shape
    blocks = field.reshape(pipe_len // 8, 8, cycle_len // 8, 8, radial_len)
    highest = lax.Precision.HIGHEST
    grad_z = jnp.einsum("im,pmqjr->piqjr", derivative, blocks, precision=highest)
    grad_a = jnp.einsum("jm,piqmr->piqjr", derivative, blocks, precision=highest)
    grad_r = radial_apply(field, radial_matrix.T)
    return (grad_z.reshape(field.shape), grad_a.reshape(field.shape), grad_r)


def divergence(flux_z, flux_a, flux_r, derivative, radial_matrix):
    pipe_len, cycle_len, radial_len = flux_z.shape
    shape5 = (pipe_len // 8, 8, cycle_len // 8, 8, radial_len)
    highest = lax.Precision.HIGHEST
    part_z = jnp.einsum(
        "mi,pmqjr->piqjr", derivative, flux_z.reshape(shape5), precision=highest
    ).reshape(flux_z.shape)
    part_a = jnp.einsum(
        "mj,piqmr->piqjr", derivative, flux_a.reshape(shape5), precision=highest
    ).reshape(flux_z.shape)
    part_r = radial_apply(flux_r, radial_matrix)
    return part_z + part_a + part_r


def element_apply(field, metric, derivative, radial_matrix):
    grad_z, grad_a, grad_r = gradients(field, derivative, radial_matrix)
    g_zz = metric[0].astype(jnp.float32)
    g_aa = metric[1].astype(jnp.float32)
    g_rr = metric[2].astype(jnp.float32)
    g_za = metric[3].astype(jnp.float32)
    g_zr = metric[4].astype(jnp.float32)
    g_ar = metric[5].astype(jnp.float32)
    flux_z = g_zz * grad_z + g_za * grad_a + g_zr * grad_r
    flux_a = g_za * grad_z + g_aa * grad_a + g_ar * grad_r
    flux_r = g_zr * grad_z + g_ar * grad_a + g_rr * grad_r
    return (
        divergence(flux_z, flux_a, flux_r, derivative, radial_matrix)
        + metric[6].astype(jnp.float32) * field
    )


def element_bound(metric, derivative, radial_count):
    pipe_len, cycle_len, radial_len = metric.shape[1:]
    absolute = jnp.abs(derivative)
    radial_absolute = jnp.kron(jnp.eye(radial_count, dtype=jnp.float32), absolute)
    row_total = jnp.sum(absolute, axis=1)
    q_z = jnp.tile(row_total, pipe_len // 8)[:, None, None]
    q_a = jnp.tile(row_total, cycle_len // 8)[None, :, None]
    q_r = jnp.tile(row_total, radial_len // 8)[None, None, :]
    g_abs = jnp.abs(metric.astype(jnp.float32))
    h_z = g_abs[0] * q_z + g_abs[3] * q_a + g_abs[4] * q_r
    h_a = g_abs[3] * q_z + g_abs[1] * q_a + g_abs[5] * q_r
    h_r = g_abs[4] * q_z + g_abs[5] * q_a + g_abs[2] * q_r
    return divergence(h_z, h_a, h_r, absolute, radial_absolute) + g_abs[6]


def pair_sum(padded, axis):
    length = padded.shape[axis] - 2
    core = lax.slice_in_dim(padded, 1, length + 1, axis=axis)
    upper = lax.slice_in_dim(padded, 2, length + 2, axis=axis)
    lower = lax.slice_in_dim(padded, 0, length, axis=axis)
    node = lax.broadcasted_iota(jnp.int32, core.shape, axis) % 8
    return core + jnp.where(node == 7, upper, 0.0) + jnp.where(node == 0, lower, 0.0)


def point_weight(pipe_len, cycle_len, radial_len):
    one = jnp.float32(1.0)
    two = jnp.float32(2.0)
    pipe_node = jnp.arange(pipe_len) % 8
    cycle_node = jnp.arange(cycle_len) % 8
    radial_index = jnp.arange(radial_len)
    radial_node = radial_index % 8
    count_z = jnp.where((pipe_node == 0) | (pipe_node == 7), two, one)
    count_a = jnp.where((cycle_node == 0) | (cycle_node == 7), two, one)
    inside = (radial_index > 0) & (radial_index < radial_len - 1)
    count_r = jnp.where(((radial_node == 0) | (radial_node == 7)) & inside, two, one)
    return one / (count_z[:, None, None] * count_a[None, :, None] * count_r[None, None, :])


def assemble(stacked):
    padded = with_halo(stacked, (("wide", 1), ("narrow", 2)), 1)
    merged = pair_sum(pair_sum(padded, 1), 2)
    radial = jnp.pad(merged, ((0, 0), (0, 0), (0, 0), (1, 1)))
    return pair_sum(radial, 3)


def local(load, geom, element_order):
    derivative = jnp.asarray(gll_derivative(), dtype=jnp.float32)
    radial_matrix = jnp.kron(jnp.eye(ER, dtype=jnp.float32), derivative)
    order_flat = element_order.reshape(-1)
    inverse = jnp.argsort(order_flat)
    pipe_len = EZ * 8
    cycle_len = EA * 8
    radial_len = ER * 8
    placed = jnp.take(load, inverse, axis=0)
    load_grid = (
        placed.reshape(EZ, EA, ER, 8, 8, 8)
        .transpose(0, 3, 1, 4, 2, 5)
        .reshape(pipe_len, cycle_len, radial_len)
    )
    placed_geom = jnp.take(geom, inverse, axis=1)
    metric = placed_geom.reshape(7, EZ, EA, ER, 8, 8, 8).transpose(0, 1, 4, 2, 5, 3, 6)
    metric = metric.reshape(7, pipe_len, cycle_len, radial_len)
    local_bound = element_bound(metric, derivative, ER)
    assembled = assemble(jnp.stack([load_grid, local_bound]))
    grid_residual = assembled[0]
    bound_inverse = 1.0 / assembled[1]
    weight = point_weight(pipe_len, cycle_len, radial_len)

    def operator(field):
        return assemble(element_apply(field, metric, derivative, radial_matrix)[None])[0]

    def inner(first_field, second_field):
        return jnp.sum(first_field * second_field * weight)

    center = (interval_high + interval_low) / 2.0
    half_width = (interval_high - interval_low) / 2.0
    sigma_ratio = center / half_width
    grid_solution = jnp.zeros_like(grid_residual)
    direction = grid_residual
    previous = jnp.float32(1.0)
    step_size = jnp.float32(1.0)
    for iteration in range(ITERS):
        rho_now = 1.0 / sigma_ratio
        update = grid_residual * bound_inverse / center
        result = update
        for degree_step in range(CHEB - 1):
            rho_next = 1.0 / (2.0 * sigma_ratio - rho_now)
            update = rho_next * rho_now * update + 2.0 * rho_next / half_width * bound_inverse * (
                grid_residual - operator(result)
            )
            result = result + update
            rho_now = rho_next
        precond_norm = lax.psum(inner(grid_residual, result), ("wide", "narrow"))
        if iteration == 0:
            direction = result
        else:
            direction = result + precond_norm / previous * direction
        image = operator(direction)
        step_size = precond_norm / lax.psum(inner(direction, image), ("wide", "narrow"))
        grid_solution = grid_solution + step_size * direction
        grid_residual = grid_residual - step_size * image
        previous = precond_norm

    def read_back(grid_field):
        rows = (
            grid_field.reshape(EZ, 8, EA, 8, ER, 8).transpose(0, 2, 4, 1, 3, 5).reshape(E_DEV, 512)
        )
        return jnp.take(rows, order_flat, axis=0)

    return (read_back(grid_solution), read_back(grid_residual))


def solution(mesh):
    placed = (
        P(("wide", "narrow"), None),
        P(None, ("wide", "narrow"), None),
        P("wide", "narrow", None),
    )
    return jax.shard_map(
        local,
        mesh=mesh,
        in_specs=placed,
        out_specs=(P(("wide", "narrow"), None), P(("wide", "narrow"), None)),
        check_vma=False,
    )
```

profile of v0, /device:TPU:1, one launch (start us, length us, event | category | flops | bytes accessed | tf_op | source)
XLA Modules:
  0.0 614.8 jit_solution(7038333651524929016)
XLA Ops:
  0.7 2.7 sort.17
  3.4 1.9 gather_fusion
  5.8 3.6 gather.10
  9.5 5.3 convert_abs_fusion
  14.7 3.1 fusion.321
  51.3 4.8 collective-permute-start
  56.1 17.6 %collective-permute-start.1 = (f32[2,1,32,128]{3,2,1,0:T(8,128)S(1)}, f32[2,1,32,128]{3,2,1,0:T(8,128)S(1)}, u32[]{:S(2)}, u32[]{:S(2)}) collective-permute-start(f32[2,1,32,128]{3,2,1,0:T(8,128)S(1)} %get-tuple-element.46), channel_id=1, source_target_pairs={{4,0},{8,4},{12,8},{16,12},{20,16},{24,20},{28,24},{32,28},{36,32}... | collective-permute-start | bytes 98312 | tf_op jit(solution)/shard_map/ppermute | solution.py:28
  73.9 5.2 slice_convert_fusion.1
  79.1 3.1 collective-permute-start.2
  82.2 1.9 collective-permute-start.3
  107.5 2.3 collective-permute-start.4
  109.9 9.1 %collective-permute-start.5 = (f32[1,1,32,128]{3,2,1,0:T(8,128)S(1)}, f32[1,1,32,128]{3,2,1,0:T(8,128)S(1)}, u32[]{:S(2)}, u32[]{:S(2)}) collective-permute-start(f32[1,1,32,128]{3,2,1,0:T(8,128)S(1)} %get-tuple-element.70), channel_id=1, source_target_pairs={{4,0},{8,4},{12,8},{16,12},{20,16},{24,20},{28,24},{32,28},{36,32}... | collective-permute-start | bytes 49160 | tf_op jit(solution)/shard_map/ppermute | solution.py:28
  119.8 4.8 collective-permute-start.6
  124.6 1.9 collective-permute-start.7
  126.5 3.0 collective-permute-done.7
  133.8 10.3 %collective-permute-start.9 = (f32[1,1,32,128]{3,2,1,0:T(8,128)S(1)}, f32[1,1,32,128]{3,2,1,0:T(8,128)S(1)}, u32[]{:S(2)}, u32[]{:S(2)}) collective-permute-start(f32[1,1,32,128]{3,2,1,0:T(8,128)S(1)} %get-tuple-element.68), channel_id=1, source_target_pairs={{4,0},{8,4},{12,8},{16,12},{20,16},{24,20},{28,24},{32,28},{36,32}... | collective-permute-start | bytes 49160 | tf_op jit(solution)/shard_map/ppermute | solution.py:28
  144.9 2.2 collective-permute-start.10
  147.1 2.1 collective-permute-start.11
  149.3 2.8 collective-permute-done.11
  154.5 1.9 collective-permute-start.12
  156.4 10.4 %collective-permute-start.13 = (f32[1,1,32,128]{3,2,1,0:T(8,128)S(1)}, f32[1,1,32,128]{3,2,1,0:T(8,128)S(1)}, u32[]{:S(2)}, u32[]{:S(2)}) collective-permute-start(f32[1,1,32,128]{3,2,1,0:T(8,128)S(1)} %get-tuple-element.66), channel_id=1, source_target_pairs={{4,0},{8,4},{12,8},{16,12},{20,16},{24,20},{28,24},{32,28},{36,32}... | collective-permute-start | bytes 49160 | tf_op jit(solution)/shard_map/ppermute | solution.py:28
  167.7 2.2 collective-permute-start.14
  169.9 2.1 collective-permute-start.15
  172.1 2.8 collective-permute-done.15
  176.0 109.7 %all-reduce.7 = (f32[]{:T(128)}, f32[]{:T(128)}) all-reduce(f32[]{:T(128)} %get-tuple-element.6, f32[]{:T(128)} %get-tuple-element.5), channel_id=1, replica_groups=mesh['wide'=192,'narrow'=4] {'wide','narrow'}, use_global_device_ids=true, to_apply=%region_3.5 | all-reduce | flops 2 | bytes 16 | tf_op jit(solution)/shard_map/psum | solution.py:210
  290.9 9.1 %collective-permute-start.17 = (f32[1,1,32,128]{3,2,1,0:T(8,128)S(1)}, f32[1,1,32,128]{3,2,1,0:T(8,128)S(1)}, u32[]{:S(2)}, u32[]{:S(2)}) collective-permute-start(f32[1,1,32,128]{3,2,1,0:T(8,128)S(1)} %get-tuple-element.64), channel_id=1, source_target_pairs={{4,0},{8,4},{12,8},{16,12},{20,16},{24,20},{28,24},{32,28},{36,32}... | collective-permute-start | bytes 49160 | tf_op jit(solution)/shard_map/ppermute | solution.py:28
  300.9 4.7 collective-permute-start.18
  305.6 1.9 collective-permute-start.19
  307.5 3.0 collective-permute-done.19
  314.9 10.3 %collective-permute-start.21 = (f32[1,1,32,128]{3,2,1,0:T(8,128)S(1)}, f32[1,1,32,128]{3,2,1,0:T(8,128)S(1)}, u32[]{:S(2)}, u32[]{:S(2)}) collective-permute-start(f32[1,1,32,128]{3,2,1,0:T(8,128)S(1)} %get-tuple-element.62), channel_id=1, source_target_pairs={{4,0},{8,4},{12,8},{16,12},{20,16},{24,20},{28,24},{32,28},{36,32}... | collective-permute-start | bytes 49160 | tf_op jit(solution)/shard_map/ppermute | solution.py:28
  326.0 2.2 collective-permute-start.22
  328.2 2.1 collective-permute-start.23
  330.9 2.3 collective-permute-done.23
  334.3 109.0 %psum.30 = f32[]{:T(128)} all-reduce(f32[]{:T(128)} %get-tuple-element.11), channel_id=1, replica_groups=mesh['wide'=192,'narrow'=4] {'wide','narrow'}, use_global_device_ids=true, to_apply=%region_7.9 | all-reduce | flops 1 | bytes 8 | tf_op jit(solution)/shard_map/psum | solution.py:210
  446.9 1.9 collective-permute-start.24
  448.8 9.1 %collective-permute-start.25 = (f32[1,1,32,128]{3,2,1,0:T(8,128)S(1)}, f32[1,1,32,128]{3,2,1,0:T(8,128)S(1)}, u32[]{:S(2)}, u32[]{:S(2)}) collective-permute-start(f32[1,1,32,128]{3,2,1,0:T(8,128)S(1)} %get-tuple-element.60), channel_id=1, source_target_pairs={{4,0},{8,4},{12,8},{16,12},{20,16},{24,20},{28,24},{32,28},{36,32}... | collective-permute-start | bytes 49160 | tf_op jit(solution)/shard_map/ppermute | solution.py:28
  458.8 5.3 collective-permute-start.26
  464.1 2.1 collective-permute-start.27
  467.4 2.5 squeeze.59
  469.9 2.4 squeeze.120
  472.3 2.5 squeeze.121
  474.8 2.5 mul.1102
  477.3 2.4 squeeze.127
  479.8 2.6 squeeze.128
  483.5 109.4 %psum.31 = f32[]{:T(128)} all-reduce(f32[]{:T(128)} %get-tuple-element.9), channel_id=1, replica_groups=mesh['wide'=192,'narrow'=4] {'wide','narrow'}, use_global_device_ids=true, to_apply=%region_9.11 | all-reduce | flops 1 | bytes 8 | tf_op jit(solution)/shard_map/psum | solution.py:216
  594.3 2.4 mul.1113
  596.7 7.7 %subtract_bitcast_fusion = (f32[1,4,16,8,8,8]{5,2,4,1,3,0:T(8,128)}, f32[1,4,16,8,8,8]{5,2,4,1,3,0:T(8,128)}) fusion(f32[1,8,4,8,16,8]{5,4,3,2,1,0:T(8,128)} %mul.1113, f32[1,8,4,8,16,8]{5,4,3,2,1,0:T(8,128)} %squeeze.59, f32[1,8,4,8,16,8]{5,4,3,2,1,0:T(8,128)} %mul.1102, f32[]{:T(128)S(6)} %div.110, f32[1,8,4,8,16,8]{5,4,3,2,1,0:T(8,128)} %squeeze.128, ...), kind=kLoop, calls=%fused_computation.7 | loop fusion | flops 1081344 | bytes 1310732 | tf_op jit(solution)/shard_map/transpose | solution.py:223
  604.4 2.8 copy.217
  (284 shorter events, 91.1 us)
Async XLA Ops:
  51.3 27.8 %collective-permute-start = (f32[2,1,32,128]{3,2,1,0:T(8,128)S(1)}, f32[2,1,32,128]{3,2,1,0:T(8,128)S(1)}, u32[]{:S(2)}, u32[]{:S(2)}) collective-permute-start(f32[2,1,32,128]{3,2,1,0:T(8,128)S(1)} %get-tuple-element.45), channel_id=1, source_target_pairs={{0,4},{4,8},{8,12},{12,16},{16,20},{20,24},{24,28},{28,32},{32,36}... | collective-permute-start | bytes 98312 | tf_op jit(solution)/shard_map/ppermute | solution.py:26
  56.1 23.0 %collective-permute-start.1 = (f32[2,1,32,128]{3,2,1,0:T(8,128)S(1)}, f32[2,1,32,128]{3,2,1,0:T(8,128)S(1)}, u32[]{:S(2)}, u32[]{:S(2)}) collective-permute-start(f32[2,1,32,128]{3,2,1,0:T(8,128)S(1)} %get-tuple-element.46), channel_id=1, source_target_pairs={{4,0},{8,4},{12,8},{16,12},{20,16},{24,20},{28,24},{32,28},{36,32}... | collective-permute-start | bytes 98312 | tf_op jit(solution)/shard_map/ppermute | solution.py:28
  73.8 236.8 %copy-start.29 = (s32[8]{0:T(128)}, s32[8]{0:T(128)S(1)}, u32[]{:S(2)}) copy-start(s32[8]{0:T(128)S(1)} %get-tuple-element.75) | copy-start | bytes 100
  73.8 236.8 %copy-start.32 = (s32[8]{0:T(128)}, s32[8]{0:T(128)S(1)}, u32[]{:S(2)}) copy-start(s32[8]{0:T(128)S(1)} %get-tuple-element.76) | copy-start | bytes 100
  73.8 236.8 %copy-start.35 = (pred[8]{0:T(512)(128)(4,1)}, pred[8]{0:T(512)(128)(4,1)S(1)}, u32[]{:S(2)}) copy-start(pred[8]{0:T(512)(128)(4,1)S(1)} %compare_and_fusion.4) | copy-start | bytes 28
  73.8 101.3 %copy-start.20 = (s32[128]{0:T(128)}, s32[128]{0:T(128)S(1)}, u32[]{:S(2)}) copy-start(s32[128]{0:T(128)S(1)} %get-tuple-element.77) | copy-start | bytes 1540
  73.8 101.3 %copy-start.23 = (s32[128]{0:T(128)}, s32[128]{0:T(128)S(1)}, u32[]{:S(2)}) copy-start(s32[128]{0:T(128)S(1)} %get-tuple-element.78) | copy-start | bytes 1540
  79.1 25.8 %collective-permute-start.2 = (f32[2,10,1,128]{3,2,1,0:T(1,128)S(1)}, f32[2,10,1,128]{3,2,1,0:T(1,128)S(1)}, u32[]{:S(2)}, u32[]{:S(2)}) collective-permute-start(f32[2,10,1,128]{3,2,1,0:T(1,128)S(1)} %get-tuple-element.41), channel_id=1, source_target_pairs={{0,1},{1,2},{2,3},{3,0},{4,5},{5,6},{6,7},{7,4},{8,9},{9,10},{10,1... | collective-permute-start | bytes 30728 | tf_op jit(solution)/shard_map/ppermute | solution.py:26
  82.2 22.8 %collective-permute-start.3 = (f32[2,10,1,128]{3,2,1,0:T(1,128)S(1)}, f32[2,10,1,128]{3,2,1,0:T(1,128)S(1)}, u32[]{:S(2)}, u32[]{:S(2)}) collective-permute-start(f32[2,10,1,128]{3,2,1,0:T(1,128)S(1)} %get-tuple-element.42), channel_id=1, source_target_pairs={{1,0},{2,1},{3,2},{0,3},{5,4},{6,5},{7,6},{4,7},{9,8},{10,9},{11,1... | collective-permute-start | bytes 30728 | tf_op jit(solution)/shard_map/ppermute | solution.py:28
  84.1 91.0 %copy-start.26 = (pred[128]{0:T(512)(128)(4,1)}, pred[128]{0:T(512)(128)(4,1)S(1)}, u32[]{:S(2)}) copy-start(pred[128]{0:T(512)(128)(4,1)S(1)} %compare_and_fusion.2) | copy-start | bytes 388
  84.7 204.0 %copy-start.7 = (f32[128,128,1]{1,0,2:T(8,128)}, f32[128,128,1]{1,0,2:T(8,128)S(1)}, u32[]{:S(2)}) copy-start(f32[128,128,1]{1,0,2:T(8,128)S(1)} %reshape.941) | copy-start | bytes 196612
  107.5 11.4 %collective-permute-start.4 = (f32[1,1,32,128]{3,2,1,0:T(8,128)S(1)}, f32[1,1,32,128]{3,2,1,0:T(8,128)S(1)}, u32[]{:S(2)}, u32[]{:S(2)}) collective-permute-start(f32[1,1,32,128]{3,2,1,0:T(8,128)S(1)} %get-tuple-element.69), channel_id=1, source_target_pairs={{0,4},{4,8},{8,12},{12,16},{16,20},{20,24},{24,28},{28,32},{32,36}... | collective-permute-start | bytes 49160 | tf_op jit(solution)/shard_map/ppermute | solution.py:26
  109.9 9.9 %collective-permute-start.5 = (f32[1,1,32,128]{3,2,1,0:T(8,128)S(1)}, f32[1,1,32,128]{3,2,1,0:T(8,128)S(1)}, u32[]{:S(2)}, u32[]{:S(2)}) collective-permute-start(f32[1,1,32,128]{3,2,1,0:T(8,128)S(1)} %get-tuple-element.70), channel_id=1, source_target_pairs={{4,0},{8,4},{12,8},{16,12},{20,16},{24,20},{28,24},{32,28},{36,32}... | collective-permute-start | bytes 49160 | tf_op jit(solution)/shard_map/ppermute | solution.py:28
  119.8 6.7 %collective-permute-start.6 = (f32[1,10,1,128]{3,2,1,0:T(1,128)S(1)}, f32[1,10,1,128]{3,2,1,0:T(1,128)S(1)}, u32[]{:S(2)}, u32[]{:S(2)}) collective-permute-start(f32[1,10,1,128]{3,2,1,0:T(1,128)S(1)} %get-tuple-element.57), channel_id=1, source_target_pairs={{0,1},{1,2},{2,3},{3,0},{4,5},{5,6},{6,7},{7,4},{8,9},{9,10},{10,1... | collective-permute-start | bytes 15368 | tf_op jit(solution)/shard_map/ppermute | solution.py:26
  124.6 4.9 collective-permute-start.7
  131.9 12.2 %collective-permute-start.8 = (f32[1,1,32,128]{3,2,1,0:T(8,128)S(1)}, f32[1,1,32,128]{3,2,1,0:T(8,128)S(1)}, u32[]{:S(2)}, u32[]{:S(2)}) collective-permute-start(f32[1,1,32,128]{3,2,1,0:T(8,128)S(1)} %get-tuple-element.67), channel_id=1, source_target_pairs={{0,4},{4,8},{8,12},{12,16},{16,20},{20,24},{24,28},{28,32},{32,36}... | collective-permute-start | bytes 49160 | tf_op jit(solution)/shard_map/ppermute | solution.py:26
  133.8 11.1 %collective-permute-start.9 = (f32[1,1,32,128]{3,2,1,0:T(8,128)S(1)}, f32[1,1,32,128]{3,2,1,0:T(8,128)S(1)}, u32[]{:S(2)}, u32[]{:S(2)}) collective-permute-start(f32[1,1,32,128]{3,2,1,0:T(8,128)S(1)} %get-tuple-element.68), channel_id=1, source_target_pairs={{4,0},{8,4},{12,8},{16,12},{20,16},{24,20},{28,24},{32,28},{36,32}... | collective-permute-start | bytes 49160 | tf_op jit(solution)/shard_map/ppermute | solution.py:28
  144.9 4.4 collective-permute-start.10
  147.1 4.9 collective-permute-start.11
  152.4 293.0 %copy-start.12 = (f32[1,8,32,128]{3,2,1,0:T(8,128)}, f32[1,8,32,128]{3,2,1,0:T(8,128)S(1)}, u32[]{:S(2)}) copy-start(f32[1,8,32,128]{3,2,1,0:T(8,128)S(1)} %get-tuple-element.20) | copy-start | bytes 393220
  152.4 294.1 %copy-start.5 = (f32[8,32,128]{2,1,0:T(8,128)}, f32[8,32,128]{2,1,0:T(8,128)S(1)}, u32[]{:S(2)}) copy-start(f32[8,32,128]{2,1,0:T(8,128)S(1)} %get-tuple-element.19) | copy-start | bytes 393220
  154.5 12.4 %collective-permute-start.12 = (f32[1,1,32,128]{3,2,1,0:T(8,128)S(1)}, f32[1,1,32,128]{3,2,1,0:T(8,128)S(1)}, u32[]{:S(2)}, u32[]{:S(2)}) collective-permute-start(f32[1,1,32,128]{3,2,1,0:T(8,128)S(1)} %get-tuple-element.65), channel_id=1, source_target_pairs={{0,4},{4,8},{8,12},{12,16},{16,20},{20,24},{24,28},{28,32},{32,36}... | collective-permute-start | bytes 49160 | tf_op jit(solution)/shard_map/ppermute | solution.py:26
  156.4 11.3 %collective-permute-start.13 = (f32[1,1,32,128]{3,2,1,0:T(8,128)S(1)}, f32[1,1,32,128]{3,2,1,0:T(8,128)S(1)}, u32[]{:S(2)}, u32[]{:S(2)}) collective-permute-start(f32[1,1,32,128]{3,2,1,0:T(8,128)S(1)} %get-tuple-element.66), channel_id=1, source_target_pairs={{4,0},{8,4},{12,8},{16,12},{20,16},{24,20},{28,24},{32,28},{36,32}... | collective-permute-start | bytes 49160 | tf_op jit(solution)/shard_map/ppermute | solution.py:28
  167.7 4.4 collective-permute-start.14
  169.9 4.9 collective-permute-start.15
  172.1 161.4 %copy-start.39 = (f32[128]{0:T(128)}, f32[128]{0:T(128)S(1)}, u32[]{:S(2)}) copy-start(f32[128]{0:T(128)S(1)} %and_select_fusion) | copy-start | bytes 1540
  287.0 158.4 %copy-start.10 = (f32[1,8,32,128]{3,2,1,0:T(8,128)}, f32[1,8,32,128]{3,2,1,0:T(8,128)S(1)}, u32[]{:S(2)}) copy-start(f32[1,8,32,128]{3,2,1,0:T(8,128)S(1)} %get-tuple-element.17) | copy-start | bytes 393220
  288.3 22.5 %copy-start.21 = (s32[128]{0:T(128)S(1)}, s32[128]{0:T(128)}, u32[]{:S(2)}) copy-start(s32[128]{0:T(128)} %copy-done.20) | copy-start | bytes 1540
  288.3 22.5 %copy-start.24 = (s32[128]{0:T(128)S(1)}, s32[128]{0:T(128)}, u32[]{:S(2)}) copy-start(s32[128]{0:T(128)} %copy-done.23) | copy-start | bytes 1540
  288.3 22.5 %copy-start.27 = (pred[128]{0:T(512)(128)(4,1)S(1)}, pred[128]{0:T(512)(128)(4,1)}, u32[]{:S(2)}) copy-start(pred[128]{0:T(512)(128)(4,1)} %copy-done.26) | copy-start | bytes 388
  289.0 22.6 %copy-start.8 = (f32[128,128,1]{1,0,2:T(8,128)S(1)}, f32[128,128,1]{1,0,2:T(8,128)}, u32[]{:S(2)}) copy-start(f32[128,128,1]{1,0,2:T(8,128)} %copy-done.7) | copy-start | bytes 196612
  289.0 11.0 %collective-permute-start.16 = (f32[1,1,32,128]{3,2,1,0:T(8,128)S(1)}, f32[1,1,32,128]{3,2,1,0:T(8,128)S(1)}, u32[]{:S(2)}, u32[]{:S(2)}) collective-permute-start(f32[1,1,32,128]{3,2,1,0:T(8,128)S(1)} %get-tuple-element.63), channel_id=1, source_target_pairs={{0,4},{4,8},{8,12},{12,16},{16,20},{20,24},{24,28},{28,32},{32,36}... | collective-permute-start | bytes 49160 | tf_op jit(solution)/shard_map/ppermute | solution.py:26
  290.9 9.9 %collective-permute-start.17 = (f32[1,1,32,128]{3,2,1,0:T(8,128)S(1)}, f32[1,1,32,128]{3,2,1,0:T(8,128)S(1)}, u32[]{:S(2)}, u32[]{:S(2)}) collective-permute-start(f32[1,1,32,128]{3,2,1,0:T(8,128)S(1)} %get-tuple-element.64), channel_id=1, source_target_pairs={{4,0},{8,4},{12,8},{16,12},{20,16},{24,20},{28,24},{32,28},{36,32}... | collective-permute-start | bytes 49160 | tf_op jit(solution)/shard_map/ppermute | solution.py:28
  300.9 6.6 %collective-permute-start.18 = (f32[1,10,1,128]{3,2,1,0:T(1,128)S(1)}, f32[1,10,1,128]{3,2,1,0:T(1,128)S(1)}, u32[]{:S(2)}, u32[]{:S(2)}) collective-permute-start(f32[1,10,1,128]{3,2,1,0:T(1,128)S(1)} %get-tuple-element.51), channel_id=1, source_target_pairs={{0,1},{1,2},{2,3},{3,0},{4,5},{5,6},{6,7},{7,4},{8,9},{9,10},{10,1... | collective-permute-start | bytes 15368 | tf_op jit(solution)/shard_map/ppermute | solution.py:26
  305.6 4.9 collective-permute-start.19
  311.9 21.3 %copy-start.30 = (s32[8]{0:T(128)S(1)}, s32[8]{0:T(128)}, u32[]{:S(2)}) copy-start(s32[8]{0:T(128)} %copy-done.29) | copy-start | bytes 100
  311.9 21.3 %copy-start.33 = (s32[8]{0:T(128)S(1)}, s32[8]{0:T(128)}, u32[]{:S(2)}) copy-start(s32[8]{0:T(128)} %copy-done.32) | copy-start | bytes 100
  311.9 21.3 %copy-start.36 = (pred[8]{0:T(512)(128)(4,1)S(1)}, pred[8]{0:T(512)(128)(4,1)}, u32[]{:S(2)}) copy-start(pred[8]{0:T(512)(128)(4,1)} %copy-done.35) | copy-start | bytes 28
  313.0 12.2 %collective-permute-start.20 = (f32[1,1,32,128]{3,2,1,0:T(8,128)S(1)}, f32[1,1,32,128]{3,2,1,0:T(8,128)S(1)}, u32[]{:S(2)}, u32[]{:S(2)}) collective-permute-start(f32[1,1,32,128]{3,2,1,0:T(8,128)S(1)} %get-tuple-element.61), channel_id=1, source_target_pairs={{0,4},{4,8},{8,12},{12,16},{16,20},{20,24},{24,28},{28,32},{32,36}... | collective-permute-start | bytes 49160 | tf_op jit(solution)/shard_map/ppermute | solution.py:26
  314.9 11.1 %collective-permute-start.21 = (f32[1,1,32,128]{3,2,1,0:T(8,128)S(1)}, f32[1,1,32,128]{3,2,1,0:T(8,128)S(1)}, u32[]{:S(2)}, u32[]{:S(2)}) collective-permute-start(f32[1,1,32,128]{3,2,1,0:T(8,128)S(1)} %get-tuple-element.62), channel_id=1, source_target_pairs={{4,0},{8,4},{12,8},{16,12},{20,16},{24,20},{28,24},{32,28},{36,32}... | collective-permute-start | bytes 49160 | tf_op jit(solution)/shard_map/ppermute | solution.py:28
  326.0 4.9 collective-permute-start.22
  328.2 4.9 collective-permute-start.23
  334.3 112.0 %copy-start.14 = (f32[1,8,32,128]{3,2,1,0:T(8,128)}, f32[1,8,32,128]{3,2,1,0:T(8,128)S(1)}, u32[]{:S(2)}) copy-start(f32[1,8,32,128]{3,2,1,0:T(8,128)S(1)} %get-tuple-element.13) | copy-start | bytes 393220
  334.3 112.4 %copy-start.16 = (f32[8,32,128]{2,1,0:T(8,128)}, f32[8,32,128]{2,1,0:T(8,128)S(1)}, u32[]{:S(2)}) copy-start(f32[8,32,128]{2,1,0:T(8,128)S(1)} %get-tuple-element.12) | copy-start | bytes 393220
  446.9 11.0 %collective-permute-start.24 = (f32[1,1,32,128]{3,2,1,0:T(8,128)S(1)}, f32[1,1,32,128]{3,2,1,0:T(8,128)S(1)}, u32[]{:S(2)}, u32[]{:S(2)}) collective-permute-start(f32[1,1,32,128]{3,2,1,0:T(8,128)S(1)} %get-tuple-element.59), channel_id=1, source_target_pairs={{0,4},{4,8},{8,12},{12,16},{16,20},{20,24},{24,28},{28,32},{32,36}... | collective-permute-start | bytes 49160 | tf_op jit(solution)/shard_map/ppermute | solution.py:26
  448.8 9.9 %collective-permute-start.25 = (f32[1,1,32,128]{3,2,1,0:T(8,128)S(1)}, f32[1,1,32,128]{3,2,1,0:T(8,128)S(1)}, u32[]{:S(2)}, u32[]{:S(2)}) collective-permute-start(f32[1,1,32,128]{3,2,1,0:T(8,128)S(1)} %get-tuple-element.60), channel_id=1, source_target_pairs={{4,0},{8,4},{12,8},{16,12},{20,16},{24,20},{28,24},{32,28},{36,32}... | collective-permute-start | bytes 49160 | tf_op jit(solution)/shard_map/ppermute | solution.py:28
  458.8 23.6 %collective-permute-start.26 = (f32[1,10,1,128]{3,2,1,0:T(1,128)S(1)}, f32[1,10,1,128]{3,2,1,0:T(1,128)S(1)}, u32[]{:S(2)}, u32[]{:S(2)}) collective-permute-start(f32[1,10,1,128]{3,2,1,0:T(1,128)S(1)} %get-tuple-element.47), channel_id=1, source_target_pairs={{0,1},{1,2},{2,3},{3,0},{4,5},{5,6},{6,7},{7,4},{8,9},{9,10},{10,1... | collective-permute-start | bytes 15368 | tf_op jit(solution)/shard_map/ppermute | solution.py:26
  464.1 18.3 %collective-permute-start.27 = (f32[1,10,1,128]{3,2,1,0:T(1,128)S(1)}, f32[1,10,1,128]{3,2,1,0:T(1,128)S(1)}, u32[]{:S(2)}, u32[]{:S(2)}) collective-permute-start(f32[1,10,1,128]{3,2,1,0:T(1,128)S(1)} %get-tuple-element.48), channel_id=1, source_target_pairs={{1,0},{2,1},{3,2},{0,3},{5,4},{6,5},{7,6},{4,7},{9,8},{10,9},{11,1... | collective-permute-start | bytes 15368 | tf_op jit(solution)/shard_map/ppermute | solution.py:28
  (25 other events, 103.5 us)
where the time goes:
time: 619 us; the launch traced here: 615 us
  blocking collectives  328 us (53%)
  starting transfers between devices  131 us (21%)
  local copies, waits for them, and re-layouts  87.9 us (14%)
  other arithmetic  29.4 us (5%)
  waiting for transfers between devices  18.8 us (3%)
  matrix products  12.8 us (2%)
  between operations  6.71 us (1%)
    psum x2, blocking collectives, local(): precond_norm = lax.psum(inner(grid_residual, result), ('wide', 'narrow'))  219 us
    psum x1, blocking collectives, local(): lax.psum(inner(direction, image), ('wide', 'narrow'))  109 us
    ppermute x14, starting transfers between devices, with_halo(): lax.ppermute(head, axis, [((i + 1) % count, i) for i in range(count)])  90 us
    ppermute x14, starting transfers between devices, with_halo(): lax.ppermute(tail, axis, [(i, (i + 1) % count) for i in range(count)])  41.1 us
    ppermute x14, waiting for transfers between devices, with_halo(): lax.ppermute(head, axis, [((i + 1) % count, i) for i in range(count)])  18.7 us
  transfers between devices with their start and end apart: 28, of which 11 were waited for; matrix products, arithmetic and copies ran while one was open for 7% of the time, Pallas kernels for 0%

commit v1 on v0

v1 whole, which is shorter than its diff:
```python
import functools

import jax
import jax.numpy as jnp
import ml_dtypes
import numpy as np
from jax import lax
from jax.experimental import pallas as pl
from jax.experimental.pallas import tpu as pltpu
from jax.sharding import PartitionSpec as P

NODES = 8
ROWS = 32
LANES = 128
HALF = 16
INTERVAL_LOW = 0.03
INTERVAL_HIGH = 1.0
FIELD = (NODES, ROWS, LANES)
WIDE = ("outer", "ring")
REST = ("outer", "narrow")


def legendre_seven(point):
    before = 1.0
    current = point
    for degree in range(1, 7):
        after = ((2.0 * degree + 1.0) * point * current - degree * before) / (degree + 1.0)
        before = current
        current = after
    return current


def gll_derivative():
    points = 8
    inner_nodes = [
        -0.8717401485096066,
        -0.5917001814331423,
        -0.2092992179024789,
        0.2092992179024789,
        0.5917001814331423,
        0.8717401485096066,
    ]
    nodes = [-1.0] + inner_nodes + [1.0]
    values_at = [legendre_seven(node) for node in nodes]
    matrix = np.zeros((points, points))
    for source in range(points):
        for target in range(points):
            if source != target:
                matrix[source, target] = values_at[source] / (
                    values_at[target] * (nodes[source] - nodes[target])
                )
    matrix[0, 0] = -(points - 1) * points / 4.0
    matrix[points - 1, points - 1] = (points - 1) * points / 4.0
    return matrix


DERIV = gll_derivative().astype(np.float32)
ABS_DERIV = np.abs(DERIV)
ROW_TOTAL = ABS_DERIV.sum(axis=1)
EYE8 = np.eye(8, dtype=np.float32)


def cycle_matrix(small):
    return np.kron(np.eye(2, dtype=np.float32), np.kron(small, EYE8))


def radial_matrix(small):
    return np.kron(np.eye(16, dtype=np.float32), small)


def split_const(matrix):
    high = matrix.astype(ml_dtypes.bfloat16)
    low = (matrix - high.astype(np.float32)).astype(ml_dtypes.bfloat16)
    return high, low


GRAD = np.concatenate([cycle_matrix(DERIV.T), radial_matrix(DERIV.T)], axis=1)
DIVER = np.concatenate([cycle_matrix(DERIV), radial_matrix(DERIV)], axis=0)
GRAD_HL = np.stack(split_const(GRAD))
DIVER_HL = np.stack(split_const(DIVER))
ABS_HL = np.stack(split_const(np.abs(DIVER)))


def split(value):
    high = value.astype(jnp.bfloat16)
    return high, (value - high.astype(jnp.float32)).astype(jnp.bfloat16)


def dot(left, right):
    return lax.dot_general(
        left, right, (((1,), (0,)), ((), ())), preferred_element_type=jnp.float32
    )


def dot_split(value, matrix_ref):
    high, low = split(value)
    return dot(high, matrix_ref[0]) + (dot(low, matrix_ref[0]) + dot(high, matrix_ref[1]))


def lane_iota(rows):
    return lax.broadcasted_iota(jnp.int32, (rows, LANES), 1)


def row_iota(rows):
    return lax.broadcasted_iota(jnp.int32, (rows, LANES), 0)


def roll(value, shift, axis):
    size = value.shape[axis]
    return pltpu.roll(value, shift % size, axis)


def along_nodes(values, small):
    out = []
    for m in range(NODES):
        total = None
        for i in range(NODES):
            scale = float(small[m][i])
            if scale != 0.0:
                term = values[i] * scale
                total = term if total is None else total + term
        out.append(total)
    return out


def own_assembly(u):
    lane = lane_iota(ROWS)
    k = lane % 8
    er = row_iota(ROWS) % HALF
    up = roll(roll(u, -1, 0), 7, 1)
    down = roll(roll(u, 1, 0), -7, 1)
    u = (
        u
        + jnp.where((k == 7) & (er < HALF - 1), up, 0.0)
        + jnp.where((k == 0) & (er > 0), down, 0.0)
    )
    top, bottom = u[:HALF], u[HALF:]
    lane = lane_iota(HALF)
    j = (lane // 8) % 8
    block = lane // 64
    new_top = (
        top
        + jnp.where(j == 7, roll(bottom, 56, 1), 0.0)
        + jnp.where((j == 0) & (block == 1), roll(bottom, 8, 1), 0.0)
    )
    new_bottom = (
        bottom
        + jnp.where(j == 0, roll(top, -56, 1), 0.0)
        + jnp.where((j == 7) & (block == 0), roll(top, -8, 1), 0.0)
    )
    return new_top, new_bottom


def ends(value):
    lane = lane_iota(HALF)
    return jnp.where(lane < 8, value[:HALF], jnp.where(lane >= 120, value[HALF:], 0.0))


def store_assembled(kv_ref, near_ref, far_ref, pack_ref, even, source, field=0):
    pack = None
    for i in range(NODES):
        top, bottom = own_assembly(source(i))
        value = jnp.concatenate([top, bottom], axis=0)
        kv_ref[i] = value
        if i == 0:
            first = value
        last = value
        piece = ends(value)
        if i:
            piece = roll(piece, 16 * i, 1)
        pack = piece if pack is None else pack + piece
    near_ref[field] = jnp.where(even, last, first)
    far_ref[field] = jnp.where(even, first, last)
    pack_ref[field] = pack


def is_even(place_ref):
    return lax.broadcast_in_dim(place_ref[0], (ROWS, LANES), ()) == 0


def pack_kernel(place_ref, pack_in, near_ref, far_ref, pack_ref):
    even = is_even(place_ref)
    for field in range(pack_ref.shape[0]):
        near, far = near_ref[field], far_ref[field]
        first = ends(jnp.where(even, far, near))
        last = ends(jnp.where(even, near, far))
        pack_ref[field] = pack_in[field] + first + roll(last, 16 * (NODES - 1), 1)


def completed(place_ref, kv, halo, field=0):
    near_ref, far_ref, packs_ref = halo
    even = is_even(place_ref)
    near, far = near_ref[field], far_ref[field]
    count = packs_ref.shape[0]
    here = place_ref[1]
    left = packs_ref[lax.rem(here + count - 1, count), field]
    right = packs_ref[lax.rem(here + 1, count), field]
    lane = lane_iota(HALF)
    side = jnp.where(lane % 16 < 8, roll(left, 8, 1), roll(right, -8, 1))

    def value(i):
        piece = roll(side, -16 * i, 1) if i else side
        u = kv[i] + jnp.concatenate(
            [jnp.where(lane < 8, piece, 0.0), jnp.where(lane >= 120, piece, 0.0)], axis=0
        )
        if i == 0:
            u = u + jnp.where(even, far, near)
        if i == NODES - 1:
            u = u + jnp.where(even, near, far)
        return u

    return value


def apply_element(v_ref, metric_ref, grad_ref, diver_ref, flux_ref, out_ref):
    side = dot_split(v_ref[...].reshape(NODES * ROWS, LANES), grad_ref)
    flux_ref[0] = side[:, :LANES]
    flux_ref[1] = side[:, LANES:]
    for chunk in range(ROWS // 8):
        rows = pl.ds(chunk * 8, 8)
        values = [v_ref[i, rows] for i in range(NODES)]
        grad_z = along_nodes(values, DERIV)
        flux_z = []
        for i in range(NODES):
            at = pl.ds(i * ROWS + chunk * 8, 8)
            g_z, g_a, g_r = grad_z[i], flux_ref[0, at], flux_ref[1, at]
            m = [metric_ref[c, i, rows] for c in range(6)]
            flux_z.append(m[0] * g_z + m[3] * g_a + m[4] * g_r)
            flux_ref[0, at] = m[3] * g_z + m[1] * g_a + m[5] * g_r
            flux_ref[1, at] = m[4] * g_z + m[5] * g_a + m[2] * g_r
        part_z = along_nodes(flux_z, DERIV.T)
        for i in range(NODES):
            out_ref[i, rows] = part_z[i] + metric_ref[6, i, rows] * values[i]
    flux = jnp.concatenate([flux_ref[0], flux_ref[1]], axis=1)
    out_ref[...] += dot_split(flux, diver_ref).reshape(FIELD)


def weight_plane():
    lane, row = lane_iota(ROWS), row_iota(ROWS)
    j, k, er = (lane // 8) % 8, lane % 8, row % HALF
    w_a = jnp.where((j == 0) | (j == 7), 0.5, 1.0)
    shared = ((k == 0) & (er > 0)) | ((k == 7) & (er < HALF - 1))
    return w_a * jnp.where(shared, 0.5, 1.0)


def node_weight(i):
    return 0.5 if i in (0, NODES - 1) else 1.0


def sum_row(sums):
    lane = lane_iota(1)
    row = jnp.zeros((1, LANES), jnp.float32)
    for d, value in enumerate(sums):
        row = jnp.where(lane == d, jnp.sum(value), row)
    return row


SIGMA = ((INTERVAL_HIGH + INTERVAL_LOW) / 2.0) / ((INTERVAL_HIGH - INTERVAL_LOW) / 2.0)
CENTER = (INTERVAL_HIGH + INTERVAL_LOW) / 2.0
HALF_WIDTH = (INTERVAL_HIGH - INTERVAL_LOW) / 2.0
RHO0 = 1.0 / SIGMA
RHO1 = 1.0 / (2.0 * SIGMA - RHO0)
RHO2 = 1.0 / (2.0 * SIGMA - RHO1)


def place_kernel(
    place_ref, order_ref, load_ref, geom_ref, abs_ref,
    metric_ref, load_kv, bound_kv, near_ref, far_ref, pack_ref, flux_ref, work_ref,
):
    pick = jnp.where(
        lax.broadcasted_iota(jnp.int32, (64, 64), 0) == order_ref[...], 1.0, 0.0
    ).astype(jnp.bfloat16)
    low = lane_iota(ROWS) < 64

    def spread(placed, store):
        for b in range(4):
            piece = placed[:, b * LANES : (b + 1) * LANES]
            first, second = piece[:ROWS], piece[ROWS:]
            store(2 * b, jnp.where(low, first, roll(second, 64, 1)))
            store(2 * b + 1, jnp.where(low, roll(first, 64, 1), second))

    for c in range(7):
        def store_metric(i, value, c=c):
            metric_ref[c, i] = value

        spread(dot(pick, geom_ref[c]), store_metric)

    load = load_ref[...]
    high, rest = split(load)
    middle = (load - high.astype(jnp.float32) - rest.astype(jnp.float32)).astype(jnp.bfloat16)

    def store_load(i, value):
        work_ref[i] = value

    spread(dot(pick, high) + (dot(pick, rest) + dot(pick, middle)), store_load)
    store_assembled(load_kv, near_ref, far_ref, pack_ref, is_even(place_ref), lambda i: work_ref[i], 0)

    lane = lane_iota(8)
    q_a = jnp.zeros((8, LANES), jnp.float32)
    q_r = jnp.zeros((8, LANES), jnp.float32)
    for m in range(NODES):
        q_a = jnp.where((lane // 8) % 8 == m, float(ROW_TOTAL[m]), q_a)
        q_r = jnp.where(lane % 8 == m, float(ROW_TOTAL[m]), q_r)
    for chunk in range(ROWS // 8):
        rows = pl.ds(chunk * 8, 8)
        h_z = []
        for i in range(NODES):
            at = pl.ds(i * ROWS + chunk * 8, 8)
            q_z = float(ROW_TOTAL[i])
            g = [jnp.abs(metric_ref[c, i, rows]) for c in range(6)]
            h_z.append(g[0] * q_z + g[3] * q_a + g[4] * q_r)
            flux_ref[0, at] = g[3] * q_z + g[1] * q_a + g[5] * q_r
            flux_ref[1, at] = g[4] * q_z + g[5] * q_a + g[2] * q_r
        part_z = along_nodes(h_z, ABS_DERIV.T)
        for i in range(NODES):
            work_ref[i, rows] = part_z[i] + jnp.abs(metric_ref[6, i, rows])
    flux = jnp.concatenate([flux_ref[0], flux_ref[1]], axis=1)
    work_ref[...] += dot_split(flux, abs_ref).reshape(FIELD)
    store_assembled(bound_kv, near_ref, far_ref, pack_ref, is_even(place_ref), lambda i: work_ref[i], 1)


def start_kernel(
    place_ref, load_kv, bound_kv, h0, h1, h2,
    metric_ref, grad_ref, diver_ref,
    residual_ref, inverse_ref, update_ref, kv_ref, near_ref, far_ref, pack_ref, flux_ref, work_ref,
):
    residual = completed(place_ref, load_kv, (h0, h1, h2), 0)
    bound = completed(place_ref, bound_kv, (h0, h1, h2), 1)
    for i in range(NODES):
        r = residual(i)
        inverse = 1.0 / bound(i)
        residual_ref[i] = r
        inverse_ref[i] = inverse
        update_ref[i] = r * inverse * (1.0 / CENTER)
    apply_element(update_ref, metric_ref, grad_ref, diver_ref, flux_ref, work_ref)
    store_assembled(kv_ref, near_ref, far_ref, pack_ref, is_even(place_ref), lambda i: work_ref[i])


def second_kernel(
    place_ref, kv_in, h0, h1, h2, source_ref, inverse_ref, update_in,
    metric_ref, grad_ref, diver_ref,
    update_ref, result_ref, kv_ref, near_ref, far_ref, pack_ref, flux_ref, work_ref,
):
    image = completed(place_ref, kv_in, (h0, h1, h2))
    for i in range(NODES):
        old = update_in[i]
        update = (RHO1 * RHO0) * old + (2.0 * RHO1 / HALF_WIDTH) * inverse_ref[i] * (
            source_ref[i] - image(i)
        )
        update_ref[i] = update
        result_ref[i] = old + update
    apply_element(result_ref, metric_ref, grad_ref, diver_ref, flux_ref, work_ref)
    store_assembled(kv_ref, near_ref, far_ref, pack_ref, is_even(place_ref), lambda i: work_ref[i])


def third_kernel(
    place_ref, kv_in, h0, h1, h2, source_ref, inverse_ref, update_in, result_in,
    metric_ref, grad_ref, diver_ref,
    result_ref, kv_ref, near_ref, far_ref, pack_ref, sums_ref, flux_ref, work_ref,
):
    image = completed(place_ref, kv_in, (h0, h1, h2))
    plane = weight_plane()
    rz = jnp.zeros((ROWS, LANES), jnp.float32)
    for i in range(NODES):
        source = source_ref[i]
        update = (RHO2 * RHO1) * update_in[i] + (2.0 * RHO2 / HALF_WIDTH) * inverse_ref[i] * (
            source - image(i)
        )
        result = result_in[i] + update
        result_ref[i] = result
        rz = rz + source * result * node_weight(i)
    apply_element(result_ref, metric_ref, grad_ref, diver_ref, flux_ref, work_ref)
    energy = jnp.zeros((ROWS, LANES), jnp.float32)
    for i in range(NODES):
        energy = energy + result_ref[i] * work_ref[i]
    sums_ref[...] = sum_row([rz * plane, energy])
    store_assembled(kv_ref, near_ref, far_ref, pack_ref, is_even(place_ref), lambda i: work_ref[i])


def fourth_kernel(
    place_ref, kv_in, h0, h1, h2, inverse_ref, metric_ref, grad_ref, diver_ref,
    image_ref, update_ref, kv_ref, near_ref, far_ref, pack_ref, flux_ref, work_ref,
):
    image = completed(place_ref, kv_in, (h0, h1, h2))
    for i in range(NODES):
        value = image(i)
        image_ref[i] = value
        update_ref[i] = value * inverse_ref[i] * (1.0 / CENTER)
    apply_element(update_ref, metric_ref, grad_ref, diver_ref, flux_ref, work_ref)
    store_assembled(kv_ref, near_ref, far_ref, pack_ref, is_even(place_ref), lambda i: work_ref[i])


def sixth_kernel(
    place_ref, kv_in, h0, h1, h2, source_ref, inverse_ref, update_in, result_in,
    residual_ref, first_ref, early_ref, metric_ref, grad_ref, diver_ref,
    result_ref, kv_ref, near_ref, far_ref, pack_ref, sums_ref, flux_ref, work_ref,
):
    image = completed(place_ref, kv_in, (h0, h1, h2))
    plane = weight_plane()
    r_y = jnp.zeros((ROWS, LANES), jnp.float32)
    w_y = jnp.zeros((ROWS, LANES), jnp.float32)
    for i in range(NODES):
        source = source_ref[i]
        update = (RHO2 * RHO1) * update_in[i] + (2.0 * RHO2 / HALF_WIDTH) * inverse_ref[i] * (
            source - image(i)
        )
        result = result_in[i] + update
        result_ref[i] = result
        r_y = r_y + residual_ref[i] * result * node_weight(i)
        w_y = w_y + source * result * node_weight(i)
    apply_element(result_ref, metric_ref, grad_ref, diver_ref, flux_ref, work_ref)
    z_ky = jnp.zeros((ROWS, LANES), jnp.float32)
    y_ky = jnp.zeros((ROWS, LANES), jnp.float32)
    for i in range(NODES):
        z_ky = z_ky + first_ref[i] * work_ref[i]
        y_ky = y_ky + result_ref[i] * work_ref[i]
    zero = jnp.zeros((1, LANES), jnp.float32)
    late = sum_row([zero, zero, r_y * plane, w_y * plane, z_ky, y_ky])
    sums_ref[...] = jnp.broadcast_to(early_ref[...] + late, sums_ref.shape)
    store_assembled(kv_ref, near_ref, far_ref, pack_ref, is_even(place_ref), lambda i: work_ref[i])


def last_kernel(
    place_ref, kv_in, h0, h1, h2, sums_ref, order_ref,
    residual_ref, first_ref, image_ref, second_ref,
    solution_ref, residual_out, spread_ref,
):
    sums = jnp.sum(sums_ref[...], axis=0, keepdims=True)
    lane = lane_iota(1)

    def total(d):
        return jnp.sum(jnp.where(lane == d, sums, 0.0), axis=1, keepdims=True)

    rz0, zw, ry, wy, zq, yq = (total(d) for d in range(6))
    alpha0 = rz0 / zw
    rz1 = rz0 - alpha0 * (zw + ry) + alpha0 * alpha0 * wy
    beta = rz1 / rz0
    share = 1.0 + beta
    energy = share * share * zw - 2.0 * share * alpha0 * zq + alpha0 * alpha0 * yq
    alpha1 = rz1 / energy
    first_scale = alpha0 + alpha1 * share
    second_scale = alpha1 * alpha0
    image = completed(place_ref, kv_in, (h0, h1, h2))
    low = lane_iota(ROWS) < 64
    for b in range(4):
        pair = []
        for i in (2 * b, 2 * b + 1):
            x = first_scale * first_ref[i] - second_scale * second_ref[i]
            r = residual_ref[i] - first_scale * image_ref[i] + second_scale * image(i)
            pair.append((x, r))
        for f in range(2):
            even, odd = pair[0][f], pair[1][f]
            lanes = pl.ds(b * LANES, LANES)
            spread_ref[f, :ROWS, lanes] = jnp.where(low, even, roll(odd, 64, 1))
            spread_ref[f, ROWS:, lanes] = jnp.where(low, roll(even, 64, 1), odd)
    pick = jnp.where(
        lax.broadcasted_iota(jnp.int32, (64, 64), 1) == order_ref[...], 1.0, 0.0
    ).astype(jnp.bfloat16)
    for f, out in ((0, solution_ref), (1, residual_out)):
        value = spread_ref[f]
        high, middle = split(value)
        rest = (value - high.astype(jnp.float32) - middle.astype(jnp.float32)).astype(jnp.bfloat16)
        out[...] = dot(pick, high) + (dot(pick, middle) + dot(pick, rest))


VMEM_LIMIT = 24 * 1024 * 1024
F32 = jnp.float32


def call(kernel, place, outs, scratch, *operands):
    vmem = pl.BlockSpec(memory_space=pltpu.VMEM)
    return pl.pallas_call(
        kernel,
        out_shape=[jax.ShapeDtypeStruct(s, F32) for s in outs],
        in_specs=[pl.BlockSpec(memory_space=pltpu.SMEM)] + [vmem] * len(operands),
        out_specs=[vmem] * len(outs),
        scratch_shapes=[pltpu.VMEM(s, F32) for s in scratch],
        compiler_params=pltpu.CompilerParams(vmem_limit_bytes=VMEM_LIMIT),
    )(place, *operands)


FLUX = (2, NODES * ROWS, LANES)


def faces(fields=1):
    return [(fields, ROWS, LANES), (fields, ROWS, LANES), (fields, HALF, LANES)]


def exchange(place, near, far, pack):
    count = lax.axis_size(WIDE)
    near = lax.ppermute(near, WIDE, [(w, w ^ 1) for w in range(count)])
    far = lax.ppermute(
        far, WIDE, [(w, (w + 1 if w % 2 else w - 1) % count) for w in range(count)]
    )
    (pack,) = call(pack_kernel, place, [pack.shape], [], pack, near, far)
    return near, far, lax.all_gather(pack, "narrow")


def local(load, geom, element_order):
    place = jnp.stack([lax.axis_index(WIDE) % 2, lax.axis_index("narrow")]).astype(jnp.int32)
    order = element_order.reshape(1, 64)
    grad = jnp.asarray(GRAD_HL)
    diver = jnp.asarray(DIVER_HL)
    metric, load_kv, bound_kv, *face = call(
        place_kernel, place,
        [(7,) + FIELD, FIELD, FIELD] + faces(2),
        [FLUX, FIELD],
        order, load, geom, jnp.asarray(ABS_HL),
    )
    halo = exchange(place, *face)
    residual, inverse, update, kv, *face = call(
        start_kernel, place,
        [FIELD, FIELD, FIELD, FIELD] + faces(),
        [FLUX, FIELD],
        load_kv, bound_kv, *halo, metric, grad, diver,
    )
    halo = exchange(place, *face)
    update, result, kv, *face = call(
        second_kernel, place,
        [FIELD, FIELD, FIELD] + faces(),
        [FLUX, FIELD],
        kv, *halo, residual, inverse, update, metric, grad, diver,
    )
    halo = exchange(place, *face)
    first, kv, *face, early = call(
        third_kernel, place,
        [FIELD, FIELD] + faces() + [(1, LANES)],
        [FLUX, FIELD],
        kv, *halo, residual, inverse, update, result, metric, grad, diver,
    )
    halo = exchange(place, *face)
    image, update, kv, *face = call(
        fourth_kernel, place,
        [FIELD, FIELD, FIELD] + faces(),
        [FLUX, FIELD],
        kv, *halo, inverse, metric, grad, diver,
    )
    halo = exchange(place, *face)
    update, result, kv, *face = call(
        second_kernel, place,
        [FIELD, FIELD, FIELD] + faces(),
        [FLUX, FIELD],
        kv, *halo, image, inverse, update, metric, grad, diver,
    )
    halo = exchange(place, *face)
    second, kv, *face, sums = call(
        sixth_kernel, place,
        [FIELD, FIELD] + faces() + [(lax.axis_size(REST), LANES)],
        [FLUX, FIELD],
        kv, *halo, image, inverse, update, result,
        residual, first, early, metric, grad, diver,
    )
    halo = exchange(place, *face)
    sums = lax.all_to_all(sums, REST, 0, 0)
    sums = jnp.broadcast_to(
        jnp.sum(sums, axis=0, keepdims=True), (lax.axis_size("ring"), LANES)
    )
    sums = lax.all_to_all(sums, "ring", 0, 0)
    return tuple(
        call(
            last_kernel, place,
            [(64, 512), (64, 512)],
            [(2, 64, 512)],
            kv, *halo, sums, element_order.reshape(64, 1), residual, first, image, second,
        )
    )


def solution(mesh):
    wide, narrow = mesh.devices.shape
    ring = 12 if wide % 12 == 0 else 2
    fine = jax.sharding.Mesh(
        mesh.devices.reshape(wide // ring, ring, narrow), ("outer", "ring", "narrow")
    )
    rows = ("outer", "ring", "narrow")
    return jax.shard_map(
        local,
        mesh=fine,
        in_specs=(P(rows, None), P(None, rows, None), P(WIDE, "narrow", None)),
        out_specs=(P(rows, None), P(rows, None)),
        check_vma=False,
    )
```

time: 619 us -> 177 us (0.29)
  blocking collectives: 328 us -> 42.7 us
  local copies, waits for them, and re-layouts: 87.9 us -> 4.19 us
  other arithmetic: 29.4 us -> 0.16 us
  starting transfers between devices: 131 us -> 102 us
  Pallas kernels: 0 us -> 17.2 us
  matrix products: 12.8 us -> 0 us
  waiting for transfers between devices: 18.8 us -> 9.21 us
    psum x3 -> x0, blocking collectives: 328 us -> none  [the longest x2 219 us: local(): precond_norm = lax.psum(inner(grid_residual, result), ('wide', 'narrow'))]
    all_gather x0 -> x7, blocking collectives: none -> 42.7 us  [exchange(): return (near, far, lax.all_gather(pack, 'narrow'))]
    ppermute x28 -> x14, starting transfers between devices: 131 us -> 93.3 us  [the longest x7 76.8 us: exchange(): lax.ppermute(far, WIDE, [(w, (w + 1 if w % 2 else w - 1) % count) for w i...]
    convert_element_type x14 -> x0, local copies, waits for them, and re-layouts: 20.2 us -> none  [the longest x2 2.91 us: element_apply(): g_za = metric[3].astype(jnp.float32)]
    slice x17 -> x0, local copies, waits for them, and re-layouts: 20 us -> none  [the longest x3 6.73 us: element_bound(): h_r = g_abs[4] * q_z + g_abs[5] * q_a + g_abs[2] * q_r]
    squeeze x11 -> x0, local copies, waits for them, and re-layouts: 19.2 us -> none  [the longest x4 9.94 us: operator(): assemble(element_apply(field, metric, derivative, radial_matrix)[None])[0]]
    pallas_call x0 -> x15, Pallas kernels: none -> 17.2 us  [call(): pl.pallas_call(kernel, out_shape=[jax.ShapeDtypeStruct(s, F32) for s in o...]
    dot_general x39 -> x0, matrix products: 12.8 us -> none  [the longest x13 4.78 us: radial_apply(): jnp.dot(flat, radial_matrix, precision=lax.Precision.HIGHEST, preferred_e...]
  transfers between devices with their start and end apart: 28 -> 16, of which waited for: 11 -> 7; matrix products, arithmetic and copies ran while one was open for 7% -> 0% of each run, Pallas kernels for 0% -> 0%
where the time goes in v1:
time: 177 us; the launch traced here: 176 us
  starting transfers between devices  102 us (58%)
  blocking collectives  42.7 us (24%)
  Pallas kernels  17.2 us (10%)
  waiting for transfers between devices  9.21 us (5%)
  local copies, waits for them, and re-layouts  4.19 us (2%)
    ppermute x7, starting transfers between devices, exchange(): lax.ppermute(far, WIDE, [(w, (w + 1 if w % 2 else w - 1) % count) for w i...  76.8 us
    all_gather x7, blocking collectives, exchange(): return (near, far, lax.all_gather(pack, 'narrow'))  42.7 us
    pallas_call x15, Pallas kernels, call(): pl.pallas_call(kernel, out_shape=[jax.ShapeDtypeStruct(s, F32) for s in o...  17.2 us
    ppermute x7, starting transfers between devices, exchange(): near = lax.ppermute(near, WIDE, [(w, w ^ 1) for w in range(count)])  16.4 us
    ppermute x7, waiting for transfers between devices, exchange(): lax.ppermute(far, WIDE, [(w, (w + 1 if w % 2 else w - 1) % count) for w i...  6.79 us
    all_to_all x1, starting transfers between devices, local(): sums = lax.all_to_all(sums, REST, 0, 0)  4.92 us
  transfers between devices with their start and end apart: 16, of which 7 were waited for; matrix products, arithmetic and copies ran while one was open for 0% of the time, Pallas kernels for 0%

profile of v1, /device:TPU:1, one launch (start us, length us, event | category | flops | bytes accessed | tf_op | source)
XLA Modules:
  0.0 176.0 jit_solution(3271620758152487606)
XLA Ops:
  0.7 0.7 copy-done.5
  1.4 1.0 copy-done.2
  2.4 0.9 copy-done.3
  3.3 0.9 copy-done.4
  4.2 1.5 shard_map.77
  5.7 5.0 %collective-permute-start = (f32[2,32,128]{2,1,0:T(8,128)S(1)}, f32[2,32,128]{2,1,0:T(8,128)S(1)}, u32[]{:S(2)}, u32[]{:S(2)}) collective-permute-start(f32[2,32,128]{2,1,0:T(8,128)S(1)} %get-tuple-element.47), channel_id=1, source_target_pairs={{0,4},{4,0},{8,12},{12,8},{16,20},{20,16},{24,28},{28,24},{32,36},... | collective-permute-start | bytes 98312 | tf_op jit(solution)/shard_map/ppermute | solution.py:491
  10.7 17.9 %collective-permute-start.1 = (f32[2,32,128]{2,1,0:T(8,128)S(1)}, f32[2,32,128]{2,1,0:T(8,128)S(1)}, u32[]{:S(2)}, u32[]{:S(2)}) collective-permute-start(f32[2,32,128]{2,1,0:T(8,128)S(1)} %get-tuple-element.48), channel_id=1, source_target_pairs={{0,764},{4,8},{8,4},{12,16},{16,12},{20,24},{24,20},{28,32},{32,28... | collective-permute-start | bytes 98312 | tf_op jit(solution)/shard_map/ppermute | solution.py:492
  28.5 1.3 collective-permute-done.1.far_ref.h1
  29.8 0.6 shard_map.78
  30.4 6.9 %all-gather = f32[8,16,128]{2,1,0:T(8,128)S(1)} all-gather(f32[2,16,128]{2,1,0:T(8,128)S(1)} %shard_map.78), channel_id=2, replica_groups=mesh['outer'=16,'ring'=12,'narrow'=4] {'narrow'}, dimensions={0}, use_global_device_ids=true | all-gather | bytes 81920 | tf_op jit(solution)/shard_map/all_gather | solution.py:496
  37.3 1.5 shard_map.79
  38.8 1.9 %collective-permute-start.2 = (f32[1,32,128]{2,1,0:T(8,128)S(1)}, f32[1,32,128]{2,1,0:T(8,128)S(1)}, u32[]{:S(2)}, u32[]{:S(2)}) collective-permute-start(f32[1,32,128]{2,1,0:T(8,128)S(1)} %get-tuple-element.52), channel_id=1, source_target_pairs={{0,4},{4,0},{8,12},{12,8},{16,20},{20,16},{24,28},{28,24},{32,36},... | collective-permute-start | bytes 49160 | tf_op jit(solution)/shard_map/ppermute | solution.py:491
  40.8 9.4 %collective-permute-start.3 = (f32[1,32,128]{2,1,0:T(8,128)S(1)}, f32[1,32,128]{2,1,0:T(8,128)S(1)}, u32[]{:S(2)}, u32[]{:S(2)}) collective-permute-start(f32[1,32,128]{2,1,0:T(8,128)S(1)} %get-tuple-element.53), channel_id=1, source_target_pairs={{0,764},{4,8},{8,4},{12,16},{16,12},{20,24},{24,20},{28,32},{32,28... | collective-permute-start | bytes 49160 | tf_op jit(solution)/shard_map/ppermute | solution.py:492
  50.1 1.1 collective-permute-done.3.far_ref.h1
  51.2 0.6 shard_map.80
  51.9 6.0 %all-gather.1 = f32[4,16,128]{2,1,0:T(8,128)S(1)} all-gather(f32[1,16,128]{2,1,0:T(8,128)S(1)} %shard_map.80), channel_id=3, replica_groups=mesh['outer'=16,'ring'=12,'narrow'=4] {'narrow'}, dimensions={0}, use_global_device_ids=true | all-gather | bytes 40960 | tf_op jit(solution)/shard_map/all_gather | solution.py:496
  57.9 1.5 shard_map.81
  59.4 1.9 %collective-permute-start.4 = (f32[1,32,128]{2,1,0:T(8,128)S(1)}, f32[1,32,128]{2,1,0:T(8,128)S(1)}, u32[]{:S(2)}, u32[]{:S(2)}) collective-permute-start(f32[1,32,128]{2,1,0:T(8,128)S(1)} %get-tuple-element.59), channel_id=1, source_target_pairs={{0,4},{4,0},{8,12},{12,8},{16,20},{20,16},{24,28},{28,24},{32,36},... | collective-permute-start | bytes 49160 | tf_op jit(solution)/shard_map/ppermute | solution.py:491
  61.3 9.4 %collective-permute-start.5 = (f32[1,32,128]{2,1,0:T(8,128)S(1)}, f32[1,32,128]{2,1,0:T(8,128)S(1)}, u32[]{:S(2)}, u32[]{:S(2)}) collective-permute-start(f32[1,32,128]{2,1,0:T(8,128)S(1)} %get-tuple-element.60), channel_id=1, source_target_pairs={{0,764},{4,8},{8,4},{12,16},{16,12},{20,24},{24,20},{28,32},{32,28... | collective-permute-start | bytes 49160 | tf_op jit(solution)/shard_map/ppermute | solution.py:492
  70.7 1.1 collective-permute-done.5.far_ref.h1
  71.8 0.6 shard_map.82
  72.4 6.0 %all-gather.2 = f32[4,16,128]{2,1,0:T(8,128)S(1)} all-gather(f32[1,16,128]{2,1,0:T(8,128)S(1)} %shard_map.82), channel_id=4, replica_groups=mesh['outer'=16,'ring'=12,'narrow'=4] {'narrow'}, dimensions={0}, use_global_device_ids=true | all-gather | bytes 40960 | tf_op jit(solution)/shard_map/all_gather | solution.py:496
  78.5 1.6 shard_map.83
  80.0 1.9 %collective-permute-start.6 = (f32[1,32,128]{2,1,0:T(8,128)S(1)}, f32[1,32,128]{2,1,0:T(8,128)S(1)}, u32[]{:S(2)}, u32[]{:S(2)}) collective-permute-start(f32[1,32,128]{2,1,0:T(8,128)S(1)} %get-tuple-element.65), channel_id=1, source_target_pairs={{0,4},{4,0},{8,12},{12,8},{16,20},{20,16},{24,28},{28,24},{32,36},... | collective-permute-start | bytes 49160 | tf_op jit(solution)/shard_map/ppermute | solution.py:491
  81.9 9.4 %collective-permute-start.7 = (f32[1,32,128]{2,1,0:T(8,128)S(1)}, f32[1,32,128]{2,1,0:T(8,128)S(1)}, u32[]{:S(2)}, u32[]{:S(2)}) collective-permute-start(f32[1,32,128]{2,1,0:T(8,128)S(1)} %get-tuple-element.66), channel_id=1, source_target_pairs={{0,764},{4,8},{8,4},{12,16},{16,12},{20,24},{24,20},{28,32},{32,28... | collective-permute-start | bytes 49160 | tf_op jit(solution)/shard_map/ppermute | solution.py:492
  91.3 1.1 collective-permute-done.7.far_ref.h1
  92.4 0.6 shard_map.84
  93.0 6.1 %all-gather.3 = f32[4,16,128]{2,1,0:T(8,128)S(1)} all-gather(f32[1,16,128]{2,1,0:T(8,128)S(1)} %shard_map.84), channel_id=5, replica_groups=mesh['outer'=16,'ring'=12,'narrow'=4] {'narrow'}, dimensions={0}, use_global_device_ids=true | all-gather | bytes 40960 | tf_op jit(solution)/shard_map/all_gather | solution.py:496
  99.1 1.5 shard_map.85
  100.6 1.9 %collective-permute-start.8 = (f32[1,32,128]{2,1,0:T(8,128)S(1)}, f32[1,32,128]{2,1,0:T(8,128)S(1)}, u32[]{:S(2)}, u32[]{:S(2)}) collective-permute-start(f32[1,32,128]{2,1,0:T(8,128)S(1)} %get-tuple-element.69), channel_id=1, source_target_pairs={{0,4},{4,0},{8,12},{12,8},{16,20},{20,16},{24,28},{28,24},{32,36},... | collective-permute-start | bytes 49160 | tf_op jit(solution)/shard_map/ppermute | solution.py:491
  102.5 9.4 %collective-permute-start.9 = (f32[1,32,128]{2,1,0:T(8,128)S(1)}, f32[1,32,128]{2,1,0:T(8,128)S(1)}, u32[]{:S(2)}, u32[]{:S(2)}) collective-permute-start(f32[1,32,128]{2,1,0:T(8,128)S(1)} %get-tuple-element.70), channel_id=1, source_target_pairs={{0,764},{4,8},{8,4},{12,16},{16,12},{20,24},{24,20},{28,32},{32,28... | collective-permute-start | bytes 49160 | tf_op jit(solution)/shard_map/ppermute | solution.py:492
  111.9 1.1 collective-permute-done.9.far_ref.h1
  113.6 6.0 %all-gather.4 = f32[4,16,128]{2,1,0:T(8,128)S(1)} all-gather(f32[1,16,128]{2,1,0:T(8,128)S(1)} %shard_map.86), channel_id=6, replica_groups=mesh['outer'=16,'ring'=12,'narrow'=4] {'narrow'}, dimensions={0}, use_global_device_ids=true | all-gather | bytes 40960 | tf_op jit(solution)/shard_map/all_gather | solution.py:496
  119.7 1.5 shard_map.87
  121.2 1.9 %collective-permute-start.10 = (f32[1,32,128]{2,1,0:T(8,128)S(1)}, f32[1,32,128]{2,1,0:T(8,128)S(1)}, u32[]{:S(2)}, u32[]{:S(2)}) collective-permute-start(f32[1,32,128]{2,1,0:T(8,128)S(1)} %get-tuple-element.75), channel_id=1, source_target_pairs={{0,4},{4,0},{8,12},{12,8},{16,20},{20,16},{24,28},{28,24},{32,36},... | collective-permute-start | bytes 49160 | tf_op jit(solution)/shard_map/ppermute | solution.py:491
  123.1 9.4 %collective-permute-start.11 = (f32[1,32,128]{2,1,0:T(8,128)S(1)}, f32[1,32,128]{2,1,0:T(8,128)S(1)}, u32[]{:S(2)}, u32[]{:S(2)}) collective-permute-start(f32[1,32,128]{2,1,0:T(8,128)S(1)} %get-tuple-element.76), channel_id=1, source_target_pairs={{0,764},{4,8},{8,4},{12,16},{16,12},{20,24},{24,20},{28,32},{32,28... | collective-permute-start | bytes 49160 | tf_op jit(solution)/shard_map/ppermute | solution.py:492
  132.5 1.1 collective-permute-done.11.far_ref.h1
  133.6 0.6 shard_map.88
  134.2 6.0 %all-gather.5 = f32[4,16,128]{2,1,0:T(8,128)S(1)} all-gather(f32[1,16,128]{2,1,0:T(8,128)S(1)} %shard_map.88), channel_id=7, replica_groups=mesh['outer'=16,'ring'=12,'narrow'=4] {'narrow'}, dimensions={0}, use_global_device_ids=true | all-gather | bytes 40960 | tf_op jit(solution)/shard_map/all_gather | solution.py:496
  140.2 2.1 %shard_map.89 = (f32[8,32,128]{2,1,0:T(8,128)S(1)}, f32[8,32,128]{2,1,0:T(8,128)S(1)}, f32[1,32,128]{2,1,0:T(8,128)S(1)}, f32[1,32,128]{2,1,0:T(8,128)S(1)}, f32...) custom-call(s32[2]{0:T(128)S(1)} %pad_add_fusion.place_ref, f32[8,32,128]{2,1,0:T(8,128)S(1)} %get-tuple-element.74.kv_in, ...), custom_call_target="tpu_custom_call" | custom-call | tf_op jit(solution)/shard_map/pallas_call | solution.py:472
  142.4 4.9 %all-to-all-start = ((f32[64,1,128]{2,1,0:T(1,128)}), f32[64,1,128]{2,1,0:T(1,128)S(1)}, u32[]{:S(2)}, u32[]{:S(2)}) async-start(f32[64,1,128]{2,1,0:T(1,128)} %bitcast.11), calls=%async_computation | async-start | bytes 65536 | tf_op jit(solution)/shard_map/all_to_all | solution.py:554
  147.3 1.9 %collective-permute-start.12 = (f32[1,32,128]{2,1,0:T(8,128)S(1)}, f32[1,32,128]{2,1,0:T(8,128)S(1)}, u32[]{:S(2)}, u32[]{:S(2)}) collective-permute-start(f32[1,32,128]{2,1,0:T(8,128)S(1)} %get-tuple-element.83), channel_id=1, source_target_pairs={{0,4},{4,0},{8,12},{12,8},{16,20},{20,16},{24,28},{28,24},{32,36},... | collective-permute-start | bytes 49160 | tf_op jit(solution)/shard_map/ppermute | solution.py:491
  149.2 12.2 %collective-permute-start.13 = (f32[1,32,128]{2,1,0:T(8,128)S(1)}, f32[1,32,128]{2,1,0:T(8,128)S(1)}, u32[]{:S(2)}, u32[]{:S(2)}) collective-permute-start(f32[1,32,128]{2,1,0:T(8,128)S(1)} %get-tuple-element.84), channel_id=1, source_target_pairs={{0,764},{4,8},{8,4},{12,16},{16,12},{20,24},{24,20},{28,32},{32,28... | collective-permute-start | bytes 49160 | tf_op jit(solution)/shard_map/ppermute | solution.py:492
  162.1 3.5 %all-to-all-start.1 = ((f32[12,1,128]{2,1,0:T(1,128)}), f32[12,1,128]{2,1,0:T(1,128)S(1)}, u32[]{:S(2)}, u32[]{:S(2)}) async-start(f32[12,1,128]{2,1,0:T(1,128)} %broadcast_in_dim.2), calls=%async_computation.1 | async-start | bytes 12288 | tf_op jit(solution)/shard_map/all_to_all | solution.py:558
  165.7 0.6 shard_map.90
  166.3 5.6 %all-gather.6 = f32[4,16,128]{2,1,0:T(8,128)S(1)} all-gather(f32[1,16,128]{2,1,0:T(8,128)S(1)} %shard_map.90), channel_id=8, replica_groups=mesh['outer'=16,'ring'=12,'narrow'=4] {'narrow'}, dimensions={0}, use_global_device_ids=true | all-gather | bytes 40960 | tf_op jit(solution)/shard_map/all_gather | solution.py:496
  171.9 2.4 %all-to-all-done.1 = f32[12,1,128]{2,1,0:T(1,128)S(1)} async-done(((f32[12,1,128]{2,1,0:T(1,128)}), f32[12,1,128]{2,1,0:T(1,128)S(1)}, u32[]{:S(2)}, u32[]{:S(2)}) %all-to-all-start.1) | async-done | bytes 6176 | tf_op jit(solution)/shard_map/all_to_all | solution.py:558
  174.3 1.7 shard_map.91
  (23 shorter events, 1.5 us)
Async XLA Ops:
  0.7 0.7 copy-start.5
  1.4 1.0 copy-start.2
  2.4 0.9 copy-start.3
  3.3 0.9 copy-start.4
  4.2 33.1 %copy-start.1 = (bf16[2,256,128]{2,1,0:T(8,128)(2,1)S(1)}, bf16[2,256,128]{2,1,0:T(8,128)(2,1)}, u32[]{:S(2)}) copy-start(bf16[2,256,128]{2,1,0:T(8,128)(2,1)} %constant.37.clone.diver_ref) | copy-start | bytes 393220
  5.7 31.6 %copy-start = (bf16[2,128,256]{2,1,0:T(8,128)(2,1)S(1)}, bf16[2,128,256]{2,1,0:T(8,128)(2,1)}, u32[]{:S(2)}) copy-start(bf16[2,128,256]{2,1,0:T(8,128)(2,1)} %constant.36.clone.grad_ref) | copy-start | bytes 393220
  5.7 22.8 %collective-permute-start = (f32[2,32,128]{2,1,0:T(8,128)S(1)}, f32[2,32,128]{2,1,0:T(8,128)S(1)}, u32[]{:S(2)}, u32[]{:S(2)}) collective-permute-start(f32[2,32,128]{2,1,0:T(8,128)S(1)} %get-tuple-element.47), channel_id=1, source_target_pairs={{0,4},{4,0},{8,12},{12,8},{16,20},{20,16},{24,28},{28,24},{32,36},... | collective-permute-start | bytes 98312 | tf_op jit(solution)/shard_map/ppermute | solution.py:491
  10.7 19.1 %collective-permute-start.1 = (f32[2,32,128]{2,1,0:T(8,128)S(1)}, f32[2,32,128]{2,1,0:T(8,128)S(1)}, u32[]{:S(2)}, u32[]{:S(2)}) collective-permute-start(f32[2,32,128]{2,1,0:T(8,128)S(1)} %get-tuple-element.48), channel_id=1, source_target_pairs={{0,764},{4,8},{8,4},{12,16},{16,12},{20,24},{24,20},{28,32},{32,28... | collective-permute-start | bytes 98312 | tf_op jit(solution)/shard_map/ppermute | solution.py:492
  38.8 11.3 %collective-permute-start.2 = (f32[1,32,128]{2,1,0:T(8,128)S(1)}, f32[1,32,128]{2,1,0:T(8,128)S(1)}, u32[]{:S(2)}, u32[]{:S(2)}) collective-permute-start(f32[1,32,128]{2,1,0:T(8,128)S(1)} %get-tuple-element.52), channel_id=1, source_target_pairs={{0,4},{4,0},{8,12},{12,8},{16,20},{20,16},{24,28},{28,24},{32,36},... | collective-permute-start | bytes 49160 | tf_op jit(solution)/shard_map/ppermute | solution.py:491
  40.8 10.5 %collective-permute-start.3 = (f32[1,32,128]{2,1,0:T(8,128)S(1)}, f32[1,32,128]{2,1,0:T(8,128)S(1)}, u32[]{:S(2)}, u32[]{:S(2)}) collective-permute-start(f32[1,32,128]{2,1,0:T(8,128)S(1)} %get-tuple-element.53), channel_id=1, source_target_pairs={{0,764},{4,8},{8,4},{12,16},{16,12},{20,24},{24,20},{28,32},{32,28... | collective-permute-start | bytes 49160 | tf_op jit(solution)/shard_map/ppermute | solution.py:492
  59.4 11.3 %collective-permute-start.4 = (f32[1,32,128]{2,1,0:T(8,128)S(1)}, f32[1,32,128]{2,1,0:T(8,128)S(1)}, u32[]{:S(2)}, u32[]{:S(2)}) collective-permute-start(f32[1,32,128]{2,1,0:T(8,128)S(1)} %get-tuple-element.59), channel_id=1, source_target_pairs={{0,4},{4,0},{8,12},{12,8},{16,20},{20,16},{24,28},{28,24},{32,36},... | collective-permute-start | bytes 49160 | tf_op jit(solution)/shard_map/ppermute | solution.py:491
  61.3 10.5 %collective-permute-start.5 = (f32[1,32,128]{2,1,0:T(8,128)S(1)}, f32[1,32,128]{2,1,0:T(8,128)S(1)}, u32[]{:S(2)}, u32[]{:S(2)}) collective-permute-start(f32[1,32,128]{2,1,0:T(8,128)S(1)} %get-tuple-element.60), channel_id=1, source_target_pairs={{0,764},{4,8},{8,4},{12,16},{16,12},{20,24},{24,20},{28,32},{32,28... | collective-permute-start | bytes 49160 | tf_op jit(solution)/shard_map/ppermute | solution.py:492
  80.0 11.3 %collective-permute-start.6 = (f32[1,32,128]{2,1,0:T(8,128)S(1)}, f32[1,32,128]{2,1,0:T(8,128)S(1)}, u32[]{:S(2)}, u32[]{:S(2)}) collective-permute-start(f32[1,32,128]{2,1,0:T(8,128)S(1)} %get-tuple-element.65), channel_id=1, source_target_pairs={{0,4},{4,0},{8,12},{12,8},{16,20},{20,16},{24,28},{28,24},{32,36},... | collective-permute-start | bytes 49160 | tf_op jit(solution)/shard_map/ppermute | solution.py:491
  81.9 10.5 %collective-permute-start.7 = (f32[1,32,128]{2,1,0:T(8,128)S(1)}, f32[1,32,128]{2,1,0:T(8,128)S(1)}, u32[]{:S(2)}, u32[]{:S(2)}) collective-permute-start(f32[1,32,128]{2,1,0:T(8,128)S(1)} %get-tuple-element.66), channel_id=1, source_target_pairs={{0,764},{4,8},{8,4},{12,16},{16,12},{20,24},{24,20},{28,32},{32,28... | collective-permute-start | bytes 49160 | tf_op jit(solution)/shard_map/ppermute | solution.py:492
  100.6 11.3 %collective-permute-start.8 = (f32[1,32,128]{2,1,0:T(8,128)S(1)}, f32[1,32,128]{2,1,0:T(8,128)S(1)}, u32[]{:S(2)}, u32[]{:S(2)}) collective-permute-start(f32[1,32,128]{2,1,0:T(8,128)S(1)} %get-tuple-element.69), channel_id=1, source_target_pairs={{0,4},{4,0},{8,12},{12,8},{16,20},{20,16},{24,28},{28,24},{32,36},... | collective-permute-start | bytes 49160 | tf_op jit(solution)/shard_map/ppermute | solution.py:491
  102.5 10.5 %collective-permute-start.9 = (f32[1,32,128]{2,1,0:T(8,128)S(1)}, f32[1,32,128]{2,1,0:T(8,128)S(1)}, u32[]{:S(2)}, u32[]{:S(2)}) collective-permute-start(f32[1,32,128]{2,1,0:T(8,128)S(1)} %get-tuple-element.70), channel_id=1, source_target_pairs={{0,764},{4,8},{8,4},{12,16},{16,12},{20,24},{24,20},{28,32},{32,28... | collective-permute-start | bytes 49160 | tf_op jit(solution)/shard_map/ppermute | solution.py:492
  121.2 11.3 %collective-permute-start.10 = (f32[1,32,128]{2,1,0:T(8,128)S(1)}, f32[1,32,128]{2,1,0:T(8,128)S(1)}, u32[]{:S(2)}, u32[]{:S(2)}) collective-permute-start(f32[1,32,128]{2,1,0:T(8,128)S(1)} %get-tuple-element.75), channel_id=1, source_target_pairs={{0,4},{4,0},{8,12},{12,8},{16,20},{20,16},{24,28},{28,24},{32,36},... | collective-permute-start | bytes 49160 | tf_op jit(solution)/shard_map/ppermute | solution.py:491
  123.1 10.5 %collective-permute-start.11 = (f32[1,32,128]{2,1,0:T(8,128)S(1)}, f32[1,32,128]{2,1,0:T(8,128)S(1)}, u32[]{:S(2)}, u32[]{:S(2)}) collective-permute-start(f32[1,32,128]{2,1,0:T(8,128)S(1)} %get-tuple-element.76), channel_id=1, source_target_pairs={{0,764},{4,8},{8,4},{12,16},{16,12},{20,24},{24,20},{28,32},{32,28... | collective-permute-start | bytes 49160 | tf_op jit(solution)/shard_map/ppermute | solution.py:492
  142.4 19.0 %all-to-all-start = ((f32[64,1,128]{2,1,0:T(1,128)}), f32[64,1,128]{2,1,0:T(1,128)S(1)}, u32[]{:S(2)}, u32[]{:S(2)}) async-start(f32[64,1,128]{2,1,0:T(1,128)} %bitcast.11), calls=%async_computation | async-start | bytes 65536 | tf_op jit(solution)/shard_map/all_to_all | solution.py:554
  147.3 18.4 %collective-permute-start.12 = (f32[1,32,128]{2,1,0:T(8,128)S(1)}, f32[1,32,128]{2,1,0:T(8,128)S(1)}, u32[]{:S(2)}, u32[]{:S(2)}) collective-permute-start(f32[1,32,128]{2,1,0:T(8,128)S(1)} %get-tuple-element.83), channel_id=1, source_target_pairs={{0,4},{4,0},{8,12},{12,8},{16,20},{20,16},{24,28},{28,24},{32,36},... | collective-permute-start | bytes 49160 | tf_op jit(solution)/shard_map/ppermute | solution.py:491
  149.2 16.4 %collective-permute-start.13 = (f32[1,32,128]{2,1,0:T(8,128)S(1)}, f32[1,32,128]{2,1,0:T(8,128)S(1)}, u32[]{:S(2)}, u32[]{:S(2)}) collective-permute-start(f32[1,32,128]{2,1,0:T(8,128)S(1)} %get-tuple-element.84), channel_id=1, source_target_pairs={{0,764},{4,8},{8,4},{12,16},{16,12},{20,24},{24,20},{28,32},{32,28... | collective-permute-start | bytes 49160 | tf_op jit(solution)/shard_map/ppermute | solution.py:492
  162.1 12.2 %all-to-all-start.1 = ((f32[12,1,128]{2,1,0:T(1,128)}), f32[12,1,128]{2,1,0:T(1,128)S(1)}, u32[]{:S(2)}, u32[]{:S(2)}) async-start(f32[12,1,128]{2,1,0:T(1,128)} %broadcast_in_dim.2), calls=%async_computation.1 | async-start | bytes 12288 | tf_op jit(solution)/shard_map/all_to_all | solution.py:558

commit v2 on v1

--- a/solution.py
+++ b/solution.py
@@ -178,7 +178,7 @@
     return lax.broadcast_in_dim(place_ref[0], (ROWS, LANES), ()) == 0
 
 
-def pack_kernel(place_ref, pack_in, near_ref, far_ref, pack_ref):
+def pack_kernel(place_ref, pack_in, far_ref, near_ref, pack_ref):
     even = is_even(place_ref)
     for field in range(pack_ref.shape[0]):
         near, far = near_ref[field], far_ref[field]
@@ -188,7 +188,7 @@
 
 
 def completed(place_ref, kv, halo, field=0):
-    near_ref, far_ref, packs_ref = halo
+    far_ref, near_ref, packs_ref = halo
     even = is_even(place_ref)
     near, far = near_ref[field], far_ref[field]
     count = packs_ref.shape[0]
@@ -488,12 +488,12 @@
 
 def exchange(place, near, far, pack):
     count = lax.axis_size(WIDE)
-    near = lax.ppermute(near, WIDE, [(w, w ^ 1) for w in range(count)])
     far = lax.ppermute(
         far, WIDE, [(w, (w + 1 if w % 2 else w - 1) % count) for w in range(count)]
     )
-    (pack,) = call(pack_kernel, place, [pack.shape], [], pack, near, far)
-    return near, far, lax.all_gather(pack, "narrow")
+    near = lax.ppermute(near, WIDE, [(w, w ^ 1) for w in range(count)])
+    (pack,) = call(pack_kernel, place, [pack.shape], [], pack, far, near)
+    return far, near, lax.all_gather(pack, "narrow")
 
 
 def local(load, geom, element_order):

time: 177 us -> 165 us (0.932)
  starting transfers between devices: 102 us -> 78.2 us
  waiting for transfers between devices: 9.21 us -> 19.4 us
    ppermute x7, starting transfers between devices: 76.8 us -> 56.4 us  [exchange(): lax.ppermute(far, WIDE, [(w, (w + 1 if w % 2 else w - 1) % count) for w i...]
    ppermute x7, waiting for transfers between devices: 6.79 us -> 13.9 us  [exchange(): lax.ppermute(far, WIDE, [(w, (w + 1 if w % 2 else w - 1) % count) for w i...]
    ppermute x7, waiting for transfers between devices: 0.02 us -> 3.07 us  [exchange(): near = lax.ppermute(near, WIDE, [(w, w ^ 1) for w in range(count)])]
    ppermute x7, starting transfers between devices: 16.4 us -> 13.4 us  [exchange(): near = lax.ppermute(near, WIDE, [(w, w ^ 1) for w in range(count)])]
  transfers between devices with their start and end apart: 16 -> 16, of which waited for: 7 -> 9; matrix products, arithmetic and copies ran while one was open for 0% -> 0% of each run, Pallas kernels for 0% -> 0%
where the time goes in v2:
time: 165 us; the launch traced here: 164 us
  starting transfers between devices  78.2 us (47%)
  blocking collectives  44.3 us (27%)
  waiting for transfers between devices  19.4 us (12%)
  Pallas kernels  17.2 us (10%)
  local copies, waits for them, and re-layouts  4.19 us (3%)
    ppermute x7, starting transfers between devices, exchange(): lax.ppermute(far, WIDE, [(w, (w + 1 if w % 2 else w - 1) % count) for w i...  56.4 us
    all_gather x7, blocking collectives, exchange(): return (far, near, lax.all_gather(pack, 'narrow'))  44.3 us
    pallas_call x15, Pallas kernels, call(): pl.pallas_call(kernel, out_shape=[jax.ShapeDtypeStruct(s, F32) for s in o...  17.2 us
    ppermute x7, waiting for transfers between devices, exchange(): lax.ppermute(far, WIDE, [(w, (w + 1 if w % 2 else w - 1) % count) for w i...  13.9 us
    ppermute x7, starting transfers between devices, exchange(): near = lax.ppermute(near, WIDE, [(w, w ^ 1) for w in range(count)])  13.4 us
    all_to_all x1, starting transfers between devices, local(): sums = lax.all_to_all(sums, REST, 0, 0)  4.91 us
    unnamed x13, local copies, waits for them, and re-layouts  3.49 us
    all_to_all x1, starting transfers between devices, local(): sums = lax.all_to_all(sums, 'ring', 0, 0)  3.47 us
  transfers between devices with their start and end apart: 16, of which 9 were waited for; matrix products, arithmetic and copies ran while one was open for 0% of the time, Pallas kernels for 0%

profile of v2, /device:TPU:1, one launch (start us, length us, event | category | flops | bytes accessed | tf_op | source)
XLA Modules:
  0.0 164.3 jit_solution(11211011645253744223)
XLA Ops:
  0.7 0.7 copy-done.5
  1.4 1.0 copy-done.2
  2.4 0.9 copy-done.3
  3.3 0.9 copy-done.4
  4.2 1.5 shard_map.77
  5.7 20.6 %collective-permute-start = (f32[2,32,128]{2,1,0:T(8,128)S(1)}, f32[2,32,128]{2,1,0:T(8,128)S(1)}, u32[]{:S(2)}, u32[]{:S(2)}) collective-permute-start(f32[2,32,128]{2,1,0:T(8,128)S(1)} %get-tuple-element.47), channel_id=1, source_target_pairs={{0,764},{4,8},{8,4},{12,16},{16,12},{20,24},{24,20},{28,32},{32,28... | collective-permute-start | bytes 98312 | tf_op jit(solution)/shard_map/ppermute | solution.py:491
  26.3 1.9 %collective-permute-start.1 = (f32[2,32,128]{2,1,0:T(8,128)S(1)}, f32[2,32,128]{2,1,0:T(8,128)S(1)}, u32[]{:S(2)}, u32[]{:S(2)}) collective-permute-start(f32[2,32,128]{2,1,0:T(8,128)S(1)} %get-tuple-element.48), channel_id=1, source_target_pairs={{0,4},{4,0},{8,12},{12,8},{16,20},{20,16},{24,28},{28,24},{32,36},... | collective-permute-start | bytes 98312 | tf_op jit(solution)/shard_map/ppermute | solution.py:494
  28.3 2.7 %collective-permute-done.1.near_ref.h1 = f32[2,32,128]{2,1,0:T(8,128)S(1)} collective-permute-done((f32[2,32,128]{2,1,0:T(8,128)S(1)}, f32[2,32,128]{2,1,0:T(8,128)S(1)}, u32[]{:S(2)}, u32[]{:S(2)}) %collective-permute-start.1) | collective-permute-done | bytes 32800 | tf_op jit(solution)/shard_map/ppermute | solution.py:494
  31.0 0.6 shard_map.78
  31.6 7.2 %all-gather = f32[8,16,128]{2,1,0:T(8,128)S(1)} all-gather(f32[2,16,128]{2,1,0:T(8,128)S(1)} %shard_map.78), channel_id=2, replica_groups=mesh['outer'=16,'ring'=12,'narrow'=4] {'narrow'}, dimensions={0}, use_global_device_ids=true | all-gather | bytes 81920 | tf_op jit(solution)/shard_map/all_gather | solution.py:496
  38.8 1.5 shard_map.79
  40.3 5.4 %collective-permute-start.2 = (f32[1,32,128]{2,1,0:T(8,128)S(1)}, f32[1,32,128]{2,1,0:T(8,128)S(1)}, u32[]{:S(2)}, u32[]{:S(2)}) collective-permute-start(f32[1,32,128]{2,1,0:T(8,128)S(1)} %get-tuple-element.52), channel_id=1, source_target_pairs={{0,764},{4,8},{8,4},{12,16},{16,12},{20,24},{24,20},{28,32},{32,28... | collective-permute-start | bytes 49160 | tf_op jit(solution)/shard_map/ppermute | solution.py:491
  45.7 1.9 %collective-permute-start.3 = (f32[1,32,128]{2,1,0:T(8,128)S(1)}, f32[1,32,128]{2,1,0:T(8,128)S(1)}, u32[]{:S(2)}, u32[]{:S(2)}) collective-permute-start(f32[1,32,128]{2,1,0:T(8,128)S(1)} %get-tuple-element.53), channel_id=1, source_target_pairs={{0,4},{4,0},{8,12},{12,8},{16,20},{20,16},{24,28},{28,24},{32,36},... | collective-permute-start | bytes 49160 | tf_op jit(solution)/shard_map/ppermute | solution.py:494
  47.7 2.8 %collective-permute-done.2.far_ref.h0 = f32[1,32,128]{2,1,0:T(8,128)S(1)} collective-permute-done((f32[1,32,128]{2,1,0:T(8,128)S(1)}, f32[1,32,128]{2,1,0:T(8,128)S(1)}, u32[]{:S(2)}, u32[]{:S(2)}) %collective-permute-start.2) | collective-permute-done | bytes 16416 | tf_op jit(solution)/shard_map/ppermute | solution.py:491
  50.5 0.6 shard_map.80
  51.1 6.3 %all-gather.1 = f32[4,16,128]{2,1,0:T(8,128)S(1)} all-gather(f32[1,16,128]{2,1,0:T(8,128)S(1)} %shard_map.80), channel_id=3, replica_groups=mesh['outer'=16,'ring'=12,'narrow'=4] {'narrow'}, dimensions={0}, use_global_device_ids=true | all-gather | bytes 40960 | tf_op jit(solution)/shard_map/all_gather | solution.py:496
  57.4 1.5 shard_map.81
  58.9 5.6 %collective-permute-start.4 = (f32[1,32,128]{2,1,0:T(8,128)S(1)}, f32[1,32,128]{2,1,0:T(8,128)S(1)}, u32[]{:S(2)}, u32[]{:S(2)}) collective-permute-start(f32[1,32,128]{2,1,0:T(8,128)S(1)} %get-tuple-element.59), channel_id=1, source_target_pairs={{0,764},{4,8},{8,4},{12,16},{16,12},{20,24},{24,20},{28,32},{32,28... | collective-permute-start | bytes 49160 | tf_op jit(solution)/shard_map/ppermute | solution.py:491
  64.5 1.9 %collective-permute-start.5 = (f32[1,32,128]{2,1,0:T(8,128)S(1)}, f32[1,32,128]{2,1,0:T(8,128)S(1)}, u32[]{:S(2)}, u32[]{:S(2)}) collective-permute-start(f32[1,32,128]{2,1,0:T(8,128)S(1)} %get-tuple-element.60), channel_id=1, source_target_pairs={{0,4},{4,0},{8,12},{12,8},{16,20},{20,16},{24,28},{28,24},{32,36},... | collective-permute-start | bytes 49160 | tf_op jit(solution)/shard_map/ppermute | solution.py:494
  66.4 2.7 %collective-permute-done.4.far_ref.h0 = f32[1,32,128]{2,1,0:T(8,128)S(1)} collective-permute-done((f32[1,32,128]{2,1,0:T(8,128)S(1)}, f32[1,32,128]{2,1,0:T(8,128)S(1)}, u32[]{:S(2)}, u32[]{:S(2)}) %collective-permute-start.4) | collective-permute-done | bytes 16416 | tf_op jit(solution)/shard_map/ppermute | solution.py:491
  69.3 0.6 shard_map.82
  69.9 6.3 %all-gather.2 = f32[4,16,128]{2,1,0:T(8,128)S(1)} all-gather(f32[1,16,128]{2,1,0:T(8,128)S(1)} %shard_map.82), channel_id=4, replica_groups=mesh['outer'=16,'ring'=12,'narrow'=4] {'narrow'}, dimensions={0}, use_global_device_ids=true | all-gather | bytes 40960 | tf_op jit(solution)/shard_map/all_gather | solution.py:496
  76.2 1.6 shard_map.83
  77.8 5.4 %collective-permute-start.6 = (f32[1,32,128]{2,1,0:T(8,128)S(1)}, f32[1,32,128]{2,1,0:T(8,128)S(1)}, u32[]{:S(2)}, u32[]{:S(2)}) collective-permute-start(f32[1,32,128]{2,1,0:T(8,128)S(1)} %get-tuple-element.65), channel_id=1, source_target_pairs={{0,764},{4,8},{8,4},{12,16},{16,12},{20,24},{24,20},{28,32},{32,28... | collective-permute-start | bytes 49160 | tf_op jit(solution)/shard_map/ppermute | solution.py:491
  83.2 1.9 %collective-permute-start.7 = (f32[1,32,128]{2,1,0:T(8,128)S(1)}, f32[1,32,128]{2,1,0:T(8,128)S(1)}, u32[]{:S(2)}, u32[]{:S(2)}) collective-permute-start(f32[1,32,128]{2,1,0:T(8,128)S(1)} %get-tuple-element.66), channel_id=1, source_target_pairs={{0,4},{4,0},{8,12},{12,8},{16,20},{20,16},{24,28},{28,24},{32,36},... | collective-permute-start | bytes 49160 | tf_op jit(solution)/shard_map/ppermute | solution.py:494
  85.1 2.8 %collective-permute-done.6.far_ref.h0 = f32[1,32,128]{2,1,0:T(8,128)S(1)} collective-permute-done((f32[1,32,128]{2,1,0:T(8,128)S(1)}, f32[1,32,128]{2,1,0:T(8,128)S(1)}, u32[]{:S(2)}, u32[]{:S(2)}) %collective-permute-start.6) | collective-permute-done | bytes 16416 | tf_op jit(solution)/shard_map/ppermute | solution.py:491
  88.6 6.3 %all-gather.3 = f32[4,16,128]{2,1,0:T(8,128)S(1)} all-gather(f32[1,16,128]{2,1,0:T(8,128)S(1)} %shard_map.84), channel_id=5, replica_groups=mesh['outer'=16,'ring'=12,'narrow'=4] {'narrow'}, dimensions={0}, use_global_device_ids=true | all-gather | bytes 40960 | tf_op jit(solution)/shard_map/all_gather | solution.py:496
  94.9 1.5 shard_map.85
  96.4 5.6 %collective-permute-start.8 = (f32[1,32,128]{2,1,0:T(8,128)S(1)}, f32[1,32,128]{2,1,0:T(8,128)S(1)}, u32[]{:S(2)}, u32[]{:S(2)}) collective-permute-start(f32[1,32,128]{2,1,0:T(8,128)S(1)} %get-tuple-element.69), channel_id=1, source_target_pairs={{0,764},{4,8},{8,4},{12,16},{16,12},{20,24},{24,20},{28,32},{32,28... | collective-permute-start | bytes 49160 | tf_op jit(solution)/shard_map/ppermute | solution.py:491
  102.0 1.9 %collective-permute-start.9 = (f32[1,32,128]{2,1,0:T(8,128)S(1)}, f32[1,32,128]{2,1,0:T(8,128)S(1)}, u32[]{:S(2)}, u32[]{:S(2)}) collective-permute-start(f32[1,32,128]{2,1,0:T(8,128)S(1)} %get-tuple-element.70), channel_id=1, source_target_pairs={{0,4},{4,0},{8,12},{12,8},{16,20},{20,16},{24,28},{28,24},{32,36},... | collective-permute-start | bytes 49160 | tf_op jit(solution)/shard_map/ppermute | solution.py:494
  103.9 2.7 %collective-permute-done.8.far_ref.h0 = f32[1,32,128]{2,1,0:T(8,128)S(1)} collective-permute-done((f32[1,32,128]{2,1,0:T(8,128)S(1)}, f32[1,32,128]{2,1,0:T(8,128)S(1)}, u32[]{:S(2)}, u32[]{:S(2)}) %collective-permute-start.8) | collective-permute-done | bytes 16416 | tf_op jit(solution)/shard_map/ppermute | solution.py:491
  106.7 0.6 shard_map.86
  107.4 6.3 %all-gather.4 = f32[4,16,128]{2,1,0:T(8,128)S(1)} all-gather(f32[1,16,128]{2,1,0:T(8,128)S(1)} %shard_map.86), channel_id=6, replica_groups=mesh['outer'=16,'ring'=12,'narrow'=4] {'narrow'}, dimensions={0}, use_global_device_ids=true | all-gather | bytes 40960 | tf_op jit(solution)/shard_map/all_gather | solution.py:496
  113.7 1.5 shard_map.87
  115.2 5.4 %collective-permute-start.10 = (f32[1,32,128]{2,1,0:T(8,128)S(1)}, f32[1,32,128]{2,1,0:T(8,128)S(1)}, u32[]{:S(2)}, u32[]{:S(2)}) collective-permute-start(f32[1,32,128]{2,1,0:T(8,128)S(1)} %get-tuple-element.75), channel_id=1, source_target_pairs={{0,764},{4,8},{8,4},{12,16},{16,12},{20,24},{24,20},{28,32},{32,28... | collective-permute-start | bytes 49160 | tf_op jit(solution)/shard_map/ppermute | solution.py:491
  120.6 1.9 %collective-permute-start.11 = (f32[1,32,128]{2,1,0:T(8,128)S(1)}, f32[1,32,128]{2,1,0:T(8,128)S(1)}, u32[]{:S(2)}, u32[]{:S(2)}) collective-permute-start(f32[1,32,128]{2,1,0:T(8,128)S(1)} %get-tuple-element.76), channel_id=1, source_target_pairs={{0,4},{4,0},{8,12},{12,8},{16,20},{20,16},{24,28},{28,24},{32,36},... | collective-permute-start | bytes 49160 | tf_op jit(solution)/shard_map/ppermute | solution.py:494
  122.6 2.8 %collective-permute-done.10.far_ref.h0 = f32[1,32,128]{2,1,0:T(8,128)S(1)} collective-permute-done((f32[1,32,128]{2,1,0:T(8,128)S(1)}, f32[1,32,128]{2,1,0:T(8,128)S(1)}, u32[]{:S(2)}, u32[]{:S(2)}) %collective-permute-start.10) | collective-permute-done | bytes 16416 | tf_op jit(solution)/shard_map/ppermute | solution.py:491
  125.4 0.6 shard_map.88
  126.0 6.3 %all-gather.5 = f32[4,16,128]{2,1,0:T(8,128)S(1)} all-gather(f32[1,16,128]{2,1,0:T(8,128)S(1)} %shard_map.88), channel_id=7, replica_groups=mesh['outer'=16,'ring'=12,'narrow'=4] {'narrow'}, dimensions={0}, use_global_device_ids=true | all-gather | bytes 40960 | tf_op jit(solution)/shard_map/all_gather | solution.py:496
  132.3 2.1 %shard_map.89 = (f32[8,32,128]{2,1,0:T(8,128)S(1)}, f32[8,32,128]{2,1,0:T(8,128)S(1)}, f32[1,32,128]{2,1,0:T(8,128)S(1)}, f32[1,32,128]{2,1,0:T(8,128)S(1)}, f32...) custom-call(s32[2]{0:T(128)S(1)} %pad_add_fusion.place_ref, f32[8,32,128]{2,1,0:T(8,128)S(1)} %get-tuple-element.74.kv_in, ...), custom_call_target="tpu_custom_call" | custom-call | tf_op jit(solution)/shard_map/pallas_call | solution.py:472
  134.4 4.9 %all-to-all-start = ((f32[64,1,128]{2,1,0:T(1,128)}), f32[64,1,128]{2,1,0:T(1,128)S(1)}, u32[]{:S(2)}, u32[]{:S(2)}) async-start(f32[64,1,128]{2,1,0:T(1,128)} %bitcast.11), calls=%async_computation | async-start | bytes 65536 | tf_op jit(solution)/shard_map/all_to_all | solution.py:554
  139.4 8.4 %collective-permute-start.12 = (f32[1,32,128]{2,1,0:T(8,128)S(1)}, f32[1,32,128]{2,1,0:T(8,128)S(1)}, u32[]{:S(2)}, u32[]{:S(2)}) collective-permute-start(f32[1,32,128]{2,1,0:T(8,128)S(1)} %get-tuple-element.83), channel_id=1, source_target_pairs={{0,764},{4,8},{8,4},{12,16},{16,12},{20,24},{24,20},{28,32},{32,28... | collective-permute-start | bytes 49160 | tf_op jit(solution)/shard_map/ppermute | solution.py:491
  147.8 1.9 %collective-permute-start.13 = (f32[1,32,128]{2,1,0:T(8,128)S(1)}, f32[1,32,128]{2,1,0:T(8,128)S(1)}, u32[]{:S(2)}, u32[]{:S(2)}) collective-permute-start(f32[1,32,128]{2,1,0:T(8,128)S(1)} %get-tuple-element.84), channel_id=1, source_target_pairs={{0,4},{4,0},{8,12},{12,8},{16,20},{20,16},{24,28},{28,24},{32,36},... | collective-permute-start | bytes 49160 | tf_op jit(solution)/shard_map/ppermute | solution.py:494
  150.4 3.5 %all-to-all-start.1 = ((f32[12,1,128]{2,1,0:T(1,128)}), f32[12,1,128]{2,1,0:T(1,128)S(1)}, u32[]{:S(2)}, u32[]{:S(2)}) async-start(f32[12,1,128]{2,1,0:T(1,128)} %broadcast_in_dim.2), calls=%async_computation.1 | async-start | bytes 12288 | tf_op jit(solution)/shard_map/all_to_all | solution.py:558
  154.0 0.6 shard_map.90
  154.6 5.6 %all-gather.6 = f32[4,16,128]{2,1,0:T(8,128)S(1)} all-gather(f32[1,16,128]{2,1,0:T(8,128)S(1)} %shard_map.90), channel_id=8, replica_groups=mesh['outer'=16,'ring'=12,'narrow'=4] {'narrow'}, dimensions={0}, use_global_device_ids=true | all-gather | bytes 40960 | tf_op jit(solution)/shard_map/all_gather | solution.py:496
  160.2 2.4 %all-to-all-done.1 = f32[12,1,128]{2,1,0:T(1,128)S(1)} async-done(((f32[12,1,128]{2,1,0:T(1,128)}), f32[12,1,128]{2,1,0:T(1,128)S(1)}, u32[]{:S(2)}, u32[]{:S(2)}) %all-to-all-start.1) | async-done | bytes 6176 | tf_op jit(solution)/shard_map/all_to_all | solution.py:558
  162.6 1.7 %shard_map.91 = (f32[64,512]{1,0:T(8,128)}, f32[64,512]{1,0:T(8,128)}) custom-call(s32[2]{0:T(128)S(1)} %pad_add_fusion.place_ref, f32[8,32,128]{2,1,0:T(8,128)S(1)} %get-tuple-element.82.kv_in, f32[1,32,128]{2,1,0:T(8,128)S(1)} %collective-permute-done.12.far_ref.h0, f32[1,32,128]{2,1,0:T(8,128)S(1)} %collective-permute-done.13.near_ref.h1, ...), custom_call_target="tpu_custom_call" | custom-call | tf_op jit(solution)/shard_map/pallas_call | solution.py:472
  (23 shorter events, 1.8 us)
Async XLA Ops:
  0.7 0.7 copy-start.5
  1.4 1.0 copy-start.2
  2.4 0.9 copy-start.3
  3.3 0.9 copy-start.4
  4.2 34.6 %copy-start.1 = (bf16[2,256,128]{2,1,0:T(8,128)(2,1)S(1)}, bf16[2,256,128]{2,1,0:T(8,128)(2,1)}, u32[]{:S(2)}) copy-start(bf16[2,256,128]{2,1,0:T(8,128)(2,1)} %constant.37.clone.diver_ref) | copy-start | bytes 393220
  5.7 33.1 %copy-start = (bf16[2,128,256]{2,1,0:T(8,128)(2,1)S(1)}, bf16[2,128,256]{2,1,0:T(8,128)(2,1)}, u32[]{:S(2)}) copy-start(bf16[2,128,256]{2,1,0:T(8,128)(2,1)} %constant.36.clone.grad_ref) | copy-start | bytes 393220
  5.7 22.6 %collective-permute-start = (f32[2,32,128]{2,1,0:T(8,128)S(1)}, f32[2,32,128]{2,1,0:T(8,128)S(1)}, u32[]{:S(2)}, u32[]{:S(2)}) collective-permute-start(f32[2,32,128]{2,1,0:T(8,128)S(1)} %get-tuple-element.47), channel_id=1, source_target_pairs={{0,764},{4,8},{8,4},{12,16},{16,12},{20,24},{24,20},{28,32},{32,28... | collective-permute-start | bytes 98312 | tf_op jit(solution)/shard_map/ppermute | solution.py:491
  26.3 4.7 %collective-permute-start.1 = (f32[2,32,128]{2,1,0:T(8,128)S(1)}, f32[2,32,128]{2,1,0:T(8,128)S(1)}, u32[]{:S(2)}, u32[]{:S(2)}) collective-permute-start(f32[2,32,128]{2,1,0:T(8,128)S(1)} %get-tuple-element.48), channel_id=1, source_target_pairs={{0,4},{4,0},{8,12},{12,8},{16,20},{20,16},{24,28},{28,24},{32,36},... | collective-permute-start | bytes 98312 | tf_op jit(solution)/shard_map/ppermute | solution.py:494
  40.3 10.2 %collective-permute-start.2 = (f32[1,32,128]{2,1,0:T(8,128)S(1)}, f32[1,32,128]{2,1,0:T(8,128)S(1)}, u32[]{:S(2)}, u32[]{:S(2)}) collective-permute-start(f32[1,32,128]{2,1,0:T(8,128)S(1)} %get-tuple-element.52), channel_id=1, source_target_pairs={{0,764},{4,8},{8,4},{12,16},{16,12},{20,24},{24,20},{28,32},{32,28... | collective-permute-start | bytes 49160 | tf_op jit(solution)/shard_map/ppermute | solution.py:491
  45.7 4.8 %collective-permute-start.3 = (f32[1,32,128]{2,1,0:T(8,128)S(1)}, f32[1,32,128]{2,1,0:T(8,128)S(1)}, u32[]{:S(2)}, u32[]{:S(2)}) collective-permute-start(f32[1,32,128]{2,1,0:T(8,128)S(1)} %get-tuple-element.53), channel_id=1, source_target_pairs={{0,4},{4,0},{8,12},{12,8},{16,20},{20,16},{24,28},{28,24},{32,36},... | collective-permute-start | bytes 49160 | tf_op jit(solution)/shard_map/ppermute | solution.py:494
  58.9 10.2 %collective-permute-start.4 = (f32[1,32,128]{2,1,0:T(8,128)S(1)}, f32[1,32,128]{2,1,0:T(8,128)S(1)}, u32[]{:S(2)}, u32[]{:S(2)}) collective-permute-start(f32[1,32,128]{2,1,0:T(8,128)S(1)} %get-tuple-element.59), channel_id=1, source_target_pairs={{0,764},{4,8},{8,4},{12,16},{16,12},{20,24},{24,20},{28,32},{32,28... | collective-permute-start | bytes 49160 | tf_op jit(solution)/shard_map/ppermute | solution.py:491
  64.5 4.8 %collective-permute-start.5 = (f32[1,32,128]{2,1,0:T(8,128)S(1)}, f32[1,32,128]{2,1,0:T(8,128)S(1)}, u32[]{:S(2)}, u32[]{:S(2)}) collective-permute-start(f32[1,32,128]{2,1,0:T(8,128)S(1)} %get-tuple-element.60), channel_id=1, source_target_pairs={{0,4},{4,0},{8,12},{12,8},{16,20},{20,16},{24,28},{28,24},{32,36},... | collective-permute-start | bytes 49160 | tf_op jit(solution)/shard_map/ppermute | solution.py:494
  77.8 10.2 %collective-permute-start.6 = (f32[1,32,128]{2,1,0:T(8,128)S(1)}, f32[1,32,128]{2,1,0:T(8,128)S(1)}, u32[]{:S(2)}, u32[]{:S(2)}) collective-permute-start(f32[1,32,128]{2,1,0:T(8,128)S(1)} %get-tuple-element.65), channel_id=1, source_target_pairs={{0,764},{4,8},{8,4},{12,16},{16,12},{20,24},{24,20},{28,32},{32,28... | collective-permute-start | bytes 49160 | tf_op jit(solution)/shard_map/ppermute | solution.py:491
  83.2 4.8 %collective-permute-start.7 = (f32[1,32,128]{2,1,0:T(8,128)S(1)}, f32[1,32,128]{2,1,0:T(8,128)S(1)}, u32[]{:S(2)}, u32[]{:S(2)}) collective-permute-start(f32[1,32,128]{2,1,0:T(8,128)S(1)} %get-tuple-element.66), channel_id=1, source_target_pairs={{0,4},{4,0},{8,12},{12,8},{16,20},{20,16},{24,28},{28,24},{32,36},... | collective-permute-start | bytes 49160 | tf_op jit(solution)/shard_map/ppermute | solution.py:494
  96.4 10.2 %collective-permute-start.8 = (f32[1,32,128]{2,1,0:T(8,128)S(1)}, f32[1,32,128]{2,1,0:T(8,128)S(1)}, u32[]{:S(2)}, u32[]{:S(2)}) collective-permute-start(f32[1,32,128]{2,1,0:T(8,128)S(1)} %get-tuple-element.69), channel_id=1, source_target_pairs={{0,764},{4,8},{8,4},{12,16},{16,12},{20,24},{24,20},{28,32},{32,28... | collective-permute-start | bytes 49160 | tf_op jit(solution)/shard_map/ppermute | solution.py:491
  102.0 4.8 %collective-permute-start.9 = (f32[1,32,128]{2,1,0:T(8,128)S(1)}, f32[1,32,128]{2,1,0:T(8,128)S(1)}, u32[]{:S(2)}, u32[]{:S(2)}) collective-permute-start(f32[1,32,128]{2,1,0:T(8,128)S(1)} %get-tuple-element.70), channel_id=1, source_target_pairs={{0,4},{4,0},{8,12},{12,8},{16,20},{20,16},{24,28},{28,24},{32,36},... | collective-permute-start | bytes 49160 | tf_op jit(solution)/shard_map/ppermute | solution.py:494
  115.2 10.2 %collective-permute-start.10 = (f32[1,32,128]{2,1,0:T(8,128)S(1)}, f32[1,32,128]{2,1,0:T(8,128)S(1)}, u32[]{:S(2)}, u32[]{:S(2)}) collective-permute-start(f32[1,32,128]{2,1,0:T(8,128)S(1)} %get-tuple-element.75), channel_id=1, source_target_pairs={{0,764},{4,8},{8,4},{12,16},{16,12},{20,24},{24,20},{28,32},{32,28... | collective-permute-start | bytes 49160 | tf_op jit(solution)/shard_map/ppermute | solution.py:491
  120.6 4.8 %collective-permute-start.11 = (f32[1,32,128]{2,1,0:T(8,128)S(1)}, f32[1,32,128]{2,1,0:T(8,128)S(1)}, u32[]{:S(2)}, u32[]{:S(2)}) collective-permute-start(f32[1,32,128]{2,1,0:T(8,128)S(1)} %get-tuple-element.76), channel_id=1, source_target_pairs={{0,4},{4,0},{8,12},{12,8},{16,20},{20,16},{24,28},{28,24},{32,36},... | collective-permute-start | bytes 49160 | tf_op jit(solution)/shard_map/ppermute | solution.py:494
  134.4 15.2 %all-to-all-start = ((f32[64,1,128]{2,1,0:T(1,128)}), f32[64,1,128]{2,1,0:T(1,128)S(1)}, u32[]{:S(2)}, u32[]{:S(2)}) async-start(f32[64,1,128]{2,1,0:T(1,128)} %bitcast.11), calls=%async_computation | async-start | bytes 65536 | tf_op jit(solution)/shard_map/all_to_all | solution.py:554
  139.4 14.6 %collective-permute-start.12 = (f32[1,32,128]{2,1,0:T(8,128)S(1)}, f32[1,32,128]{2,1,0:T(8,128)S(1)}, u32[]{:S(2)}, u32[]{:S(2)}) collective-permute-start(f32[1,32,128]{2,1,0:T(8,128)S(1)} %get-tuple-element.83), channel_id=1, source_target_pairs={{0,764},{4,8},{8,4},{12,16},{16,12},{20,24},{24,20},{28,32},{32,28... | collective-permute-start | bytes 49160 | tf_op jit(solution)/shard_map/ppermute | solution.py:491
  147.8 6.2 %collective-permute-start.13 = (f32[1,32,128]{2,1,0:T(8,128)S(1)}, f32[1,32,128]{2,1,0:T(8,128)S(1)}, u32[]{:S(2)}, u32[]{:S(2)}) collective-permute-start(f32[1,32,128]{2,1,0:T(8,128)S(1)} %get-tuple-element.84), channel_id=1, source_target_pairs={{0,4},{4,0},{8,12},{12,8},{16,20},{20,16},{24,28},{28,24},{32,36},... | collective-permute-start | bytes 49160 | tf_op jit(solution)/shard_map/ppermute | solution.py:494
  150.4 12.2 %all-to-all-start.1 = ((f32[12,1,128]{2,1,0:T(1,128)}), f32[12,1,128]{2,1,0:T(1,128)S(1)}, u32[]{:S(2)}, u32[]{:S(2)}) async-start(f32[12,1,128]{2,1,0:T(1,128)} %broadcast_in_dim.2), calls=%async_computation.1 | async-start | bytes 12288 | tf_op jit(solution)/shard_map/all_to_all | solution.py:558

commit v3 on v2

v3 whole, which is shorter than its diff:
```python
import functools

import jax
import jax.numpy as jnp
import ml_dtypes
import numpy as np
from jax import lax
from jax.experimental import pallas as pl
from jax.experimental.pallas import tpu as pltpu
from jax.sharding import PartitionSpec as P

NODES = 8
ROWS = 32
LANES = 128
HALF = 16
GROWS = ROWS + HALF
INTERVAL_LOW = 0.03
INTERVAL_HIGH = 1.0
FIELD = (NODES, ROWS, LANES)
GHOST = (NODES, HALF, LANES)
BIG = (NODES, GROWS, LANES)
WIDE = ("outer", "ring")
REST = ("outer", "narrow")


def legendre_seven(point):
    before = 1.0
    current = point
    for degree in range(1, 7):
        after = ((2.0 * degree + 1.0) * point * current - degree * before) / (degree + 1.0)
        before = current
        current = after
    return current


def gll_derivative():
    points = 8
    inner_nodes = [
        -0.8717401485096066,
        -0.5917001814331423,
        -0.2092992179024789,
        0.2092992179024789,
        0.5917001814331423,
        0.8717401485096066,
    ]
    nodes = [-1.0] + inner_nodes + [1.0]
    values_at = [legendre_seven(node) for node in nodes]
    matrix = np.zeros((points, points))
    for source in range(points):
        for target in range(points):
            if source != target:
                matrix[source, target] = values_at[source] / (
                    values_at[target] * (nodes[source] - nodes[target])
                )
    matrix[0, 0] = -(points - 1) * points / 4.0
    matrix[points - 1, points - 1] = (points - 1) * points / 4.0
    return matrix


DERIV = gll_derivative().astype(np.float32)
ABS_DERIV = np.abs(DERIV)
ROW_TOTAL = ABS_DERIV.sum(axis=1)
EYE8 = np.eye(8, dtype=np.float32)


def cycle_matrix(small):
    return np.kron(np.eye(2, dtype=np.float32), np.kron(small, EYE8))


def radial_matrix(small):
    return np.kron(np.eye(16, dtype=np.float32), small)


def split_const(matrix):
    high = matrix.astype(ml_dtypes.bfloat16)
    low = (matrix - high.astype(np.float32)).astype(ml_dtypes.bfloat16)
    return high, low


GRAD = np.concatenate([cycle_matrix(DERIV.T), radial_matrix(DERIV.T)], axis=1)
DIVER = np.concatenate([cycle_matrix(DERIV), radial_matrix(DERIV)], axis=0)
GRAD_HL = np.stack(split_const(GRAD))
DIVER_HL = np.stack(split_const(DIVER))
ABS_HL = np.stack(split_const(np.abs(DIVER)))


def split(value):
    high = value.astype(jnp.bfloat16)
    return high, (value - high.astype(jnp.float32)).astype(jnp.bfloat16)


def dot(left, right):
    return lax.dot_general(
        left, right, (((1,), (0,)), ((), ())), preferred_element_type=jnp.float32
    )


def dot_split(value, matrix_ref):
    high, low = split(value)
    return dot(high, matrix_ref[0]) + (dot(low, matrix_ref[0]) + dot(high, matrix_ref[1]))


def lane_iota(rows):
    return lax.broadcasted_iota(jnp.int32, (rows, LANES), 1)


def row_iota(rows):
    return lax.broadcasted_iota(jnp.int32, (rows, LANES), 0)


def roll(value, shift, axis):
    size = value.shape[axis]
    return pltpu.roll(value, shift % size, axis)


def along_nodes(values, small):
    half = NODES // 2
    even = [values[i] + values[NODES - 1 - i] for i in range(half)]
    odd = [values[i] - values[NODES - 1 - i] for i in range(half)]
    out = [None] * NODES
    for m in range(half):
        from_even, from_odd = None, None
        for i in range(half):
            near, far = float(small[m][i]), float(small[m][NODES - 1 - i])
            one = even[i] * (0.5 * (near + far))
            two = odd[i] * (0.5 * (near - far))
            from_even = one if from_even is None else from_even + one
            from_odd = two if from_odd is None else from_odd + two
        out[m] = from_odd + from_even
        out[NODES - 1 - m] = from_odd - from_even
    return out


def along_nodes_plain(values, small):
    out = []
    for m in range(NODES):
        total = None
        for i in range(NODES):
            term = values[i] * float(small[m][i])
            total = term if total is None else total + term
        out.append(total)
    return out


def edge(value):
    return jnp.where(lane_iota(HALF) < 64, value[:HALF], value[HALF:])


def packed_edges(even, odd):
    low = lane_iota(HALF) < 64
    return jnp.where(low, even, roll(odd, 64, 1)), jnp.where(low, roll(even, 64, 1), odd)


def store_edges(lo_ref, hi_ref, c, values):
    for b in range(NODES // 2):
        lo_ref[c, b], hi_ref[c, b] = packed_edges(values[2 * b], values[2 * b + 1])


def ghost_columns(left_ref, right_ref, c):
    low = lane_iota(HALF) < 64
    out = []
    for b in range(NODES // 2):
        left, right = left_ref[c, b], right_ref[c, b]
        out.append(jnp.where(low, left, roll(right, 64, 1)))
        out.append(jnp.where(low, roll(left, 64, 1), right))
    return out


def facing(left, right):
    return roll(jnp.where(lane_iota(HALF) < 64, right, left), 64, 1)


def own_assembly(u):
    count = u.shape[0]
    k = lane_iota(count) % 8
    er = row_iota(count) % HALF
    up = roll(roll(u, -1, 0), 7, 1)
    down = roll(roll(u, 1, 0), -7, 1)
    u = (
        u
        + jnp.where((k == 7) & (er < HALF - 1), up, 0.0)
        + jnp.where((k == 0) & (er > 0), down, 0.0)
    )
    top, bottom = u[:HALF], u[HALF:ROWS]
    lane = lane_iota(HALF)
    j = (lane // 8) % 8
    block = lane // 64
    new_top = (
        top
        + jnp.where(j == 7, roll(bottom, 56, 1), 0.0)
        + jnp.where((j == 0) & (block == 1), roll(bottom, 8, 1), 0.0)
    )
    new_bottom = (
        bottom
        + jnp.where(j == 0, roll(top, -56, 1), 0.0)
        + jnp.where((j == 7) & (block == 0), roll(top, -8, 1), 0.0)
    )
    if count == GROWS:
        ghost = u[ROWS:]
        new_top = new_top + jnp.where(lane < 8, roll(ghost, -56, 1), 0.0)
        new_bottom = new_bottom + jnp.where(lane >= 120, roll(ghost, 56, 1), 0.0)
    return jnp.concatenate([new_top, new_bottom], axis=0)


def ends(value):
    lane = lane_iota(HALF)
    return jnp.where(lane < 8, value[:HALF], jnp.where(lane >= 120, value[HALF:], 0.0))


def store_assembled(kv_ref, far_ref, near_ref, even, source, field=0, pack_ref=None):
    pack = None
    for i in range(NODES):
        value = own_assembly(source(i))
        kv_ref[i] = value
        if i == 0:
            first = value
        last = value
        if pack_ref is not None:
            piece = ends(value)
            if i:
                piece = roll(piece, 16 * i, 1)
            pack = piece if pack is None else pack + piece
    near_ref[field] = jnp.where(even, last, first)
    far_ref[field] = jnp.where(even, first, last)
    if pack_ref is not None:
        pack_ref[field] = pack


def is_even(place_ref):
    return lax.broadcast_in_dim(place_ref[0], (ROWS, LANES), ()) == 0


def pack_kernel(place_ref, pack_in, far_ref, near_ref, pack_ref):
    even = is_even(place_ref)
    for field in range(pack_ref.shape[0]):
        near, far = near_ref[field], far_ref[field]
        first = jnp.where(even, far, near)
        last = jnp.where(even, near, far)
        pack_ref[field, :HALF] = (
            pack_in[field] + ends(first) + roll(ends(last), 16 * (NODES - 1), 1)
        )
        if pack_ref.shape[1] > HALF:
            pack_ref[field, HALF:ROWS] = edge(first)
            pack_ref[field, ROWS:] = edge(last)


def beside(place_ref, packs_ref):
    count = packs_ref.shape[0]
    here = place_ref[1]
    return lax.rem(here + count - 1, count), lax.rem(here + 1, count)


def completed(place_ref, kv, halo, field=0):
    far_ref, near_ref = halo[:2]
    even = is_even(place_ref)
    near, far = near_ref[field], far_ref[field]
    lane = lane_iota(HALF)
    if len(halo) > 2:
        left, right = beside(place_ref, halo[2])
        side = jnp.where(
            lane % 16 < 8,
            roll(halo[2][left, field, :HALF], 8, 1),
            roll(halo[2][right, field, :HALF], -8, 1),
        )

    def value(i):
        u = kv[i]
        if len(halo) > 2:
            piece = roll(side, -16 * i, 1) if i else side
            u = u + jnp.concatenate(
                [jnp.where(lane < 8, piece, 0.0), jnp.where(lane >= 120, piece, 0.0)], axis=0
            )
        if i == 0:
            u = u + jnp.where(even, far, near)
        if i == NODES - 1:
            u = u + jnp.where(even, near, far)
        return u

    return value


def ghost_sums(place_ref, packs_ref, field=0):
    left, right = beside(place_ref, packs_ref)
    lane = lane_iota(HALF)
    own = packs_ref[place_ref[1], field, :HALF]
    lines = jnp.where(lane % 16 < 8, own, roll(own, 16, 1))
    inner = (lane >= 56) & (lane < 72)

    def value(i):
        u = jnp.where(inner, roll(lines, 56 - 16 * i, 1), 0.0)
        if i in (0, NODES - 1):
            rows = slice(HALF, ROWS) if i == 0 else slice(ROWS, GROWS)
            u = u + facing(packs_ref[left, field, rows], packs_ref[right, field, rows])
        return u

    return value


def apply_element(v_ref, metric_ref, ghost_ref, grad_ref, diver_ref, flux_ref, out_ref):
    count = v_ref.shape[1]
    side = dot_split(v_ref[...].reshape(NODES * count, LANES), grad_ref)
    flux_ref[0] = side[:, :LANES]
    flux_ref[1] = side[:, LANES:]
    for chunk in range(count // 8):
        rows = pl.ds(chunk * 8, 8)
        if chunk < ROWS // 8:
            geometry, there = metric_ref, rows
        else:
            geometry, there = ghost_ref, pl.ds(chunk * 8 - ROWS, 8)
        values = [v_ref[i, rows] for i in range(NODES)]
        grad_z = along_nodes(values, DERIV)
        flux_z = []
        for i in range(NODES):
            at = pl.ds(i * count + chunk * 8, 8)
            g_z, g_a, g_r = grad_z[i], flux_ref[0, at], flux_ref[1, at]
            m = [geometry[c, i, there] for c in range(6)]
            flux_z.append(m[0] * g_z + m[3] * g_a + m[4] * g_r)
            flux_ref[0, at] = m[3] * g_z + m[1] * g_a + m[5] * g_r
            flux_ref[1, at] = m[4] * g_z + m[5] * g_a + m[2] * g_r
        part_z = along_nodes(flux_z, DERIV.T)
        for i in range(NODES):
            out_ref[i, rows] = part_z[i] + geometry[6, i, there] * values[i]
    flux = jnp.concatenate([flux_ref[0], flux_ref[1]], axis=1)
    out_ref[...] += dot_split(flux, diver_ref).reshape(out_ref.shape)


def weight_plane():
    lane, row = lane_iota(ROWS), row_iota(ROWS)
    j, k, er = (lane // 8) % 8, lane % 8, row % HALF
    w_a = jnp.where((j == 0) | (j == 7), 0.5, 1.0)
    shared = ((k == 0) & (er > 0)) | ((k == 7) & (er < HALF - 1))
    return w_a * jnp.where(shared, 0.5, 1.0)


def node_weight(i):
    return 0.5 if i in (0, NODES - 1) else 1.0


def sum_row(sums):
    lane = lane_iota(1)
    row = jnp.zeros((1, LANES), jnp.float32)
    for d, value in enumerate(sums):
        row = jnp.where(lane == d, jnp.sum(value), row)
    return row


SIGMA = ((INTERVAL_HIGH + INTERVAL_LOW) / 2.0) / ((INTERVAL_HIGH - INTERVAL_LOW) / 2.0)
CENTER = (INTERVAL_HIGH + INTERVAL_LOW) / 2.0
HALF_WIDTH = (INTERVAL_HIGH - INTERVAL_LOW) / 2.0
RHO0 = 1.0 / SIGMA
RHO1 = 1.0 / (2.0 * SIGMA - RHO0)
RHO2 = 1.0 / (2.0 * SIGMA - RHO1)


STEP1 = 2.0 * RHO1 / HALF_WIDTH
STEP2 = 2.0 * RHO2 / HALF_WIDTH


def place_kernel(
    place_ref, order_hbm, load_hbm, geom_hbm, abs_hbm,
    metric_ref, load_kv, bound_kv, far_ref, near_ref, pack_ref, lo_ref, hi_ref,
    flux_ref, work_ref, order_ref, load_ref, geom_ref, abs_ref, sems,
):
    copies = [
        pltpu.make_async_copy(source, target, sems.at[c])
        for c, (source, target) in enumerate(
            [(order_hbm, order_ref), (load_hbm, load_ref), (geom_hbm, geom_ref), (abs_hbm, abs_ref)]
        )
    ]
    for copy in copies:
        copy.start()
    copies[0].wait()
    copies[1].wait()
    pick = jnp.where(
        lax.broadcasted_iota(jnp.int32, (64, 64), 0) == order_ref[...], 1.0, 0.0
    ).astype(jnp.bfloat16)
    low = lane_iota(ROWS) < 64

    def spread(placed, store):
        for b in range(4):
            piece = placed[:, b * LANES : (b + 1) * LANES]
            first, second = piece[:ROWS], piece[ROWS:]
            store(2 * b, jnp.where(low, first, roll(second, 64, 1)))
            store(2 * b + 1, jnp.where(low, roll(first, 64, 1), second))

    load = load_ref[...]
    high, rest = split(load)
    middle = (load - high.astype(jnp.float32) - rest.astype(jnp.float32)).astype(jnp.bfloat16)

    def store_load(i, value):
        work_ref[i] = value

    spread(dot(pick, high) + (dot(pick, rest) + dot(pick, middle)), store_load)
    even = is_even(place_ref)
    store_assembled(
        load_kv, far_ref, near_ref, even, lambda i: work_ref[i], 0, pack_ref
    )
    store_edges(lo_ref, hi_ref, 7, [edge(load_kv[i]) for i in range(NODES)])

    copies[2].wait()
    for c in range(7):

        def store_metric(i, value, c=c):
            metric_ref[c, i] = value

        spread(dot(pick, geom_ref[c]), store_metric)
        store_edges(lo_ref, hi_ref, c, [edge(metric_ref[c, i]) for i in range(NODES)])

    lane = lane_iota(8)
    q_a = jnp.zeros((8, LANES), jnp.float32)
    q_r = jnp.zeros((8, LANES), jnp.float32)
    for m in range(NODES):
        q_a = jnp.where((lane // 8) % 8 == m, float(ROW_TOTAL[m]), q_a)
        q_r = jnp.where(lane % 8 == m, float(ROW_TOTAL[m]), q_r)
    for chunk in range(ROWS // 8):
        rows = pl.ds(chunk * 8, 8)
        h_z = []
        for i in range(NODES):
            at = pl.ds(i * ROWS + chunk * 8, 8)
            q_z = float(ROW_TOTAL[i])
            g = [jnp.abs(metric_ref[c, i, rows]) for c in range(6)]
            h_z.append(g[0] * q_z + g[3] * q_a + g[4] * q_r)
            flux_ref[0, at] = g[3] * q_z + g[1] * q_a + g[5] * q_r
            flux_ref[1, at] = g[4] * q_z + g[5] * q_a + g[2] * q_r
        part_z = along_nodes_plain(h_z, ABS_DERIV.T)
        for i in range(NODES):
            work_ref[i, rows] = part_z[i] + jnp.abs(metric_ref[6, i, rows])
    flux = jnp.concatenate([flux_ref[0], flux_ref[1]], axis=1)
    copies[3].wait()
    work_ref[...] += dot_split(flux, abs_ref).reshape(FIELD)
    store_assembled(
        bound_kv, far_ref, near_ref, even, lambda i: work_ref[i], 1, pack_ref
    )
    store_edges(lo_ref, hi_ref, 8, [edge(bound_kv[i]) for i in range(NODES)])


def first_kernel(
    place_ref, load_kv, bound_kv, h0, h1, h2, left_ref, right_ref, metric_ref, grad_ref, diver_ref,
    residual_ref, inverse_ref, update_ref, ghost_inverse, ghost_metric, kv_ref, far_ref, near_ref,
    v_ref, flux_ref, work_ref,
):
    residual = completed(place_ref, load_kv, (h0, h1, h2), 0)
    bound = completed(place_ref, bound_kv, (h0, h1, h2), 1)
    for i in range(NODES):
        r = residual(i)
        inverse = 1.0 / bound(i)
        update = r * inverse * (1.0 / CENTER)
        residual_ref[i] = r
        inverse_ref[i] = inverse
        update_ref[i] = update
        v_ref[i, :ROWS] = update
    residual, residual_sums = ghost_columns(left_ref, right_ref, 7), ghost_sums(place_ref, h2, 0)
    bound, bound_sums = ghost_columns(left_ref, right_ref, 8), ghost_sums(place_ref, h2, 1)
    for i in range(NODES):
        inverse = 1.0 / (bound[i] + bound_sums(i))
        ghost_inverse[i] = inverse
        v_ref[i, ROWS:] = (residual[i] + residual_sums(i)) * inverse * (1.0 / CENTER)
    for c in range(7):
        for i, value in enumerate(ghost_columns(left_ref, right_ref, c)):
            ghost_metric[c, i] = value
    apply_element(v_ref, metric_ref, ghost_metric, grad_ref, diver_ref, flux_ref, work_ref)
    store_assembled(kv_ref, far_ref, near_ref, is_even(place_ref), lambda i: work_ref[i])


def second_kernel(
    place_ref, kv_in, h0, h1, source_ref, inverse_ref, update_in, metric_ref, grad_ref, diver_ref,
    start_ref, kv_ref, far_ref, near_ref, pack_ref, lo_ref, hi_ref, v_ref, flux_ref, work_ref,
):
    image = completed(place_ref, kv_in, (h0, h1))
    for i in range(NODES):
        old = update_in[i]
        inverse = inverse_ref[i]
        source = source_ref[i]
        update = (RHO1 * RHO0) * old + STEP1 * inverse * (source - image(i))
        result = old + update
        v_ref[i] = result
        start_ref[i] = result + (RHO2 * RHO1) * update + STEP2 * inverse * source
    apply_element(v_ref, metric_ref, None, grad_ref, diver_ref, flux_ref, work_ref)
    store_assembled(
        kv_ref, far_ref, near_ref, is_even(place_ref), lambda i: work_ref[i], 0, pack_ref
    )
    store_edges(
        lo_ref, hi_ref, 0,
        [edge(start_ref[i] - STEP2 * inverse_ref[i] * kv_ref[i]) for i in range(NODES)],
    )


def third_kernel(
    place_ref, kv_in, h0, h1, h2, left_ref, right_ref, source_ref, inverse_ref, start_ref,
    ghost_inverse, ghost_metric, metric_ref, grad_ref, diver_ref,
    result_ref, kv_ref, far_ref, near_ref, sums_ref, v_ref, flux_ref, work_ref,
):
    image = completed(place_ref, kv_in, (h0, h1, h2))
    plane = weight_plane()
    rz = jnp.zeros((ROWS, LANES), jnp.float32)
    for i in range(NODES):
        result = start_ref[i] - STEP2 * inverse_ref[i] * image(i)
        result_ref[i] = result
        v_ref[i, :ROWS] = result
        rz = rz + source_ref[i] * result * node_weight(i)
    start, sums = ghost_columns(left_ref, right_ref, 0), ghost_sums(place_ref, h2)
    for i in range(NODES):
        v_ref[i, ROWS:] = start[i] - STEP2 * ghost_inverse[i] * sums(i)
    apply_element(v_ref, metric_ref, ghost_metric, grad_ref, diver_ref, flux_ref, work_ref)
    energy = jnp.zeros((ROWS, LANES), jnp.float32)
    for i in range(NODES):
        energy = energy + result_ref[i] * work_ref[i, :ROWS]
    sums_ref[...] = sum_row([rz * plane, energy])
    store_assembled(kv_ref, far_ref, near_ref, is_even(place_ref), lambda i: work_ref[i])


def fourth_kernel(
    place_ref, kv_in, h0, h1, inverse_ref, metric_ref, grad_ref, diver_ref,
    image_ref, update_ref, kv_ref, far_ref, near_ref, pack_ref, lo_ref, hi_ref, flux_ref, work_ref,
):
    image = completed(place_ref, kv_in, (h0, h1))
    for i in range(NODES):
        value = image(i)
        image_ref[i] = value
        update_ref[i] = value * inverse_ref[i] * (1.0 / CENTER)
    apply_element(update_ref, metric_ref, None, grad_ref, diver_ref, flux_ref, work_ref)
    store_assembled(
        kv_ref, far_ref, near_ref, is_even(place_ref), lambda i: work_ref[i], 0, pack_ref
    )
    scale = 1.0 + RHO1 * RHO0 + STEP1 * CENTER
    store_edges(
        lo_ref, hi_ref, 0,
        [edge(scale * update_ref[i] - STEP1 * inverse_ref[i] * kv_ref[i]) for i in range(NODES)],
    )


def fifth_kernel(
    place_ref, kv_in, h0, h1, h2, left_ref, right_ref, source_ref, inverse_ref, update_in,
    ghost_inverse, ghost_metric, metric_ref, grad_ref, diver_ref,
    start_ref, kv_ref, far_ref, near_ref, v_ref, flux_ref, work_ref,
):
    image = completed(place_ref, kv_in, (h0, h1, h2))
    for i in range(NODES):
        old = update_in[i]
        inverse = inverse_ref[i]
        source = source_ref[i]
        update = (RHO1 * RHO0) * old + STEP1 * inverse * (source - image(i))
        result = old + update
        v_ref[i, :ROWS] = result
        start_ref[i] = result + (RHO2 * RHO1) * update + STEP2 * inverse * source
    start, sums = ghost_columns(left_ref, right_ref, 0), ghost_sums(place_ref, h2)
    for i in range(NODES):
        v_ref[i, ROWS:] = start[i] - STEP1 * ghost_inverse[i] * sums(i)
    apply_element(v_ref, metric_ref, ghost_metric, grad_ref, diver_ref, flux_ref, work_ref)
    store_assembled(kv_ref, far_ref, near_ref, is_even(place_ref), lambda i: work_ref[i])


def sixth_kernel(
    place_ref, kv_in, h0, h1, source_ref, inverse_ref, start_ref, residual_ref, first_ref, early_ref,
    metric_ref, grad_ref, diver_ref,
    result_ref, kv_ref, far_ref, near_ref, pack_ref, sums_ref, flux_ref, work_ref,
):
    image = completed(place_ref, kv_in, (h0, h1))
    plane = weight_plane()
    r_y = jnp.zeros((ROWS, LANES), jnp.float32)
    w_y = jnp.zeros((ROWS, LANES), jnp.float32)
    for i in range(NODES):
        result = start_ref[i] - STEP2 * inverse_ref[i] * image(i)
        result_ref[i] = result
        r_y = r_y + residual_ref[i] * result * node_weight(i)
        w_y = w_y + source_ref[i] * result * node_weight(i)
    apply_element(result_ref, metric_ref, None, grad_ref, diver_ref, flux_ref, work_ref)
    z_ky = jnp.zeros((ROWS, LANES), jnp.float32)
    y_ky = jnp.zeros((ROWS, LANES), jnp.float32)
    for i in range(NODES):
        z_ky = z_ky + first_ref[i] * work_ref[i]
        y_ky = y_ky + result_ref[i] * work_ref[i]
    zero = jnp.zeros((1, LANES), jnp.float32)
    late = sum_row([zero, zero, r_y * plane, w_y * plane, z_ky, y_ky])
    sums_ref[...] = jnp.broadcast_to(early_ref[...] + late, sums_ref.shape)
    store_assembled(
        kv_ref, far_ref, near_ref, is_even(place_ref), lambda i: work_ref[i], 0, pack_ref
    )


def last_kernel(
    place_ref, kv_in, h0, h1, h2, sums_ref, order_ref,
    residual_ref, first_ref, image_ref, second_ref,
    solution_ref, residual_out, spread_ref,
):
    sums = jnp.sum(sums_ref[...], axis=0, keepdims=True)
    lane = lane_iota(1)

    def total(d):
        return jnp.sum(jnp.where(lane == d, sums, 0.0), axis=1, keepdims=True)

    rz0, zw, ry, wy, zq, yq = (total(d) for d in range(6))
    alpha0 = rz0 / zw
    rz1 = rz0 - alpha0 * (zw + ry) + alpha0 * alpha0 * wy
    beta = rz1 / rz0
    share = 1.0 + beta
    energy = share * share * zw - 2.0 * share * alpha0 * zq + alpha0 * alpha0 * yq
    alpha1 = rz1 / energy
    first_scale = alpha0 + alpha1 * share
    second_scale = alpha1 * alpha0
    image = completed(place_ref, kv_in, (h0, h1, h2))
    low = lane_iota(ROWS) < 64
    for b in range(4):
        pair = []
        for i in (2 * b, 2 * b + 1):
            x = first_scale * first_ref[i] - second_scale * second_ref[i]
            r = residual_ref[i] - first_scale * image_ref[i] + second_scale * image(i)
            pair.append((x, r))
        for f in range(2):
            even, odd = pair[0][f], pair[1][f]
            lanes = pl.ds(b * LANES, LANES)
            spread_ref[f, :ROWS, lanes] = jnp.where(low, even, roll(odd, 64, 1))
            spread_ref[f, ROWS:, lanes] = jnp.where(low, roll(even, 64, 1), odd)
    pick = jnp.where(
        lax.broadcasted_iota(jnp.int32, (64, 64), 1) == order_ref[...], 1.0, 0.0
    ).astype(jnp.bfloat16)
    for f, out in ((0, solution_ref), (1, residual_out)):
        value = spread_ref[f]
        high, middle = split(value)
        rest = (value - high.astype(jnp.float32) - middle.astype(jnp.float32)).astype(jnp.bfloat16)
        out[...] = dot(pick, high) + (dot(pick, middle) + dot(pick, rest))


VMEM_LIMIT = 24 * 1024 * 1024
F32 = jnp.float32


def call(kernel, place, outs, scratch, *operands, space=pltpu.VMEM):
    vmem = pl.BlockSpec(memory_space=pltpu.VMEM)
    return pl.pallas_call(
        kernel,
        out_shape=[jax.ShapeDtypeStruct(s, F32) for s in outs],
        in_specs=[pl.BlockSpec(memory_space=pltpu.SMEM)]
        + [pl.BlockSpec(memory_space=space)] * len(operands),
        out_specs=[vmem] * len(outs),
        scratch_shapes=[pltpu.VMEM(s, F32) if isinstance(s, tuple) else s for s in scratch],
        compiler_params=pltpu.CompilerParams(vmem_limit_bytes=VMEM_LIMIT),
    )(place, *operands)


FLUX = (2, NODES * ROWS, LANES)
BIG_FLUX = (2, NODES * GROWS, LANES)


def faces(fields=1):
    return [(fields, ROWS, LANES), (fields, ROWS, LANES)]


def packs(fields=1):
    return [(fields, HALF, LANES)]


def swap_wide(far, near):
    count = lax.axis_size(WIDE)
    far = lax.ppermute(
        far, WIDE, [(w, (w + 1 if w % 2 else w - 1) % count) for w in range(count)]
    )
    near = lax.ppermute(near, WIDE, [(w, w ^ 1) for w in range(count)])
    return far, near


def swap_all(place, far, near, pack, rows):
    far, near = swap_wide(far, near)
    (pack,) = call(pack_kernel, place, [(pack.shape[0], rows, LANES)], [], pack, far, near)
    return far, near, lax.all_gather(pack, "narrow")


def edges(fields=1):
    return [(fields, NODES // 2, HALF, LANES)] * 2


def swap_edges(lo, hi):
    count = lax.axis_size("narrow")
    left = lax.ppermute(hi, "narrow", [(n, (n + 1) % count) for n in range(count)])
    right = lax.ppermute(lo, "narrow", [(n, (n - 1) % count) for n in range(count)])
    return left, right


def local(load, geom, element_order):
    place = jnp.stack([lax.axis_index(WIDE) % 2, lax.axis_index("narrow")]).astype(jnp.int32)
    grad = jnp.asarray(GRAD_HL)
    diver = jnp.asarray(DIVER_HL)
    metric, load_kv, bound_kv, *face, lo, hi = call(
        place_kernel, place,
        [(7,) + FIELD, FIELD, FIELD] + faces(2) + packs(2) + edges(9),
        [
            FLUX, FIELD,
            pltpu.VMEM((1, 64), jnp.int32), pltpu.VMEM(load.shape, load.dtype),
            pltpu.VMEM(geom.shape, geom.dtype), pltpu.VMEM(ABS_HL.shape, jnp.bfloat16),
            pltpu.SemaphoreType.DMA((4,)),
        ],
        *(pltpu.with_memory_space_constraint(x, pltpu.HBM) for x in (element_order.reshape(1, 64), load, geom, jnp.asarray(ABS_HL))),
        space=pltpu.HBM,
    )
    sides = swap_edges(lo, hi)
    halo = swap_all(place, *face, GROWS)
    residual, inverse, update, ghost_inverse, ghost_metric, kv, *face = call(
        first_kernel, place,
        [FIELD, FIELD, FIELD, GHOST, (7,) + GHOST, FIELD] + faces(),
        [BIG, BIG_FLUX, BIG],
        load_kv, bound_kv, *halo, *sides, metric, grad, diver,
    )
    halo = swap_wide(*face)
    start, kv, *face, lo, hi = call(
        second_kernel, place,
        [FIELD, FIELD] + faces() + packs() + edges(),
        [FIELD, FLUX, FIELD],
        kv, *halo, residual, inverse, update, metric, grad, diver,
    )
    sides = swap_edges(lo, hi)
    halo = swap_all(place, *face, GROWS)
    first, kv, *face, early = call(
        third_kernel, place,
        [FIELD, FIELD] + faces() + [(1, LANES)],
        [BIG, BIG_FLUX, BIG],
        kv, *halo, *sides, residual, inverse, start, ghost_inverse, ghost_metric, metric, grad, diver,
    )
    halo = swap_wide(*face)
    image, update, kv, *face, lo, hi = call(
        fourth_kernel, place,
        [FIELD, FIELD, FIELD] + faces() + packs() + edges(),
        [FLUX, FIELD],
        kv, *halo, inverse, metric, grad, diver,
    )
    sides = swap_edges(lo, hi)
    halo = swap_all(place, *face, GROWS)
    start, kv, *face = call(
        fifth_kernel, place,
        [FIELD, FIELD] + faces(),
        [BIG, BIG_FLUX, BIG],
        kv, *halo, *sides, image, inverse, update, ghost_inverse, ghost_metric, metric, grad, diver,
    )
    halo = swap_wide(*face)
    second, kv, *face, sums = call(
        sixth_kernel, place,
        [FIELD, FIELD] + faces() + packs() + [(lax.axis_size(REST), LANES)],
        [FLUX, FIELD],
        kv, *halo, image, inverse, start, residual, first, early, metric, grad, diver,
    )
    halo = swap_all(place, *face, HALF)
    sums = lax.all_to_all(sums, REST, 0, 0)
    sums = jnp.broadcast_to(
        jnp.sum(sums, axis=0, keepdims=True), (lax.axis_size("ring"), LANES)
    )
    sums = lax.all_to_all(sums, "ring", 0, 0)
    return tuple(
        call(
            last_kernel, place,
            [(64, 512), (64, 512)],
            [(2, 64, 512)],
            kv, *halo, sums, element_order.reshape(64, 1), residual, first, image, second,
        )
    )


def solution(mesh):
    wide, narrow = mesh.devices.shape
    ring = 12 if wide % 12 == 0 else 2
    fine = jax.sharding.Mesh(
        mesh.devices.reshape(wide // ring, ring, narrow), ("outer", "ring", "narrow")
    )
    rows = ("outer", "ring", "narrow")
    return jax.shard_map(
        local,
        mesh=fine,
        in_specs=(P(rows, None), P(None, rows, None), P(WIDE, "narrow", None)),
        out_specs=(P(rows, None), P(rows, None)),
        check_vma=False,
    )
```

time: 165 us -> 156 us (0.945)
  starting transfers between devices: 78.2 us -> 95.8 us
  blocking collectives: 44.3 us -> 26.9 us
  waiting for transfers between devices: 19.4 us -> 13 us
  local copies, waits for them, and re-layouts: 4.19 us -> 1.35 us
    all_gather x7 -> x4, blocking collectives: 44.3 us -> 26.9 us  [swap_all(): return (far, near, lax.all_gather(pack, 'narrow'))]
    ppermute x14 -> x20, starting transfers between devices: 69.9 us -> 86.4 us  [the longest x7 47.4 us: swap_wide(): lax.ppermute(far, WIDE, [(w, (w + 1 if w % 2 else w - 1) % count) for w i...]
    ppermute x14 -> x20, waiting for transfers between devices: 17 us -> 11.3 us  [the longest x7 8.5 us: swap_wide(): lax.ppermute(far, WIDE, [(w, (w + 1 if w % 2 else w - 1) % count) for w i...]
    unnamed x13 -> x7, local copies, waits for them, and re-layouts: 3.49 us -> 0.66 us
    pallas_call x15 -> x12, Pallas kernels: 17.2 us -> 17.2 us  [call(): pl.pallas_call(kernel, out_shape=[jax.ShapeDtypeStruct(s, F32) for s in o...]
  transfers between devices with their start and end apart: 16 -> 22, of which waited for: 9 -> 5; matrix products, arithmetic and copies ran while one was open for 0% -> 1% of each run, Pallas kernels for 0% -> 2%
where the time goes in v3:
time: 156 us; the launch traced here: 155 us
  starting transfers between devices  95.8 us (61%)
  blocking collectives  26.9 us (17%)
  Pallas kernels  17.2 us (11%)
  waiting for transfers between devices  13 us (8%)
    ppermute x7, starting transfers between devices, swap_wide(): lax.ppermute(far, WIDE, [(w, (w + 1 if w % 2 else w - 1) % count) for w i...  47.4 us
    all_gather x4, blocking collectives, swap_all(): return (far, near, lax.all_gather(pack, 'narrow'))  26.9 us
    pallas_call x12, Pallas kernels, call(): pl.pallas_call(kernel, out_shape=[jax.ShapeDtypeStruct(s, F32) for s in o...  17.2 us
    ppermute x3, starting transfers between devices, swap_edges(): lax.ppermute(lo, 'narrow', [(n, (n - 1) % count) for n in range(count)])  13.7 us
    ppermute x7, starting transfers between devices, swap_wide(): near = lax.ppermute(near, WIDE, [(w, w ^ 1) for w in range(count)])  13.4 us
    ppermute x3, starting transfers between devices, swap_edges(): lax.ppermute(hi, 'narrow', [(n, (n + 1) % count) for n in range(count)])  11.9 us
    ppermute x7, waiting for transfers between devices, swap_wide(): lax.ppermute(far, WIDE, [(w, (w + 1 if w % 2 else w - 1) % count) for w i...  8.5 us
    all_to_all x1, starting transfers between devices, local(): sums = lax.all_to_all(sums, REST, 0, 0)  5.96 us
  transfers between devices with their start and end apart: 22, of which 5 were waited for; matrix products, arithmetic and copies ran while one was open for 1% of the time, Pallas kernels for 2%

profile of v3, /device:TPU:1, one launch (start us, length us, event | category | flops | bytes accessed | tf_op | source)
XLA Modules:
  0.0 155.4 jit_solution(10526876943268358319)
XLA Ops:
  0.6 0.1 pad_add_fusion.place_ref
  0.7 3.2 %shard_map.77 = (f32[7,8,32,128]{3,2,1,0:T(8,128)S(1)}, f32[8,32,128]{2,1,0:T(8,128)S(1)}, f32[8,32,128]{2,1,0:T(8,128)S(1)}, f32[2,32,128]{2,1,0:T(8,128)S(1)},...) custom-call(s32[2]{0:T(128)S(1)} %pad_add_fusion.place_ref, ...), custom_call_target="tpu_custom_call" | custom-call | tf_op jit(solution)/shard_map/pallas_call | solution.py:630
  4.0 4.5 %collective-permute-start.2 = (f32[9,4,16,128]{3,2,1,0:T(8,128)S(1)}, f32[9,4,16,128]{3,2,1,0:T(8,128)S(1)}, u32[]{:S(2)}, u32[]{:S(2)}) collective-permute-start(f32[9,4,16,128]{3,2,1,0:T(8,128)S(1)} %get-tuple-element.53), channel_id=1, source_target_pairs={{0,1},{1,2},{2,3},{3,0},{4,5},{5,6},{6,7},{7,4},{8,9},{9,10},{10,1... | collective-permute-start | bytes 884744 | tf_op jit(solution)/shard_map/ppermute | solution.py:674
  8.5 9.8 %collective-permute-start.3 = (f32[9,4,16,128]{3,2,1,0:T(8,128)S(1)}, f32[9,4,16,128]{3,2,1,0:T(8,128)S(1)}, u32[]{:S(2)}, u32[]{:S(2)}) collective-permute-start(f32[9,4,16,128]{3,2,1,0:T(8,128)S(1)} %get-tuple-element.54), channel_id=1, source_target_pairs={{0,3},{1,0},{2,1},{3,2},{4,7},{5,4},{6,5},{7,6},{8,11},{9,8},{10,9... | collective-permute-start | bytes 884744 | tf_op jit(solution)/shard_map/ppermute | solution.py:675
  18.3 11.5 %collective-permute-start = (f32[2,32,128]{2,1,0:T(8,128)S(1)}, f32[2,32,128]{2,1,0:T(8,128)S(1)}, u32[]{:S(2)}, u32[]{:S(2)}) collective-permute-start(f32[2,32,128]{2,1,0:T(8,128)S(1)} %get-tuple-element.50), channel_id=1, source_target_pairs={{0,764},{4,8},{8,4},{12,16},{16,12},{20,24},{24,20},{28,32},{32,28... | collective-permute-start | bytes 98312 | tf_op jit(solution)/shard_map/ppermute | solution.py:655
  29.8 1.9 %collective-permute-start.1 = (f32[2,32,128]{2,1,0:T(8,128)S(1)}, f32[2,32,128]{2,1,0:T(8,128)S(1)}, u32[]{:S(2)}, u32[]{:S(2)}) collective-permute-start(f32[2,32,128]{2,1,0:T(8,128)S(1)} %get-tuple-element.51), channel_id=1, source_target_pairs={{0,4},{4,0},{8,12},{12,8},{16,20},{20,16},{24,28},{28,24},{32,36},... | collective-permute-start | bytes 98312 | tf_op jit(solution)/shard_map/ppermute | solution.py:658
  31.7 2.7 %collective-permute-done.1.near_ref.h1 = f32[2,32,128]{2,1,0:T(8,128)S(1)} collective-permute-done((f32[2,32,128]{2,1,0:T(8,128)S(1)}, f32[2,32,128]{2,1,0:T(8,128)S(1)}, u32[]{:S(2)}, u32[]{:S(2)}) %collective-permute-start.1) | collective-permute-done | bytes 32800 | tf_op jit(solution)/shard_map/ppermute | solution.py:658
  34.5 0.6 shard_map.78
  35.1 7.9 %all-gather = f32[8,48,128]{2,1,0:T(8,128)S(1)} all-gather(f32[2,48,128]{2,1,0:T(8,128)S(1)} %shard_map.78), channel_id=2, replica_groups=mesh['outer'=16,'ring'=12,'narrow'=4] {'narrow'}, dimensions={0}, use_global_device_ids=true | all-gather | bytes 245760 | tf_op jit(solution)/shard_map/all_gather | solution.py:665
  43.0 1.7 %shard_map.79 = (f32[8,32,128]{2,1,0:T(8,128)S(1)}, f32[8,32,128]{2,1,0:T(8,128)S(1)}, f32[8,32,128]{2,1,0:T(8,128)S(1)}, f32[8,16,128]{2,1,0:T(8,128)S(1)}, f32...) custom-call(s32[2]{0:T(128)S(1)} %pad_add_fusion.place_ref, ...), custom_call_target="tpu_custom_call" | custom-call | tf_op jit(solution)/shard_map/pallas_call | solution.py:630
  44.7 5.4 %collective-permute-start.4 = (f32[1,32,128]{2,1,0:T(8,128)S(1)}, f32[1,32,128]{2,1,0:T(8,128)S(1)}, u32[]{:S(2)}, u32[]{:S(2)}) collective-permute-start(f32[1,32,128]{2,1,0:T(8,128)S(1)} %get-tuple-element.57), channel_id=1, source_target_pairs={{0,764},{4,8},{8,4},{12,16},{16,12},{20,24},{24,20},{28,32},{32,28... | collective-permute-start | bytes 49160 | tf_op jit(solution)/shard_map/ppermute | solution.py:655
  50.1 1.9 %collective-permute-start.5 = (f32[1,32,128]{2,1,0:T(8,128)S(1)}, f32[1,32,128]{2,1,0:T(8,128)S(1)}, u32[]{:S(2)}, u32[]{:S(2)}) collective-permute-start(f32[1,32,128]{2,1,0:T(8,128)S(1)} %get-tuple-element.58), channel_id=1, source_target_pairs={{0,4},{4,0},{8,12},{12,8},{16,20},{20,16},{24,28},{28,24},{32,36},... | collective-permute-start | bytes 49160 | tf_op jit(solution)/shard_map/ppermute | solution.py:658
  52.1 2.8 %collective-permute-done.4.h0 = f32[1,32,128]{2,1,0:T(8,128)S(1)} collective-permute-done((f32[1,32,128]{2,1,0:T(8,128)S(1)}, f32[1,32,128]{2,1,0:T(8,128)S(1)}, u32[]{:S(2)}, u32[]{:S(2)}) %collective-permute-start.4) | collective-permute-done | bytes 16416 | tf_op jit(solution)/shard_map/ppermute | solution.py:655
  54.9 1.4 shard_map.80
  56.3 5.6 %collective-permute-start.6 = (f32[1,32,128]{2,1,0:T(8,128)S(1)}, f32[1,32,128]{2,1,0:T(8,128)S(1)}, u32[]{:S(2)}, u32[]{:S(2)}) collective-permute-start(f32[1,32,128]{2,1,0:T(8,128)S(1)} %get-tuple-element.63), channel_id=1, source_target_pairs={{0,764},{4,8},{8,4},{12,16},{16,12},{20,24},{24,20},{28,32},{32,28... | collective-permute-start | bytes 49160 | tf_op jit(solution)/shard_map/ppermute | solution.py:655
  61.9 1.9 %collective-permute-start.7 = (f32[1,32,128]{2,1,0:T(8,128)S(1)}, f32[1,32,128]{2,1,0:T(8,128)S(1)}, u32[]{:S(2)}, u32[]{:S(2)}) collective-permute-start(f32[1,32,128]{2,1,0:T(8,128)S(1)} %get-tuple-element.64), channel_id=1, source_target_pairs={{0,4},{4,0},{8,12},{12,8},{16,20},{20,16},{24,28},{28,24},{32,36},... | collective-permute-start | bytes 49160 | tf_op jit(solution)/shard_map/ppermute | solution.py:658
  63.8 3.7 %collective-permute-start.8 = (f32[1,4,16,128]{3,2,1,0:T(8,128)S(1)}, f32[1,4,16,128]{3,2,1,0:T(8,128)S(1)}, u32[]{:S(2)}, u32[]{:S(2)}) collective-permute-start(f32[1,4,16,128]{3,2,1,0:T(8,128)S(1)} %get-tuple-element.66), channel_id=1, source_target_pairs={{0,1},{1,2},{2,3},{3,0},{4,5},{5,6},{6,7},{7,4},{8,9},{9,10},{10,1... | collective-permute-start | bytes 98312 | tf_op jit(solution)/shard_map/ppermute | solution.py:674
  67.5 1.9 %collective-permute-start.9 = (f32[1,4,16,128]{3,2,1,0:T(8,128)S(1)}, f32[1,4,16,128]{3,2,1,0:T(8,128)S(1)}, u32[]{:S(2)}, u32[]{:S(2)}) collective-permute-start(f32[1,4,16,128]{3,2,1,0:T(8,128)S(1)} %get-tuple-element.67), channel_id=1, source_target_pairs={{0,3},{1,0},{2,1},{3,2},{4,7},{5,4},{6,5},{7,6},{8,11},{9,8},{10,9... | collective-permute-start | bytes 98312 | tf_op jit(solution)/shard_map/ppermute | solution.py:675
  69.5 0.6 shard_map.81
  70.1 6.7 %all-gather.1 = f32[4,48,128]{2,1,0:T(8,128)S(1)} all-gather(f32[1,48,128]{2,1,0:T(8,128)S(1)} %shard_map.81), channel_id=3, replica_groups=mesh['outer'=16,'ring'=12,'narrow'=4] {'narrow'}, dimensions={0}, use_global_device_ids=true | all-gather | bytes 122880 | tf_op jit(solution)/shard_map/all_gather | solution.py:665
  76.8 1.7 %shard_map.82 = (f32[8,32,128]{2,1,0:T(8,128)S(1)}, f32[8,32,128]{2,1,0:T(8,128)S(1)}, f32[1,32,128]{2,1,0:T(8,128)S(1)}, f32[1,32,128]{2,1,0:T(8,128)S(1)}, f32[1,128]{1,0:T(1,128)S(1)}) custom-call(s32[2]{0:T(128)S(1)} %pad_add_fusion.place_ref, f32[8,32,128]{2,1,0:T(8,128)S(1)} %get-tuple-element.62.kv_in, ...), custom_call_target="tpu_custom_call" | custom-call | tf_op jit(solution)/shard_map/pallas_call | solution.py:630
  78.5 5.4 %collective-permute-start.10 = (f32[1,32,128]{2,1,0:T(8,128)S(1)}, f32[1,32,128]{2,1,0:T(8,128)S(1)}, u32[]{:S(2)}, u32[]{:S(2)}) collective-permute-start(f32[1,32,128]{2,1,0:T(8,128)S(1)} %get-tuple-element.72), channel_id=1, source_target_pairs={{0,764},{4,8},{8,4},{12,16},{16,12},{20,24},{24,20},{28,32},{32,28... | collective-permute-start | bytes 49160 | tf_op jit(solution)/shard_map/ppermute | solution.py:655
  83.9 1.9 %collective-permute-start.11 = (f32[1,32,128]{2,1,0:T(8,128)S(1)}, f32[1,32,128]{2,1,0:T(8,128)S(1)}, u32[]{:S(2)}, u32[]{:S(2)}) collective-permute-start(f32[1,32,128]{2,1,0:T(8,128)S(1)} %get-tuple-element.73), channel_id=1, source_target_pairs={{0,4},{4,0},{8,12},{12,8},{16,20},{20,16},{24,28},{28,24},{32,36},... | collective-permute-start | bytes 49160 | tf_op jit(solution)/shard_map/ppermute | solution.py:658
  85.8 2.8 %collective-permute-done.10.h0 = f32[1,32,128]{2,1,0:T(8,128)S(1)} collective-permute-done((f32[1,32,128]{2,1,0:T(8,128)S(1)}, f32[1,32,128]{2,1,0:T(8,128)S(1)}, u32[]{:S(2)}, u32[]{:S(2)}) %collective-permute-start.10) | collective-permute-done | bytes 16416 | tf_op jit(solution)/shard_map/ppermute | solution.py:655
  88.7 1.4 shard_map.83
  90.1 5.6 %collective-permute-start.12 = (f32[1,32,128]{2,1,0:T(8,128)S(1)}, f32[1,32,128]{2,1,0:T(8,128)S(1)}, u32[]{:S(2)}, u32[]{:S(2)}) collective-permute-start(f32[1,32,128]{2,1,0:T(8,128)S(1)} %get-tuple-element.75), channel_id=1, source_target_pairs={{0,764},{4,8},{8,4},{12,16},{16,12},{20,24},{24,20},{28,32},{32,28... | collective-permute-start | bytes 49160 | tf_op jit(solution)/shard_map/ppermute | solution.py:655
  95.7 1.9 %collective-permute-start.13 = (f32[1,32,128]{2,1,0:T(8,128)S(1)}, f32[1,32,128]{2,1,0:T(8,128)S(1)}, u32[]{:S(2)}, u32[]{:S(2)}) collective-permute-start(f32[1,32,128]{2,1,0:T(8,128)S(1)} %get-tuple-element.76), channel_id=1, source_target_pairs={{0,4},{4,0},{8,12},{12,8},{16,20},{20,16},{24,28},{28,24},{32,36},... | collective-permute-start | bytes 49160 | tf_op jit(solution)/shard_map/ppermute | solution.py:658
  97.6 3.7 %collective-permute-start.14 = (f32[1,4,16,128]{3,2,1,0:T(8,128)S(1)}, f32[1,4,16,128]{3,2,1,0:T(8,128)S(1)}, u32[]{:S(2)}, u32[]{:S(2)}) collective-permute-start(f32[1,4,16,128]{3,2,1,0:T(8,128)S(1)} %get-tuple-element.78), channel_id=1, source_target_pairs={{0,1},{1,2},{2,3},{3,0},{4,5},{5,6},{6,7},{7,4},{8,9},{9,10},{10,1... | collective-permute-start | bytes 98312 | tf_op jit(solution)/shard_map/ppermute | solution.py:674
  101.3 1.9 %collective-permute-start.15 = (f32[1,4,16,128]{3,2,1,0:T(8,128)S(1)}, f32[1,4,16,128]{3,2,1,0:T(8,128)S(1)}, u32[]{:S(2)}, u32[]{:S(2)}) collective-permute-start(f32[1,4,16,128]{3,2,1,0:T(8,128)S(1)} %get-tuple-element.79), channel_id=1, source_target_pairs={{0,3},{1,0},{2,1},{3,2},{4,7},{5,4},{6,5},{7,6},{8,11},{9,8},{10,9... | collective-permute-start | bytes 98312 | tf_op jit(solution)/shard_map/ppermute | solution.py:675
  103.2 0.6 shard_map.84
  103.9 6.7 %all-gather.2 = f32[4,48,128]{2,1,0:T(8,128)S(1)} all-gather(f32[1,48,128]{2,1,0:T(8,128)S(1)} %shard_map.84), channel_id=4, replica_groups=mesh['outer'=16,'ring'=12,'narrow'=4] {'narrow'}, dimensions={0}, use_global_device_ids=true | all-gather | bytes 122880 | tf_op jit(solution)/shard_map/all_gather | solution.py:665
  110.5 1.7 %shard_map.85 = (f32[8,32,128]{2,1,0:T(8,128)S(1)}, f32[8,32,128]{2,1,0:T(8,128)S(1)}, f32[1,32,128]{2,1,0:T(8,128)S(1)}, f32[1,32,128]{2,1,0:T(8,128)S(1)}) custom-call(s32[2]{0:T(128)S(1)} %pad_add_fusion.place_ref, f32[8,32,128]{2,1,0:T(8,128)S(1)} %get-tuple-element.74.kv_in, f32[1,32,128]{2,1,0:T(8,128)S(1)} %collective-permute-done.12.far_ref.h0, ...), custom_call_target="tpu_custom_call" | custom-call | tf_op jit(solution)/shard_map/pallas_call | solution.py:630
  112.2 5.4 %collective-permute-start.16 = (f32[1,32,128]{2,1,0:T(8,128)S(1)}, f32[1,32,128]{2,1,0:T(8,128)S(1)}, u32[]{:S(2)}, u32[]{:S(2)}) collective-permute-start(f32[1,32,128]{2,1,0:T(8,128)S(1)} %get-tuple-element.83), channel_id=1, source_target_pairs={{0,764},{4,8},{8,4},{12,16},{16,12},{20,24},{24,20},{28,32},{32,28... | collective-permute-start | bytes 49160 | tf_op jit(solution)/shard_map/ppermute | solution.py:655
  117.7 1.9 %collective-permute-start.17 = (f32[1,32,128]{2,1,0:T(8,128)S(1)}, f32[1,32,128]{2,1,0:T(8,128)S(1)}, u32[]{:S(2)}, u32[]{:S(2)}) collective-permute-start(f32[1,32,128]{2,1,0:T(8,128)S(1)} %get-tuple-element.84), channel_id=1, source_target_pairs={{0,4},{4,0},{8,12},{12,8},{16,20},{20,16},{24,28},{28,24},{32,36},... | collective-permute-start | bytes 49160 | tf_op jit(solution)/shard_map/ppermute | solution.py:658
  119.6 2.8 %collective-permute-done.16.h0 = f32[1,32,128]{2,1,0:T(8,128)S(1)} collective-permute-done((f32[1,32,128]{2,1,0:T(8,128)S(1)}, f32[1,32,128]{2,1,0:T(8,128)S(1)}, u32[]{:S(2)}, u32[]{:S(2)}) %collective-permute-start.16) | collective-permute-done | bytes 16416 | tf_op jit(solution)/shard_map/ppermute | solution.py:655
  122.4 2.0 %shard_map.86 = (f32[8,32,128]{2,1,0:T(8,128)S(1)}, f32[8,32,128]{2,1,0:T(8,128)S(1)}, f32[1,32,128]{2,1,0:T(8,128)S(1)}, f32[1,32,128]{2,1,0:T(8,128)S(1)}, f32...) custom-call(s32[2]{0:T(128)S(1)} %pad_add_fusion.place_ref, f32[8,32,128]{2,1,0:T(8,128)S(1)} %get-tuple-element.82.kv_in, ...), custom_call_target="tpu_custom_call" | custom-call | tf_op jit(solution)/shard_map/pallas_call | solution.py:630
  124.4 6.0 %all-to-all-start = ((f32[64,1,128]{2,1,0:T(1,128)}), f32[64,1,128]{2,1,0:T(1,128)S(1)}, u32[]{:S(2)}, u32[]{:S(2)}) async-start(f32[64,1,128]{2,1,0:T(1,128)} %bitcast.8), calls=%async_computation | async-start | bytes 65536 | tf_op jit(solution)/shard_map/all_to_all | solution.py:741
  130.4 8.4 %collective-permute-start.18 = (f32[1,32,128]{2,1,0:T(8,128)S(1)}, f32[1,32,128]{2,1,0:T(8,128)S(1)}, u32[]{:S(2)}, u32[]{:S(2)}) collective-permute-start(f32[1,32,128]{2,1,0:T(8,128)S(1)} %get-tuple-element.89), channel_id=1, source_target_pairs={{0,764},{4,8},{8,4},{12,16},{16,12},{20,24},{24,20},{28,32},{32,28... | collective-permute-start | bytes 49160 | tf_op jit(solution)/shard_map/ppermute | solution.py:655
  138.8 1.9 %collective-permute-start.19 = (f32[1,32,128]{2,1,0:T(8,128)S(1)}, f32[1,32,128]{2,1,0:T(8,128)S(1)}, u32[]{:S(2)}, u32[]{:S(2)}) collective-permute-start(f32[1,32,128]{2,1,0:T(8,128)S(1)} %get-tuple-element.90), channel_id=1, source_target_pairs={{0,4},{4,0},{8,12},{12,8},{16,20},{20,16},{24,28},{28,24},{32,36},... | collective-permute-start | bytes 49160 | tf_op jit(solution)/shard_map/ppermute | solution.py:658
  140.8 0.1 reduce_sum.9
  140.8 0.6 broadcast_in_dim.2
  141.4 3.5 %all-to-all-start.1 = ((f32[12,1,128]{2,1,0:T(1,128)}), f32[12,1,128]{2,1,0:T(1,128)S(1)}, u32[]{:S(2)}, u32[]{:S(2)}) async-start(f32[12,1,128]{2,1,0:T(1,128)} %broadcast_in_dim.2), calls=%async_computation.1 | async-start | bytes 12288 | tf_op jit(solution)/shard_map/all_to_all | solution.py:745
  144.9 0.6 copy-done.2
  145.6 0.1 copy.10.order_ref
  145.7 0.6 shard_map.87
  146.3 5.6 %all-gather.3 = f32[4,16,128]{2,1,0:T(8,128)S(1)} all-gather(f32[1,16,128]{2,1,0:T(8,128)S(1)} %shard_map.87), channel_id=5, replica_groups=mesh['outer'=16,'ring'=12,'narrow'=4] {'narrow'}, dimensions={0}, use_global_device_ids=true | all-gather | bytes 40960 | tf_op jit(solution)/shard_map/all_gather | solution.py:665
  151.9 1.7 %all-to-all-done.1 = f32[12,1,128]{2,1,0:T(1,128)S(1)} async-done(((f32[12,1,128]{2,1,0:T(1,128)}), f32[12,1,128]{2,1,0:T(1,128)S(1)}, u32[]{:S(2)}, u32[]{:S(2)}) %all-to-all-start.1) | async-done | bytes 6176 | tf_op jit(solution)/shard_map/all_to_all | solution.py:745
  153.7 1.7 %shard_map.88 = (f32[64,512]{1,0:T(8,128)}, f32[64,512]{1,0:T(8,128)}) custom-call(s32[2]{0:T(128)S(1)} %pad_add_fusion.place_ref, f32[8,32,128]{2,1,0:T(8,128)S(1)} %get-tuple-element.88.kv_in, f32[1,32,128]{2,1,0:T(8,128)S(1)} %collective-permute-done.18.far_ref.h0, f32[1,32,128]{2,1,0:T(8,128)S(1)} %collective-permute-done.19.near_ref.h1, ...), custom_call_target="tpu_custom_call" | custom-call | tf_op jit(solution)/shard_map/pallas_call | solution.py:630
  (23 shorter events, 0.1 us)
Async XLA Ops:
  4.0 39.0 %collective-permute-start.2 = (f32[9,4,16,128]{3,2,1,0:T(8,128)S(1)}, f32[9,4,16,128]{3,2,1,0:T(8,128)S(1)}, u32[]{:S(2)}, u32[]{:S(2)}) collective-permute-start(f32[9,4,16,128]{3,2,1,0:T(8,128)S(1)} %get-tuple-element.53), channel_id=1, source_target_pairs={{0,1},{1,2},{2,3},{3,0},{4,5},{5,6},{6,7},{7,4},{8,9},{9,10},{10,1... | collective-permute-start | bytes 884744 | tf_op jit(solution)/shard_map/ppermute | solution.py:674
  8.5 34.5 %collective-permute-start.3 = (f32[9,4,16,128]{3,2,1,0:T(8,128)S(1)}, f32[9,4,16,128]{3,2,1,0:T(8,128)S(1)}, u32[]{:S(2)}, u32[]{:S(2)}) collective-permute-start(f32[9,4,16,128]{3,2,1,0:T(8,128)S(1)} %get-tuple-element.54), channel_id=1, source_target_pairs={{0,3},{1,0},{2,1},{3,2},{4,7},{5,4},{6,5},{7,6},{8,11},{9,8},{10,9... | collective-permute-start | bytes 884744 | tf_op jit(solution)/shard_map/ppermute | solution.py:675
  18.3 13.4 %collective-permute-start = (f32[2,32,128]{2,1,0:T(8,128)S(1)}, f32[2,32,128]{2,1,0:T(8,128)S(1)}, u32[]{:S(2)}, u32[]{:S(2)}) collective-permute-start(f32[2,32,128]{2,1,0:T(8,128)S(1)} %get-tuple-element.50), channel_id=1, source_target_pairs={{0,764},{4,8},{8,4},{12,16},{16,12},{20,24},{24,20},{28,32},{32,28... | collective-permute-start | bytes 98312 | tf_op jit(solution)/shard_map/ppermute | solution.py:655
  29.8 4.7 %collective-permute-start.1 = (f32[2,32,128]{2,1,0:T(8,128)S(1)}, f32[2,32,128]{2,1,0:T(8,128)S(1)}, u32[]{:S(2)}, u32[]{:S(2)}) collective-permute-start(f32[2,32,128]{2,1,0:T(8,128)S(1)} %get-tuple-element.51), channel_id=1, source_target_pairs={{0,4},{4,0},{8,12},{12,8},{16,20},{20,16},{24,28},{28,24},{32,36},... | collective-permute-start | bytes 98312 | tf_op jit(solution)/shard_map/ppermute | solution.py:658
  34.5 8.5 %copy-start.1 = (bf16[2,256,128]{2,1,0:T(8,128)(2,1)S(1)}, bf16[2,256,128]{2,1,0:T(8,128)(2,1)}, u32[]{:S(2)}) copy-start(bf16[2,256,128]{2,1,0:T(8,128)(2,1)} %constant.37.clone.diver_ref) | copy-start | bytes 393220
  35.1 7.9 %copy-start = (bf16[2,128,256]{2,1,0:T(8,128)(2,1)S(1)}, bf16[2,128,256]{2,1,0:T(8,128)(2,1)}, u32[]{:S(2)}) copy-start(bf16[2,128,256]{2,1,0:T(8,128)(2,1)} %constant.36.clone.grad_ref) | copy-start | bytes 393220
  44.7 10.2 %collective-permute-start.4 = (f32[1,32,128]{2,1,0:T(8,128)S(1)}, f32[1,32,128]{2,1,0:T(8,128)S(1)}, u32[]{:S(2)}, u32[]{:S(2)}) collective-permute-start(f32[1,32,128]{2,1,0:T(8,128)S(1)} %get-tuple-element.57), channel_id=1, source_target_pairs={{0,764},{4,8},{8,4},{12,16},{16,12},{20,24},{24,20},{28,32},{32,28... | collective-permute-start | bytes 49160 | tf_op jit(solution)/shard_map/ppermute | solution.py:655
  50.1 4.8 %collective-permute-start.5 = (f32[1,32,128]{2,1,0:T(8,128)S(1)}, f32[1,32,128]{2,1,0:T(8,128)S(1)}, u32[]{:S(2)}, u32[]{:S(2)}) collective-permute-start(f32[1,32,128]{2,1,0:T(8,128)S(1)} %get-tuple-element.58), channel_id=1, source_target_pairs={{0,4},{4,0},{8,12},{12,8},{16,20},{20,16},{24,28},{28,24},{32,36},... | collective-permute-start | bytes 49160 | tf_op jit(solution)/shard_map/ppermute | solution.py:658
  56.3 13.1 %collective-permute-start.6 = (f32[1,32,128]{2,1,0:T(8,128)S(1)}, f32[1,32,128]{2,1,0:T(8,128)S(1)}, u32[]{:S(2)}, u32[]{:S(2)}) collective-permute-start(f32[1,32,128]{2,1,0:T(8,128)S(1)} %get-tuple-element.63), channel_id=1, source_target_pairs={{0,764},{4,8},{8,4},{12,16},{16,12},{20,24},{24,20},{28,32},{32,28... | collective-permute-start | bytes 49160 | tf_op jit(solution)/shard_map/ppermute | solution.py:655
  61.9 7.6 %collective-permute-start.7 = (f32[1,32,128]{2,1,0:T(8,128)S(1)}, f32[1,32,128]{2,1,0:T(8,128)S(1)}, u32[]{:S(2)}, u32[]{:S(2)}) collective-permute-start(f32[1,32,128]{2,1,0:T(8,128)S(1)} %get-tuple-element.64), channel_id=1, source_target_pairs={{0,4},{4,0},{8,12},{12,8},{16,20},{20,16},{24,28},{28,24},{32,36},... | collective-permute-start | bytes 49160 | tf_op jit(solution)/shard_map/ppermute | solution.py:658
  63.8 13.0 %collective-permute-start.8 = (f32[1,4,16,128]{3,2,1,0:T(8,128)S(1)}, f32[1,4,16,128]{3,2,1,0:T(8,128)S(1)}, u32[]{:S(2)}, u32[]{:S(2)}) collective-permute-start(f32[1,4,16,128]{3,2,1,0:T(8,128)S(1)} %get-tuple-element.66), channel_id=1, source_target_pairs={{0,1},{1,2},{2,3},{3,0},{4,5},{5,6},{6,7},{7,4},{8,9},{9,10},{10,1... | collective-permute-start | bytes 98312 | tf_op jit(solution)/shard_map/ppermute | solution.py:674
  67.5 9.2 %collective-permute-start.9 = (f32[1,4,16,128]{3,2,1,0:T(8,128)S(1)}, f32[1,4,16,128]{3,2,1,0:T(8,128)S(1)}, u32[]{:S(2)}, u32[]{:S(2)}) collective-permute-start(f32[1,4,16,128]{3,2,1,0:T(8,128)S(1)} %get-tuple-element.67), channel_id=1, source_target_pairs={{0,3},{1,0},{2,1},{3,2},{4,7},{5,4},{6,5},{7,6},{8,11},{9,8},{10,9... | collective-permute-start | bytes 98312 | tf_op jit(solution)/shard_map/ppermute | solution.py:675
  78.5 10.2 %collective-permute-start.10 = (f32[1,32,128]{2,1,0:T(8,128)S(1)}, f32[1,32,128]{2,1,0:T(8,128)S(1)}, u32[]{:S(2)}, u32[]{:S(2)}) collective-permute-start(f32[1,32,128]{2,1,0:T(8,128)S(1)} %get-tuple-element.72), channel_id=1, source_target_pairs={{0,764},{4,8},{8,4},{12,16},{16,12},{20,24},{24,20},{28,32},{32,28... | collective-permute-start | bytes 49160 | tf_op jit(solution)/shard_map/ppermute | solution.py:655
  83.9 4.8 %collective-permute-start.11 = (f32[1,32,128]{2,1,0:T(8,128)S(1)}, f32[1,32,128]{2,1,0:T(8,128)S(1)}, u32[]{:S(2)}, u32[]{:S(2)}) collective-permute-start(f32[1,32,128]{2,1,0:T(8,128)S(1)} %get-tuple-element.73), channel_id=1, source_target_pairs={{0,4},{4,0},{8,12},{12,8},{16,20},{20,16},{24,28},{28,24},{32,36},... | collective-permute-start | bytes 49160 | tf_op jit(solution)/shard_map/ppermute | solution.py:658
  90.1 13.1 %collective-permute-start.12 = (f32[1,32,128]{2,1,0:T(8,128)S(1)}, f32[1,32,128]{2,1,0:T(8,128)S(1)}, u32[]{:S(2)}, u32[]{:S(2)}) collective-permute-start(f32[1,32,128]{2,1,0:T(8,128)S(1)} %get-tuple-element.75), channel_id=1, source_target_pairs={{0,764},{4,8},{8,4},{12,16},{16,12},{20,24},{24,20},{28,32},{32,28... | collective-permute-start | bytes 49160 | tf_op jit(solution)/shard_map/ppermute | solution.py:655
  95.7 7.6 %collective-permute-start.13 = (f32[1,32,128]{2,1,0:T(8,128)S(1)}, f32[1,32,128]{2,1,0:T(8,128)S(1)}, u32[]{:S(2)}, u32[]{:S(2)}) collective-permute-start(f32[1,32,128]{2,1,0:T(8,128)S(1)} %get-tuple-element.76), channel_id=1, source_target_pairs={{0,4},{4,0},{8,12},{12,8},{16,20},{20,16},{24,28},{28,24},{32,36},... | collective-permute-start | bytes 49160 | tf_op jit(solution)/shard_map/ppermute | solution.py:658
  97.6 13.0 %collective-permute-start.14 = (f32[1,4,16,128]{3,2,1,0:T(8,128)S(1)}, f32[1,4,16,128]{3,2,1,0:T(8,128)S(1)}, u32[]{:S(2)}, u32[]{:S(2)}) collective-permute-start(f32[1,4,16,128]{3,2,1,0:T(8,128)S(1)} %get-tuple-element.78), channel_id=1, source_target_pairs={{0,1},{1,2},{2,3},{3,0},{4,5},{5,6},{6,7},{7,4},{8,9},{9,10},{10,1... | collective-permute-start | bytes 98312 | tf_op jit(solution)/shard_map/ppermute | solution.py:674
  101.3 9.2 %collective-permute-start.15 = (f32[1,4,16,128]{3,2,1,0:T(8,128)S(1)}, f32[1,4,16,128]{3,2,1,0:T(8,128)S(1)}, u32[]{:S(2)}, u32[]{:S(2)}) collective-permute-start(f32[1,4,16,128]{3,2,1,0:T(8,128)S(1)} %get-tuple-element.79), channel_id=1, source_target_pairs={{0,3},{1,0},{2,1},{3,2},{4,7},{5,4},{6,5},{7,6},{8,11},{9,8},{10,9... | collective-permute-start | bytes 98312 | tf_op jit(solution)/shard_map/ppermute | solution.py:675
  112.2 10.2 %collective-permute-start.16 = (f32[1,32,128]{2,1,0:T(8,128)S(1)}, f32[1,32,128]{2,1,0:T(8,128)S(1)}, u32[]{:S(2)}, u32[]{:S(2)}) collective-permute-start(f32[1,32,128]{2,1,0:T(8,128)S(1)} %get-tuple-element.83), channel_id=1, source_target_pairs={{0,764},{4,8},{8,4},{12,16},{16,12},{20,24},{24,20},{28,32},{32,28... | collective-permute-start | bytes 49160 | tf_op jit(solution)/shard_map/ppermute | solution.py:655
  117.7 4.8 %collective-permute-start.17 = (f32[1,32,128]{2,1,0:T(8,128)S(1)}, f32[1,32,128]{2,1,0:T(8,128)S(1)}, u32[]{:S(2)}, u32[]{:S(2)}) collective-permute-start(f32[1,32,128]{2,1,0:T(8,128)S(1)} %get-tuple-element.84), channel_id=1, source_target_pairs={{0,4},{4,0},{8,12},{12,8},{16,20},{20,16},{24,28},{28,24},{32,36},... | collective-permute-start | bytes 49160 | tf_op jit(solution)/shard_map/ppermute | solution.py:658
  124.4 16.3 %all-to-all-start = ((f32[64,1,128]{2,1,0:T(1,128)}), f32[64,1,128]{2,1,0:T(1,128)S(1)}, u32[]{:S(2)}, u32[]{:S(2)}) async-start(f32[64,1,128]{2,1,0:T(1,128)} %bitcast.8), calls=%async_computation | async-start | bytes 65536 | tf_op jit(solution)/shard_map/all_to_all | solution.py:741
  130.4 15.3 %collective-permute-start.18 = (f32[1,32,128]{2,1,0:T(8,128)S(1)}, f32[1,32,128]{2,1,0:T(8,128)S(1)}, u32[]{:S(2)}, u32[]{:S(2)}) collective-permute-start(f32[1,32,128]{2,1,0:T(8,128)S(1)} %get-tuple-element.89), channel_id=1, source_target_pairs={{0,764},{4,8},{8,4},{12,16},{16,12},{20,24},{24,20},{28,32},{32,28... | collective-permute-start | bytes 49160 | tf_op jit(solution)/shard_map/ppermute | solution.py:655
  138.8 6.9 %collective-permute-start.19 = (f32[1,32,128]{2,1,0:T(8,128)S(1)}, f32[1,32,128]{2,1,0:T(8,128)S(1)}, u32[]{:S(2)}, u32[]{:S(2)}) collective-permute-start(f32[1,32,128]{2,1,0:T(8,128)S(1)} %get-tuple-element.90), channel_id=1, source_target_pairs={{0,4},{4,0},{8,12},{12,8},{16,20},{20,16},{24,28},{28,24},{32,36},... | collective-permute-start | bytes 49160 | tf_op jit(solution)/shard_map/ppermute | solution.py:658
  141.4 12.2 %all-to-all-start.1 = ((f32[12,1,128]{2,1,0:T(1,128)}), f32[12,1,128]{2,1,0:T(1,128)S(1)}, u32[]{:S(2)}, u32[]{:S(2)}) async-start(f32[12,1,128]{2,1,0:T(1,128)} %broadcast_in_dim.2), calls=%async_computation.1 | async-start | bytes 12288 | tf_op jit(solution)/shard_map/all_to_all | solution.py:745
  144.9 0.7 copy-start.2

commit v4 on v3

--- a/solution.py
+++ b/solution.py
@@ -79,8 +79,9 @@
 
 GRAD = np.concatenate([cycle_matrix(DERIV.T), radial_matrix(DERIV.T)], axis=1)
 DIVER = np.concatenate([cycle_matrix(DERIV), radial_matrix(DERIV)], axis=0)
-GRAD_HL = np.stack(split_const(GRAD))
-DIVER_HL = np.stack(split_const(DIVER))
+GRAD_PARTS = split_const(GRAD)
+GRAD_HL = np.concatenate([GRAD_PARTS[0], GRAD_PARTS[0], GRAD_PARTS[1]], axis=0)
+DIVER_HL = np.concatenate(split_const(DIVER), axis=1)
 ABS_HL = np.stack(split_const(np.abs(DIVER)))
 
 
@@ -98,6 +99,18 @@
 def dot_split(value, matrix_ref):
     high, low = split(value)
     return dot(high, matrix_ref[0]) + (dot(low, matrix_ref[0]) + dot(high, matrix_ref[1]))
+
+
+def dot_grad(value, grad_ref):
+    high, low = split(value)
+    both = jnp.concatenate([high, low], axis=1)
+    return dot(both, grad_ref[: 2 * LANES]) + dot(high, grad_ref[2 * LANES :])
+
+
+def dot_diver(value, diver_ref):
+    high, low = split(value)
+    both = dot(high, diver_ref[...])
+    return both[:, :LANES] + (both[:, LANES:] + dot(low, diver_ref[:, :LANES]))
 
 
 def lane_iota(rows):
@@ -226,12 +239,12 @@
         pack_ref[field] = pack
 
 
-def is_even(place_ref):
-    return lax.broadcast_in_dim(place_ref[0], (ROWS, LANES), ()) == 0
-
-
-def pack_kernel(place_ref, pack_in, far_ref, near_ref, pack_ref):
-    even = is_even(place_ref)
+def is_even():
+    return lax.broadcast_in_dim(lax.rem(lax.axis_index("ring"), 2), (ROWS, LANES), ()) == 0
+
+
+def pack_kernel(pack_in, far_ref, near_ref, pack_ref):
+    even = is_even()
     for field in range(pack_ref.shape[0]):
         near, far = near_ref[field], far_ref[field]
         first = jnp.where(even, far, near)
@@ -244,19 +257,19 @@
             pack_ref[field, ROWS:] = edge(last)
 
 
-def beside(place_ref, packs_ref):
+def beside(packs_ref):
     count = packs_ref.shape[0]
-    here = place_ref[1]
+    here = lax.axis_index("narrow")
     return lax.rem(here + count - 1, count), lax.rem(here + 1, count)
 
 
-def completed(place_ref, kv, halo, field=0):
+def completed(kv, halo, field=0):
     far_ref, near_ref = halo[:2]
-    even = is_even(place_ref)
+    even = is_even()
     near, far = near_ref[field], far_ref[field]
     lane = lane_iota(HALF)
     if len(halo) > 2:
-        left, right = beside(place_ref, halo[2])
+        left, right = beside(halo[2])
         side = jnp.where(
             lane % 16 < 8,
             roll(halo[2][left, field, :HALF], 8, 1),
@@ -279,10 +292,10 @@
     return value
 
 
-def ghost_sums(place_ref, packs_ref, field=0):
-    left, right = beside(place_ref, packs_ref)
+def ghost_sums(packs_ref, field=0):
+    left, right = beside(packs_ref)
     lane = lane_iota(HALF)
-    own = packs_ref[place_ref[1], field, :HALF]
+    own = packs_ref[lax.axis_index("narrow"), field, :HALF]
     lines = jnp.where(lane % 16 < 8, own, roll(own, 16, 1))
     inner = (lane >= 56) & (lane < 72)
 
@@ -298,7 +311,7 @@
 
 def apply_element(v_ref, metric_ref, ghost_ref, grad_ref, diver_ref, flux_ref, out_ref):
     count = v_ref.shape[1]
-    side = dot_split(v_ref[...].reshape(NODES * count, LANES), grad_ref)
+    side = dot_grad(v_ref[...].reshape(NODES * count, LANES), grad_ref)
     flux_ref[0] = side[:, :LANES]
     flux_ref[1] = side[:, LANES:]
     for chunk in range(count // 8):
@@ -321,7 +334,7 @@
         for i in range(NODES):
             out_ref[i, rows] = part_z[i] + geometry[6, i, there] * values[i]
     flux = jnp.concatenate([flux_ref[0], flux_ref[1]], axis=1)
-    out_ref[...] += dot_split(flux, diver_ref).reshape(out_ref.shape)
+    out_ref[...] += dot_diver(flux, diver_ref).reshape(out_ref.shape)
 
 
 def weight_plane():
@@ -357,7 +370,7 @@
 
 
 def place_kernel(
-    place_ref, order_hbm, load_hbm, geom_hbm, abs_hbm,
+    order_hbm, load_hbm, geom_hbm, abs_hbm,
     metric_ref, load_kv, bound_kv, far_ref, near_ref, pack_ref, lo_ref, hi_ref,
     flux_ref, work_ref, order_ref, load_ref, geom_ref, abs_ref, sems,
 ):
@@ -391,7 +404,7 @@
         work_ref[i] = value
 
     spread(dot(pick, high) + (dot(pick, rest) + dot(pick, middle)), store_load)
-    even = is_even(place_ref)
+    even = is_even()
     store_assembled(
         load_kv, far_ref, near_ref, even, lambda i: work_ref[i], 0, pack_ref
     )
@@ -435,12 +448,12 @@
 
 
 def first_kernel(
-    place_ref, load_kv, bound_kv, h0, h1, h2, left_ref, right_ref, metric_ref, grad_ref, diver_ref,
+    load_kv, bound_kv, h0, h1, h2, left_ref, right_ref, metric_ref, grad_ref, diver_ref,
     residual_ref, inverse_ref, update_ref, ghost_inverse, ghost_metric, kv_ref, far_ref, near_ref,
     v_ref, flux_ref, work_ref,
 ):
-    residual = completed(place_ref, load_kv, (h0, h1, h2), 0)
-    bound = completed(place_ref, bound_kv, (h0, h1, h2), 1)
+    residual = completed(load_kv, (h0, h1, h2), 0)
+    bound = completed(bound_kv, (h0, h1, h2), 1)
     for i in range(NODES):
         r = residual(i)
         inverse = 1.0 / bound(i)
@@ -449,8 +462,8 @@
         inverse_ref[i] = inverse
         update_ref[i] = update
         v_ref[i, :ROWS] = update
-    residual, residual_sums = ghost_columns(left_ref, right_ref, 7), ghost_sums(place_ref, h2, 0)
-    bound, bound_sums = ghost_columns(left_ref, right_ref, 8), ghost_sums(place_ref, h2, 1)
+    residual, residual_sums = ghost_columns(left_ref, right_ref, 7), ghost_sums(h2, 0)
+    bound, bound_sums = ghost_columns(left_ref, right_ref, 8), ghost_sums(h2, 1)
     for i in range(NODES):
         inverse = 1.0 / (bound[i] + bound_sums(i))
         ghost_inverse[i] = inverse
@@ -459,14 +472,14 @@
         for i, value in enumerate(ghost_columns(left_ref, right_ref, c)):
             ghost_metric[c, i] = value
     apply_element(v_ref, metric_ref, ghost_metric, grad_ref, diver_ref, flux_ref, work_ref)
-    store_assembled(kv_ref, far_ref, near_ref, is_even(place_ref), lambda i: work_ref[i])
+    store_assembled(kv_ref, far_ref, near_ref, is_even(), lambda i: work_ref[i])
 
 
 def second_kernel(
-    place_ref, kv_in, h0, h1, source_ref, inverse_ref, update_in, metric_ref, grad_ref, diver_ref,
+    kv_in, h0, h1, source_ref, inverse_ref, update_in, metric_ref, grad_ref, diver_ref,
     start_ref, kv_ref, far_ref, near_ref, pack_ref, lo_ref, hi_ref, v_ref, flux_ref, work_ref,
 ):
-    image = completed(place_ref, kv_in, (h0, h1))
+    image = completed(kv_in, (h0, h1))
     for i in range(NODES):
         old = update_in[i]
         inverse = inverse_ref[i]
@@ -477,7 +490,7 @@
         start_ref[i] = result + (RHO2 * RHO1) * update + STEP2 * inverse * source
     apply_element(v_ref, metric_ref, None, grad_ref, diver_ref, flux_ref, work_ref)
     store_assembled(
-        kv_ref, far_ref, near_ref, is_even(place_ref), lambda i: work_ref[i], 0, pack_ref
+        kv_ref, far_ref, near_ref, is_even(), lambda i: work_ref[i], 0, pack_ref
     )
     store_edges(
         lo_ref, hi_ref, 0,
@@ -486,11 +499,11 @@
 
 
 def third_kernel(
-    place_ref, kv_in, h0, h1, h2, left_ref, right_ref, source_ref, inverse_ref, start_ref,
+    kv_in, h0, h1, h2, left_ref, right_ref, source_ref, inverse_ref, start_ref,
     ghost_inverse, ghost_metric, metric_ref, grad_ref, diver_ref,
     result_ref, kv_ref, far_ref, near_ref, sums_ref, v_ref, flux_ref, work_ref,
 ):
-    image = completed(place_ref, kv_in, (h0, h1, h2))
+    image = completed(kv_in, (h0, h1, h2))
     plane = weight_plane()
     rz = jnp.zeros((ROWS, LANES), jnp.float32)
     for i in range(NODES):
@@ -498,7 +511,7 @@
         result_ref[i] = result
         v_ref[i, :ROWS] = result
         rz = rz + source_ref[i] * result * node_weight(i)
-    start, sums = ghost_columns(left_ref, right_ref, 0), ghost_sums(place_ref, h2)
+    start, sums = ghost_columns(left_ref, right_ref, 0), ghost_sums(h2)
     for i in range(NODES):
         v_ref[i, ROWS:] = start[i] - STEP2 * ghost_inverse[i] * sums(i)
     apply_element(v_ref, metric_ref, ghost_metric, grad_ref, diver_ref, flux_ref, work_ref)
@@ -506,21 +519,21 @@
     for i in range(NODES):
         energy = energy + result_ref[i] * work_ref[i, :ROWS]
     sums_ref[...] = sum_row([rz * plane, energy])
-    store_assembled(kv_ref, far_ref, near_ref, is_even(place_ref), lambda i: work_ref[i])
+    store_assembled(kv_ref, far_ref, near_ref, is_even(), lambda i: work_ref[i])
 
 
 def fourth_kernel(
-    place_ref, kv_in, h0, h1, inverse_ref, metric_ref, grad_ref, diver_ref,
+    kv_in, h0, h1, inverse_ref, metric_ref, grad_ref, diver_ref,
     image_ref, update_ref, kv_ref, far_ref, near_ref, pack_ref, lo_ref, hi_ref, flux_ref, work_ref,
 ):
-    image = completed(place_ref, kv_in, (h0, h1))
+    image = completed(kv_in, (h0, h1))
     for i in range(NODES):
         value = image(i)
         image_ref[i] = value
         update_ref[i] = value * inverse_ref[i] * (1.0 / CENTER)
     apply_element(update_ref, metric_ref, None, grad_ref, diver_ref, flux_ref, work_ref)
     store_assembled(
-        kv_ref, far_ref, near_ref, is_even(place_ref), lambda i: work_ref[i], 0, pack_ref
+        kv_ref, far_ref, near_ref, is_even(), lambda i: work_ref[i], 0, pack_ref
     )
     scale = 1.0 + RHO1 * RHO0 + STEP1 * CENTER
     store_edges(
@@ -530,11 +543,11 @@
 
 
 def fifth_kernel(
-    place_ref, kv_in, h0, h1, h2, left_ref, right_ref, source_ref, inverse_ref, update_in,
+    kv_in, h0, h1, h2, left_ref, right_ref, source_ref, inverse_ref, update_in,
     ghost_inverse, ghost_metric, metric_ref, grad_ref, diver_ref,
     start_ref, kv_ref, far_ref, near_ref, v_ref, flux_ref, work_ref,
 ):
-    image = completed(place_ref, kv_in, (h0, h1, h2))
+    image = completed(kv_in, (h0, h1, h2))
     for i in range(NODES):
         old = update_in[i]
         inverse = inverse_ref[i]
@@ -543,19 +556,19 @@
         result = old + update
         v_ref[i, :ROWS] = result
         start_ref[i] = result + (RHO2 * RHO1) * update + STEP2 * inverse * source
-    start, sums = ghost_columns(left_ref, right_ref, 0), ghost_sums(place_ref, h2)
+    start, sums = ghost_columns(left_ref, right_ref, 0), ghost_sums(h2)
     for i in range(NODES):
         v_ref[i, ROWS:] = start[i] - STEP1 * ghost_inverse[i] * sums(i)
     apply_element(v_ref, metric_ref, ghost_metric, grad_ref, diver_ref, flux_ref, work_ref)
-    store_assembled(kv_ref, far_ref, near_ref, is_even(place_ref), lambda i: work_ref[i])
+    store_assembled(kv_ref, far_ref, near_ref, is_even(), lambda i: work_ref[i])
 
 
 def sixth_kernel(
-    place_ref, kv_in, h0, h1, source_ref, inverse_ref, start_ref, residual_ref, first_ref, early_ref,
+    kv_in, h0, h1, source_ref, inverse_ref, start_ref, residual_ref, first_ref, early_ref,
     metric_ref, grad_ref, diver_ref,
     result_ref, kv_ref, far_ref, near_ref, pack_ref, sums_ref, flux_ref, work_ref,
 ):
-    image = completed(place_ref, kv_in, (h0, h1))
+    image = completed(kv_in, (h0, h1))
     plane = weight_plane()
     r_y = jnp.zeros((ROWS, LANES), jnp.float32)
     w_y = jnp.zeros((ROWS, LANES), jnp.float32)
@@ -574,15 +587,32 @@
     late = sum_row([zero, zero, r_y * plane, w_y * plane, z_ky, y_ky])
     sums_ref[...] = jnp.broadcast_to(early_ref[...] + late, sums_ref.shape)
     store_assembled(
-        kv_ref, far_ref, near_ref, is_even(place_ref), lambda i: work_ref[i], 0, pack_ref
-    )
-
-
-def last_kernel(
-    place_ref, kv_in, h0, h1, h2, sums_ref, order_ref,
-    residual_ref, first_ref, image_ref, second_ref,
-    solution_ref, residual_out, spread_ref,
+        kv_ref, far_ref, near_ref, is_even(), lambda i: work_ref[i], 0, pack_ref
+    )
+
+
+def spread_kernel(
+    kv_in, h0, h1, h2, order_ref, residual_ref, first_ref, image_ref, second_ref, out_ref, spread_ref
 ):
+    image = completed(kv_in, (h0, h1, h2))
+    low = lane_iota(ROWS) < 64
+    pick = jnp.where(
+        lax.broadcasted_iota(jnp.int32, (64, 64), 1) == order_ref[...], 1.0, 0.0
+    ).astype(jnp.bfloat16)
+    fields = [lambda i, ref=ref: ref[i] for ref in (first_ref, second_ref, residual_ref, image_ref)]
+    for f, field in enumerate(fields + [image]):
+        for b in range(NODES // 2):
+            even, odd = field(2 * b), field(2 * b + 1)
+            lanes = pl.ds(b * LANES, LANES)
+            spread_ref[:ROWS, lanes] = jnp.where(low, even, roll(odd, 64, 1))
+            spread_ref[ROWS:, lanes] = jnp.where(low, roll(even, 64, 1), odd)
+        value = spread_ref[...]
+        high, middle = split(value)
+        rest = (value - high.astype(jnp.float32) - middle.astype(jnp.float32)).astype(jnp.bfloat16)
+        out_ref[f] = dot(pick, high) + (dot(pick, middle) + dot(pick, rest))
+
+
+def last_kernel(sums_ref, spread_ref, solution_ref, residual_ref):
     sums = jnp.sum(sums_ref[...], axis=0, keepdims=True)
     lane = lane_iota(1)
 
@@ -598,47 +628,31 @@
     alpha1 = rz1 / energy
     first_scale = alpha0 + alpha1 * share
     second_scale = alpha1 * alpha0
-    image = completed(place_ref, kv_in, (h0, h1, h2))
-    low = lane_iota(ROWS) < 64
-    for b in range(4):
-        pair = []
-        for i in (2 * b, 2 * b + 1):
-            x = first_scale * first_ref[i] - second_scale * second_ref[i]
-            r = residual_ref[i] - first_scale * image_ref[i] + second_scale * image(i)
-            pair.append((x, r))
-        for f in range(2):
-            even, odd = pair[0][f], pair[1][f]
-            lanes = pl.ds(b * LANES, LANES)
-            spread_ref[f, :ROWS, lanes] = jnp.where(low, even, roll(odd, 64, 1))
-            spread_ref[f, ROWS:, lanes] = jnp.where(low, roll(even, 64, 1), odd)
-    pick = jnp.where(
-        lax.broadcasted_iota(jnp.int32, (64, 64), 1) == order_ref[...], 1.0, 0.0
-    ).astype(jnp.bfloat16)
-    for f, out in ((0, solution_ref), (1, residual_out)):
-        value = spread_ref[f]
-        high, middle = split(value)
-        rest = (value - high.astype(jnp.float32) - middle.astype(jnp.float32)).astype(jnp.bfloat16)
-        out[...] = dot(pick, high) + (dot(pick, middle) + dot(pick, rest))
+    solution_ref[...] = first_scale * spread_ref[0] - second_scale * spread_ref[1]
+    residual_ref[...] = (
+        spread_ref[2] - first_scale * spread_ref[3] + second_scale * spread_ref[4]
+    )
 
 
 VMEM_LIMIT = 24 * 1024 * 1024
 F32 = jnp.float32
 
 
-def call(kernel, place, outs, scratch, *operands, space=pltpu.VMEM):
+def call(kernel, outs, scratch, *operands, space=pltpu.VMEM, cost=None):
     vmem = pl.BlockSpec(memory_space=pltpu.VMEM)
     return pl.pallas_call(
         kernel,
         out_shape=[jax.ShapeDtypeStruct(s, F32) for s in outs],
-        in_specs=[pl.BlockSpec(memory_space=pltpu.SMEM)]
-        + [pl.BlockSpec(memory_space=space)] * len(operands),
+        in_specs=[pl.BlockSpec(memory_space=space)] * len(operands),
         out_specs=[vmem] * len(outs),
         scratch_shapes=[pltpu.VMEM(s, F32) if isinstance(s, tuple) else s for s in scratch],
+        cost_estimate=cost,
         compiler_params=pltpu.CompilerParams(vmem_limit_bytes=VMEM_LIMIT),
-    )(place, *operands)
+    )(*operands)
 
 
 FLUX = (2, NODES * ROWS, LANES)
+COST = pl.CostEstimate(flops=10**11, transcendentals=0, bytes_accessed=10**8)
 BIG_FLUX = (2, NODES * GROWS, LANES)
 
 
@@ -659,9 +673,9 @@
     return far, near
 
 
-def swap_all(place, far, near, pack, rows):
+def swap_all(far, near, pack, rows):
     far, near = swap_wide(far, near)
-    (pack,) = call(pack_kernel, place, [(pack.shape[0], rows, LANES)], [], pack, far, near)
+    (pack,) = call(pack_kernel, [(pack.shape[0], rows, LANES)], [], pack, far, near, cost=COST)
     return far, near, lax.all_gather(pack, "narrow")
 
 
@@ -677,11 +691,10 @@
 
 
 def local(load, geom, element_order):
-    place = jnp.stack([lax.axis_index(WIDE) % 2, lax.axis_index("narrow")]).astype(jnp.int32)
     grad = jnp.asarray(GRAD_HL)
     diver = jnp.asarray(DIVER_HL)
     metric, load_kv, bound_kv, *face, lo, hi = call(
-        place_kernel, place,
+        place_kernel,
         [(7,) + FIELD, FIELD, FIELD] + faces(2) + packs(2) + edges(9),
         [
             FLUX, FIELD,
@@ -693,64 +706,63 @@
         space=pltpu.HBM,
     )
     sides = swap_edges(lo, hi)
-    halo = swap_all(place, *face, GROWS)
+    halo = swap_all(*face, GROWS)
     residual, inverse, update, ghost_inverse, ghost_metric, kv, *face = call(
-        first_kernel, place,
+        first_kernel,
         [FIELD, FIELD, FIELD, GHOST, (7,) + GHOST, FIELD] + faces(),
         [BIG, BIG_FLUX, BIG],
         load_kv, bound_kv, *halo, *sides, metric, grad, diver,
     )
     halo = swap_wide(*face)
     start, kv, *face, lo, hi = call(
-        second_kernel, place,
+        second_kernel,
         [FIELD, FIELD] + faces() + packs() + edges(),
         [FIELD, FLUX, FIELD],
         kv, *halo, residual, inverse, update, metric, grad, diver,
     )
     sides = swap_edges(lo, hi)
-    halo = swap_all(place, *face, GROWS)
+    halo = swap_all(*face, GROWS)
     first, kv, *face, early = call(
-        third_kernel, place,
+        third_kernel,
         [FIELD, FIELD] + faces() + [(1, LANES)],
         [BIG, BIG_FLUX, BIG],
         kv, *halo, *sides, residual, inverse, start, ghost_inverse, ghost_metric, metric, grad, diver,
     )
     halo = swap_wide(*face)
     image, update, kv, *face, lo, hi = call(
-        fourth_kernel, place,
+        fourth_kernel,
         [FIELD, FIELD, FIELD] + faces() + packs() + edges(),
         [FLUX, FIELD],
         kv, *halo, inverse, metric, grad, diver,
     )
     sides = swap_edges(lo, hi)
-    halo = swap_all(place, *face, GROWS)
+    halo = swap_all(*face, GROWS)
     start, kv, *face = call(
-        fifth_kernel, place,
+        fifth_kernel,
         [FIELD, FIELD] + faces(),
         [BIG, BIG_FLUX, BIG],
         kv, *halo, *sides, image, inverse, update, ghost_inverse, ghost_metric, metric, grad, diver,
     )
     halo = swap_wide(*face)
     second, kv, *face, sums = call(
-        sixth_kernel, place,
+        sixth_kernel,
         [FIELD, FIELD] + faces() + packs() + [(lax.axis_size(REST), LANES)],
         [FLUX, FIELD],
         kv, *halo, image, inverse, start, residual, first, early, metric, grad, diver,
     )
-    halo = swap_all(place, *face, HALF)
+    halo = swap_all(*face, HALF)
     sums = lax.all_to_all(sums, REST, 0, 0)
     sums = jnp.broadcast_to(
         jnp.sum(sums, axis=0, keepdims=True), (lax.axis_size("ring"), LANES)
     )
     sums = lax.all_to_all(sums, "ring", 0, 0)
-    return tuple(
-        call(
-            last_kernel, place,
-            [(64, 512), (64, 512)],
-            [(2, 64, 512)],
-            kv, *halo, sums, element_order.reshape(64, 1), residual, first, image, second,
-        )
-    )
+    (spread,) = call(
+        spread_kernel,
+        [(5, 64, 512)],
+        [(64, 512)],
+        kv, *halo, element_order.reshape(64, 1), residual, first, image, second,
+    )
+    return tuple(call(last_kernel, [(64, 512), (64, 512)], [], sums, spread))
 
 
 def solution(mesh):

time: 156 us -> 147 us (0.942)
  Pallas kernels: 17.2 us -> 9.94 us
    ppermute x3, starting transfers between devices: 13.7 us -> 5.76 us  [swap_edges(): lax.ppermute(lo, 'narrow', [(n, (n - 1) % count) for n in range(count)])]
    pallas_call x12 -> x13, Pallas kernels: 17.2 us -> 9.94 us  [call(): pl.pallas_call(kernel, out_shape=[jax.ShapeDtypeStruct(s, F32) for s in o...]
    ppermute x7, starting transfers between devices: 47.4 us -> 53.4 us  [swap_wide(): lax.ppermute(far, WIDE, [(w, (w + 1 if w % 2 else w - 1) % count) for w i...]
    ppermute x7, waiting for transfers between devices: 2.78 us -> 0.05 us  [swap_wide(): near = lax.ppermute(near, WIDE, [(w, w ^ 1) for w in range(count)])]
    ppermute x7, waiting for transfers between devices: 8.5 us -> 10.3 us  [swap_wide(): lax.ppermute(far, WIDE, [(w, (w + 1 if w % 2 else w - 1) % count) for w i...]
  transfers between devices with their start and end apart: 22 -> 22, of which waited for: 5 -> 4; matrix products, arithmetic and copies ran while one was open for 1% -> 1% of each run, Pallas kernels for 2% -> 1%
where the time goes in v4:
time: 147 us; the launch traced here: 146 us
  starting transfers between devices  94.9 us (65%)
  blocking collectives  26.8 us (18%)
  waiting for transfers between devices  12.8 us (9%)
  Pallas kernels  9.94 us (7%)
    ppermute x7, starting transfers between devices, swap_wide(): lax.ppermute(far, WIDE, [(w, (w + 1 if w % 2 else w - 1) % count) for w i...  53.4 us
    all_gather x4, blocking collectives, swap_all(): return (far, near, lax.all_gather(pack, 'narrow'))  26.8 us
    ppermute x7, starting transfers between devices, swap_wide(): near = lax.ppermute(near, WIDE, [(w, w ^ 1) for w in range(count)])  14.1 us
    ppermute x3, starting transfers between devices, swap_edges(): lax.ppermute(hi, 'narrow', [(n, (n + 1) % count) for n in range(count)])  11.7 us
    ppermute x7, waiting for transfers between devices, swap_wide(): lax.ppermute(far, WIDE, [(w, (w + 1 if w % 2 else w - 1) % count) for w i...  10.3 us
    pallas_call x13, Pallas kernels, call(): pl.pallas_call(kernel, out_shape=[jax.ShapeDtypeStruct(s, F32) for s in o...  9.94 us
    all_to_all x1, starting transfers between devices, local(): sums = lax.all_to_all(sums, REST, 0, 0)  6.46 us
    ppermute x3, starting transfers between devices, swap_edges(): lax.ppermute(lo, 'narrow', [(n, (n - 1) % count) for n in range(count)])  5.76 us
  transfers between devices with their start and end apart: 22, of which 4 were waited for; matrix products, arithmetic and copies ran while one was open for 1% of the time, Pallas kernels for 1%

profile of v4, /device:TPU:1, one launch (start us, length us, event | category | flops | bytes accessed | tf_op | source)
XLA Modules:
  0.0 146.2 jit_solution(379939922835028723)
XLA Ops:
  0.6 2.7 %shard_map.77 = (f32[7,8,32,128]{3,2,1,0:T(8,128)S(1)}, f32[8,32,128]{2,1,0:T(8,128)S(1)}, f32[8,32,128]{2,1,0:T(8,128)S(1)}, f32[2,32,128]{2,1,0:T(8,128)S(1)},...) custom-call(s32[1,64]{1,0:T(1,128)} %bitcast.17, ...), custom_call_target="tpu_custom_call" | custom-call | tf_op jit(solution)/shard_map/pallas_call | solution.py:643
  3.3 20.5 %collective-permute-start = (f32[2,32,128]{2,1,0:T(8,128)S(1)}, f32[2,32,128]{2,1,0:T(8,128)S(1)}, u32[]{:S(2)}, u32[]{:S(2)}) collective-permute-start(f32[2,32,128]{2,1,0:T(8,128)S(1)} %get-tuple-element.50), channel_id=1, source_target_pairs={{0,764},{4,8},{8,4},{12,16},{16,12},{20,24},{24,20},{28,32},{32,28... | collective-permute-start | bytes 98312 | tf_op jit(solution)/shard_map/ppermute | solution.py:669
  23.8 1.9 %collective-permute-start.1 = (f32[2,32,128]{2,1,0:T(8,128)S(1)}, f32[2,32,128]{2,1,0:T(8,128)S(1)}, u32[]{:S(2)}, u32[]{:S(2)}) collective-permute-start(f32[2,32,128]{2,1,0:T(8,128)S(1)} %get-tuple-element.51), channel_id=1, source_target_pairs={{0,4},{4,0},{8,12},{12,8},{16,20},{20,16},{24,28},{28,24},{32,36},... | collective-permute-start | bytes 98312 | tf_op jit(solution)/shard_map/ppermute | solution.py:672
  25.7 3.1 %collective-permute-start.2 = (f32[9,4,16,128]{3,2,1,0:T(8,128)S(1)}, f32[9,4,16,128]{3,2,1,0:T(8,128)S(1)}, u32[]{:S(2)}, u32[]{:S(2)}) collective-permute-start(f32[9,4,16,128]{3,2,1,0:T(8,128)S(1)} %get-tuple-element.53), channel_id=1, source_target_pairs={{0,1},{1,2},{2,3},{3,0},{4,5},{5,6},{6,7},{7,4},{8,9},{9,10},{10,1... | collective-permute-start | bytes 884744 | tf_op jit(solution)/shard_map/ppermute | solution.py:688
  28.8 1.9 %collective-permute-start.3 = (f32[9,4,16,128]{3,2,1,0:T(8,128)S(1)}, f32[9,4,16,128]{3,2,1,0:T(8,128)S(1)}, u32[]{:S(2)}, u32[]{:S(2)}) collective-permute-start(f32[9,4,16,128]{3,2,1,0:T(8,128)S(1)} %get-tuple-element.54), channel_id=1, source_target_pairs={{0,3},{1,0},{2,1},{3,2},{4,7},{5,4},{6,5},{7,6},{8,11},{9,8},{10,9... | collective-permute-start | bytes 884744 | tf_op jit(solution)/shard_map/ppermute | solution.py:689
  30.8 0.1 shard_map.78
  30.9 8.8 %all-gather = f32[8,48,128]{2,1,0:T(8,128)S(1)} all-gather(f32[2,48,128]{2,1,0:T(8,128)S(1)} %shard_map.78), channel_id=2, replica_groups=mesh['outer'=16,'ring'=12,'narrow'=4] {'narrow'}, dimensions={0}, use_global_device_ids=true | all-gather | bytes 245760 | tf_op jit(solution)/shard_map/all_gather | solution.py:679
  39.6 0.9 shard_map.79
  40.6 3.0 %collective-permute-start.4 = (f32[1,32,128]{2,1,0:T(8,128)S(1)}, f32[1,32,128]{2,1,0:T(8,128)S(1)}, u32[]{:S(2)}, u32[]{:S(2)}) collective-permute-start(f32[1,32,128]{2,1,0:T(8,128)S(1)} %get-tuple-element.57), channel_id=1, source_target_pairs={{0,764},{4,8},{8,4},{12,16},{16,12},{20,24},{24,20},{28,32},{32,28... | collective-permute-start | bytes 49160 | tf_op jit(solution)/shard_map/ppermute | solution.py:669
  43.6 2.6 %collective-permute-start.5 = (f32[1,32,128]{2,1,0:T(8,128)S(1)}, f32[1,32,128]{2,1,0:T(8,128)S(1)}, u32[]{:S(2)}, u32[]{:S(2)}) collective-permute-start(f32[1,32,128]{2,1,0:T(8,128)S(1)} %get-tuple-element.58), channel_id=1, source_target_pairs={{0,4},{4,0},{8,12},{12,8},{16,20},{20,16},{24,28},{28,24},{32,36},... | collective-permute-start | bytes 49160 | tf_op jit(solution)/shard_map/ppermute | solution.py:672
  46.2 4.6 %collective-permute-done.4.h0 = f32[1,32,128]{2,1,0:T(8,128)S(1)} collective-permute-done((f32[1,32,128]{2,1,0:T(8,128)S(1)}, f32[1,32,128]{2,1,0:T(8,128)S(1)}, u32[]{:S(2)}, u32[]{:S(2)}) %collective-permute-start.4) | collective-permute-done | bytes 16416 | tf_op jit(solution)/shard_map/ppermute | solution.py:669
  50.8 0.7 shard_map.80
  51.5 5.3 %collective-permute-start.6 = (f32[1,32,128]{2,1,0:T(8,128)S(1)}, f32[1,32,128]{2,1,0:T(8,128)S(1)}, u32[]{:S(2)}, u32[]{:S(2)}) collective-permute-start(f32[1,32,128]{2,1,0:T(8,128)S(1)} %get-tuple-element.63), channel_id=1, source_target_pairs={{0,764},{4,8},{8,4},{12,16},{16,12},{20,24},{24,20},{28,32},{32,28... | collective-permute-start | bytes 49160 | tf_op jit(solution)/shard_map/ppermute | solution.py:669
  56.8 1.9 %collective-permute-start.7 = (f32[1,32,128]{2,1,0:T(8,128)S(1)}, f32[1,32,128]{2,1,0:T(8,128)S(1)}, u32[]{:S(2)}, u32[]{:S(2)}) collective-permute-start(f32[1,32,128]{2,1,0:T(8,128)S(1)} %get-tuple-element.64), channel_id=1, source_target_pairs={{0,4},{4,0},{8,12},{12,8},{16,20},{20,16},{24,28},{28,24},{32,36},... | collective-permute-start | bytes 49160 | tf_op jit(solution)/shard_map/ppermute | solution.py:672
  58.7 4.5 %collective-permute-start.8 = (f32[1,4,16,128]{3,2,1,0:T(8,128)S(1)}, f32[1,4,16,128]{3,2,1,0:T(8,128)S(1)}, u32[]{:S(2)}, u32[]{:S(2)}) collective-permute-start(f32[1,4,16,128]{3,2,1,0:T(8,128)S(1)} %get-tuple-element.66), channel_id=1, source_target_pairs={{0,1},{1,2},{2,3},{3,0},{4,5},{5,6},{6,7},{7,4},{8,9},{9,10},{10,1... | collective-permute-start | bytes 98312 | tf_op jit(solution)/shard_map/ppermute | solution.py:688
  63.2 1.9 %collective-permute-start.9 = (f32[1,4,16,128]{3,2,1,0:T(8,128)S(1)}, f32[1,4,16,128]{3,2,1,0:T(8,128)S(1)}, u32[]{:S(2)}, u32[]{:S(2)}) collective-permute-start(f32[1,4,16,128]{3,2,1,0:T(8,128)S(1)} %get-tuple-element.67), channel_id=1, source_target_pairs={{0,3},{1,0},{2,1},{3,2},{4,7},{5,4},{6,5},{7,6},{8,11},{9,8},{10,9... | collective-permute-start | bytes 98312 | tf_op jit(solution)/shard_map/ppermute | solution.py:689
  65.2 0.1 shard_map.81
  65.3 6.2 %all-gather.1 = f32[4,48,128]{2,1,0:T(8,128)S(1)} all-gather(f32[1,48,128]{2,1,0:T(8,128)S(1)} %shard_map.81), channel_id=3, replica_groups=mesh['outer'=16,'ring'=12,'narrow'=4] {'narrow'}, dimensions={0}, use_global_device_ids=true | all-gather | bytes 122880 | tf_op jit(solution)/shard_map/all_gather | solution.py:679
  71.5 0.9 shard_map.82
  72.4 5.4 %collective-permute-start.10 = (f32[1,32,128]{2,1,0:T(8,128)S(1)}, f32[1,32,128]{2,1,0:T(8,128)S(1)}, u32[]{:S(2)}, u32[]{:S(2)}) collective-permute-start(f32[1,32,128]{2,1,0:T(8,128)S(1)} %get-tuple-element.72), channel_id=1, source_target_pairs={{0,764},{4,8},{8,4},{12,16},{16,12},{20,24},{24,20},{28,32},{32,28... | collective-permute-start | bytes 49160 | tf_op jit(solution)/shard_map/ppermute | solution.py:669
  77.9 1.9 %collective-permute-start.11 = (f32[1,32,128]{2,1,0:T(8,128)S(1)}, f32[1,32,128]{2,1,0:T(8,128)S(1)}, u32[]{:S(2)}, u32[]{:S(2)}) collective-permute-start(f32[1,32,128]{2,1,0:T(8,128)S(1)} %get-tuple-element.73), channel_id=1, source_target_pairs={{0,4},{4,0},{8,12},{12,8},{16,20},{20,16},{24,28},{28,24},{32,36},... | collective-permute-start | bytes 49160 | tf_op jit(solution)/shard_map/ppermute | solution.py:672
  79.8 2.8 %collective-permute-done.10.h0 = f32[1,32,128]{2,1,0:T(8,128)S(1)} collective-permute-done((f32[1,32,128]{2,1,0:T(8,128)S(1)}, f32[1,32,128]{2,1,0:T(8,128)S(1)}, u32[]{:S(2)}, u32[]{:S(2)}) %collective-permute-start.10) | collective-permute-done | bytes 16416 | tf_op jit(solution)/shard_map/ppermute | solution.py:669
  82.6 0.0 collective-permute-done.11.h1
  82.6 0.7 shard_map.83
  83.3 5.6 %collective-permute-start.12 = (f32[1,32,128]{2,1,0:T(8,128)S(1)}, f32[1,32,128]{2,1,0:T(8,128)S(1)}, u32[]{:S(2)}, u32[]{:S(2)}) collective-permute-start(f32[1,32,128]{2,1,0:T(8,128)S(1)} %get-tuple-element.75), channel_id=1, source_target_pairs={{0,764},{4,8},{8,4},{12,16},{16,12},{20,24},{24,20},{28,32},{32,28... | collective-permute-start | bytes 49160 | tf_op jit(solution)/shard_map/ppermute | solution.py:669
  88.9 1.9 %collective-permute-start.13 = (f32[1,32,128]{2,1,0:T(8,128)S(1)}, f32[1,32,128]{2,1,0:T(8,128)S(1)}, u32[]{:S(2)}, u32[]{:S(2)}) collective-permute-start(f32[1,32,128]{2,1,0:T(8,128)S(1)} %get-tuple-element.76), channel_id=1, source_target_pairs={{0,4},{4,0},{8,12},{12,8},{16,20},{20,16},{24,28},{28,24},{32,36},... | collective-permute-start | bytes 49160 | tf_op jit(solution)/shard_map/ppermute | solution.py:672
  90.8 4.2 %collective-permute-start.14 = (f32[1,4,16,128]{3,2,1,0:T(8,128)S(1)}, f32[1,4,16,128]{3,2,1,0:T(8,128)S(1)}, u32[]{:S(2)}, u32[]{:S(2)}) collective-permute-start(f32[1,4,16,128]{3,2,1,0:T(8,128)S(1)} %get-tuple-element.78), channel_id=1, source_target_pairs={{0,1},{1,2},{2,3},{3,0},{4,5},{5,6},{6,7},{7,4},{8,9},{9,10},{10,1... | collective-permute-start | bytes 98312 | tf_op jit(solution)/shard_map/ppermute | solution.py:688
  95.0 1.9 %collective-permute-start.15 = (f32[1,4,16,128]{3,2,1,0:T(8,128)S(1)}, f32[1,4,16,128]{3,2,1,0:T(8,128)S(1)}, u32[]{:S(2)}, u32[]{:S(2)}) collective-permute-start(f32[1,4,16,128]{3,2,1,0:T(8,128)S(1)} %get-tuple-element.79), channel_id=1, source_target_pairs={{0,3},{1,0},{2,1},{3,2},{4,7},{5,4},{6,5},{7,6},{8,11},{9,8},{10,9... | collective-permute-start | bytes 98312 | tf_op jit(solution)/shard_map/ppermute | solution.py:689
  97.0 0.1 shard_map.84
  97.1 6.2 %all-gather.2 = f32[4,48,128]{2,1,0:T(8,128)S(1)} all-gather(f32[1,48,128]{2,1,0:T(8,128)S(1)} %shard_map.84), channel_id=4, replica_groups=mesh['outer'=16,'ring'=12,'narrow'=4] {'narrow'}, dimensions={0}, use_global_device_ids=true | all-gather | bytes 122880 | tf_op jit(solution)/shard_map/all_gather | solution.py:679
  103.3 0.9 shard_map.85
  104.2 5.4 %collective-permute-start.16 = (f32[1,32,128]{2,1,0:T(8,128)S(1)}, f32[1,32,128]{2,1,0:T(8,128)S(1)}, u32[]{:S(2)}, u32[]{:S(2)}) collective-permute-start(f32[1,32,128]{2,1,0:T(8,128)S(1)} %get-tuple-element.83), channel_id=1, source_target_pairs={{0,764},{4,8},{8,4},{12,16},{16,12},{20,24},{24,20},{28,32},{32,28... | collective-permute-start | bytes 49160 | tf_op jit(solution)/shard_map/ppermute | solution.py:669
  109.7 1.9 %collective-permute-start.17 = (f32[1,32,128]{2,1,0:T(8,128)S(1)}, f32[1,32,128]{2,1,0:T(8,128)S(1)}, u32[]{:S(2)}, u32[]{:S(2)}) collective-permute-start(f32[1,32,128]{2,1,0:T(8,128)S(1)} %get-tuple-element.84), channel_id=1, source_target_pairs={{0,4},{4,0},{8,12},{12,8},{16,20},{20,16},{24,28},{28,24},{32,36},... | collective-permute-start | bytes 49160 | tf_op jit(solution)/shard_map/ppermute | solution.py:672
  111.6 2.8 %collective-permute-done.16.h0 = f32[1,32,128]{2,1,0:T(8,128)S(1)} collective-permute-done((f32[1,32,128]{2,1,0:T(8,128)S(1)}, f32[1,32,128]{2,1,0:T(8,128)S(1)}, u32[]{:S(2)}, u32[]{:S(2)}) %collective-permute-start.16) | collective-permute-done | bytes 16416 | tf_op jit(solution)/shard_map/ppermute | solution.py:669
  114.4 0.0 collective-permute-done.17.h1
  114.4 1.3 shard_map.86
  115.7 6.5 %all-to-all-start = ((f32[64,1,128]{2,1,0:T(1,128)}), f32[64,1,128]{2,1,0:T(1,128)S(1)}, u32[]{:S(2)}, u32[]{:S(2)}) async-start(f32[64,1,128]{2,1,0:T(1,128)} %bitcast.5), calls=%async_computation | async-start | bytes 65536 | tf_op jit(solution)/shard_map/all_to_all | solution.py:754
  122.2 8.2 %collective-permute-start.18 = (f32[1,32,128]{2,1,0:T(8,128)S(1)}, f32[1,32,128]{2,1,0:T(8,128)S(1)}, u32[]{:S(2)}, u32[]{:S(2)}) collective-permute-start(f32[1,32,128]{2,1,0:T(8,128)S(1)} %get-tuple-element.90), channel_id=1, source_target_pairs={{0,764},{4,8},{8,4},{12,16},{16,12},{20,24},{24,20},{28,32},{32,28... | collective-permute-start | bytes 49160 | tf_op jit(solution)/shard_map/ppermute | solution.py:669
  130.4 1.9 %collective-permute-start.19 = (f32[1,32,128]{2,1,0:T(8,128)S(1)}, f32[1,32,128]{2,1,0:T(8,128)S(1)}, u32[]{:S(2)}, u32[]{:S(2)}) collective-permute-start(f32[1,32,128]{2,1,0:T(8,128)S(1)} %get-tuple-element.91), channel_id=1, source_target_pairs={{0,4},{4,0},{8,12},{12,8},{16,20},{20,16},{24,28},{28,24},{32,36},... | collective-permute-start | bytes 49160 | tf_op jit(solution)/shard_map/ppermute | solution.py:672
  132.3 0.1 copy.10.order_ref
  132.4 0.1 reduce_sum.9
  132.5 0.6 broadcast_in_dim.2
  133.1 3.5 %all-to-all-start.1 = ((f32[12,1,128]{2,1,0:T(1,128)}), f32[12,1,128]{2,1,0:T(1,128)S(1)}, u32[]{:S(2)}, u32[]{:S(2)}) async-start(f32[12,1,128]{2,1,0:T(1,128)} %broadcast_in_dim.2), calls=%async_computation.1 | async-start | bytes 12288 | tf_op jit(solution)/shard_map/all_to_all | solution.py:758
  136.6 0.1 shard_map.87
  136.7 5.6 %all-gather.3 = f32[4,16,128]{2,1,0:T(8,128)S(1)} all-gather(f32[1,16,128]{2,1,0:T(8,128)S(1)} %shard_map.87), channel_id=5, replica_groups=mesh['outer'=16,'ring'=12,'narrow'=4] {'narrow'}, dimensions={0}, use_global_device_ids=true | all-gather | bytes 40960 | tf_op jit(solution)/shard_map/all_gather | solution.py:679
  142.3 0.6 shard_map.88.spread_ref
  142.9 2.4 %all-to-all-done.1 = f32[12,1,128]{2,1,0:T(1,128)S(1)} async-done(((f32[12,1,128]{2,1,0:T(1,128)}), f32[12,1,128]{2,1,0:T(1,128)S(1)}, u32[]{:S(2)}, u32[]{:S(2)}) %all-to-all-start.1) | async-done | bytes 6176 | tf_op jit(solution)/shard_map/all_to_all | solution.py:758
  145.3 0.8 shard_map.89
  (23 shorter events, 0.1 us)
Async XLA Ops:
  3.3 27.4 %collective-permute-start = (f32[2,32,128]{2,1,0:T(8,128)S(1)}, f32[2,32,128]{2,1,0:T(8,128)S(1)}, u32[]{:S(2)}, u32[]{:S(2)}) collective-permute-start(f32[2,32,128]{2,1,0:T(8,128)S(1)} %get-tuple-element.50), channel_id=1, source_target_pairs={{0,764},{4,8},{8,4},{12,16},{16,12},{20,24},{24,20},{28,32},{32,28... | collective-permute-start | bytes 98312 | tf_op jit(solution)/shard_map/ppermute | solution.py:669
  23.8 6.9 %collective-permute-start.1 = (f32[2,32,128]{2,1,0:T(8,128)S(1)}, f32[2,32,128]{2,1,0:T(8,128)S(1)}, u32[]{:S(2)}, u32[]{:S(2)}) collective-permute-start(f32[2,32,128]{2,1,0:T(8,128)S(1)} %get-tuple-element.51), channel_id=1, source_target_pairs={{0,4},{4,0},{8,12},{12,8},{16,20},{20,16},{24,28},{28,24},{32,36},... | collective-permute-start | bytes 98312 | tf_op jit(solution)/shard_map/ppermute | solution.py:672
  25.7 13.9 %collective-permute-start.2 = (f32[9,4,16,128]{3,2,1,0:T(8,128)S(1)}, f32[9,4,16,128]{3,2,1,0:T(8,128)S(1)}, u32[]{:S(2)}, u32[]{:S(2)}) collective-permute-start(f32[9,4,16,128]{3,2,1,0:T(8,128)S(1)} %get-tuple-element.53), channel_id=1, source_target_pairs={{0,1},{1,2},{2,3},{3,0},{4,5},{5,6},{6,7},{7,4},{8,9},{9,10},{10,1... | collective-permute-start | bytes 884744 | tf_op jit(solution)/shard_map/ppermute | solution.py:688
  28.8 10.8 %collective-permute-start.3 = (f32[9,4,16,128]{3,2,1,0:T(8,128)S(1)}, f32[9,4,16,128]{3,2,1,0:T(8,128)S(1)}, u32[]{:S(2)}, u32[]{:S(2)}) collective-permute-start(f32[9,4,16,128]{3,2,1,0:T(8,128)S(1)} %get-tuple-element.54), channel_id=1, source_target_pairs={{0,3},{1,0},{2,1},{3,2},{4,7},{5,4},{6,5},{7,6},{8,11},{9,8},{10,9... | collective-permute-start | bytes 884744 | tf_op jit(solution)/shard_map/ppermute | solution.py:689
  30.8 8.9 %copy-start.1 = (bf16[256,256]{1,0:T(8,128)(2,1)S(1)}, bf16[256,256]{1,0:T(8,128)(2,1)}, u32[]{:S(2)}) copy-start(bf16[256,256]{1,0:T(8,128)(2,1)} %constant.9.clone.diver_ref) | copy-start | bytes 393220
  30.9 8.8 %copy-start = (bf16[384,256]{1,0:T(8,128)(2,1)S(1)}, bf16[384,256]{1,0:T(8,128)(2,1)}, u32[]{:S(2)}) copy-start(bf16[384,256]{1,0:T(8,128)(2,1)} %constant.8.clone.grad_ref) | copy-start | bytes 589828
  40.6 10.2 %collective-permute-start.4 = (f32[1,32,128]{2,1,0:T(8,128)S(1)}, f32[1,32,128]{2,1,0:T(8,128)S(1)}, u32[]{:S(2)}, u32[]{:S(2)}) collective-permute-start(f32[1,32,128]{2,1,0:T(8,128)S(1)} %get-tuple-element.57), channel_id=1, source_target_pairs={{0,764},{4,8},{8,4},{12,16},{16,12},{20,24},{24,20},{28,32},{32,28... | collective-permute-start | bytes 49160 | tf_op jit(solution)/shard_map/ppermute | solution.py:669
  43.6 7.2 %collective-permute-start.5 = (f32[1,32,128]{2,1,0:T(8,128)S(1)}, f32[1,32,128]{2,1,0:T(8,128)S(1)}, u32[]{:S(2)}, u32[]{:S(2)}) collective-permute-start(f32[1,32,128]{2,1,0:T(8,128)S(1)} %get-tuple-element.58), channel_id=1, source_target_pairs={{0,4},{4,0},{8,12},{12,8},{16,20},{20,16},{24,28},{28,24},{32,36},... | collective-permute-start | bytes 49160 | tf_op jit(solution)/shard_map/ppermute | solution.py:672
  51.5 13.6 %collective-permute-start.6 = (f32[1,32,128]{2,1,0:T(8,128)S(1)}, f32[1,32,128]{2,1,0:T(8,128)S(1)}, u32[]{:S(2)}, u32[]{:S(2)}) collective-permute-start(f32[1,32,128]{2,1,0:T(8,128)S(1)} %get-tuple-element.63), channel_id=1, source_target_pairs={{0,764},{4,8},{8,4},{12,16},{16,12},{20,24},{24,20},{28,32},{32,28... | collective-permute-start | bytes 49160 | tf_op jit(solution)/shard_map/ppermute | solution.py:669
  56.8 8.3 %collective-permute-start.7 = (f32[1,32,128]{2,1,0:T(8,128)S(1)}, f32[1,32,128]{2,1,0:T(8,128)S(1)}, u32[]{:S(2)}, u32[]{:S(2)}) collective-permute-start(f32[1,32,128]{2,1,0:T(8,128)S(1)} %get-tuple-element.64), channel_id=1, source_target_pairs={{0,4},{4,0},{8,12},{12,8},{16,20},{20,16},{24,28},{28,24},{32,36},... | collective-permute-start | bytes 49160 | tf_op jit(solution)/shard_map/ppermute | solution.py:672
  58.7 12.7 %collective-permute-start.8 = (f32[1,4,16,128]{3,2,1,0:T(8,128)S(1)}, f32[1,4,16,128]{3,2,1,0:T(8,128)S(1)}, u32[]{:S(2)}, u32[]{:S(2)}) collective-permute-start(f32[1,4,16,128]{3,2,1,0:T(8,128)S(1)} %get-tuple-element.66), channel_id=1, source_target_pairs={{0,1},{1,2},{2,3},{3,0},{4,5},{5,6},{6,7},{7,4},{8,9},{9,10},{10,1... | collective-permute-start | bytes 98312 | tf_op jit(solution)/shard_map/ppermute | solution.py:688
  63.2 8.3 %collective-permute-start.9 = (f32[1,4,16,128]{3,2,1,0:T(8,128)S(1)}, f32[1,4,16,128]{3,2,1,0:T(8,128)S(1)}, u32[]{:S(2)}, u32[]{:S(2)}) collective-permute-start(f32[1,4,16,128]{3,2,1,0:T(8,128)S(1)} %get-tuple-element.67), channel_id=1, source_target_pairs={{0,3},{1,0},{2,1},{3,2},{4,7},{5,4},{6,5},{7,6},{8,11},{9,8},{10,9... | collective-permute-start | bytes 98312 | tf_op jit(solution)/shard_map/ppermute | solution.py:689
  72.4 10.2 %collective-permute-start.10 = (f32[1,32,128]{2,1,0:T(8,128)S(1)}, f32[1,32,128]{2,1,0:T(8,128)S(1)}, u32[]{:S(2)}, u32[]{:S(2)}) collective-permute-start(f32[1,32,128]{2,1,0:T(8,128)S(1)} %get-tuple-element.72), channel_id=1, source_target_pairs={{0,764},{4,8},{8,4},{12,16},{16,12},{20,24},{24,20},{28,32},{32,28... | collective-permute-start | bytes 49160 | tf_op jit(solution)/shard_map/ppermute | solution.py:669
  77.9 4.8 %collective-permute-start.11 = (f32[1,32,128]{2,1,0:T(8,128)S(1)}, f32[1,32,128]{2,1,0:T(8,128)S(1)}, u32[]{:S(2)}, u32[]{:S(2)}) collective-permute-start(f32[1,32,128]{2,1,0:T(8,128)S(1)} %get-tuple-element.73), channel_id=1, source_target_pairs={{0,4},{4,0},{8,12},{12,8},{16,20},{20,16},{24,28},{28,24},{32,36},... | collective-permute-start | bytes 49160 | tf_op jit(solution)/shard_map/ppermute | solution.py:672
  83.3 13.6 %collective-permute-start.12 = (f32[1,32,128]{2,1,0:T(8,128)S(1)}, f32[1,32,128]{2,1,0:T(8,128)S(1)}, u32[]{:S(2)}, u32[]{:S(2)}) collective-permute-start(f32[1,32,128]{2,1,0:T(8,128)S(1)} %get-tuple-element.75), channel_id=1, source_target_pairs={{0,764},{4,8},{8,4},{12,16},{16,12},{20,24},{24,20},{28,32},{32,28... | collective-permute-start | bytes 49160 | tf_op jit(solution)/shard_map/ppermute | solution.py:669
  88.9 8.1 %collective-permute-start.13 = (f32[1,32,128]{2,1,0:T(8,128)S(1)}, f32[1,32,128]{2,1,0:T(8,128)S(1)}, u32[]{:S(2)}, u32[]{:S(2)}) collective-permute-start(f32[1,32,128]{2,1,0:T(8,128)S(1)} %get-tuple-element.76), channel_id=1, source_target_pairs={{0,4},{4,0},{8,12},{12,8},{16,20},{20,16},{24,28},{28,24},{32,36},... | collective-permute-start | bytes 49160 | tf_op jit(solution)/shard_map/ppermute | solution.py:672
  90.8 12.4 %collective-permute-start.14 = (f32[1,4,16,128]{3,2,1,0:T(8,128)S(1)}, f32[1,4,16,128]{3,2,1,0:T(8,128)S(1)}, u32[]{:S(2)}, u32[]{:S(2)}) collective-permute-start(f32[1,4,16,128]{3,2,1,0:T(8,128)S(1)} %get-tuple-element.78), channel_id=1, source_target_pairs={{0,1},{1,2},{2,3},{3,0},{4,5},{5,6},{6,7},{7,4},{8,9},{9,10},{10,1... | collective-permute-start | bytes 98312 | tf_op jit(solution)/shard_map/ppermute | solution.py:688
  95.0 8.3 %collective-permute-start.15 = (f32[1,4,16,128]{3,2,1,0:T(8,128)S(1)}, f32[1,4,16,128]{3,2,1,0:T(8,128)S(1)}, u32[]{:S(2)}, u32[]{:S(2)}) collective-permute-start(f32[1,4,16,128]{3,2,1,0:T(8,128)S(1)} %get-tuple-element.79), channel_id=1, source_target_pairs={{0,3},{1,0},{2,1},{3,2},{4,7},{5,4},{6,5},{7,6},{8,11},{9,8},{10,9... | collective-permute-start | bytes 98312 | tf_op jit(solution)/shard_map/ppermute | solution.py:689
  104.2 10.2 %collective-permute-start.16 = (f32[1,32,128]{2,1,0:T(8,128)S(1)}, f32[1,32,128]{2,1,0:T(8,128)S(1)}, u32[]{:S(2)}, u32[]{:S(2)}) collective-permute-start(f32[1,32,128]{2,1,0:T(8,128)S(1)} %get-tuple-element.83), channel_id=1, source_target_pairs={{0,764},{4,8},{8,4},{12,16},{16,12},{20,24},{24,20},{28,32},{32,28... | collective-permute-start | bytes 49160 | tf_op jit(solution)/shard_map/ppermute | solution.py:669
  109.7 4.8 %collective-permute-start.17 = (f32[1,32,128]{2,1,0:T(8,128)S(1)}, f32[1,32,128]{2,1,0:T(8,128)S(1)}, u32[]{:S(2)}, u32[]{:S(2)}) collective-permute-start(f32[1,32,128]{2,1,0:T(8,128)S(1)} %get-tuple-element.84), channel_id=1, source_target_pairs={{0,4},{4,0},{8,12},{12,8},{16,20},{20,16},{24,28},{28,24},{32,36},... | collective-permute-start | bytes 49160 | tf_op jit(solution)/shard_map/ppermute | solution.py:672
  115.7 16.7 %all-to-all-start = ((f32[64,1,128]{2,1,0:T(1,128)}), f32[64,1,128]{2,1,0:T(1,128)S(1)}, u32[]{:S(2)}, u32[]{:S(2)}) async-start(f32[64,1,128]{2,1,0:T(1,128)} %bitcast.5), calls=%async_computation | async-start | bytes 65536 | tf_op jit(solution)/shard_map/all_to_all | solution.py:754
  122.2 14.4 %collective-permute-start.18 = (f32[1,32,128]{2,1,0:T(8,128)S(1)}, f32[1,32,128]{2,1,0:T(8,128)S(1)}, u32[]{:S(2)}, u32[]{:S(2)}) collective-permute-start(f32[1,32,128]{2,1,0:T(8,128)S(1)} %get-tuple-element.90), channel_id=1, source_target_pairs={{0,764},{4,8},{8,4},{12,16},{16,12},{20,24},{24,20},{28,32},{32,28... | collective-permute-start | bytes 49160 | tf_op jit(solution)/shard_map/ppermute | solution.py:669
  130.4 1.9 %copy-start.2 = (s32[1,1,64]{2,1,0:T(1,128)S(1)}, s32[1,1,64]{2,1,0:T(1,128)}, u32[]{:S(2)}) copy-start(s32[1,1,64]{2,1,0:T(1,128)} %param.8) | copy-start | bytes 772
  130.4 6.2 %collective-permute-start.19 = (f32[1,32,128]{2,1,0:T(8,128)S(1)}, f32[1,32,128]{2,1,0:T(8,128)S(1)}, u32[]{:S(2)}, u32[]{:S(2)}) collective-permute-start(f32[1,32,128]{2,1,0:T(8,128)S(1)} %get-tuple-element.91), channel_id=1, source_target_pairs={{0,4},{4,0},{8,12},{12,8},{16,20},{20,16},{24,28},{28,24},{32,36},... | collective-permute-start | bytes 49160 | tf_op jit(solution)/shard_map/ppermute | solution.py:672
  133.1 12.2 %all-to-all-start.1 = ((f32[12,1,128]{2,1,0:T(1,128)}), f32[12,1,128]{2,1,0:T(1,128)S(1)}, u32[]{:S(2)}, u32[]{:S(2)}) async-start(f32[12,1,128]{2,1,0:T(1,128)} %broadcast_in_dim.2), calls=%async_computation.1 | async-start | bytes 12288 | tf_op jit(solution)/shard_map/all_to_all | solution.py:758

commit v5 on v4

--- a/solution.py
+++ b/solution.py
@@ -164,19 +164,28 @@
     return jnp.where(low, even, roll(odd, 64, 1)), jnp.where(low, roll(even, 64, 1), odd)
 
 
-def store_edges(lo_ref, hi_ref, c, values):
+def store_edges(lo_ref, hi_ref, lo_at, hi_at, values):
     for b in range(NODES // 2):
-        lo_ref[c, b], hi_ref[c, b] = packed_edges(values[2 * b], values[2 * b + 1])
-
-
-def ghost_columns(left_ref, right_ref, c):
+        lo_ref[lo_at, b], hi_ref[hi_at, b] = packed_edges(values[2 * b], values[2 * b + 1])
+
+
+def ghost_columns(lefts, rights):
     low = lane_iota(HALF) < 64
     out = []
     for b in range(NODES // 2):
-        left, right = left_ref[c, b], right_ref[c, b]
+        left, right = lefts[b], rights[b]
         out.append(jnp.where(low, left, roll(right, 64, 1)))
         out.append(jnp.where(low, roll(left, 64, 1), right))
     return out
+
+
+def gathered_ghost(packs_ref):
+    left, right = beside(packs_ref)
+    half = range(NODES // 2)
+    return ghost_columns(
+        [packs_ref[left, 0, HALF * (5 + b) : HALF * (6 + b)] for b in half],
+        [packs_ref[right, 0, HALF * (1 + b) : HALF * (2 + b)] for b in half],
+    )
 
 
 def facing(left, right):
@@ -243,10 +252,16 @@
     return lax.broadcast_in_dim(lax.rem(lax.axis_index("ring"), 2), (ROWS, LANES), ()) == 0
 
 
+def near_face(near_ref, field, even):
+    if near_ref.ndim == 4:
+        return jnp.where(even, near_ref[1, field], near_ref[0, field])
+    return near_ref[field]
+
+
 def pack_kernel(pack_in, far_ref, near_ref, pack_ref):
     even = is_even()
     for field in range(pack_ref.shape[0]):
-        near, far = near_ref[field], far_ref[field]
+        near, far = near_face(near_ref, field, even), far_ref[field]
         first = jnp.where(even, far, near)
         last = jnp.where(even, near, far)
         pack_ref[field, :HALF] = (
@@ -257,6 +272,25 @@
             pack_ref[field, ROWS:] = edge(last)
 
 
+def pack_edges_kernel(step, pack_in, edges_in, inverse_ref, far_ref, near_ref, pack_ref):
+    even = is_even()
+    near, far = near_ref[0], far_ref[0]
+    first = jnp.where(even, far, near)
+    last = jnp.where(even, near, far)
+    pack_ref[0, :HALF] = pack_in[0] + ends(first) + roll(ends(last), 16 * (NODES - 1), 1)
+    zero = jnp.zeros((HALF, LANES), jnp.float32)
+    for b in range(NODES // 2):
+        lo, hi = edges_in[0, b], edges_in[1, b]
+        if b == 0:
+            add = packed_edges(edge(-step * inverse_ref[0] * first), zero)
+            lo, hi = lo + add[0], hi + add[1]
+        if b == NODES // 2 - 1:
+            add = packed_edges(zero, edge(-step * inverse_ref[NODES - 1] * last))
+            lo, hi = lo + add[0], hi + add[1]
+        pack_ref[0, HALF * (1 + b) : HALF * (2 + b)] = lo
+        pack_ref[0, HALF * (5 + b) : HALF * (6 + b)] = hi
+
+
 def beside(packs_ref):
     count = packs_ref.shape[0]
     here = lax.axis_index("narrow")
@@ -266,7 +300,7 @@
 def completed(kv, halo, field=0):
     far_ref, near_ref = halo[:2]
     even = is_even()
-    near, far = near_ref[field], far_ref[field]
+    near, far = near_face(near_ref, field, even), far_ref[field]
     lane = lane_iota(HALF)
     if len(halo) > 2:
         left, right = beside(halo[2])
@@ -292,7 +326,7 @@
     return value
 
 
-def ghost_sums(packs_ref, field=0):
+def ghost_sums(packs_ref, field=0, wide_too=False):
     left, right = beside(packs_ref)
     lane = lane_iota(HALF)
     own = packs_ref[lax.axis_index("narrow"), field, :HALF]
@@ -301,7 +335,7 @@
 
     def value(i):
         u = jnp.where(inner, roll(lines, 56 - 16 * i, 1), 0.0)
-        if i in (0, NODES - 1):
+        if wide_too and i in (0, NODES - 1):
             rows = slice(HALF, ROWS) if i == 0 else slice(ROWS, GROWS)
             u = u + facing(packs_ref[left, field, rows], packs_ref[right, field, rows])
         return u
@@ -408,7 +442,7 @@
     store_assembled(
         load_kv, far_ref, near_ref, even, lambda i: work_ref[i], 0, pack_ref
     )
-    store_edges(lo_ref, hi_ref, 7, [edge(load_kv[i]) for i in range(NODES)])
+    store_edges(lo_ref, hi_ref, 7, 7, [edge(load_kv[i]) for i in range(NODES)])
 
     copies[2].wait()
     for c in range(7):
@@ -417,7 +451,7 @@
             metric_ref[c, i] = value
 
         spread(dot(pick, geom_ref[c]), store_metric)
-        store_edges(lo_ref, hi_ref, c, [edge(metric_ref[c, i]) for i in range(NODES)])
+        store_edges(lo_ref, hi_ref, c, c, [edge(metric_ref[c, i]) for i in range(NODES)])
 
     lane = lane_iota(8)
     q_a = jnp.zeros((8, LANES), jnp.float32)
@@ -444,7 +478,7 @@
     store_assembled(
         bound_kv, far_ref, near_ref, even, lambda i: work_ref[i], 1, pack_ref
     )
-    store_edges(lo_ref, hi_ref, 8, [edge(bound_kv[i]) for i in range(NODES)])
+    store_edges(lo_ref, hi_ref, 8, 8, [edge(bound_kv[i]) for i in range(NODES)])
 
 
 def first_kernel(
@@ -462,14 +496,14 @@
         inverse_ref[i] = inverse
         update_ref[i] = update
         v_ref[i, :ROWS] = update
-    residual, residual_sums = ghost_columns(left_ref, right_ref, 7), ghost_sums(h2, 0)
-    bound, bound_sums = ghost_columns(left_ref, right_ref, 8), ghost_sums(h2, 1)
+    residual, residual_sums = ghost_columns(left_ref[7], right_ref[7]), ghost_sums(h2, 0, True)
+    bound, bound_sums = ghost_columns(left_ref[8], right_ref[8]), ghost_sums(h2, 1, True)
     for i in range(NODES):
         inverse = 1.0 / (bound[i] + bound_sums(i))
         ghost_inverse[i] = inverse
         v_ref[i, ROWS:] = (residual[i] + residual_sums(i)) * inverse * (1.0 / CENTER)
     for c in range(7):
-        for i, value in enumerate(ghost_columns(left_ref, right_ref, c)):
+        for i, value in enumerate(ghost_columns(left_ref[c], right_ref[c])):
             ghost_metric[c, i] = value
     apply_element(v_ref, metric_ref, ghost_metric, grad_ref, diver_ref, flux_ref, work_ref)
     store_assembled(kv_ref, far_ref, near_ref, is_even(), lambda i: work_ref[i])
@@ -477,7 +511,7 @@
 
 def second_kernel(
     kv_in, h0, h1, source_ref, inverse_ref, update_in, metric_ref, grad_ref, diver_ref,
-    start_ref, kv_ref, far_ref, near_ref, pack_ref, lo_ref, hi_ref, v_ref, flux_ref, work_ref,
+    start_ref, kv_ref, far_ref, near_ref, pack_ref, edges_ref, v_ref, flux_ref, work_ref,
 ):
     image = completed(kv_in, (h0, h1))
     for i in range(NODES):
@@ -493,13 +527,13 @@
         kv_ref, far_ref, near_ref, is_even(), lambda i: work_ref[i], 0, pack_ref
     )
     store_edges(
-        lo_ref, hi_ref, 0,
+        edges_ref, edges_ref, 0, 1,
         [edge(start_ref[i] - STEP2 * inverse_ref[i] * kv_ref[i]) for i in range(NODES)],
     )
 
 
 def third_kernel(
-    kv_in, h0, h1, h2, left_ref, right_ref, source_ref, inverse_ref, start_ref,
+    kv_in, h0, h1, h2, source_ref, inverse_ref, start_ref,
     ghost_inverse, ghost_metric, metric_ref, grad_ref, diver_ref,
     result_ref, kv_ref, far_ref, near_ref, sums_ref, v_ref, flux_ref, work_ref,
 ):
@@ -511,7 +545,7 @@
         result_ref[i] = result
         v_ref[i, :ROWS] = result
         rz = rz + source_ref[i] * result * node_weight(i)
-    start, sums = ghost_columns(left_ref, right_ref, 0), ghost_sums(h2)
+    start, sums = gathered_ghost(h2), ghost_sums(h2)
     for i in range(NODES):
         v_ref[i, ROWS:] = start[i] - STEP2 * ghost_inverse[i] * sums(i)
     apply_element(v_ref, metric_ref, ghost_metric, grad_ref, diver_ref, flux_ref, work_ref)
@@ -524,7 +558,7 @@
 
 def fourth_kernel(
     kv_in, h0, h1, inverse_ref, metric_ref, grad_ref, diver_ref,
-    image_ref, update_ref, kv_ref, far_ref, near_ref, pack_ref, lo_ref, hi_ref, flux_ref, work_ref,
+    image_ref, update_ref, kv_ref, far_ref, near_ref, pack_ref, edges_ref, flux_ref, work_ref,
 ):
     image = completed(kv_in, (h0, h1))
     for i in range(NODES):
@@ -537,13 +571,13 @@
     )
     scale = 1.0 + RHO1 * RHO0 + STEP1 * CENTER
     store_edges(
-        lo_ref, hi_ref, 0,
+        edges_ref, edges_ref, 0, 1,
         [edge(scale * update_ref[i] - STEP1 * inverse_ref[i] * kv_ref[i]) for i in range(NODES)],
     )
 
 
 def fifth_kernel(
-    kv_in, h0, h1, h2, left_ref, right_ref, source_ref, inverse_ref, update_in,
+    kv_in, h0, h1, h2, source_ref, inverse_ref, update_in,
     ghost_inverse, ghost_metric, metric_ref, grad_ref, diver_ref,
     start_ref, kv_ref, far_ref, near_ref, v_ref, flux_ref, work_ref,
 ):
@@ -556,7 +590,7 @@
         result = old + update
         v_ref[i, :ROWS] = result
         start_ref[i] = result + (RHO2 * RHO1) * update + STEP2 * inverse * source
-    start, sums = ghost_columns(left_ref, right_ref, 0), ghost_sums(h2)
+    start, sums = gathered_ghost(h2), ghost_sums(h2)
     for i in range(NODES):
         v_ref[i, ROWS:] = start[i] - STEP1 * ghost_inverse[i] * sums(i)
     apply_element(v_ref, metric_ref, ghost_metric, grad_ref, diver_ref, flux_ref, work_ref)
@@ -664,13 +698,16 @@
     return [(fields, HALF, LANES)]
 
 
+def swap_far(far):
+    count = lax.axis_size(WIDE)
+    return lax.ppermute(
+        far, WIDE, [(w, (w + 1 if w % 2 else w - 1) % count) for w in range(count)]
+    )
+
+
 def swap_wide(far, near):
     count = lax.axis_size(WIDE)
-    far = lax.ppermute(
-        far, WIDE, [(w, (w + 1 if w % 2 else w - 1) % count) for w in range(count)]
-    )
-    near = lax.ppermute(near, WIDE, [(w, w ^ 1) for w in range(count)])
-    return far, near
+    return swap_far(far), lax.ppermute(near, WIDE, [(w, w ^ 1) for w in range(count)])
 
 
 def swap_all(far, near, pack, rows):
@@ -679,8 +716,19 @@
     return far, near, lax.all_gather(pack, "narrow")
 
 
-def edges(fields=1):
-    return [(fields, NODES // 2, HALF, LANES)] * 2
+def edges(fields):
+    return (fields, NODES // 2, HALF, LANES)
+
+
+def swap_edged(step, inverse, far, near, pack, edges_out):
+    far, near = swap_wide(far, near)
+    (pack,) = call(
+        functools.partial(pack_edges_kernel, step),
+        [(1, HALF * (1 + NODES), LANES)],
+        [],
+        pack, edges_out, inverse, far, near,
+    )
+    return far, near, lax.all_gather(pack, "narrow")
 
 
 def swap_edges(lo, hi):
@@ -695,7 +743,7 @@
     diver = jnp.asarray(DIVER_HL)
     metric, load_kv, bound_kv, *face, lo, hi = call(
         place_kernel,
-        [(7,) + FIELD, FIELD, FIELD] + faces(2) + packs(2) + edges(9),
+        [(7,) + FIELD, FIELD, FIELD] + faces(2) + packs(2) + [edges(9)] * 2,
         [
             FLUX, FIELD,
             pltpu.VMEM((1, 64), jnp.int32), pltpu.VMEM(load.shape, load.dtype),
@@ -714,34 +762,32 @@
         load_kv, bound_kv, *halo, *sides, metric, grad, diver,
     )
     halo = swap_wide(*face)
-    start, kv, *face, lo, hi = call(
+    start, kv, *face = call(
         second_kernel,
-        [FIELD, FIELD] + faces() + packs() + edges(),
+        [FIELD, FIELD] + faces() + packs() + [edges(2)],
         [FIELD, FLUX, FIELD],
         kv, *halo, residual, inverse, update, metric, grad, diver,
     )
-    sides = swap_edges(lo, hi)
-    halo = swap_all(*face, GROWS)
+    halo = swap_edged(STEP2, inverse, *face)
     first, kv, *face, early = call(
         third_kernel,
         [FIELD, FIELD] + faces() + [(1, LANES)],
         [BIG, BIG_FLUX, BIG],
-        kv, *halo, *sides, residual, inverse, start, ghost_inverse, ghost_metric, metric, grad, diver,
+        kv, *halo, residual, inverse, start, ghost_inverse, ghost_metric, metric, grad, diver,
     )
     halo = swap_wide(*face)
-    image, update, kv, *face, lo, hi = call(
+    image, update, kv, *face = call(
         fourth_kernel,
-        [FIELD, FIELD, FIELD] + faces() + packs() + edges(),
+        [FIELD, FIELD, FIELD] + faces() + packs() + [edges(2)],
         [FLUX, FIELD],
         kv, *halo, inverse, metric, grad, diver,
     )
-    sides = swap_edges(lo, hi)
-    halo = swap_all(*face, GROWS)
+    halo = swap_edged(STEP1, inverse, *face)
     start, kv, *face = call(
         fifth_kernel,
         [FIELD, FIELD] + faces(),
         [BIG, BIG_FLUX, BIG],
-        kv, *halo, *sides, image, inverse, update, ghost_inverse, ghost_metric, metric, grad, diver,
+        kv, *halo, image, inverse, update, ghost_inverse, ghost_metric, metric, grad, diver,
     )
     halo = swap_wide(*face)
     second, kv, *face, sums = call(
@@ -750,12 +796,18 @@
         [FLUX, FIELD],
         kv, *halo, image, inverse, start, residual, first, early, metric, grad, diver,
     )
-    halo = swap_all(*face, HALF)
+    far, near, pack = face
+    far = swap_far(far)
+    ring = lax.axis_size("ring")
     sums = lax.all_to_all(sums, REST, 0, 0)
-    sums = jnp.broadcast_to(
-        jnp.sum(sums, axis=0, keepdims=True), (lax.axis_size("ring"), LANES)
-    )
+    sums = jnp.broadcast_to(jnp.sum(sums, axis=0, keepdims=True), (ring, LANES))
+    near, sums = lax.optimization_barrier((near, sums))
     sums = lax.all_to_all(sums, "ring", 0, 0)
+    near = lax.all_gather(
+        near, "ring", axis_index_groups=[[v, v + 1] for v in range(0, ring, 2)]
+    )
+    (pack,) = call(pack_kernel, [pack.shape], [], pack, far, near)
+    halo = far, near, lax.all_gather(pack, "narrow")
     (spread,) = call(
         spread_kernel,
         [(5, 64, 512)],

time: 147 us -> 145 us (0.986)
  starting transfers between devices: 94.9 us -> 80.5 us
  blocking collectives: 26.8 us -> 35.2 us
  waiting for transfers between devices: 12.8 us -> 17.3 us
    all_gather x0 -> x4, blocking collectives: none -> 26.4 us  [the longest x2 16.3 us: swap_edged(): return (far, near, lax.all_gather(pack, 'narrow'))]
    all_gather x4 -> x1, blocking collectives: 26.8 us -> 8.75 us  [swap_all(): return (far, near, lax.all_gather(pack, 'narrow'))]
    ppermute x3 -> x1, starting transfers between devices: 11.7 us -> 3.06 us  [swap_edges(): lax.ppermute(hi, 'narrow', [(n, (n + 1) % count) for n in range(count)])]
    ppermute x14 -> x13, waiting for transfers between devices: 10.4 us -> 16.3 us  [the longest x7 15.9 us: swap_far(): lax.ppermute(far, WIDE, [(w, (w + 1 if w % 2 else w - 1) % count) for w i...]
    ppermute x3 -> x1, starting transfers between devices: 5.76 us -> 1.92 us  [swap_edges(): lax.ppermute(lo, 'narrow', [(n, (n - 1) % count) for n in range(count)])]
    all_to_all x1, waiting for transfers between devices: 2.44 us -> 0.01 us  [local(): sums = lax.all_to_all(sums, 'ring', 0, 0)]
    ppermute x14 -> x13, starting transfers between devices: 67.5 us -> 65.8 us  [the longest x7 53.6 us: swap_far(): lax.ppermute(far, WIDE, [(w, (w + 1 if w % 2 else w - 1) % count) for w i...]
  transfers between devices with their start and end apart: 22 -> 17, of which waited for: 4 -> 8; matrix products, arithmetic and copies ran while one was open for 1% -> 0% of each run, Pallas kernels for 1% -> 1%
where the time goes in v5:
time: 145 us
  starting transfers between devices  80.5 us (56%)
  blocking collectives  35.2 us (24%)
  waiting for transfers between devices  17.3 us (12%)
  Pallas kernels  9.91 us (7%)
    ppermute x7, starting transfers between devices, swap_far(): lax.ppermute(far, WIDE, [(w, (w + 1 if w % 2 else w - 1) % count) for w i...  53.6 us
    all_gather x2, blocking collectives, swap_edged(): return (far, near, lax.all_gather(pack, 'narrow'))  16.3 us
    ppermute x7, waiting for transfers between devices, swap_far(): lax.ppermute(far, WIDE, [(w, (w + 1 if w % 2 else w - 1) % count) for w i...  15.9 us
    ppermute x6, starting transfers between devices, swap_wide(): lax.ppermute(near, WIDE, [(w, w ^ 1) for w in range(count)])  12.2 us
    pallas_call x13, Pallas kernels, call(): pl.pallas_call(kernel, out_shape=[jax.ShapeDtypeStruct(s, F32) for s in o...  9.91 us
    all_gather x1, blocking collectives, swap_all(): return (far, near, lax.all_gather(pack, 'narrow'))  8.75 us
    all_gather x1, blocking collectives, local(): halo = (far, near, lax.all_gather(pack, 'narrow'))  6.82 us
    all_to_all x1, starting transfers between devices, local(): sums = lax.all_to_all(sums, REST, 0, 0)  6.22 us
  transfers between devices with their start and end apart: 17, of which 8 were waited for; matrix products, arithmetic and copies ran while one was open for 0% of the time, Pallas kernels for 1%

profile of v5, /device:TPU:1, one launch (start us, length us, event | category | flops | bytes accessed | tf_op | source)
XLA Modules:
  0.0 144.5 jit_solution(14082337924463828277)
XLA Ops:
  0.6 2.7 %shard_map.77 = (f32[7,8,32,128]{3,2,1,0:T(8,128)S(1)}, f32[8,32,128]{2,1,0:T(8,128)S(1)}, f32[8,32,128]{2,1,0:T(8,128)S(1)}, f32[2,32,128]{2,1,0:T(8,128)S(1)},...) custom-call(s32[1,64]{1,0:T(1,128)} %bitcast.20, ...), custom_call_target="tpu_custom_call" | custom-call | tf_op jit(solution)/shard_map/pallas_call | solution.py:677
  3.3 20.5 %collective-permute-start = (f32[2,32,128]{2,1,0:T(8,128)S(1)}, f32[2,32,128]{2,1,0:T(8,128)S(1)}, u32[]{:S(2)}, u32[]{:S(2)}) collective-permute-start(f32[2,32,128]{2,1,0:T(8,128)S(1)} %get-tuple-element.50), channel_id=1, source_target_pairs={{0,764},{4,8},{8,4},{12,16},{16,12},{20,24},{24,20},{28,32},{32,28... | collective-permute-start | bytes 98312 | tf_op jit(solution)/shard_map/ppermute | solution.py:703
  23.8 1.9 %collective-permute-start.1 = (f32[2,32,128]{2,1,0:T(8,128)S(1)}, f32[2,32,128]{2,1,0:T(8,128)S(1)}, u32[]{:S(2)}, u32[]{:S(2)}) collective-permute-start(f32[2,32,128]{2,1,0:T(8,128)S(1)} %get-tuple-element.51), channel_id=1, source_target_pairs={{0,4},{4,0},{8,12},{12,8},{16,20},{20,16},{24,28},{28,24},{32,36},... | collective-permute-start | bytes 98312 | tf_op jit(solution)/shard_map/ppermute | solution.py:710
  25.7 3.1 %collective-permute-start.2 = (f32[9,4,16,128]{3,2,1,0:T(8,128)S(1)}, f32[9,4,16,128]{3,2,1,0:T(8,128)S(1)}, u32[]{:S(2)}, u32[]{:S(2)}) collective-permute-start(f32[9,4,16,128]{3,2,1,0:T(8,128)S(1)} %get-tuple-element.53), channel_id=1, source_target_pairs={{0,1},{1,2},{2,3},{3,0},{4,5},{5,6},{6,7},{7,4},{8,9},{9,10},{10,1... | collective-permute-start | bytes 884744 | tf_op jit(solution)/shard_map/ppermute | solution.py:736
  28.8 1.9 %collective-permute-start.3 = (f32[9,4,16,128]{3,2,1,0:T(8,128)S(1)}, f32[9,4,16,128]{3,2,1,0:T(8,128)S(1)}, u32[]{:S(2)}, u32[]{:S(2)}) collective-permute-start(f32[9,4,16,128]{3,2,1,0:T(8,128)S(1)} %get-tuple-element.54), channel_id=1, source_target_pairs={{0,3},{1,0},{2,1},{3,2},{4,7},{5,4},{6,5},{7,6},{8,11},{9,8},{10,9... | collective-permute-start | bytes 884744 | tf_op jit(solution)/shard_map/ppermute | solution.py:737
  30.8 0.0 copy-start.1
  30.8 0.1 shard_map.78
  30.9 8.8 %all-gather = f32[8,48,128]{2,1,0:T(8,128)S(1)} all-gather(f32[2,48,128]{2,1,0:T(8,128)S(1)} %shard_map.78), channel_id=2, replica_groups=mesh['outer'=16,'ring'=12,'narrow'=4] {'narrow'}, dimensions={0}, use_global_device_ids=true | all-gather | bytes 245760 | tf_op jit(solution)/shard_map/all_gather | solution.py:716
  39.6 0.9 shard_map.79
  40.6 3.0 %collective-permute-start.4 = (f32[1,32,128]{2,1,0:T(8,128)S(1)}, f32[1,32,128]{2,1,0:T(8,128)S(1)}, u32[]{:S(2)}, u32[]{:S(2)}) collective-permute-start(f32[1,32,128]{2,1,0:T(8,128)S(1)} %get-tuple-element.57), channel_id=1, source_target_pairs={{0,764},{4,8},{8,4},{12,16},{16,12},{20,24},{24,20},{28,32},{32,28... | collective-permute-start | bytes 49160 | tf_op jit(solution)/shard_map/ppermute | solution.py:703
  43.6 2.6 %collective-permute-start.5 = (f32[1,32,128]{2,1,0:T(8,128)S(1)}, f32[1,32,128]{2,1,0:T(8,128)S(1)}, u32[]{:S(2)}, u32[]{:S(2)}) collective-permute-start(f32[1,32,128]{2,1,0:T(8,128)S(1)} %get-tuple-element.58), channel_id=1, source_target_pairs={{0,4},{4,0},{8,12},{12,8},{16,20},{20,16},{24,28},{28,24},{32,36},... | collective-permute-start | bytes 49160 | tf_op jit(solution)/shard_map/ppermute | solution.py:710
  46.2 4.6 %collective-permute-done.4.h0 = f32[1,32,128]{2,1,0:T(8,128)S(1)} collective-permute-done((f32[1,32,128]{2,1,0:T(8,128)S(1)}, f32[1,32,128]{2,1,0:T(8,128)S(1)}, u32[]{:S(2)}, u32[]{:S(2)}) %collective-permute-start.4) | collective-permute-done | bytes 16416 | tf_op jit(solution)/shard_map/ppermute | solution.py:703
  50.8 0.7 shard_map.80
  51.5 5.3 %collective-permute-start.6 = (f32[1,32,128]{2,1,0:T(8,128)S(1)}, f32[1,32,128]{2,1,0:T(8,128)S(1)}, u32[]{:S(2)}, u32[]{:S(2)}) collective-permute-start(f32[1,32,128]{2,1,0:T(8,128)S(1)} %get-tuple-element.63), channel_id=1, source_target_pairs={{0,764},{4,8},{8,4},{12,16},{16,12},{20,24},{24,20},{28,32},{32,28... | collective-permute-start | bytes 49160 | tf_op jit(solution)/shard_map/ppermute | solution.py:703
  56.8 1.9 %collective-permute-start.7 = (f32[1,32,128]{2,1,0:T(8,128)S(1)}, f32[1,32,128]{2,1,0:T(8,128)S(1)}, u32[]{:S(2)}, u32[]{:S(2)}) collective-permute-start(f32[1,32,128]{2,1,0:T(8,128)S(1)} %get-tuple-element.64), channel_id=1, source_target_pairs={{0,4},{4,0},{8,12},{12,8},{16,20},{20,16},{24,28},{28,24},{32,36},... | collective-permute-start | bytes 49160 | tf_op jit(solution)/shard_map/ppermute | solution.py:710
  58.7 3.0 %collective-permute-done.6.far_ref.h0 = f32[1,32,128]{2,1,0:T(8,128)S(1)} collective-permute-done((f32[1,32,128]{2,1,0:T(8,128)S(1)}, f32[1,32,128]{2,1,0:T(8,128)S(1)}, u32[]{:S(2)}, u32[]{:S(2)}) %collective-permute-start.6) | collective-permute-done | bytes 16416 | tf_op jit(solution)/shard_map/ppermute | solution.py:703
  61.7 0.1 shard_map.81
  61.8 8.3 %all-gather.1 = f32[4,144,128]{2,1,0:T(8,128)S(1)} all-gather(f32[1,144,128]{2,1,0:T(8,128)S(1)} %shard_map.81), channel_id=3, replica_groups=mesh['outer'=16,'ring'=12,'narrow'=4] {'narrow'}, dimensions={0}, use_global_device_ids=true | all-gather | bytes 368640 | tf_op jit(solution)/shard_map/all_gather | solution.py:731
  70.1 1.0 shard_map.82
  71.0 5.7 %collective-permute-start.8 = (f32[1,32,128]{2,1,0:T(8,128)S(1)}, f32[1,32,128]{2,1,0:T(8,128)S(1)}, u32[]{:S(2)}, u32[]{:S(2)}) collective-permute-start(f32[1,32,128]{2,1,0:T(8,128)S(1)} %get-tuple-element.71), channel_id=1, source_target_pairs={{0,764},{4,8},{8,4},{12,16},{16,12},{20,24},{24,20},{28,32},{32,28... | collective-permute-start | bytes 49160 | tf_op jit(solution)/shard_map/ppermute | solution.py:703
  76.7 1.9 %collective-permute-start.9 = (f32[1,32,128]{2,1,0:T(8,128)S(1)}, f32[1,32,128]{2,1,0:T(8,128)S(1)}, u32[]{:S(2)}, u32[]{:S(2)}) collective-permute-start(f32[1,32,128]{2,1,0:T(8,128)S(1)} %get-tuple-element.72), channel_id=1, source_target_pairs={{0,4},{4,0},{8,12},{12,8},{16,20},{20,16},{24,28},{28,24},{32,36},... | collective-permute-start | bytes 49160 | tf_op jit(solution)/shard_map/ppermute | solution.py:710
  78.7 2.6 %collective-permute-done.8.h0 = f32[1,32,128]{2,1,0:T(8,128)S(1)} collective-permute-done((f32[1,32,128]{2,1,0:T(8,128)S(1)}, f32[1,32,128]{2,1,0:T(8,128)S(1)}, u32[]{:S(2)}, u32[]{:S(2)}) %collective-permute-start.8) | collective-permute-done | bytes 16416 | tf_op jit(solution)/shard_map/ppermute | solution.py:703
  81.2 0.3 collective-permute-done.9.h1
  81.5 0.7 shard_map.83
  82.2 5.4 %collective-permute-start.10 = (f32[1,32,128]{2,1,0:T(8,128)S(1)}, f32[1,32,128]{2,1,0:T(8,128)S(1)}, u32[]{:S(2)}, u32[]{:S(2)}) collective-permute-start(f32[1,32,128]{2,1,0:T(8,128)S(1)} %get-tuple-element.74), channel_id=1, source_target_pairs={{0,764},{4,8},{8,4},{12,16},{16,12},{20,24},{24,20},{28,32},{32,28... | collective-permute-start | bytes 49160 | tf_op jit(solution)/shard_map/ppermute | solution.py:703
  87.6 1.9 %collective-permute-start.11 = (f32[1,32,128]{2,1,0:T(8,128)S(1)}, f32[1,32,128]{2,1,0:T(8,128)S(1)}, u32[]{:S(2)}, u32[]{:S(2)}) collective-permute-start(f32[1,32,128]{2,1,0:T(8,128)S(1)} %get-tuple-element.75), channel_id=1, source_target_pairs={{0,4},{4,0},{8,12},{12,8},{16,20},{20,16},{24,28},{28,24},{32,36},... | collective-permute-start | bytes 49160 | tf_op jit(solution)/shard_map/ppermute | solution.py:710
  89.6 3.0 %collective-permute-done.10.far_ref.h0 = f32[1,32,128]{2,1,0:T(8,128)S(1)} collective-permute-done((f32[1,32,128]{2,1,0:T(8,128)S(1)}, f32[1,32,128]{2,1,0:T(8,128)S(1)}, u32[]{:S(2)}, u32[]{:S(2)}) %collective-permute-start.10) | collective-permute-done | bytes 16416 | tf_op jit(solution)/shard_map/ppermute | solution.py:703
  92.5 0.1 shard_map.84
  92.6 8.0 %all-gather.2 = f32[4,144,128]{2,1,0:T(8,128)S(1)} all-gather(f32[1,144,128]{2,1,0:T(8,128)S(1)} %shard_map.84), channel_id=4, replica_groups=mesh['outer'=16,'ring'=12,'narrow'=4] {'narrow'}, dimensions={0}, use_global_device_ids=true | all-gather | bytes 368640 | tf_op jit(solution)/shard_map/all_gather | solution.py:731
  100.7 0.9 shard_map.85
  101.6 5.6 %collective-permute-start.12 = (f32[1,32,128]{2,1,0:T(8,128)S(1)}, f32[1,32,128]{2,1,0:T(8,128)S(1)}, u32[]{:S(2)}, u32[]{:S(2)}) collective-permute-start(f32[1,32,128]{2,1,0:T(8,128)S(1)} %get-tuple-element.81), channel_id=1, source_target_pairs={{0,764},{4,8},{8,4},{12,16},{16,12},{20,24},{24,20},{28,32},{32,28... | collective-permute-start | bytes 49160 | tf_op jit(solution)/shard_map/ppermute | solution.py:703
  107.2 1.9 %collective-permute-start.13 = (f32[1,32,128]{2,1,0:T(8,128)S(1)}, f32[1,32,128]{2,1,0:T(8,128)S(1)}, u32[]{:S(2)}, u32[]{:S(2)}) collective-permute-start(f32[1,32,128]{2,1,0:T(8,128)S(1)} %get-tuple-element.82), channel_id=1, source_target_pairs={{0,4},{4,0},{8,12},{12,8},{16,20},{20,16},{24,28},{28,24},{32,36},... | collective-permute-start | bytes 49160 | tf_op jit(solution)/shard_map/ppermute | solution.py:710
  109.1 2.7 %collective-permute-done.12.h0 = f32[1,32,128]{2,1,0:T(8,128)S(1)} collective-permute-done((f32[1,32,128]{2,1,0:T(8,128)S(1)}, f32[1,32,128]{2,1,0:T(8,128)S(1)}, u32[]{:S(2)}, u32[]{:S(2)}) %collective-permute-start.12) | collective-permute-done | bytes 16416 | tf_op jit(solution)/shard_map/ppermute | solution.py:703
  111.8 0.1 collective-permute-done.13.h1
  111.9 1.3 shard_map.86
  113.2 6.2 %all-to-all-start = ((f32[64,1,128]{2,1,0:T(1,128)}), f32[64,1,128]{2,1,0:T(1,128)S(1)}, u32[]{:S(2)}, u32[]{:S(2)}) async-start(f32[64,1,128]{2,1,0:T(1,128)} %bitcast.5), calls=%async_computation | async-start | bytes 65536 | tf_op jit(solution)/shard_map/all_to_all | solution.py:802
  119.5 0.0 copy-start.2
  119.5 8.2 %collective-permute-start.14 = (f32[1,32,128]{2,1,0:T(8,128)S(1)}, f32[1,32,128]{2,1,0:T(8,128)S(1)}, u32[]{:S(2)}, u32[]{:S(2)}) collective-permute-start(f32[1,32,128]{2,1,0:T(8,128)S(1)} %get-tuple-element.90), channel_id=1, source_target_pairs={{0,764},{4,8},{8,4},{12,16},{16,12},{20,24},{24,20},{28,32},{32,28... | collective-permute-start | bytes 49160 | tf_op jit(solution)/shard_map/ppermute | solution.py:703
  127.7 0.1 copy.10.order_ref
  127.7 1.0 all-to-all-done
  128.8 0.1 reduce_sum.9
  128.8 0.6 all_to_all.15
  129.4 3.5 %all-to-all-start.1 = ((f32[12,1,128]{2,1,0:T(1,128)}), f32[12,1,128]{2,1,0:T(1,128)S(1)}, u32[]{:S(2)}, u32[]{:S(2)}) async-start(f32[12,1,128]{2,1,0:T(1,128)} %all_to_all.15), calls=%async_computation.1 | async-start | bytes 12288 | tf_op jit(solution)/shard_map/all_to_all | solution.py:805
  132.9 3.3 %all-gather.3 = f32[2,32,128]{2,1,0:T(8,128)S(1)} all-gather(f32[1,32,128]{2,1,0:T(8,128)S(1)} %get-tuple-element.91), channel_id=5, replica_groups={{0,4},{8,12},{16,20},{24,28},{32,36},{40,44},{1,5},{9,13},{17,21},{25,2..., dimensions={0}, use_global_device_ids=true | all-gather | bytes 49152 | tf_op jit(solution)/shard_map/all_gather | solution.py:806
  136.2 0.1 shard_map.87
  136.3 6.8 %all-gather.4 = f32[4,16,128]{2,1,0:T(8,128)S(1)} all-gather(f32[1,16,128]{2,1,0:T(8,128)S(1)} %shard_map.87), channel_id=6, replica_groups=mesh['outer'=16,'ring'=12,'narrow'=4] {'narrow'}, dimensions={0}, use_global_device_ids=true | all-gather | bytes 40960 | tf_op jit(solution)/shard_map/all_gather | solution.py:810
  143.1 0.6 shard_map.88.spread_ref
  143.7 0.8 shard_map.89
  (15 shorter events, 0.0 us)
Async XLA Ops:
  3.3 27.4 %collective-permute-start = (f32[2,32,128]{2,1,0:T(8,128)S(1)}, f32[2,32,128]{2,1,0:T(8,128)S(1)}, u32[]{:S(2)}, u32[]{:S(2)}) collective-permute-start(f32[2,32,128]{2,1,0:T(8,128)S(1)} %get-tuple-element.50), channel_id=1, source_target_pairs={{0,764},{4,8},{8,4},{12,16},{16,12},{20,24},{24,20},{28,32},{32,28... | collective-permute-start | bytes 98312 | tf_op jit(solution)/shard_map/ppermute | solution.py:703
  23.8 6.9 %collective-permute-start.1 = (f32[2,32,128]{2,1,0:T(8,128)S(1)}, f32[2,32,128]{2,1,0:T(8,128)S(1)}, u32[]{:S(2)}, u32[]{:S(2)}) collective-permute-start(f32[2,32,128]{2,1,0:T(8,128)S(1)} %get-tuple-element.51), channel_id=1, source_target_pairs={{0,4},{4,0},{8,12},{12,8},{16,20},{20,16},{24,28},{28,24},{32,36},... | collective-permute-start | bytes 98312 | tf_op jit(solution)/shard_map/ppermute | solution.py:710
  25.7 13.9 %collective-permute-start.2 = (f32[9,4,16,128]{3,2,1,0:T(8,128)S(1)}, f32[9,4,16,128]{3,2,1,0:T(8,128)S(1)}, u32[]{:S(2)}, u32[]{:S(2)}) collective-permute-start(f32[9,4,16,128]{3,2,1,0:T(8,128)S(1)} %get-tuple-element.53), channel_id=1, source_target_pairs={{0,1},{1,2},{2,3},{3,0},{4,5},{5,6},{6,7},{7,4},{8,9},{9,10},{10,1... | collective-permute-start | bytes 884744 | tf_op jit(solution)/shard_map/ppermute | solution.py:736
  28.8 10.8 %collective-permute-start.3 = (f32[9,4,16,128]{3,2,1,0:T(8,128)S(1)}, f32[9,4,16,128]{3,2,1,0:T(8,128)S(1)}, u32[]{:S(2)}, u32[]{:S(2)}) collective-permute-start(f32[9,4,16,128]{3,2,1,0:T(8,128)S(1)} %get-tuple-element.54), channel_id=1, source_target_pairs={{0,3},{1,0},{2,1},{3,2},{4,7},{5,4},{6,5},{7,6},{8,11},{9,8},{10,9... | collective-permute-start | bytes 884744 | tf_op jit(solution)/shard_map/ppermute | solution.py:737
  30.8 8.9 %copy-start.1 = (bf16[256,256]{1,0:T(8,128)(2,1)S(1)}, bf16[256,256]{1,0:T(8,128)(2,1)}, u32[]{:S(2)}) copy-start(bf16[256,256]{1,0:T(8,128)(2,1)} %constant.9.clone.diver_ref) | copy-start | bytes 393220
  30.9 8.8 %copy-start = (bf16[384,256]{1,0:T(8,128)(2,1)S(1)}, bf16[384,256]{1,0:T(8,128)(2,1)}, u32[]{:S(2)}) copy-start(bf16[384,256]{1,0:T(8,128)(2,1)} %constant.8.clone.grad_ref) | copy-start | bytes 589828
  40.6 10.2 %collective-permute-start.4 = (f32[1,32,128]{2,1,0:T(8,128)S(1)}, f32[1,32,128]{2,1,0:T(8,128)S(1)}, u32[]{:S(2)}, u32[]{:S(2)}) collective-permute-start(f32[1,32,128]{2,1,0:T(8,128)S(1)} %get-tuple-element.57), channel_id=1, source_target_pairs={{0,764},{4,8},{8,4},{12,16},{16,12},{20,24},{24,20},{28,32},{32,28... | collective-permute-start | bytes 49160 | tf_op jit(solution)/shard_map/ppermute | solution.py:703
  43.6 7.2 %collective-permute-start.5 = (f32[1,32,128]{2,1,0:T(8,128)S(1)}, f32[1,32,128]{2,1,0:T(8,128)S(1)}, u32[]{:S(2)}, u32[]{:S(2)}) collective-permute-start(f32[1,32,128]{2,1,0:T(8,128)S(1)} %get-tuple-element.58), channel_id=1, source_target_pairs={{0,4},{4,0},{8,12},{12,8},{16,20},{20,16},{24,28},{28,24},{32,36},... | collective-permute-start | bytes 49160 | tf_op jit(solution)/shard_map/ppermute | solution.py:710
  51.5 10.2 %collective-permute-start.6 = (f32[1,32,128]{2,1,0:T(8,128)S(1)}, f32[1,32,128]{2,1,0:T(8,128)S(1)}, u32[]{:S(2)}, u32[]{:S(2)}) collective-permute-start(f32[1,32,128]{2,1,0:T(8,128)S(1)} %get-tuple-element.63), channel_id=1, source_target_pairs={{0,764},{4,8},{8,4},{12,16},{16,12},{20,24},{24,20},{28,32},{32,28... | collective-permute-start | bytes 49160 | tf_op jit(solution)/shard_map/ppermute | solution.py:703
  56.8 4.9 %collective-permute-start.7 = (f32[1,32,128]{2,1,0:T(8,128)S(1)}, f32[1,32,128]{2,1,0:T(8,128)S(1)}, u32[]{:S(2)}, u32[]{:S(2)}) collective-permute-start(f32[1,32,128]{2,1,0:T(8,128)S(1)} %get-tuple-element.64), channel_id=1, source_target_pairs={{0,4},{4,0},{8,12},{12,8},{16,20},{20,16},{24,28},{28,24},{32,36},... | collective-permute-start | bytes 49160 | tf_op jit(solution)/shard_map/ppermute | solution.py:710
  71.0 10.2 %collective-permute-start.8 = (f32[1,32,128]{2,1,0:T(8,128)S(1)}, f32[1,32,128]{2,1,0:T(8,128)S(1)}, u32[]{:S(2)}, u32[]{:S(2)}) collective-permute-start(f32[1,32,128]{2,1,0:T(8,128)S(1)} %get-tuple-element.71), channel_id=1, source_target_pairs={{0,764},{4,8},{8,4},{12,16},{16,12},{20,24},{24,20},{28,32},{32,28... | collective-permute-start | bytes 49160 | tf_op jit(solution)/shard_map/ppermute | solution.py:703
  76.7 4.8 %collective-permute-start.9 = (f32[1,32,128]{2,1,0:T(8,128)S(1)}, f32[1,32,128]{2,1,0:T(8,128)S(1)}, u32[]{:S(2)}, u32[]{:S(2)}) collective-permute-start(f32[1,32,128]{2,1,0:T(8,128)S(1)} %get-tuple-element.72), channel_id=1, source_target_pairs={{0,4},{4,0},{8,12},{12,8},{16,20},{20,16},{24,28},{28,24},{32,36},... | collective-permute-start | bytes 49160 | tf_op jit(solution)/shard_map/ppermute | solution.py:710
  82.2 10.3 %collective-permute-start.10 = (f32[1,32,128]{2,1,0:T(8,128)S(1)}, f32[1,32,128]{2,1,0:T(8,128)S(1)}, u32[]{:S(2)}, u32[]{:S(2)}) collective-permute-start(f32[1,32,128]{2,1,0:T(8,128)S(1)} %get-tuple-element.74), channel_id=1, source_target_pairs={{0,764},{4,8},{8,4},{12,16},{16,12},{20,24},{24,20},{28,32},{32,28... | collective-permute-start | bytes 49160 | tf_op jit(solution)/shard_map/ppermute | solution.py:703
  87.6 4.9 %collective-permute-start.11 = (f32[1,32,128]{2,1,0:T(8,128)S(1)}, f32[1,32,128]{2,1,0:T(8,128)S(1)}, u32[]{:S(2)}, u32[]{:S(2)}) collective-permute-start(f32[1,32,128]{2,1,0:T(8,128)S(1)} %get-tuple-element.75), channel_id=1, source_target_pairs={{0,4},{4,0},{8,12},{12,8},{16,20},{20,16},{24,28},{28,24},{32,36},... | collective-permute-start | bytes 49160 | tf_op jit(solution)/shard_map/ppermute | solution.py:710
  101.6 10.2 %collective-permute-start.12 = (f32[1,32,128]{2,1,0:T(8,128)S(1)}, f32[1,32,128]{2,1,0:T(8,128)S(1)}, u32[]{:S(2)}, u32[]{:S(2)}) collective-permute-start(f32[1,32,128]{2,1,0:T(8,128)S(1)} %get-tuple-element.81), channel_id=1, source_target_pairs={{0,764},{4,8},{8,4},{12,16},{16,12},{20,24},{24,20},{28,32},{32,28... | collective-permute-start | bytes 49160 | tf_op jit(solution)/shard_map/ppermute | solution.py:703
  107.2 4.8 %collective-permute-start.13 = (f32[1,32,128]{2,1,0:T(8,128)S(1)}, f32[1,32,128]{2,1,0:T(8,128)S(1)}, u32[]{:S(2)}, u32[]{:S(2)}) collective-permute-start(f32[1,32,128]{2,1,0:T(8,128)S(1)} %get-tuple-element.82), channel_id=1, source_target_pairs={{0,4},{4,0},{8,12},{12,8},{16,20},{20,16},{24,28},{28,24},{32,36},... | collective-permute-start | bytes 49160 | tf_op jit(solution)/shard_map/ppermute | solution.py:710
  113.2 15.5 %all-to-all-start = ((f32[64,1,128]{2,1,0:T(1,128)}), f32[64,1,128]{2,1,0:T(1,128)S(1)}, u32[]{:S(2)}, u32[]{:S(2)}) async-start(f32[64,1,128]{2,1,0:T(1,128)} %bitcast.5), calls=%async_computation | async-start | bytes 65536 | tf_op jit(solution)/shard_map/all_to_all | solution.py:802
  119.5 8.2 %copy-start.2 = (s32[1,1,64]{2,1,0:T(1,128)S(1)}, s32[1,1,64]{2,1,0:T(1,128)}, u32[]{:S(2)}) copy-start(s32[1,1,64]{2,1,0:T(1,128)} %param.8) | copy-start | bytes 772
  119.5 16.7 %collective-permute-start.14 = (f32[1,32,128]{2,1,0:T(8,128)S(1)}, f32[1,32,128]{2,1,0:T(8,128)S(1)}, u32[]{:S(2)}, u32[]{:S(2)}) collective-permute-start(f32[1,32,128]{2,1,0:T(8,128)S(1)} %get-tuple-element.90), channel_id=1, source_target_pairs={{0,764},{4,8},{8,4},{12,16},{16,12},{20,24},{24,20},{28,32},{32,28... | collective-permute-start | bytes 49160 | tf_op jit(solution)/shard_map/ppermute | solution.py:703
  129.4 14.2 %all-to-all-start.1 = ((f32[12,1,128]{2,1,0:T(1,128)}), f32[12,1,128]{2,1,0:T(1,128)S(1)}, u32[]{:S(2)}, u32[]{:S(2)}) async-start(f32[12,1,128]{2,1,0:T(1,128)} %all_to_all.15), calls=%async_computation.1 | async-start | bytes 12288 | tf_op jit(solution)/shard_map/all_to_all | solution.py:805

commit v6 on v5

--- a/solution.py
+++ b/solution.py
@@ -291,6 +291,27 @@
         pack_ref[0, HALF * (5 + b) : HALF * (6 + b)] = hi
 
 
+WHOLE = (1, 3, 5)
+LINES = (0, 2, 4, 6)
+
+
+def line_pack(field):
+    pack = None
+    for i in range(NODES):
+        piece = ends(field(i))
+        if i:
+            piece = roll(piece, 16 * i, 1)
+        pack = piece if pack is None else pack + piece
+    return pack
+
+
+def ghost_lines(left, right):
+    lane = lane_iota(HALF)
+    both = jnp.where(lane % 16 >= 8, left, right)
+    inner = (lane >= 56) & (lane < 72)
+    return [jnp.where(inner, roll(both, 64 - 16 * i, 1), 0.0) for i in range(NODES)]
+
+
 def beside(packs_ref):
     count = packs_ref.shape[0]
     here = lax.axis_index("narrow")
@@ -343,7 +364,7 @@
     return value
 
 
-def apply_element(v_ref, metric_ref, ghost_ref, grad_ref, diver_ref, flux_ref, out_ref):
+def apply_flux(v_ref, metric_ref, ghost_ref, grad_ref, flux_ref, part_ref):
     count = v_ref.shape[1]
     side = dot_grad(v_ref[...].reshape(NODES * count, LANES), grad_ref)
     flux_ref[0] = side[:, :LANES]
@@ -366,9 +387,62 @@
             flux_ref[1, at] = m[4] * g_z + m[5] * g_a + m[2] * g_r
         part_z = along_nodes(flux_z, DERIV.T)
         for i in range(NODES):
-            out_ref[i, rows] = part_z[i] + geometry[6, i, there] * values[i]
-    flux = jnp.concatenate([flux_ref[0], flux_ref[1]], axis=1)
-    out_ref[...] += dot_diver(flux, diver_ref).reshape(out_ref.shape)
+            part_ref[i, rows] = part_z[i] + geometry[6, i, there] * values[i]
+
+
+def whole_planes(flux_ref, part_ref, diver_ref, planes):
+    count = part_ref.shape[1]
+
+    def flux(f):
+        if len(planes) == NODES:
+            return flux_ref[f]
+        return jnp.concatenate([flux_ref[f, i * count : (i + 1) * count] for i in planes], axis=0)
+
+    total = dot_diver(jnp.concatenate([flux(0), flux(1)], axis=1), diver_ref)
+    return [
+        part_ref[i] + total[n * count : (n + 1) * count] for n, i in enumerate(planes)
+    ]
+
+
+def store_faces(flux_ref, part_ref, diver_ref, far_ref, near_ref):
+    first, last = (
+        own_assembly(u) for u in whole_planes(flux_ref, part_ref, diver_ref, (0, NODES - 1))
+    )
+    even = is_even()
+    near_ref[0] = jnp.where(even, last, first)
+    far_ref[0] = jnp.where(even, first, last)
+
+
+def apply_element(v_ref, metric_ref, ghost_ref, grad_ref, diver_ref, flux_ref, out_ref):
+    apply_flux(v_ref, metric_ref, ghost_ref, grad_ref, flux_ref, out_ref)
+    planes = whole_planes(flux_ref, out_ref, diver_ref, range(NODES))
+    for i in range(NODES):
+        out_ref[i] = planes[i]
+
+
+def rest_kernel(flux_ref, part_ref, diver_ref, kv_ref):
+    for i, u in enumerate(whole_planes(flux_ref, part_ref, diver_ref, range(NODES))):
+        kv_ref[i] = own_assembly(u)
+
+
+def rest_energy_kernel(flux_ref, part_ref, diver_ref, v_ref, sums_in, kv_ref, sums_ref):
+    energy = jnp.zeros((ROWS, LANES), jnp.float32)
+    for i, u in enumerate(whole_planes(flux_ref, part_ref, diver_ref, range(NODES))):
+        kv_ref[i] = own_assembly(u)
+        energy = energy + v_ref[i] * u[:ROWS]
+    sums_ref[...] = sums_in[...] + sum_row([jnp.zeros((1, LANES), jnp.float32), energy])
+
+
+def rest_edges_kernel(
+    step, flux_ref, part_ref, diver_ref, start_ref, inverse_ref, kv_ref, pack_ref, edges_ref
+):
+    for i, u in enumerate(whole_planes(flux_ref, part_ref, diver_ref, range(NODES))):
+        kv_ref[i] = own_assembly(u)
+    pack_ref[0] = line_pack(lambda i: kv_ref[i])
+    store_edges(
+        edges_ref, edges_ref, 0, 1,
+        [edge(start_ref[i] - step * inverse_ref[i] * kv_ref[i]) for i in range(NODES)],
+    )
 
 
 def weight_plane():
@@ -442,7 +516,7 @@
     store_assembled(
         load_kv, far_ref, near_ref, even, lambda i: work_ref[i], 0, pack_ref
     )
-    store_edges(lo_ref, hi_ref, 7, 7, [edge(load_kv[i]) for i in range(NODES)])
+    store_edges(lo_ref, hi_ref, 3, 3, [edge(load_kv[i]) for i in range(NODES)])
 
     copies[2].wait()
     for c in range(7):
@@ -451,7 +525,12 @@
             metric_ref[c, i] = value
 
         spread(dot(pick, geom_ref[c]), store_metric)
-        store_edges(lo_ref, hi_ref, c, c, [edge(metric_ref[c, i]) for i in range(NODES)])
+    for slot, c in enumerate(WHOLE):
+        store_edges(lo_ref, hi_ref, slot, slot, [edge(metric_ref[c, i]) for i in range(NODES)])
+    for slot, c in enumerate(LINES):
+        lines = line_pack(lambda i, c=c: metric_ref[c, i])
+        lo_ref[5, slot] = lines
+        hi_ref[5, slot] = lines
 
     lane = lane_iota(8)
     q_a = jnp.zeros((8, LANES), jnp.float32)
@@ -478,13 +557,13 @@
     store_assembled(
         bound_kv, far_ref, near_ref, even, lambda i: work_ref[i], 1, pack_ref
     )
-    store_edges(lo_ref, hi_ref, 8, 8, [edge(bound_kv[i]) for i in range(NODES)])
+    store_edges(lo_ref, hi_ref, 4, 4, [edge(bound_kv[i]) for i in range(NODES)])
 
 
 def first_kernel(
     load_kv, bound_kv, h0, h1, h2, left_ref, right_ref, metric_ref, grad_ref, diver_ref,
-    residual_ref, inverse_ref, update_ref, ghost_inverse, ghost_metric, kv_ref, far_ref, near_ref,
-    v_ref, flux_ref, work_ref,
+    residual_ref, inverse_ref, update_ref, ghost_inverse, ghost_metric, flux_ref, part_ref, far_ref, near_ref,
+    v_ref,
 ):
     residual = completed(load_kv, (h0, h1, h2), 0)
     bound = completed(bound_kv, (h0, h1, h2), 1)
@@ -496,22 +575,25 @@
         inverse_ref[i] = inverse
         update_ref[i] = update
         v_ref[i, :ROWS] = update
-    residual, residual_sums = ghost_columns(left_ref[7], right_ref[7]), ghost_sums(h2, 0, True)
-    bound, bound_sums = ghost_columns(left_ref[8], right_ref[8]), ghost_sums(h2, 1, True)
+    residual, residual_sums = ghost_columns(left_ref[3], right_ref[3]), ghost_sums(h2, 0, True)
+    bound, bound_sums = ghost_columns(left_ref[4], right_ref[4]), ghost_sums(h2, 1, True)
     for i in range(NODES):
         inverse = 1.0 / (bound[i] + bound_sums(i))
         ghost_inverse[i] = inverse
         v_ref[i, ROWS:] = (residual[i] + residual_sums(i)) * inverse * (1.0 / CENTER)
-    for c in range(7):
-        for i, value in enumerate(ghost_columns(left_ref[c], right_ref[c])):
+    for slot, c in enumerate(WHOLE):
+        for i, value in enumerate(ghost_columns(left_ref[slot], right_ref[slot])):
             ghost_metric[c, i] = value
-    apply_element(v_ref, metric_ref, ghost_metric, grad_ref, diver_ref, flux_ref, work_ref)
-    store_assembled(kv_ref, far_ref, near_ref, is_even(), lambda i: work_ref[i])
+    for slot, c in enumerate(LINES):
+        for i, value in enumerate(ghost_lines(left_ref[5, slot], right_ref[5, slot])):
+            ghost_metric[c, i] = value
+    apply_flux(v_ref, metric_ref, ghost_metric, grad_ref, flux_ref, part_ref)
+    store_faces(flux_ref, part_ref, diver_ref, far_ref, near_ref)
 
 
 def second_kernel(
     kv_in, h0, h1, source_ref, inverse_ref, update_in, metric_ref, grad_ref, diver_ref,
-    start_ref, kv_ref, far_ref, near_ref, pack_ref, edges_ref, v_ref, flux_ref, work_ref,
+    start_ref, flux_ref, part_ref, far_ref, near_ref, v_ref,
 ):
     image = completed(kv_in, (h0, h1))
     for i in range(NODES):
@@ -522,20 +604,14 @@
         result = old + update
         v_ref[i] = result
         start_ref[i] = result + (RHO2 * RHO1) * update + STEP2 * inverse * source
-    apply_element(v_ref, metric_ref, None, grad_ref, diver_ref, flux_ref, work_ref)
-    store_assembled(
-        kv_ref, far_ref, near_ref, is_even(), lambda i: work_ref[i], 0, pack_ref
-    )
-    store_edges(
-        edges_ref, edges_ref, 0, 1,
-        [edge(start_ref[i] - STEP2 * inverse_ref[i] * kv_ref[i]) for i in range(NODES)],
-    )
+    apply_flux(v_ref, metric_ref, None, grad_ref, flux_ref, part_ref)
+    store_faces(flux_ref, part_ref, diver_ref, far_ref, near_ref)
 
 
 def third_kernel(
     kv_in, h0, h1, h2, source_ref, inverse_ref, start_ref,
     ghost_inverse, ghost_metric, metric_ref, grad_ref, diver_ref,
-    result_ref, kv_ref, far_ref, near_ref, sums_ref, v_ref, flux_ref, work_ref,
+    result_ref, flux_ref, part_ref, far_ref, near_ref, sums_ref, v_ref,
 ):
     image = completed(kv_in, (h0, h1, h2))
     plane = weight_plane()
@@ -548,38 +624,30 @@
     start, sums = gathered_ghost(h2), ghost_sums(h2)
     for i in range(NODES):
         v_ref[i, ROWS:] = start[i] - STEP2 * ghost_inverse[i] * sums(i)
-    apply_element(v_ref, metric_ref, ghost_metric, grad_ref, diver_ref, flux_ref, work_ref)
-    energy = jnp.zeros((ROWS, LANES), jnp.float32)
-    for i in range(NODES):
-        energy = energy + result_ref[i] * work_ref[i, :ROWS]
-    sums_ref[...] = sum_row([rz * plane, energy])
-    store_assembled(kv_ref, far_ref, near_ref, is_even(), lambda i: work_ref[i])
+    apply_flux(v_ref, metric_ref, ghost_metric, grad_ref, flux_ref, part_ref)
+    store_faces(flux_ref, part_ref, diver_ref, far_ref, near_ref)
+    sums_ref[...] = sum_row([rz * plane])
 
 
 def fourth_kernel(
     kv_in, h0, h1, inverse_ref, metric_ref, grad_ref, diver_ref,
-    image_ref, update_ref, kv_ref, far_ref, near_ref, pack_ref, edges_ref, flux_ref, work_ref,
+    image_ref, update_ref, start_ref, flux_ref, part_ref, far_ref, near_ref,
 ):
     image = completed(kv_in, (h0, h1))
     for i in range(NODES):
         value = image(i)
         image_ref[i] = value
-        update_ref[i] = value * inverse_ref[i] * (1.0 / CENTER)
-    apply_element(update_ref, metric_ref, None, grad_ref, diver_ref, flux_ref, work_ref)
-    store_assembled(
-        kv_ref, far_ref, near_ref, is_even(), lambda i: work_ref[i], 0, pack_ref
-    )
-    scale = 1.0 + RHO1 * RHO0 + STEP1 * CENTER
-    store_edges(
-        edges_ref, edges_ref, 0, 1,
-        [edge(scale * update_ref[i] - STEP1 * inverse_ref[i] * kv_ref[i]) for i in range(NODES)],
-    )
+        update = value * inverse_ref[i] * (1.0 / CENTER)
+        update_ref[i] = update
+        start_ref[i] = (1.0 + RHO1 * RHO0 + STEP1 * CENTER) * update
+    apply_flux(update_ref, metric_ref, None, grad_ref, flux_ref, part_ref)
+    store_faces(flux_ref, part_ref, diver_ref, far_ref, near_ref)
 
 
 def fifth_kernel(
     kv_in, h0, h1, h2, source_ref, inverse_ref, update_in,
     ghost_inverse, ghost_metric, metric_ref, grad_ref, diver_ref,
-    start_ref, kv_ref, far_ref, near_ref, v_ref, flux_ref, work_ref,
+    start_ref, flux_ref, part_ref, far_ref, near_ref, v_ref,
 ):
     image = completed(kv_in, (h0, h1, h2))
     for i in range(NODES):
@@ -593,8 +661,8 @@
     start, sums = gathered_ghost(h2), ghost_sums(h2)
     for i in range(NODES):
         v_ref[i, ROWS:] = start[i] - STEP1 * ghost_inverse[i] * sums(i)
-    apply_element(v_ref, metric_ref, ghost_metric, grad_ref, diver_ref, flux_ref, work_ref)
-    store_assembled(kv_ref, far_ref, near_ref, is_even(), lambda i: work_ref[i])
+    apply_flux(v_ref, metric_ref, ghost_metric, grad_ref, flux_ref, part_ref)
+    store_faces(flux_ref, part_ref, diver_ref, far_ref, near_ref)
 
 
 def sixth_kernel(
@@ -743,7 +811,7 @@
     diver = jnp.asarray(DIVER_HL)
     metric, load_kv, bound_kv, *face, lo, hi = call(
         place_kernel,
-        [(7,) + FIELD, FIELD, FIELD] + faces(2) + packs(2) + [edges(9)] * 2,
+        [(7,) + FIELD, FIELD, FIELD] + faces(2) + packs(2) + [edges(6)] * 2,
         [
             FLUX, FIELD,
             pltpu.VMEM((1, 64), jnp.int32), pltpu.VMEM(load.shape, load.dtype),
@@ -755,41 +823,56 @@
     )
     sides = swap_edges(lo, hi)
     halo = swap_all(*face, GROWS)
-    residual, inverse, update, ghost_inverse, ghost_metric, kv, *face = call(
+    residual, inverse, update, ghost_inverse, ghost_metric, *parts, far, near = call(
         first_kernel,
-        [FIELD, FIELD, FIELD, GHOST, (7,) + GHOST, FIELD] + faces(),
-        [BIG, BIG_FLUX, BIG],
+        [FIELD, FIELD, FIELD, GHOST, (7,) + GHOST, BIG_FLUX, BIG] + faces(),
+        [BIG],
         load_kv, bound_kv, *halo, *sides, metric, grad, diver,
     )
-    halo = swap_wide(*face)
-    start, kv, *face = call(
+    (kv,) = call(rest_kernel, [FIELD], [], *parts, diver)
+    halo = swap_wide(far, near)
+    start, *parts, far, near = call(
         second_kernel,
-        [FIELD, FIELD] + faces() + packs() + [edges(2)],
-        [FIELD, FLUX, FIELD],
+        [FIELD, FLUX, FIELD] + faces(),
+        [FIELD],
         kv, *halo, residual, inverse, update, metric, grad, diver,
     )
-    halo = swap_edged(STEP2, inverse, *face)
-    first, kv, *face, early = call(
+    kv, *side = call(
+        functools.partial(rest_edges_kernel, STEP2),
+        [FIELD] + packs() + [edges(2)],
+        [],
+        *parts, diver, start, inverse,
+    )
+    halo = swap_edged(STEP2, inverse, far, near, *side)
+    first, *parts, far, near, early = call(
         third_kernel,
-        [FIELD, FIELD] + faces() + [(1, LANES)],
-        [BIG, BIG_FLUX, BIG],
+        [FIELD, BIG_FLUX, BIG] + faces() + [(1, LANES)],
+        [BIG],
         kv, *halo, residual, inverse, start, ghost_inverse, ghost_metric, metric, grad, diver,
     )
-    halo = swap_wide(*face)
-    image, update, kv, *face = call(
+    kv, early = call(rest_energy_kernel, [FIELD, (1, LANES)], [], *parts, diver, first, early)
+    halo = swap_wide(far, near)
+    image, update, start, *parts, far, near = call(
         fourth_kernel,
-        [FIELD, FIELD, FIELD] + faces() + packs() + [edges(2)],
-        [FLUX, FIELD],
+        [FIELD, FIELD, FIELD, FLUX, FIELD] + faces(),
+        [],
         kv, *halo, inverse, metric, grad, diver,
     )
-    halo = swap_edged(STEP1, inverse, *face)
-    start, kv, *face = call(
+    kv, *side = call(
+        functools.partial(rest_edges_kernel, STEP1),
+        [FIELD] + packs() + [edges(2)],
+        [],
+        *parts, diver, start, inverse,
+    )
+    halo = swap_edged(STEP1, inverse, far, near, *side)
+    start, *parts, far, near = call(
         fifth_kernel,
-        [FIELD, FIELD] + faces(),
-        [BIG, BIG_FLUX, BIG],
+        [FIELD, BIG_FLUX, BIG] + faces(),
+        [BIG],
         kv, *halo, image, inverse, update, ghost_inverse, ghost_metric, metric, grad, diver,
     )
-    halo = swap_wide(*face)
+    (kv,) = call(rest_kernel, [FIELD], [], *parts, diver)
+    halo = swap_wide(far, near)
     second, kv, *face, sums = call(
         sixth_kernel,
         [FIELD, FIELD] + faces() + packs() + [(lax.axis_size(REST), LANES)],

time: 145 us -> 144 us (level)
  waiting for transfers between devices: 17.3 us -> 15 us
  Pallas kernels: 9.91 us -> 11.6 us
    ppermute x7, waiting for transfers between devices: 15.9 us -> 13.2 us  [swap_far(): lax.ppermute(far, WIDE, [(w, (w + 1 if w % 2 else w - 1) % count) for w i...]
    pallas_call x13 -> x18, Pallas kernels: 9.91 us -> 11.6 us  [call(): pl.pallas_call(kernel, out_shape=[jax.ShapeDtypeStruct(s, F32) for s in o...]
  transfers between devices with their start and end apart: 17 -> 17, of which waited for: 8 -> 8; matrix products, arithmetic and copies ran while one was open for 0% -> 0% of each run, Pallas kernels for 1% -> 2%
where the time goes in v6:
time: 144 us; the launch traced here: 143 us
  starting transfers between devices  80.8 us (56%)
  blocking collectives  33.8 us (23%)
  waiting for transfers between devices  15 us (10%)
  Pallas kernels  11.6 us (8%)
    ppermute x7, starting transfers between devices, swap_far(): lax.ppermute(far, WIDE, [(w, (w + 1 if w % 2 else w - 1) % count) for w i...  54.5 us
    all_gather x2, blocking collectives, swap_edged(): return (far, near, lax.all_gather(pack, 'narrow'))  16.3 us
    ppermute x7, waiting for transfers between devices, swap_far(): lax.ppermute(far, WIDE, [(w, (w + 1 if w % 2 else w - 1) % count) for w i...  13.2 us
    pallas_call x18, Pallas kernels, call(): pl.pallas_call(kernel, out_shape=[jax.ShapeDtypeStruct(s, F32) for s in o...  11.6 us
    ppermute x6, starting transfers between devices, swap_wide(): lax.ppermute(near, WIDE, [(w, w ^ 1) for w in range(count)])  11.6 us
    all_gather x1, blocking collectives, swap_all(): return (far, near, lax.all_gather(pack, 'narrow'))  7.34 us
    all_gather x1, blocking collectives, local(): halo = (far, near, lax.all_gather(pack, 'narrow'))  6.82 us
    all_to_all x1, starting transfers between devices, local(): sums = lax.all_to_all(sums, REST, 0, 0)  6.21 us
  transfers between devices with their start and end apart: 17, of which 8 were waited for; matrix products, arithmetic and copies ran while one was open for 0% of the time, Pallas kernels for 2%

profile of v6, /device:TPU:1, one launch (start us, length us, event | category | flops | bytes accessed | tf_op | source)
XLA Modules:
  0.0 142.9 jit_solution(6039417820094161556)
XLA Ops:
  0.6 2.6 %shard_map.77 = (f32[7,8,32,128]{3,2,1,0:T(8,128)S(1)}, f32[8,32,128]{2,1,0:T(8,128)S(1)}, f32[8,32,128]{2,1,0:T(8,128)S(1)}, f32[2,32,128]{2,1,0:T(8,128)S(1)},...) custom-call(s32[1,64]{1,0:T(1,128)} %bitcast.20, ...), custom_call_target="tpu_custom_call" | custom-call | tf_op jit(solution)/shard_map/pallas_call | solution.py:745
  3.3 20.5 %collective-permute-start = (f32[2,32,128]{2,1,0:T(8,128)S(1)}, f32[2,32,128]{2,1,0:T(8,128)S(1)}, u32[]{:S(2)}, u32[]{:S(2)}) collective-permute-start(f32[2,32,128]{2,1,0:T(8,128)S(1)} %get-tuple-element.60), channel_id=1, source_target_pairs={{0,764},{4,8},{8,4},{12,16},{16,12},{20,24},{24,20},{28,32},{32,28... | collective-permute-start | bytes 98312 | tf_op jit(solution)/shard_map/ppermute | solution.py:771
  23.8 1.9 %collective-permute-start.1 = (f32[2,32,128]{2,1,0:T(8,128)S(1)}, f32[2,32,128]{2,1,0:T(8,128)S(1)}, u32[]{:S(2)}, u32[]{:S(2)}) collective-permute-start(f32[2,32,128]{2,1,0:T(8,128)S(1)} %get-tuple-element.61), channel_id=1, source_target_pairs={{0,4},{4,0},{8,12},{12,8},{16,20},{20,16},{24,28},{28,24},{32,36},... | collective-permute-start | bytes 98312 | tf_op jit(solution)/shard_map/ppermute | solution.py:778
  25.7 3.1 %collective-permute-start.2 = (f32[6,4,16,128]{3,2,1,0:T(8,128)S(1)}, f32[6,4,16,128]{3,2,1,0:T(8,128)S(1)}, u32[]{:S(2)}, u32[]{:S(2)}) collective-permute-start(f32[6,4,16,128]{3,2,1,0:T(8,128)S(1)} %get-tuple-element.63), channel_id=1, source_target_pairs={{0,1},{1,2},{2,3},{3,0},{4,5},{5,6},{6,7},{7,4},{8,9},{9,10},{10,1... | collective-permute-start | bytes 589832 | tf_op jit(solution)/shard_map/ppermute | solution.py:804
  28.8 1.9 %collective-permute-start.3 = (f32[6,4,16,128]{3,2,1,0:T(8,128)S(1)}, f32[6,4,16,128]{3,2,1,0:T(8,128)S(1)}, u32[]{:S(2)}, u32[]{:S(2)}) collective-permute-start(f32[6,4,16,128]{3,2,1,0:T(8,128)S(1)} %get-tuple-element.64), channel_id=1, source_target_pairs={{0,3},{1,0},{2,1},{3,2},{4,7},{5,4},{6,5},{7,6},{8,11},{9,8},{10,9... | collective-permute-start | bytes 589832 | tf_op jit(solution)/shard_map/ppermute | solution.py:805
  30.7 0.1 shard_map.78
  30.8 7.3 %all-gather = f32[8,48,128]{2,1,0:T(8,128)S(1)} all-gather(f32[2,48,128]{2,1,0:T(8,128)S(1)} %shard_map.78), channel_id=2, replica_groups=mesh['outer'=16,'ring'=12,'narrow'=4] {'narrow'}, dimensions={0}, use_global_device_ids=true | all-gather | bytes 245760 | tf_op jit(solution)/shard_map/all_gather | solution.py:784
  38.2 0.8 shard_map.79
  39.1 3.6 %collective-permute-start.4 = (f32[1,32,128]{2,1,0:T(8,128)S(1)}, f32[1,32,128]{2,1,0:T(8,128)S(1)}, u32[]{:S(2)}, u32[]{:S(2)}) collective-permute-start(f32[1,32,128]{2,1,0:T(8,128)S(1)} %get-tuple-element.68), channel_id=1, source_target_pairs={{0,764},{4,8},{8,4},{12,16},{16,12},{20,24},{24,20},{28,32},{32,28... | collective-permute-start | bytes 49160 | tf_op jit(solution)/shard_map/ppermute | solution.py:771
  42.6 2.0 %collective-permute-start.5 = (f32[1,32,128]{2,1,0:T(8,128)S(1)}, f32[1,32,128]{2,1,0:T(8,128)S(1)}, u32[]{:S(2)}, u32[]{:S(2)}) collective-permute-start(f32[1,32,128]{2,1,0:T(8,128)S(1)} %get-tuple-element.69), channel_id=1, source_target_pairs={{0,4},{4,0},{8,12},{12,8},{16,20},{20,16},{24,28},{28,24},{32,36},... | collective-permute-start | bytes 49160 | tf_op jit(solution)/shard_map/ppermute | solution.py:778
  44.6 0.4 shard_map.80.kv_in
  45.1 4.2 %collective-permute-done.4.h0 = f32[1,32,128]{2,1,0:T(8,128)S(1)} collective-permute-done((f32[1,32,128]{2,1,0:T(8,128)S(1)}, f32[1,32,128]{2,1,0:T(8,128)S(1)}, u32[]{:S(2)}, u32[]{:S(2)}) %collective-permute-start.4) | collective-permute-done | bytes 16416 | tf_op jit(solution)/shard_map/ppermute | solution.py:771
  49.3 0.6 shard_map.81
  49.9 5.3 %collective-permute-start.6 = (f32[1,32,128]{2,1,0:T(8,128)S(1)}, f32[1,32,128]{2,1,0:T(8,128)S(1)}, u32[]{:S(2)}, u32[]{:S(2)}) collective-permute-start(f32[1,32,128]{2,1,0:T(8,128)S(1)} %get-tuple-element.77), channel_id=1, source_target_pairs={{0,764},{4,8},{8,4},{12,16},{16,12},{20,24},{24,20},{28,32},{32,28... | collective-permute-start | bytes 49160 | tf_op jit(solution)/shard_map/ppermute | solution.py:771
  55.1 1.9 %collective-permute-start.7 = (f32[1,32,128]{2,1,0:T(8,128)S(1)}, f32[1,32,128]{2,1,0:T(8,128)S(1)}, u32[]{:S(2)}, u32[]{:S(2)}) collective-permute-start(f32[1,32,128]{2,1,0:T(8,128)S(1)} %get-tuple-element.78), channel_id=1, source_target_pairs={{0,4},{4,0},{8,12},{12,8},{16,20},{20,16},{24,28},{28,24},{32,36},... | collective-permute-start | bytes 49160 | tf_op jit(solution)/shard_map/ppermute | solution.py:778
  57.1 0.4 shard_map.82
  57.5 2.5 %collective-permute-done.6.far_ref.h0 = f32[1,32,128]{2,1,0:T(8,128)S(1)} collective-permute-done((f32[1,32,128]{2,1,0:T(8,128)S(1)}, f32[1,32,128]{2,1,0:T(8,128)S(1)}, u32[]{:S(2)}, u32[]{:S(2)}) %collective-permute-start.6) | collective-permute-done | bytes 16416 | tf_op jit(solution)/shard_map/ppermute | solution.py:771
  60.1 0.1 shard_map.83
  60.2 8.3 %all-gather.1 = f32[4,144,128]{2,1,0:T(8,128)S(1)} all-gather(f32[1,144,128]{2,1,0:T(8,128)S(1)} %shard_map.83), channel_id=3, replica_groups=mesh['outer'=16,'ring'=12,'narrow'=4] {'narrow'}, dimensions={0}, use_global_device_ids=true | all-gather | bytes 368640 | tf_op jit(solution)/shard_map/all_gather | solution.py:799
  68.4 0.8 shard_map.84
  69.3 6.0 %collective-permute-start.8 = (f32[1,32,128]{2,1,0:T(8,128)S(1)}, f32[1,32,128]{2,1,0:T(8,128)S(1)}, u32[]{:S(2)}, u32[]{:S(2)}) collective-permute-start(f32[1,32,128]{2,1,0:T(8,128)S(1)} %get-tuple-element.88), channel_id=1, source_target_pairs={{0,764},{4,8},{8,4},{12,16},{16,12},{20,24},{24,20},{28,32},{32,28... | collective-permute-start | bytes 49160 | tf_op jit(solution)/shard_map/ppermute | solution.py:771
  75.3 1.9 %collective-permute-start.9 = (f32[1,32,128]{2,1,0:T(8,128)S(1)}, f32[1,32,128]{2,1,0:T(8,128)S(1)}, u32[]{:S(2)}, u32[]{:S(2)}) collective-permute-start(f32[1,32,128]{2,1,0:T(8,128)S(1)} %get-tuple-element.89), channel_id=1, source_target_pairs={{0,4},{4,0},{8,12},{12,8},{16,20},{20,16},{24,28},{28,24},{32,36},... | collective-permute-start | bytes 49160 | tf_op jit(solution)/shard_map/ppermute | solution.py:778
  77.2 0.5 shard_map.85
  77.7 1.7 %collective-permute-done.8.h0 = f32[1,32,128]{2,1,0:T(8,128)S(1)} collective-permute-done((f32[1,32,128]{2,1,0:T(8,128)S(1)}, f32[1,32,128]{2,1,0:T(8,128)S(1)}, u32[]{:S(2)}, u32[]{:S(2)}) %collective-permute-start.8) | collective-permute-done | bytes 16416 | tf_op jit(solution)/shard_map/ppermute | solution.py:771
  79.5 0.6 collective-permute-done.9.h1
  80.1 0.6 shard_map.86
  80.7 5.4 %collective-permute-start.10 = (f32[1,32,128]{2,1,0:T(8,128)S(1)}, f32[1,32,128]{2,1,0:T(8,128)S(1)}, u32[]{:S(2)}, u32[]{:S(2)}) collective-permute-start(f32[1,32,128]{2,1,0:T(8,128)S(1)} %get-tuple-element.94), channel_id=1, source_target_pairs={{0,764},{4,8},{8,4},{12,16},{16,12},{20,24},{24,20},{28,32},{32,28... | collective-permute-start | bytes 49160 | tf_op jit(solution)/shard_map/ppermute | solution.py:771
  86.1 1.9 %collective-permute-start.11 = (f32[1,32,128]{2,1,0:T(8,128)S(1)}, f32[1,32,128]{2,1,0:T(8,128)S(1)}, u32[]{:S(2)}, u32[]{:S(2)}) collective-permute-start(f32[1,32,128]{2,1,0:T(8,128)S(1)} %get-tuple-element.95), channel_id=1, source_target_pairs={{0,4},{4,0},{8,12},{12,8},{16,20},{20,16},{24,28},{28,24},{32,36},... | collective-permute-start | bytes 49160 | tf_op jit(solution)/shard_map/ppermute | solution.py:778
  88.0 0.4 shard_map.87
  88.5 2.5 %collective-permute-done.10.far_ref.h0 = f32[1,32,128]{2,1,0:T(8,128)S(1)} collective-permute-done((f32[1,32,128]{2,1,0:T(8,128)S(1)}, f32[1,32,128]{2,1,0:T(8,128)S(1)}, u32[]{:S(2)}, u32[]{:S(2)}) %collective-permute-start.10) | collective-permute-done | bytes 16416 | tf_op jit(solution)/shard_map/ppermute | solution.py:771
  91.1 8.0 %all-gather.2 = f32[4,144,128]{2,1,0:T(8,128)S(1)} all-gather(f32[1,144,128]{2,1,0:T(8,128)S(1)} %shard_map.88), channel_id=4, replica_groups=mesh['outer'=16,'ring'=12,'narrow'=4] {'narrow'}, dimensions={0}, use_global_device_ids=true | all-gather | bytes 368640 | tf_op jit(solution)/shard_map/all_gather | solution.py:799
  99.1 0.8 shard_map.89
  100.0 5.6 %collective-permute-start.12 = (f32[1,32,128]{2,1,0:T(8,128)S(1)}, f32[1,32,128]{2,1,0:T(8,128)S(1)}, u32[]{:S(2)}, u32[]{:S(2)}) collective-permute-start(f32[1,32,128]{2,1,0:T(8,128)S(1)} %get-tuple-element.102), channel_id=1, source_target_pairs={{0,764},{4,8},{8,4},{12,16},{16,12},{20,24},{24,20},{28,32},{32,28... | collective-permute-start | bytes 49160 | tf_op jit(solution)/shard_map/ppermute | solution.py:771
  105.5 1.9 %collective-permute-start.13 = (f32[1,32,128]{2,1,0:T(8,128)S(1)}, f32[1,32,128]{2,1,0:T(8,128)S(1)}, u32[]{:S(2)}, u32[]{:S(2)}) collective-permute-start(f32[1,32,128]{2,1,0:T(8,128)S(1)} %get-tuple-element.103), channel_id=1, source_target_pairs={{0,4},{4,0},{8,12},{12,8},{16,20},{20,16},{24,28},{28,24},{32,36},... | collective-permute-start | bytes 49160 | tf_op jit(solution)/shard_map/ppermute | solution.py:778
  107.5 0.5 shard_map.90.kv_in
  107.9 2.2 %collective-permute-done.12.h0 = f32[1,32,128]{2,1,0:T(8,128)S(1)} collective-permute-done((f32[1,32,128]{2,1,0:T(8,128)S(1)}, f32[1,32,128]{2,1,0:T(8,128)S(1)}, u32[]{:S(2)}, u32[]{:S(2)}) %collective-permute-start.12) | collective-permute-done | bytes 16416 | tf_op jit(solution)/shard_map/ppermute | solution.py:771
  110.2 0.1 collective-permute-done.13.h1
  110.3 1.3 shard_map.91
  111.6 6.2 %all-to-all-start = ((f32[64,1,128]{2,1,0:T(1,128)}), f32[64,1,128]{2,1,0:T(1,128)S(1)}, u32[]{:S(2)}, u32[]{:S(2)}) async-start(f32[64,1,128]{2,1,0:T(1,128)} %bitcast.5), calls=%async_computation | async-start | bytes 65536 | tf_op jit(solution)/shard_map/all_to_all | solution.py:885
  117.8 8.2 %collective-permute-start.14 = (f32[1,32,128]{2,1,0:T(8,128)S(1)}, f32[1,32,128]{2,1,0:T(8,128)S(1)}, u32[]{:S(2)}, u32[]{:S(2)}) collective-permute-start(f32[1,32,128]{2,1,0:T(8,128)S(1)} %get-tuple-element.110), channel_id=1, source_target_pairs={{0,764},{4,8},{8,4},{12,16},{16,12},{20,24},{24,20},{28,32},{32,28... | collective-permute-start | bytes 49160 | tf_op jit(solution)/shard_map/ppermute | solution.py:771
  126.0 0.1 copy.10.order_ref
  126.1 1.0 all-to-all-done
  127.2 0.6 all_to_all.15
  127.8 3.5 %all-to-all-start.1 = ((f32[12,1,128]{2,1,0:T(1,128)}), f32[12,1,128]{2,1,0:T(1,128)S(1)}, u32[]{:S(2)}, u32[]{:S(2)}) async-start(f32[12,1,128]{2,1,0:T(1,128)} %all_to_all.15), calls=%async_computation.1 | async-start | bytes 12288 | tf_op jit(solution)/shard_map/all_to_all | solution.py:888
  131.3 3.3 %all-gather.3 = f32[2,32,128]{2,1,0:T(8,128)S(1)} all-gather(f32[1,32,128]{2,1,0:T(8,128)S(1)} %get-tuple-element.111), channel_id=5, replica_groups={{0,4},{8,12},{16,20},{24,28},{32,36},{40,44},{1,5},{9,13},{17,21},{25,2..., dimensions={0}, use_global_device_ids=true | all-gather | bytes 49152 | tf_op jit(solution)/shard_map/all_gather | solution.py:889
  134.6 6.8 %all-gather.4 = f32[4,16,128]{2,1,0:T(8,128)S(1)} all-gather(f32[1,16,128]{2,1,0:T(8,128)S(1)} %shard_map.92), channel_id=6, replica_groups=mesh['outer'=16,'ring'=12,'narrow'=4] {'narrow'}, dimensions={0}, use_global_device_ids=true | all-gather | bytes 40960 | tf_op jit(solution)/shard_map/all_gather | solution.py:893
  141.5 0.6 shard_map.93.spread_ref
  142.1 0.8 shard_map.94
  (20 shorter events, 0.3 us)
Async XLA Ops:
  3.3 27.4 %collective-permute-start = (f32[2,32,128]{2,1,0:T(8,128)S(1)}, f32[2,32,128]{2,1,0:T(8,128)S(1)}, u32[]{:S(2)}, u32[]{:S(2)}) collective-permute-start(f32[2,32,128]{2,1,0:T(8,128)S(1)} %get-tuple-element.60), channel_id=1, source_target_pairs={{0,764},{4,8},{8,4},{12,16},{16,12},{20,24},{24,20},{28,32},{32,28... | collective-permute-start | bytes 98312 | tf_op jit(solution)/shard_map/ppermute | solution.py:771
  23.8 6.9 %collective-permute-start.1 = (f32[2,32,128]{2,1,0:T(8,128)S(1)}, f32[2,32,128]{2,1,0:T(8,128)S(1)}, u32[]{:S(2)}, u32[]{:S(2)}) collective-permute-start(f32[2,32,128]{2,1,0:T(8,128)S(1)} %get-tuple-element.61), channel_id=1, source_target_pairs={{0,4},{4,0},{8,12},{12,8},{16,20},{20,16},{24,28},{28,24},{32,36},... | collective-permute-start | bytes 98312 | tf_op jit(solution)/shard_map/ppermute | solution.py:778
  25.7 12.5 %collective-permute-start.2 = (f32[6,4,16,128]{3,2,1,0:T(8,128)S(1)}, f32[6,4,16,128]{3,2,1,0:T(8,128)S(1)}, u32[]{:S(2)}, u32[]{:S(2)}) collective-permute-start(f32[6,4,16,128]{3,2,1,0:T(8,128)S(1)} %get-tuple-element.63), channel_id=1, source_target_pairs={{0,1},{1,2},{2,3},{3,0},{4,5},{5,6},{6,7},{7,4},{8,9},{9,10},{10,1... | collective-permute-start | bytes 589832 | tf_op jit(solution)/shard_map/ppermute | solution.py:804
  28.8 9.4 %collective-permute-start.3 = (f32[6,4,16,128]{3,2,1,0:T(8,128)S(1)}, f32[6,4,16,128]{3,2,1,0:T(8,128)S(1)}, u32[]{:S(2)}, u32[]{:S(2)}) collective-permute-start(f32[6,4,16,128]{3,2,1,0:T(8,128)S(1)} %get-tuple-element.64), channel_id=1, source_target_pairs={{0,3},{1,0},{2,1},{3,2},{4,7},{5,4},{6,5},{7,6},{8,11},{9,8},{10,9... | collective-permute-start | bytes 589832 | tf_op jit(solution)/shard_map/ppermute | solution.py:805
  30.7 7.5 %copy-start.1 = (bf16[384,256]{1,0:T(8,128)(2,1)S(1)}, bf16[384,256]{1,0:T(8,128)(2,1)}, u32[]{:S(2)}) copy-start(bf16[384,256]{1,0:T(8,128)(2,1)} %constant.8.clone.grad_ref) | copy-start | bytes 589828
  30.8 7.4 %copy-start = (bf16[256,256]{1,0:T(8,128)(2,1)S(1)}, bf16[256,256]{1,0:T(8,128)(2,1)}, u32[]{:S(2)}) copy-start(bf16[256,256]{1,0:T(8,128)(2,1)} %constant.9.clone.diver_ref) | copy-start | bytes 393220
  39.1 10.2 %collective-permute-start.4 = (f32[1,32,128]{2,1,0:T(8,128)S(1)}, f32[1,32,128]{2,1,0:T(8,128)S(1)}, u32[]{:S(2)}, u32[]{:S(2)}) collective-permute-start(f32[1,32,128]{2,1,0:T(8,128)S(1)} %get-tuple-element.68), channel_id=1, source_target_pairs={{0,764},{4,8},{8,4},{12,16},{16,12},{20,24},{24,20},{28,32},{32,28... | collective-permute-start | bytes 49160 | tf_op jit(solution)/shard_map/ppermute | solution.py:771
  42.6 6.6 %collective-permute-start.5 = (f32[1,32,128]{2,1,0:T(8,128)S(1)}, f32[1,32,128]{2,1,0:T(8,128)S(1)}, u32[]{:S(2)}, u32[]{:S(2)}) collective-permute-start(f32[1,32,128]{2,1,0:T(8,128)S(1)} %get-tuple-element.69), channel_id=1, source_target_pairs={{0,4},{4,0},{8,12},{12,8},{16,20},{20,16},{24,28},{28,24},{32,36},... | collective-permute-start | bytes 49160 | tf_op jit(solution)/shard_map/ppermute | solution.py:778
  49.9 10.2 %collective-permute-start.6 = (f32[1,32,128]{2,1,0:T(8,128)S(1)}, f32[1,32,128]{2,1,0:T(8,128)S(1)}, u32[]{:S(2)}, u32[]{:S(2)}) collective-permute-start(f32[1,32,128]{2,1,0:T(8,128)S(1)} %get-tuple-element.77), channel_id=1, source_target_pairs={{0,764},{4,8},{8,4},{12,16},{16,12},{20,24},{24,20},{28,32},{32,28... | collective-permute-start | bytes 49160 | tf_op jit(solution)/shard_map/ppermute | solution.py:771
  55.1 4.9 %collective-permute-start.7 = (f32[1,32,128]{2,1,0:T(8,128)S(1)}, f32[1,32,128]{2,1,0:T(8,128)S(1)}, u32[]{:S(2)}, u32[]{:S(2)}) collective-permute-start(f32[1,32,128]{2,1,0:T(8,128)S(1)} %get-tuple-element.78), channel_id=1, source_target_pairs={{0,4},{4,0},{8,12},{12,8},{16,20},{20,16},{24,28},{28,24},{32,36},... | collective-permute-start | bytes 49160 | tf_op jit(solution)/shard_map/ppermute | solution.py:778
  69.3 10.2 %collective-permute-start.8 = (f32[1,32,128]{2,1,0:T(8,128)S(1)}, f32[1,32,128]{2,1,0:T(8,128)S(1)}, u32[]{:S(2)}, u32[]{:S(2)}) collective-permute-start(f32[1,32,128]{2,1,0:T(8,128)S(1)} %get-tuple-element.88), channel_id=1, source_target_pairs={{0,764},{4,8},{8,4},{12,16},{16,12},{20,24},{24,20},{28,32},{32,28... | collective-permute-start | bytes 49160 | tf_op jit(solution)/shard_map/ppermute | solution.py:771
  75.3 4.8 %collective-permute-start.9 = (f32[1,32,128]{2,1,0:T(8,128)S(1)}, f32[1,32,128]{2,1,0:T(8,128)S(1)}, u32[]{:S(2)}, u32[]{:S(2)}) collective-permute-start(f32[1,32,128]{2,1,0:T(8,128)S(1)} %get-tuple-element.89), channel_id=1, source_target_pairs={{0,4},{4,0},{8,12},{12,8},{16,20},{20,16},{24,28},{28,24},{32,36},... | collective-permute-start | bytes 49160 | tf_op jit(solution)/shard_map/ppermute | solution.py:778
  80.7 10.3 %collective-permute-start.10 = (f32[1,32,128]{2,1,0:T(8,128)S(1)}, f32[1,32,128]{2,1,0:T(8,128)S(1)}, u32[]{:S(2)}, u32[]{:S(2)}) collective-permute-start(f32[1,32,128]{2,1,0:T(8,128)S(1)} %get-tuple-element.94), channel_id=1, source_target_pairs={{0,764},{4,8},{8,4},{12,16},{16,12},{20,24},{24,20},{28,32},{32,28... | collective-permute-start | bytes 49160 | tf_op jit(solution)/shard_map/ppermute | solution.py:771
  86.1 4.9 %collective-permute-start.11 = (f32[1,32,128]{2,1,0:T(8,128)S(1)}, f32[1,32,128]{2,1,0:T(8,128)S(1)}, u32[]{:S(2)}, u32[]{:S(2)}) collective-permute-start(f32[1,32,128]{2,1,0:T(8,128)S(1)} %get-tuple-element.95), channel_id=1, source_target_pairs={{0,4},{4,0},{8,12},{12,8},{16,20},{20,16},{24,28},{28,24},{32,36},... | collective-permute-start | bytes 49160 | tf_op jit(solution)/shard_map/ppermute | solution.py:778
  100.0 10.2 %collective-permute-start.12 = (f32[1,32,128]{2,1,0:T(8,128)S(1)}, f32[1,32,128]{2,1,0:T(8,128)S(1)}, u32[]{:S(2)}, u32[]{:S(2)}) collective-permute-start(f32[1,32,128]{2,1,0:T(8,128)S(1)} %get-tuple-element.102), channel_id=1, source_target_pairs={{0,764},{4,8},{8,4},{12,16},{16,12},{20,24},{24,20},{28,32},{32,28... | collective-permute-start | bytes 49160 | tf_op jit(solution)/shard_map/ppermute | solution.py:771
  105.5 4.8 %collective-permute-start.13 = (f32[1,32,128]{2,1,0:T(8,128)S(1)}, f32[1,32,128]{2,1,0:T(8,128)S(1)}, u32[]{:S(2)}, u32[]{:S(2)}) collective-permute-start(f32[1,32,128]{2,1,0:T(8,128)S(1)} %get-tuple-element.103), channel_id=1, source_target_pairs={{0,4},{4,0},{8,12},{12,8},{16,20},{20,16},{24,28},{28,24},{32,36},... | collective-permute-start | bytes 49160 | tf_op jit(solution)/shard_map/ppermute | solution.py:778
  111.6 15.5 %all-to-all-start = ((f32[64,1,128]{2,1,0:T(1,128)}), f32[64,1,128]{2,1,0:T(1,128)S(1)}, u32[]{:S(2)}, u32[]{:S(2)}) async-start(f32[64,1,128]{2,1,0:T(1,128)} %bitcast.5), calls=%async_computation | async-start | bytes 65536 | tf_op jit(solution)/shard_map/all_to_all | solution.py:885
  117.8 8.2 %copy-start.2 = (s32[1,1,64]{2,1,0:T(1,128)S(1)}, s32[1,1,64]{2,1,0:T(1,128)}, u32[]{:S(2)}) copy-start(s32[1,1,64]{2,1,0:T(1,128)} %param.8) | copy-start | bytes 772
  117.8 16.7 %collective-permute-start.14 = (f32[1,32,128]{2,1,0:T(8,128)S(1)}, f32[1,32,128]{2,1,0:T(8,128)S(1)}, u32[]{:S(2)}, u32[]{:S(2)}) collective-permute-start(f32[1,32,128]{2,1,0:T(8,128)S(1)} %get-tuple-element.110), channel_id=1, source_target_pairs={{0,764},{4,8},{8,4},{12,16},{16,12},{20,24},{24,20},{28,32},{32,28... | collective-permute-start | bytes 49160 | tf_op jit(solution)/shard_map/ppermute | solution.py:771
  127.8 14.2 %all-to-all-start.1 = ((f32[12,1,128]{2,1,0:T(1,128)}), f32[12,1,128]{2,1,0:T(1,128)S(1)}, u32[]{:S(2)}, u32[]{:S(2)}) async-start(f32[12,1,128]{2,1,0:T(1,128)} %all_to_all.15), calls=%async_computation.1 | async-start | bytes 12288 | tf_op jit(solution)/shard_map/all_to_all | solution.py:888

commit v7 on v6

--- a/solution.py
+++ b/solution.py
@@ -364,8 +364,9 @@
     return value
 
 
-def apply_flux(v_ref, metric_ref, ghost_ref, grad_ref, flux_ref, part_ref):
+def apply_flux(v_ref, metric_ref, ghost_ref, grad_ref, flux_ref, part_ref, with_energy=False):
     count = v_ref.shape[1]
+    energy = jnp.zeros((8, LANES), jnp.float32)
     side = dot_grad(v_ref[...].reshape(NODES * count, LANES), grad_ref)
     flux_ref[0] = side[:, :LANES]
     flux_ref[1] = side[:, LANES:]
@@ -382,12 +383,21 @@
             at = pl.ds(i * count + chunk * 8, 8)
             g_z, g_a, g_r = grad_z[i], flux_ref[0, at], flux_ref[1, at]
             m = [geometry[c, i, there] for c in range(6)]
-            flux_z.append(m[0] * g_z + m[3] * g_a + m[4] * g_r)
-            flux_ref[0, at] = m[3] * g_z + m[1] * g_a + m[5] * g_r
-            flux_ref[1, at] = m[4] * g_z + m[5] * g_a + m[2] * g_r
+            f_z = m[0] * g_z + m[3] * g_a + m[4] * g_r
+            f_a = m[3] * g_z + m[1] * g_a + m[5] * g_r
+            f_r = m[4] * g_z + m[5] * g_a + m[2] * g_r
+            flux_z.append(f_z)
+            flux_ref[0, at] = f_a
+            flux_ref[1, at] = f_r
+            if with_energy:
+                energy = energy + (g_z * f_z + g_a * f_a + g_r * f_r)
         part_z = along_nodes(flux_z, DERIV.T)
         for i in range(NODES):
-            part_ref[i, rows] = part_z[i] + geometry[6, i, there] * values[i]
+            screened = geometry[6, i, there] * values[i]
+            part_ref[i, rows] = part_z[i] + screened
+            if with_energy:
+                energy = energy + screened * values[i]
+    return energy
 
 
 def whole_planes(flux_ref, part_ref, diver_ref, planes):
@@ -411,13 +421,6 @@
     even = is_even()
     near_ref[0] = jnp.where(even, last, first)
     far_ref[0] = jnp.where(even, first, last)
-
-
-def apply_element(v_ref, metric_ref, ghost_ref, grad_ref, diver_ref, flux_ref, out_ref):
-    apply_flux(v_ref, metric_ref, ghost_ref, grad_ref, flux_ref, out_ref)
-    planes = whole_planes(flux_ref, out_ref, diver_ref, range(NODES))
-    for i in range(NODES):
-        out_ref[i] = planes[i]
 
 
 def rest_kernel(flux_ref, part_ref, diver_ref, kv_ref):
@@ -666,9 +669,9 @@
 
 
 def sixth_kernel(
-    kv_in, h0, h1, source_ref, inverse_ref, start_ref, residual_ref, first_ref, early_ref,
+    kv_in, h0, h1, source_ref, inverse_ref, start_ref, residual_ref, early_ref,
     metric_ref, grad_ref, diver_ref,
-    result_ref, kv_ref, far_ref, near_ref, pack_ref, sums_ref, flux_ref, work_ref,
+    result_ref, kv_ref, far_ref, near_ref, pack_ref, sums_hbm, flux_ref, work_ref, sums_ref, sem,
 ):
     image = completed(kv_in, (h0, h1))
     plane = weight_plane()
@@ -679,30 +682,25 @@
         result_ref[i] = result
         r_y = r_y + residual_ref[i] * result * node_weight(i)
         w_y = w_y + source_ref[i] * result * node_weight(i)
-    apply_element(result_ref, metric_ref, None, grad_ref, diver_ref, flux_ref, work_ref)
-    z_ky = jnp.zeros((ROWS, LANES), jnp.float32)
-    y_ky = jnp.zeros((ROWS, LANES), jnp.float32)
-    for i in range(NODES):
-        z_ky = z_ky + first_ref[i] * work_ref[i]
-        y_ky = y_ky + result_ref[i] * work_ref[i]
+    energy = apply_flux(
+        result_ref, metric_ref, None, grad_ref, flux_ref, work_ref, with_energy=True
+    )
     zero = jnp.zeros((1, LANES), jnp.float32)
-    late = sum_row([zero, zero, r_y * plane, w_y * plane, z_ky, y_ky])
+    late = sum_row([zero, zero, r_y * plane, w_y * plane, energy])
     sums_ref[...] = jnp.broadcast_to(early_ref[...] + late, sums_ref.shape)
-    store_assembled(
-        kv_ref, far_ref, near_ref, is_even(), lambda i: work_ref[i], 0, pack_ref
-    )
-
-
-def spread_kernel(
-    kv_in, h0, h1, h2, order_ref, residual_ref, first_ref, image_ref, second_ref, out_ref, spread_ref
-):
-    image = completed(kv_in, (h0, h1, h2))
+    leave = pltpu.make_async_copy(sums_ref, sums_hbm, sem)
+    leave.start()
+    planes = whole_planes(flux_ref, work_ref, diver_ref, range(NODES))
+    store_assembled(kv_ref, far_ref, near_ref, is_even(), lambda i: planes[i], 0, pack_ref)
+    leave.wait()
+
+
+def spread_fields(order_ref, fields, out_ref, spread_ref):
     low = lane_iota(ROWS) < 64
     pick = jnp.where(
         lax.broadcasted_iota(jnp.int32, (64, 64), 1) == order_ref[...], 1.0, 0.0
     ).astype(jnp.bfloat16)
-    fields = [lambda i, ref=ref: ref[i] for ref in (first_ref, second_ref, residual_ref, image_ref)]
-    for f, field in enumerate(fields + [image]):
+    for f, field in enumerate(fields):
         for b in range(NODES // 2):
             even, odd = field(2 * b), field(2 * b + 1)
             lanes = pl.ds(b * LANES, LANES)
@@ -714,25 +712,36 @@
         out_ref[f] = dot(pick, high) + (dot(pick, middle) + dot(pick, rest))
 
 
-def last_kernel(sums_ref, spread_ref, solution_ref, residual_ref):
+def spread_early_kernel(
+    order_ref, first_ref, second_ref, residual_ref, image_ref, out_ref, spread_ref
+):
+    refs = (first_ref, second_ref, residual_ref, image_ref)
+    spread_fields(order_ref, [lambda i, ref=ref: ref[i] for ref in refs], out_ref, spread_ref)
+
+
+def spread_late_kernel(kv_in, h0, h1, h2, order_ref, out_ref, spread_ref):
+    spread_fields(order_ref, [completed(kv_in, (h0, h1, h2))], out_ref, spread_ref)
+
+
+def last_kernel(sums_ref, spread_ref, late_ref, solution_ref, residual_ref):
     sums = jnp.sum(sums_ref[...], axis=0, keepdims=True)
     lane = lane_iota(1)
 
     def total(d):
         return jnp.sum(jnp.where(lane == d, sums, 0.0), axis=1, keepdims=True)
 
-    rz0, zw, ry, wy, zq, yq = (total(d) for d in range(6))
+    rz0, zw, ry, wy, yq = (total(d) for d in range(5))
     alpha0 = rz0 / zw
     rz1 = rz0 - alpha0 * (zw + ry) + alpha0 * alpha0 * wy
     beta = rz1 / rz0
     share = 1.0 + beta
-    energy = share * share * zw - 2.0 * share * alpha0 * zq + alpha0 * alpha0 * yq
+    energy = share * share * zw - 2.0 * share * alpha0 * wy + alpha0 * alpha0 * yq
     alpha1 = rz1 / energy
     first_scale = alpha0 + alpha1 * share
     second_scale = alpha1 * alpha0
     solution_ref[...] = first_scale * spread_ref[0] - second_scale * spread_ref[1]
     residual_ref[...] = (
-        spread_ref[2] - first_scale * spread_ref[3] + second_scale * spread_ref[4]
+        spread_ref[2] - first_scale * spread_ref[3] + second_scale * late_ref[0]
     )
 
 
@@ -740,13 +749,13 @@
 F32 = jnp.float32
 
 
-def call(kernel, outs, scratch, *operands, space=pltpu.VMEM, cost=None):
-    vmem = pl.BlockSpec(memory_space=pltpu.VMEM)
+def call(kernel, outs, scratch, *operands, space=pltpu.VMEM, out_spaces=None, cost=None):
+    out_spaces = out_spaces or [pltpu.VMEM] * len(outs)
     return pl.pallas_call(
         kernel,
         out_shape=[jax.ShapeDtypeStruct(s, F32) for s in outs],
         in_specs=[pl.BlockSpec(memory_space=space)] * len(operands),
-        out_specs=[vmem] * len(outs),
+        out_specs=[pl.BlockSpec(memory_space=s) for s in out_spaces],
         scratch_shapes=[pltpu.VMEM(s, F32) if isinstance(s, tuple) else s for s in scratch],
         cost_estimate=cost,
         compiler_params=pltpu.CompilerParams(vmem_limit_bytes=VMEM_LIMIT),
@@ -873,11 +882,17 @@
     )
     (kv,) = call(rest_kernel, [FIELD], [], *parts, diver)
     halo = swap_wide(far, near)
+    sums_shape = (lax.axis_size(REST), LANES)
     second, kv, *face, sums = call(
         sixth_kernel,
-        [FIELD, FIELD] + faces() + packs() + [(lax.axis_size(REST), LANES)],
-        [FLUX, FIELD],
-        kv, *halo, image, inverse, start, residual, first, early, metric, grad, diver,
+        [FIELD, FIELD] + faces() + packs() + [sums_shape],
+        [FLUX, FIELD, sums_shape, pltpu.SemaphoreType.DMA(())],
+        kv, *halo, image, inverse, start, residual, early, metric, grad, diver,
+        out_spaces=[pltpu.VMEM] * 5 + [pltpu.HBM],
+    )
+    order = element_order.reshape(64, 1)
+    (spread,) = call(
+        spread_early_kernel, [(4, 64, 512)], [(64, 512)], order, first, second, residual, image
     )
     far, near, pack = face
     far = swap_far(far)
@@ -891,13 +906,8 @@
     )
     (pack,) = call(pack_kernel, [pack.shape], [], pack, far, near)
     halo = far, near, lax.all_gather(pack, "narrow")
-    (spread,) = call(
-        spread_kernel,
-        [(5, 64, 512)],
-        [(64, 512)],
-        kv, *halo, element_order.reshape(64, 1), residual, first, image, second,
-    )
-    return tuple(call(last_kernel, [(64, 512), (64, 512)], [], sums, spread))
+    (late,) = call(spread_late_kernel, [(1, 64, 512)], [(64, 512)], kv, *halo, order)
+    return tuple(call(last_kernel, [(64, 512), (64, 512)], [], sums, spread, late))
 
 
 def solution(mesh):

time: 144 us -> 143 us (level)
    pallas_call x18 -> x19, Pallas kernels: 11.6 us -> 11.9 us  [call(): pl.pallas_call(kernel, out_shape=[jax.ShapeDtypeStruct(s, F32) for s in o...]
where the time goes in v7:
time: 143 us
  starting transfers between devices  80.8 us (57%)
  blocking collectives  33.8 us (24%)
  waiting for transfers between devices  14.5 us (10%)
  Pallas kernels  11.9 us (8%)
    ppermute x7, starting transfers between devices, swap_far(): lax.ppermute(far, WIDE, [(w, (w + 1 if w % 2 else w - 1) % count) for w i...  54.5 us
    all_gather x2, blocking collectives, swap_edged(): return (far, near, lax.all_gather(pack, 'narrow'))  16.3 us
    ppermute x7, waiting for transfers between devices, swap_far(): lax.ppermute(far, WIDE, [(w, (w + 1 if w % 2 else w - 1) % count) for w i...  13.2 us
    pallas_call x19, Pallas kernels, call(): pl.pallas_call(kernel, out_shape=[jax.ShapeDtypeStruct(s, F32) for s in o...  11.9 us
    ppermute x6, starting transfers between devices, swap_wide(): lax.ppermute(near, WIDE, [(w, w ^ 1) for w in range(count)])  11.6 us
    all_gather x1, blocking collectives, swap_all(): return (far, near, lax.all_gather(pack, 'narrow'))  7.34 us
    all_gather x1, blocking collectives, local(): halo = (far, near, lax.all_gather(pack, 'narrow'))  6.82 us
    all_to_all x1, starting transfers between devices, local(): sums = lax.all_to_all(sums, REST, 0, 0)  6.23 us
  transfers between devices with their start and end apart: 17, of which 8 were waited for; matrix products, arithmetic and copies ran while one was open for 0% of the time, Pallas kernels for 2%

profile of v7, /device:TPU:1, one launch (start us, length us, event | category | flops | bytes accessed | tf_op | source)
XLA Modules:
  0.0 142.8 jit_solution(13093891451142384199)
XLA Ops:
  0.6 2.6 %shard_map.77 = (f32[7,8,32,128]{3,2,1,0:T(8,128)S(1)}, f32[8,32,128]{2,1,0:T(8,128)S(1)}, f32[8,32,128]{2,1,0:T(8,128)S(1)}, f32[2,32,128]{2,1,0:T(8,128)S(1)},...) custom-call(s32[1,64]{1,0:T(1,128)} %bitcast.20, ...), custom_call_target="tpu_custom_call" | custom-call | tf_op jit(solution)/shard_map/pallas_call | solution.py:754
  3.3 20.5 %collective-permute-start = (f32[2,32,128]{2,1,0:T(8,128)S(1)}, f32[2,32,128]{2,1,0:T(8,128)S(1)}, u32[]{:S(2)}, u32[]{:S(2)}) collective-permute-start(f32[2,32,128]{2,1,0:T(8,128)S(1)} %get-tuple-element.60), channel_id=1, source_target_pairs={{0,764},{4,8},{8,4},{12,16},{16,12},{20,24},{24,20},{28,32},{32,28... | collective-permute-start | bytes 98312 | tf_op jit(solution)/shard_map/ppermute | solution.py:780
  23.8 1.9 %collective-permute-start.1 = (f32[2,32,128]{2,1,0:T(8,128)S(1)}, f32[2,32,128]{2,1,0:T(8,128)S(1)}, u32[]{:S(2)}, u32[]{:S(2)}) collective-permute-start(f32[2,32,128]{2,1,0:T(8,128)S(1)} %get-tuple-element.61), channel_id=1, source_target_pairs={{0,4},{4,0},{8,12},{12,8},{16,20},{20,16},{24,28},{28,24},{32,36},... | collective-permute-start | bytes 98312 | tf_op jit(solution)/shard_map/ppermute | solution.py:787
  25.7 3.1 %collective-permute-start.2 = (f32[6,4,16,128]{3,2,1,0:T(8,128)S(1)}, f32[6,4,16,128]{3,2,1,0:T(8,128)S(1)}, u32[]{:S(2)}, u32[]{:S(2)}) collective-permute-start(f32[6,4,16,128]{3,2,1,0:T(8,128)S(1)} %get-tuple-element.63), channel_id=1, source_target_pairs={{0,1},{1,2},{2,3},{3,0},{4,5},{5,6},{6,7},{7,4},{8,9},{9,10},{10,1... | collective-permute-start | bytes 589832 | tf_op jit(solution)/shard_map/ppermute | solution.py:813
  28.8 1.9 %collective-permute-start.3 = (f32[6,4,16,128]{3,2,1,0:T(8,128)S(1)}, f32[6,4,16,128]{3,2,1,0:T(8,128)S(1)}, u32[]{:S(2)}, u32[]{:S(2)}) collective-permute-start(f32[6,4,16,128]{3,2,1,0:T(8,128)S(1)} %get-tuple-element.64), channel_id=1, source_target_pairs={{0,3},{1,0},{2,1},{3,2},{4,7},{5,4},{6,5},{7,6},{8,11},{9,8},{10,9... | collective-permute-start | bytes 589832 | tf_op jit(solution)/shard_map/ppermute | solution.py:814
  30.7 0.1 shard_map.78
  30.8 7.3 %all-gather = f32[8,48,128]{2,1,0:T(8,128)S(1)} all-gather(f32[2,48,128]{2,1,0:T(8,128)S(1)} %shard_map.78), channel_id=2, replica_groups=mesh['outer'=16,'ring'=12,'narrow'=4] {'narrow'}, dimensions={0}, use_global_device_ids=true | all-gather | bytes 245760 | tf_op jit(solution)/shard_map/all_gather | solution.py:793
  38.2 0.8 shard_map.79
  39.1 3.6 %collective-permute-start.4 = (f32[1,32,128]{2,1,0:T(8,128)S(1)}, f32[1,32,128]{2,1,0:T(8,128)S(1)}, u32[]{:S(2)}, u32[]{:S(2)}) collective-permute-start(f32[1,32,128]{2,1,0:T(8,128)S(1)} %get-tuple-element.68), channel_id=1, source_target_pairs={{0,764},{4,8},{8,4},{12,16},{16,12},{20,24},{24,20},{28,32},{32,28... | collective-permute-start | bytes 49160 | tf_op jit(solution)/shard_map/ppermute | solution.py:780
  42.6 2.0 %collective-permute-start.5 = (f32[1,32,128]{2,1,0:T(8,128)S(1)}, f32[1,32,128]{2,1,0:T(8,128)S(1)}, u32[]{:S(2)}, u32[]{:S(2)}) collective-permute-start(f32[1,32,128]{2,1,0:T(8,128)S(1)} %get-tuple-element.69), channel_id=1, source_target_pairs={{0,4},{4,0},{8,12},{12,8},{16,20},{20,16},{24,28},{28,24},{32,36},... | collective-permute-start | bytes 49160 | tf_op jit(solution)/shard_map/ppermute | solution.py:787
  44.6 0.4 shard_map.80.kv_in
  45.1 4.2 %collective-permute-done.4.h0 = f32[1,32,128]{2,1,0:T(8,128)S(1)} collective-permute-done((f32[1,32,128]{2,1,0:T(8,128)S(1)}, f32[1,32,128]{2,1,0:T(8,128)S(1)}, u32[]{:S(2)}, u32[]{:S(2)}) %collective-permute-start.4) | collective-permute-done | bytes 16416 | tf_op jit(solution)/shard_map/ppermute | solution.py:780
  49.3 0.6 shard_map.81
  49.9 5.3 %collective-permute-start.6 = (f32[1,32,128]{2,1,0:T(8,128)S(1)}, f32[1,32,128]{2,1,0:T(8,128)S(1)}, u32[]{:S(2)}, u32[]{:S(2)}) collective-permute-start(f32[1,32,128]{2,1,0:T(8,128)S(1)} %get-tuple-element.77), channel_id=1, source_target_pairs={{0,764},{4,8},{8,4},{12,16},{16,12},{20,24},{24,20},{28,32},{32,28... | collective-permute-start | bytes 49160 | tf_op jit(solution)/shard_map/ppermute | solution.py:780
  55.1 1.9 %collective-permute-start.7 = (f32[1,32,128]{2,1,0:T(8,128)S(1)}, f32[1,32,128]{2,1,0:T(8,128)S(1)}, u32[]{:S(2)}, u32[]{:S(2)}) collective-permute-start(f32[1,32,128]{2,1,0:T(8,128)S(1)} %get-tuple-element.78), channel_id=1, source_target_pairs={{0,4},{4,0},{8,12},{12,8},{16,20},{20,16},{24,28},{28,24},{32,36},... | collective-permute-start | bytes 49160 | tf_op jit(solution)/shard_map/ppermute | solution.py:787
  57.1 0.4 shard_map.82
  57.5 2.5 %collective-permute-done.6.far_ref.h0 = f32[1,32,128]{2,1,0:T(8,128)S(1)} collective-permute-done((f32[1,32,128]{2,1,0:T(8,128)S(1)}, f32[1,32,128]{2,1,0:T(8,128)S(1)}, u32[]{:S(2)}, u32[]{:S(2)}) %collective-permute-start.6) | collective-permute-done | bytes 16416 | tf_op jit(solution)/shard_map/ppermute | solution.py:780
  60.2 8.3 %all-gather.1 = f32[4,144,128]{2,1,0:T(8,128)S(1)} all-gather(f32[1,144,128]{2,1,0:T(8,128)S(1)} %shard_map.83), channel_id=3, replica_groups=mesh['outer'=16,'ring'=12,'narrow'=4] {'narrow'}, dimensions={0}, use_global_device_ids=true | all-gather | bytes 368640 | tf_op jit(solution)/shard_map/all_gather | solution.py:808
  68.4 0.8 shard_map.84
  69.3 6.0 %collective-permute-start.8 = (f32[1,32,128]{2,1,0:T(8,128)S(1)}, f32[1,32,128]{2,1,0:T(8,128)S(1)}, u32[]{:S(2)}, u32[]{:S(2)}) collective-permute-start(f32[1,32,128]{2,1,0:T(8,128)S(1)} %get-tuple-element.88), channel_id=1, source_target_pairs={{0,764},{4,8},{8,4},{12,16},{16,12},{20,24},{24,20},{28,32},{32,28... | collective-permute-start | bytes 49160 | tf_op jit(solution)/shard_map/ppermute | solution.py:780
  75.3 1.9 %collective-permute-start.9 = (f32[1,32,128]{2,1,0:T(8,128)S(1)}, f32[1,32,128]{2,1,0:T(8,128)S(1)}, u32[]{:S(2)}, u32[]{:S(2)}) collective-permute-start(f32[1,32,128]{2,1,0:T(8,128)S(1)} %get-tuple-element.89), channel_id=1, source_target_pairs={{0,4},{4,0},{8,12},{12,8},{16,20},{20,16},{24,28},{28,24},{32,36},... | collective-permute-start | bytes 49160 | tf_op jit(solution)/shard_map/ppermute | solution.py:787
  77.2 0.5 shard_map.85
  77.7 1.8 %collective-permute-done.8.h0 = f32[1,32,128]{2,1,0:T(8,128)S(1)} collective-permute-done((f32[1,32,128]{2,1,0:T(8,128)S(1)}, f32[1,32,128]{2,1,0:T(8,128)S(1)}, u32[]{:S(2)}, u32[]{:S(2)}) %collective-permute-start.8) | collective-permute-done | bytes 16416 | tf_op jit(solution)/shard_map/ppermute | solution.py:780
  79.5 0.6 collective-permute-done.9.h1
  80.1 0.6 shard_map.86
  80.7 5.4 %collective-permute-start.10 = (f32[1,32,128]{2,1,0:T(8,128)S(1)}, f32[1,32,128]{2,1,0:T(8,128)S(1)}, u32[]{:S(2)}, u32[]{:S(2)}) collective-permute-start(f32[1,32,128]{2,1,0:T(8,128)S(1)} %get-tuple-element.94), channel_id=1, source_target_pairs={{0,764},{4,8},{8,4},{12,16},{16,12},{20,24},{24,20},{28,32},{32,28... | collective-permute-start | bytes 49160 | tf_op jit(solution)/shard_map/ppermute | solution.py:780
  86.1 1.9 %collective-permute-start.11 = (f32[1,32,128]{2,1,0:T(8,128)S(1)}, f32[1,32,128]{2,1,0:T(8,128)S(1)}, u32[]{:S(2)}, u32[]{:S(2)}) collective-permute-start(f32[1,32,128]{2,1,0:T(8,128)S(1)} %get-tuple-element.95), channel_id=1, source_target_pairs={{0,4},{4,0},{8,12},{12,8},{16,20},{20,16},{24,28},{28,24},{32,36},... | collective-permute-start | bytes 49160 | tf_op jit(solution)/shard_map/ppermute | solution.py:787
  88.0 0.4 shard_map.87
  88.5 2.5 %collective-permute-done.10.far_ref.h0 = f32[1,32,128]{2,1,0:T(8,128)S(1)} collective-permute-done((f32[1,32,128]{2,1,0:T(8,128)S(1)}, f32[1,32,128]{2,1,0:T(8,128)S(1)}, u32[]{:S(2)}, u32[]{:S(2)}) %collective-permute-start.10) | collective-permute-done | bytes 16416 | tf_op jit(solution)/shard_map/ppermute | solution.py:780
  91.1 8.0 %all-gather.2 = f32[4,144,128]{2,1,0:T(8,128)S(1)} all-gather(f32[1,144,128]{2,1,0:T(8,128)S(1)} %shard_map.88), channel_id=4, replica_groups=mesh['outer'=16,'ring'=12,'narrow'=4] {'narrow'}, dimensions={0}, use_global_device_ids=true | all-gather | bytes 368640 | tf_op jit(solution)/shard_map/all_gather | solution.py:808
  99.1 0.8 shard_map.89
  100.0 5.6 %collective-permute-start.12 = (f32[1,32,128]{2,1,0:T(8,128)S(1)}, f32[1,32,128]{2,1,0:T(8,128)S(1)}, u32[]{:S(2)}, u32[]{:S(2)}) collective-permute-start(f32[1,32,128]{2,1,0:T(8,128)S(1)} %get-tuple-element.102), channel_id=1, source_target_pairs={{0,764},{4,8},{8,4},{12,16},{16,12},{20,24},{24,20},{28,32},{32,28... | collective-permute-start | bytes 49160 | tf_op jit(solution)/shard_map/ppermute | solution.py:780
  105.5 1.9 %collective-permute-start.13 = (f32[1,32,128]{2,1,0:T(8,128)S(1)}, f32[1,32,128]{2,1,0:T(8,128)S(1)}, u32[]{:S(2)}, u32[]{:S(2)}) collective-permute-start(f32[1,32,128]{2,1,0:T(8,128)S(1)} %get-tuple-element.103), channel_id=1, source_target_pairs={{0,4},{4,0},{8,12},{12,8},{16,20},{20,16},{24,28},{28,24},{32,36},... | collective-permute-start | bytes 49160 | tf_op jit(solution)/shard_map/ppermute | solution.py:787
  107.5 0.5 shard_map.90.kv_in
  107.9 2.2 %collective-permute-done.12.h0 = f32[1,32,128]{2,1,0:T(8,128)S(1)} collective-permute-done((f32[1,32,128]{2,1,0:T(8,128)S(1)}, f32[1,32,128]{2,1,0:T(8,128)S(1)}, u32[]{:S(2)}, u32[]{:S(2)}) %collective-permute-start.12) | collective-permute-done | bytes 16416 | tf_op jit(solution)/shard_map/ppermute | solution.py:780
  110.2 0.1 collective-permute-done.13.h1
  110.3 1.3 shard_map.91
  111.6 6.2 %all-to-all-start = ((f32[64,1,128]{2,1,0:T(1,128)}), f32[64,1,128]{2,1,0:T(1,128)S(1)}, u32[]{:S(2)}, u32[]{:S(2)}) async-start(f32[64,1,128]{2,1,0:T(1,128)} %bitcast.5), calls=%async_computation | async-start | bytes 65536 | tf_op jit(solution)/shard_map/all_to_all | solution.py:900
  117.9 8.2 %collective-permute-start.14 = (f32[1,32,128]{2,1,0:T(8,128)S(1)}, f32[1,32,128]{2,1,0:T(8,128)S(1)}, u32[]{:S(2)}, u32[]{:S(2)}) collective-permute-start(f32[1,32,128]{2,1,0:T(8,128)S(1)} %get-tuple-element.111), channel_id=1, source_target_pairs={{0,764},{4,8},{8,4},{12,16},{16,12},{20,24},{24,20},{28,32},{32,28... | collective-permute-start | bytes 49160 | tf_op jit(solution)/shard_map/ppermute | solution.py:780
  126.1 0.1 copy.11.order_ref
  126.1 0.5 shard_map.92.spread_ref
  126.6 0.5 all-to-all-done
  127.2 0.6 all_to_all.15
  127.8 3.5 %all-to-all-start.1 = ((f32[12,1,128]{2,1,0:T(1,128)}), f32[12,1,128]{2,1,0:T(1,128)S(1)}, u32[]{:S(2)}, u32[]{:S(2)}) async-start(f32[12,1,128]{2,1,0:T(1,128)} %all_to_all.15), calls=%async_computation.1 | async-start | bytes 12288 | tf_op jit(solution)/shard_map/all_to_all | solution.py:903
  131.3 3.3 %all-gather.3 = f32[2,32,128]{2,1,0:T(8,128)S(1)} all-gather(f32[1,32,128]{2,1,0:T(8,128)S(1)} %get-tuple-element.112), channel_id=5, replica_groups={{0,4},{8,12},{16,20},{24,28},{32,36},{40,44},{1,5},{9,13},{17,21},{25,2..., dimensions={0}, use_global_device_ids=true | all-gather | bytes 49152 | tf_op jit(solution)/shard_map/all_gather | solution.py:904
  134.7 6.8 %all-gather.4 = f32[4,16,128]{2,1,0:T(8,128)S(1)} all-gather(f32[1,16,128]{2,1,0:T(8,128)S(1)} %shard_map.93), channel_id=6, replica_groups=mesh['outer'=16,'ring'=12,'narrow'=4] {'narrow'}, dimensions={0}, use_global_device_ids=true | all-gather | bytes 40960 | tf_op jit(solution)/shard_map/all_gather | solution.py:908
  141.5 0.4 shard_map.94.late_ref
  141.9 0.8 shard_map.95
  (21 shorter events, 0.4 us)
Async XLA Ops:
  3.3 27.4 %collective-permute-start = (f32[2,32,128]{2,1,0:T(8,128)S(1)}, f32[2,32,128]{2,1,0:T(8,128)S(1)}, u32[]{:S(2)}, u32[]{:S(2)}) collective-permute-start(f32[2,32,128]{2,1,0:T(8,128)S(1)} %get-tuple-element.60), channel_id=1, source_target_pairs={{0,764},{4,8},{8,4},{12,16},{16,12},{20,24},{24,20},{28,32},{32,28... | collective-permute-start | bytes 98312 | tf_op jit(solution)/shard_map/ppermute | solution.py:780
  23.8 6.9 %collective-permute-start.1 = (f32[2,32,128]{2,1,0:T(8,128)S(1)}, f32[2,32,128]{2,1,0:T(8,128)S(1)}, u32[]{:S(2)}, u32[]{:S(2)}) collective-permute-start(f32[2,32,128]{2,1,0:T(8,128)S(1)} %get-tuple-element.61), channel_id=1, source_target_pairs={{0,4},{4,0},{8,12},{12,8},{16,20},{20,16},{24,28},{28,24},{32,36},... | collective-permute-start | bytes 98312 | tf_op jit(solution)/shard_map/ppermute | solution.py:787
  25.7 12.5 %collective-permute-start.2 = (f32[6,4,16,128]{3,2,1,0:T(8,128)S(1)}, f32[6,4,16,128]{3,2,1,0:T(8,128)S(1)}, u32[]{:S(2)}, u32[]{:S(2)}) collective-permute-start(f32[6,4,16,128]{3,2,1,0:T(8,128)S(1)} %get-tuple-element.63), channel_id=1, source_target_pairs={{0,1},{1,2},{2,3},{3,0},{4,5},{5,6},{6,7},{7,4},{8,9},{9,10},{10,1... | collective-permute-start | bytes 589832 | tf_op jit(solution)/shard_map/ppermute | solution.py:813
  28.8 9.4 %collective-permute-start.3 = (f32[6,4,16,128]{3,2,1,0:T(8,128)S(1)}, f32[6,4,16,128]{3,2,1,0:T(8,128)S(1)}, u32[]{:S(2)}, u32[]{:S(2)}) collective-permute-start(f32[6,4,16,128]{3,2,1,0:T(8,128)S(1)} %get-tuple-element.64), channel_id=1, source_target_pairs={{0,3},{1,0},{2,1},{3,2},{4,7},{5,4},{6,5},{7,6},{8,11},{9,8},{10,9... | collective-permute-start | bytes 589832 | tf_op jit(solution)/shard_map/ppermute | solution.py:814
  30.7 7.5 %copy-start.1 = (bf16[384,256]{1,0:T(8,128)(2,1)S(1)}, bf16[384,256]{1,0:T(8,128)(2,1)}, u32[]{:S(2)}) copy-start(bf16[384,256]{1,0:T(8,128)(2,1)} %constant.8.clone.grad_ref) | copy-start | bytes 589828
  30.8 7.4 %copy-start = (bf16[256,256]{1,0:T(8,128)(2,1)S(1)}, bf16[256,256]{1,0:T(8,128)(2,1)}, u32[]{:S(2)}) copy-start(bf16[256,256]{1,0:T(8,128)(2,1)} %constant.9.clone.diver_ref) | copy-start | bytes 393220
  39.1 10.2 %collective-permute-start.4 = (f32[1,32,128]{2,1,0:T(8,128)S(1)}, f32[1,32,128]{2,1,0:T(8,128)S(1)}, u32[]{:S(2)}, u32[]{:S(2)}) collective-permute-start(f32[1,32,128]{2,1,0:T(8,128)S(1)} %get-tuple-element.68), channel_id=1, source_target_pairs={{0,764},{4,8},{8,4},{12,16},{16,12},{20,24},{24,20},{28,32},{32,28... | collective-permute-start | bytes 49160 | tf_op jit(solution)/shard_map/ppermute | solution.py:780
  42.6 6.6 %collective-permute-start.5 = (f32[1,32,128]{2,1,0:T(8,128)S(1)}, f32[1,32,128]{2,1,0:T(8,128)S(1)}, u32[]{:S(2)}, u32[]{:S(2)}) collective-permute-start(f32[1,32,128]{2,1,0:T(8,128)S(1)} %get-tuple-element.69), channel_id=1, source_target_pairs={{0,4},{4,0},{8,12},{12,8},{16,20},{20,16},{24,28},{28,24},{32,36},... | collective-permute-start | bytes 49160 | tf_op jit(solution)/shard_map/ppermute | solution.py:787
  49.9 10.2 %collective-permute-start.6 = (f32[1,32,128]{2,1,0:T(8,128)S(1)}, f32[1,32,128]{2,1,0:T(8,128)S(1)}, u32[]{:S(2)}, u32[]{:S(2)}) collective-permute-start(f32[1,32,128]{2,1,0:T(8,128)S(1)} %get-tuple-element.77), channel_id=1, source_target_pairs={{0,764},{4,8},{8,4},{12,16},{16,12},{20,24},{24,20},{28,32},{32,28... | collective-permute-start | bytes 49160 | tf_op jit(solution)/shard_map/ppermute | solution.py:780
  55.1 4.9 %collective-permute-start.7 = (f32[1,32,128]{2,1,0:T(8,128)S(1)}, f32[1,32,128]{2,1,0:T(8,128)S(1)}, u32[]{:S(2)}, u32[]{:S(2)}) collective-permute-start(f32[1,32,128]{2,1,0:T(8,128)S(1)} %get-tuple-element.78), channel_id=1, source_target_pairs={{0,4},{4,0},{8,12},{12,8},{16,20},{20,16},{24,28},{28,24},{32,36},... | collective-permute-start | bytes 49160 | tf_op jit(solution)/shard_map/ppermute | solution.py:787
  69.3 10.2 %collective-permute-start.8 = (f32[1,32,128]{2,1,0:T(8,128)S(1)}, f32[1,32,128]{2,1,0:T(8,128)S(1)}, u32[]{:S(2)}, u32[]{:S(2)}) collective-permute-start(f32[1,32,128]{2,1,0:T(8,128)S(1)} %get-tuple-element.88), channel_id=1, source_target_pairs={{0,764},{4,8},{8,4},{12,16},{16,12},{20,24},{24,20},{28,32},{32,28... | collective-permute-start | bytes 49160 | tf_op jit(solution)/shard_map/ppermute | solution.py:780
  75.3 4.8 %collective-permute-start.9 = (f32[1,32,128]{2,1,0:T(8,128)S(1)}, f32[1,32,128]{2,1,0:T(8,128)S(1)}, u32[]{:S(2)}, u32[]{:S(2)}) collective-permute-start(f32[1,32,128]{2,1,0:T(8,128)S(1)} %get-tuple-element.89), channel_id=1, source_target_pairs={{0,4},{4,0},{8,12},{12,8},{16,20},{20,16},{24,28},{28,24},{32,36},... | collective-permute-start | bytes 49160 | tf_op jit(solution)/shard_map/ppermute | solution.py:787
  80.7 10.3 %collective-permute-start.10 = (f32[1,32,128]{2,1,0:T(8,128)S(1)}, f32[1,32,128]{2,1,0:T(8,128)S(1)}, u32[]{:S(2)}, u32[]{:S(2)}) collective-permute-start(f32[1,32,128]{2,1,0:T(8,128)S(1)} %get-tuple-element.94), channel_id=1, source_target_pairs={{0,764},{4,8},{8,4},{12,16},{16,12},{20,24},{24,20},{28,32},{32,28... | collective-permute-start | bytes 49160 | tf_op jit(solution)/shard_map/ppermute | solution.py:780
  86.1 4.9 %collective-permute-start.11 = (f32[1,32,128]{2,1,0:T(8,128)S(1)}, f32[1,32,128]{2,1,0:T(8,128)S(1)}, u32[]{:S(2)}, u32[]{:S(2)}) collective-permute-start(f32[1,32,128]{2,1,0:T(8,128)S(1)} %get-tuple-element.95), channel_id=1, source_target_pairs={{0,4},{4,0},{8,12},{12,8},{16,20},{20,16},{24,28},{28,24},{32,36},... | collective-permute-start | bytes 49160 | tf_op jit(solution)/shard_map/ppermute | solution.py:787
  100.0 10.2 %collective-permute-start.12 = (f32[1,32,128]{2,1,0:T(8,128)S(1)}, f32[1,32,128]{2,1,0:T(8,128)S(1)}, u32[]{:S(2)}, u32[]{:S(2)}) collective-permute-start(f32[1,32,128]{2,1,0:T(8,128)S(1)} %get-tuple-element.102), channel_id=1, source_target_pairs={{0,764},{4,8},{8,4},{12,16},{16,12},{20,24},{24,20},{28,32},{32,28... | collective-permute-start | bytes 49160 | tf_op jit(solution)/shard_map/ppermute | solution.py:780
  105.5 4.8 %collective-permute-start.13 = (f32[1,32,128]{2,1,0:T(8,128)S(1)}, f32[1,32,128]{2,1,0:T(8,128)S(1)}, u32[]{:S(2)}, u32[]{:S(2)}) collective-permute-start(f32[1,32,128]{2,1,0:T(8,128)S(1)} %get-tuple-element.103), channel_id=1, source_target_pairs={{0,4},{4,0},{8,12},{12,8},{16,20},{20,16},{24,28},{28,24},{32,36},... | collective-permute-start | bytes 49160 | tf_op jit(solution)/shard_map/ppermute | solution.py:787
  111.6 15.5 %all-to-all-start = ((f32[64,1,128]{2,1,0:T(1,128)}), f32[64,1,128]{2,1,0:T(1,128)S(1)}, u32[]{:S(2)}, u32[]{:S(2)}) async-start(f32[64,1,128]{2,1,0:T(1,128)} %bitcast.5), calls=%async_computation | async-start | bytes 65536 | tf_op jit(solution)/shard_map/all_to_all | solution.py:900
  117.9 8.2 %copy-start.2 = (s32[1,1,64]{2,1,0:T(1,128)S(1)}, s32[1,1,64]{2,1,0:T(1,128)}, u32[]{:S(2)}) copy-start(s32[1,1,64]{2,1,0:T(1,128)} %param.8) | copy-start | bytes 772
  117.9 16.7 %collective-permute-start.14 = (f32[1,32,128]{2,1,0:T(8,128)S(1)}, f32[1,32,128]{2,1,0:T(8,128)S(1)}, u32[]{:S(2)}, u32[]{:S(2)}) collective-permute-start(f32[1,32,128]{2,1,0:T(8,128)S(1)} %get-tuple-element.111), channel_id=1, source_target_pairs={{0,764},{4,8},{8,4},{12,16},{16,12},{20,24},{24,20},{28,32},{32,28... | collective-permute-start | bytes 49160 | tf_op jit(solution)/shard_map/ppermute | solution.py:780
  127.8 14.1 %all-to-all-start.1 = ((f32[12,1,128]{2,1,0:T(1,128)}), f32[12,1,128]{2,1,0:T(1,128)S(1)}, u32[]{:S(2)}, u32[]{:S(2)}) async-start(f32[12,1,128]{2,1,0:T(1,128)} %all_to_all.15), calls=%async_computation.1 | async-start | bytes 12288 | tf_op jit(solution)/shard_map/all_to_all | solution.py:903

commit v8 on v7

--- a/solution.py
+++ b/solution.py
@@ -670,8 +670,8 @@
 
 def sixth_kernel(
     kv_in, h0, h1, source_ref, inverse_ref, start_ref, residual_ref, early_ref,
-    metric_ref, grad_ref, diver_ref,
-    result_ref, kv_ref, far_ref, near_ref, pack_ref, sums_hbm, flux_ref, work_ref, sums_ref, sem,
+    metric_ref, grad_ref,
+    result_ref, flux_ref, part_ref, sums_hbm, sums_ref, sem,
 ):
     image = completed(kv_in, (h0, h1))
     plane = weight_plane()
@@ -683,16 +683,19 @@
         r_y = r_y + residual_ref[i] * result * node_weight(i)
         w_y = w_y + source_ref[i] * result * node_weight(i)
     energy = apply_flux(
-        result_ref, metric_ref, None, grad_ref, flux_ref, work_ref, with_energy=True
+        result_ref, metric_ref, None, grad_ref, flux_ref, part_ref, with_energy=True
     )
     zero = jnp.zeros((1, LANES), jnp.float32)
     late = sum_row([zero, zero, r_y * plane, w_y * plane, energy])
     sums_ref[...] = jnp.broadcast_to(early_ref[...] + late, sums_ref.shape)
     leave = pltpu.make_async_copy(sums_ref, sums_hbm, sem)
     leave.start()
-    planes = whole_planes(flux_ref, work_ref, diver_ref, range(NODES))
+    leave.wait()
+
+
+def rest_faces_kernel(flux_ref, part_ref, diver_ref, kv_ref, far_ref, near_ref, pack_ref):
+    planes = whole_planes(flux_ref, part_ref, diver_ref, range(NODES))
     store_assembled(kv_ref, far_ref, near_ref, is_even(), lambda i: planes[i], 0, pack_ref)
-    leave.wait()
 
 
 def spread_fields(order_ref, fields, out_ref, spread_ref):
@@ -883,21 +886,23 @@
     (kv,) = call(rest_kernel, [FIELD], [], *parts, diver)
     halo = swap_wide(far, near)
     sums_shape = (lax.axis_size(REST), LANES)
-    second, kv, *face, sums = call(
+    second, *parts, sums = call(
         sixth_kernel,
-        [FIELD, FIELD] + faces() + packs() + [sums_shape],
-        [FLUX, FIELD, sums_shape, pltpu.SemaphoreType.DMA(())],
-        kv, *halo, image, inverse, start, residual, early, metric, grad, diver,
-        out_spaces=[pltpu.VMEM] * 5 + [pltpu.HBM],
+        [FIELD, FLUX, FIELD, sums_shape],
+        [sums_shape, pltpu.SemaphoreType.DMA(())],
+        kv, *halo, image, inverse, start, residual, early, metric, grad,
+        out_spaces=[pltpu.VMEM] * 3 + [pltpu.HBM],
+    )
+    sums = lax.all_to_all(sums, REST, 0, 0)
+    kv, far, near, pack = call(
+        rest_faces_kernel, [FIELD] + faces() + packs(), [], *parts, diver
     )
     order = element_order.reshape(64, 1)
     (spread,) = call(
         spread_early_kernel, [(4, 64, 512)], [(64, 512)], order, first, second, residual, image
     )
-    far, near, pack = face
     far = swap_far(far)
     ring = lax.axis_size("ring")
-    sums = lax.all_to_all(sums, REST, 0, 0)
     sums = jnp.broadcast_to(jnp.sum(sums, axis=0, keepdims=True), (ring, LANES))
     near, sums = lax.optimization_barrier((near, sums))
     sums = lax.all_to_all(sums, "ring", 0, 0)

time: 143 us -> 143 us (level)
    pallas_call x19 -> x20, Pallas kernels: 11.9 us -> 12.2 us  [call(): pl.pallas_call(kernel, out_shape=[jax.ShapeDtypeStruct(s, F32) for s in o...]
  transfers between devices with their start and end apart: 17 -> 17, of which waited for: 8 -> 7; matrix products, arithmetic and copies ran while one was open for 0% -> 0% of each run, Pallas kernels for 2% -> 3%
where the time goes in v8:
time: 143 us
  starting transfers between devices  80.9 us (57%)
  blocking collectives  33.7 us (24%)
  waiting for transfers between devices  14 us (10%)
  Pallas kernels  12.2 us (9%)
    ppermute x7, starting transfers between devices, swap_far(): lax.ppermute(far, WIDE, [(w, (w + 1 if w % 2 else w - 1) % count) for w i...  54.7 us
    all_gather x2, blocking collectives, swap_edged(): return (far, near, lax.all_gather(pack, 'narrow'))  16.3 us
    ppermute x7, waiting for transfers between devices, swap_far(): lax.ppermute(far, WIDE, [(w, (w + 1 if w % 2 else w - 1) % count) for w i...  13.2 us
    pallas_call x20, Pallas kernels, call(): pl.pallas_call(kernel, out_shape=[jax.ShapeDtypeStruct(s, F32) for s in o...  12.2 us
    ppermute x6, starting transfers between devices, swap_wide(): lax.ppermute(near, WIDE, [(w, w ^ 1) for w in range(count)])  11.6 us
    all_gather x1, blocking collectives, swap_all(): return (far, near, lax.all_gather(pack, 'narrow'))  7.34 us
    all_gather x1, blocking collectives, local(): halo = (far, near, lax.all_gather(pack, 'narrow'))  6.8 us
    all_to_all x1, starting transfers between devices, local(): sums = lax.all_to_all(sums, REST, 0, 0)  6.22 us
  transfers between devices with their start and end apart: 17, of which 7 were waited for; matrix products, arithmetic and copies ran while one was open for 0% of the time, Pallas kernels for 3%

profile of v8, /device:TPU:1, one launch (start us, length us, event | category | flops | bytes accessed | tf_op | source)
XLA Modules:
  0.0 142.6 jit_solution(4360845269025627309)
XLA Ops:
  0.6 2.6 %shard_map.77 = (f32[7,8,32,128]{3,2,1,0:T(8,128)S(1)}, f32[8,32,128]{2,1,0:T(8,128)S(1)}, f32[8,32,128]{2,1,0:T(8,128)S(1)}, f32[2,32,128]{2,1,0:T(8,128)S(1)},...) custom-call(s32[1,64]{1,0:T(1,128)} %bitcast.20, ...), custom_call_target="tpu_custom_call" | custom-call | tf_op jit(solution)/shard_map/pallas_call | solution.py:757
  3.3 20.5 %collective-permute-start = (f32[2,32,128]{2,1,0:T(8,128)S(1)}, f32[2,32,128]{2,1,0:T(8,128)S(1)}, u32[]{:S(2)}, u32[]{:S(2)}) collective-permute-start(f32[2,32,128]{2,1,0:T(8,128)S(1)} %get-tuple-element.62), channel_id=1, source_target_pairs={{0,764},{4,8},{8,4},{12,16},{16,12},{20,24},{24,20},{28,32},{32,28... | collective-permute-start | bytes 98312 | tf_op jit(solution)/shard_map/ppermute | solution.py:783
  23.8 1.9 %collective-permute-start.1 = (f32[2,32,128]{2,1,0:T(8,128)S(1)}, f32[2,32,128]{2,1,0:T(8,128)S(1)}, u32[]{:S(2)}, u32[]{:S(2)}) collective-permute-start(f32[2,32,128]{2,1,0:T(8,128)S(1)} %get-tuple-element.63), channel_id=1, source_target_pairs={{0,4},{4,0},{8,12},{12,8},{16,20},{20,16},{24,28},{28,24},{32,36},... | collective-permute-start | bytes 98312 | tf_op jit(solution)/shard_map/ppermute | solution.py:790
  25.7 3.1 %collective-permute-start.2 = (f32[6,4,16,128]{3,2,1,0:T(8,128)S(1)}, f32[6,4,16,128]{3,2,1,0:T(8,128)S(1)}, u32[]{:S(2)}, u32[]{:S(2)}) collective-permute-start(f32[6,4,16,128]{3,2,1,0:T(8,128)S(1)} %get-tuple-element.65), channel_id=1, source_target_pairs={{0,1},{1,2},{2,3},{3,0},{4,5},{5,6},{6,7},{7,4},{8,9},{9,10},{10,1... | collective-permute-start | bytes 589832 | tf_op jit(solution)/shard_map/ppermute | solution.py:816
  28.8 1.9 %collective-permute-start.3 = (f32[6,4,16,128]{3,2,1,0:T(8,128)S(1)}, f32[6,4,16,128]{3,2,1,0:T(8,128)S(1)}, u32[]{:S(2)}, u32[]{:S(2)}) collective-permute-start(f32[6,4,16,128]{3,2,1,0:T(8,128)S(1)} %get-tuple-element.66), channel_id=1, source_target_pairs={{0,3},{1,0},{2,1},{3,2},{4,7},{5,4},{6,5},{7,6},{8,11},{9,8},{10,9... | collective-permute-start | bytes 589832 | tf_op jit(solution)/shard_map/ppermute | solution.py:817
  30.7 0.1 shard_map.78
  30.8 7.3 %all-gather = f32[8,48,128]{2,1,0:T(8,128)S(1)} all-gather(f32[2,48,128]{2,1,0:T(8,128)S(1)} %shard_map.78), channel_id=2, replica_groups=mesh['outer'=16,'ring'=12,'narrow'=4] {'narrow'}, dimensions={0}, use_global_device_ids=true | all-gather | bytes 245760 | tf_op jit(solution)/shard_map/all_gather | solution.py:796
  38.2 0.8 shard_map.79
  39.1 3.6 %collective-permute-start.4 = (f32[1,32,128]{2,1,0:T(8,128)S(1)}, f32[1,32,128]{2,1,0:T(8,128)S(1)}, u32[]{:S(2)}, u32[]{:S(2)}) collective-permute-start(f32[1,32,128]{2,1,0:T(8,128)S(1)} %get-tuple-element.70), channel_id=1, source_target_pairs={{0,764},{4,8},{8,4},{12,16},{16,12},{20,24},{24,20},{28,32},{32,28... | collective-permute-start | bytes 49160 | tf_op jit(solution)/shard_map/ppermute | solution.py:783
  42.6 2.0 %collective-permute-start.5 = (f32[1,32,128]{2,1,0:T(8,128)S(1)}, f32[1,32,128]{2,1,0:T(8,128)S(1)}, u32[]{:S(2)}, u32[]{:S(2)}) collective-permute-start(f32[1,32,128]{2,1,0:T(8,128)S(1)} %get-tuple-element.71), channel_id=1, source_target_pairs={{0,4},{4,0},{8,12},{12,8},{16,20},{20,16},{24,28},{28,24},{32,36},... | collective-permute-start | bytes 49160 | tf_op jit(solution)/shard_map/ppermute | solution.py:790
  44.6 0.4 shard_map.80.kv_in
  45.1 4.2 %collective-permute-done.4.h0 = f32[1,32,128]{2,1,0:T(8,128)S(1)} collective-permute-done((f32[1,32,128]{2,1,0:T(8,128)S(1)}, f32[1,32,128]{2,1,0:T(8,128)S(1)}, u32[]{:S(2)}, u32[]{:S(2)}) %collective-permute-start.4) | collective-permute-done | bytes 16416 | tf_op jit(solution)/shard_map/ppermute | solution.py:783
  49.3 0.6 shard_map.81
  49.9 5.3 %collective-permute-start.6 = (f32[1,32,128]{2,1,0:T(8,128)S(1)}, f32[1,32,128]{2,1,0:T(8,128)S(1)}, u32[]{:S(2)}, u32[]{:S(2)}) collective-permute-start(f32[1,32,128]{2,1,0:T(8,128)S(1)} %get-tuple-element.79), channel_id=1, source_target_pairs={{0,764},{4,8},{8,4},{12,16},{16,12},{20,24},{24,20},{28,32},{32,28... | collective-permute-start | bytes 49160 | tf_op jit(solution)/shard_map/ppermute | solution.py:783
  55.1 1.9 %collective-permute-start.7 = (f32[1,32,128]{2,1,0:T(8,128)S(1)}, f32[1,32,128]{2,1,0:T(8,128)S(1)}, u32[]{:S(2)}, u32[]{:S(2)}) collective-permute-start(f32[1,32,128]{2,1,0:T(8,128)S(1)} %get-tuple-element.80), channel_id=1, source_target_pairs={{0,4},{4,0},{8,12},{12,8},{16,20},{20,16},{24,28},{28,24},{32,36},... | collective-permute-start | bytes 49160 | tf_op jit(solution)/shard_map/ppermute | solution.py:790
  57.1 0.4 shard_map.82
  57.5 2.5 %collective-permute-done.6.far_ref.h0 = f32[1,32,128]{2,1,0:T(8,128)S(1)} collective-permute-done((f32[1,32,128]{2,1,0:T(8,128)S(1)}, f32[1,32,128]{2,1,0:T(8,128)S(1)}, u32[]{:S(2)}, u32[]{:S(2)}) %collective-permute-start.6) | collective-permute-done | bytes 16416 | tf_op jit(solution)/shard_map/ppermute | solution.py:783
  60.2 8.3 %all-gather.1 = f32[4,144,128]{2,1,0:T(8,128)S(1)} all-gather(f32[1,144,128]{2,1,0:T(8,128)S(1)} %shard_map.83), channel_id=3, replica_groups=mesh['outer'=16,'ring'=12,'narrow'=4] {'narrow'}, dimensions={0}, use_global_device_ids=true | all-gather | bytes 368640 | tf_op jit(solution)/shard_map/all_gather | solution.py:811
  68.4 0.8 shard_map.84
  69.3 6.0 %collective-permute-start.8 = (f32[1,32,128]{2,1,0:T(8,128)S(1)}, f32[1,32,128]{2,1,0:T(8,128)S(1)}, u32[]{:S(2)}, u32[]{:S(2)}) collective-permute-start(f32[1,32,128]{2,1,0:T(8,128)S(1)} %get-tuple-element.90), channel_id=1, source_target_pairs={{0,764},{4,8},{8,4},{12,16},{16,12},{20,24},{24,20},{28,32},{32,28... | collective-permute-start | bytes 49160 | tf_op jit(solution)/shard_map/ppermute | solution.py:783
  75.3 1.9 %collective-permute-start.9 = (f32[1,32,128]{2,1,0:T(8,128)S(1)}, f32[1,32,128]{2,1,0:T(8,128)S(1)}, u32[]{:S(2)}, u32[]{:S(2)}) collective-permute-start(f32[1,32,128]{2,1,0:T(8,128)S(1)} %get-tuple-element.91), channel_id=1, source_target_pairs={{0,4},{4,0},{8,12},{12,8},{16,20},{20,16},{24,28},{28,24},{32,36},... | collective-permute-start | bytes 49160 | tf_op jit(solution)/shard_map/ppermute | solution.py:790
  77.2 0.5 shard_map.85
  77.7 1.8 %collective-permute-done.8.h0 = f32[1,32,128]{2,1,0:T(8,128)S(1)} collective-permute-done((f32[1,32,128]{2,1,0:T(8,128)S(1)}, f32[1,32,128]{2,1,0:T(8,128)S(1)}, u32[]{:S(2)}, u32[]{:S(2)}) %collective-permute-start.8) | collective-permute-done | bytes 16416 | tf_op jit(solution)/shard_map/ppermute | solution.py:783
  79.5 0.6 collective-permute-done.9.h1
  80.1 0.6 shard_map.86
  80.7 5.4 %collective-permute-start.10 = (f32[1,32,128]{2,1,0:T(8,128)S(1)}, f32[1,32,128]{2,1,0:T(8,128)S(1)}, u32[]{:S(2)}, u32[]{:S(2)}) collective-permute-start(f32[1,32,128]{2,1,0:T(8,128)S(1)} %get-tuple-element.96), channel_id=1, source_target_pairs={{0,764},{4,8},{8,4},{12,16},{16,12},{20,24},{24,20},{28,32},{32,28... | collective-permute-start | bytes 49160 | tf_op jit(solution)/shard_map/ppermute | solution.py:783
  86.1 1.9 %collective-permute-start.11 = (f32[1,32,128]{2,1,0:T(8,128)S(1)}, f32[1,32,128]{2,1,0:T(8,128)S(1)}, u32[]{:S(2)}, u32[]{:S(2)}) collective-permute-start(f32[1,32,128]{2,1,0:T(8,128)S(1)} %get-tuple-element.97), channel_id=1, source_target_pairs={{0,4},{4,0},{8,12},{12,8},{16,20},{20,16},{24,28},{28,24},{32,36},... | collective-permute-start | bytes 49160 | tf_op jit(solution)/shard_map/ppermute | solution.py:790
  88.0 0.4 shard_map.87
  88.5 2.5 %collective-permute-done.10.far_ref.h0 = f32[1,32,128]{2,1,0:T(8,128)S(1)} collective-permute-done((f32[1,32,128]{2,1,0:T(8,128)S(1)}, f32[1,32,128]{2,1,0:T(8,128)S(1)}, u32[]{:S(2)}, u32[]{:S(2)}) %collective-permute-start.10) | collective-permute-done | bytes 16416 | tf_op jit(solution)/shard_map/ppermute | solution.py:783
  91.1 8.0 %all-gather.2 = f32[4,144,128]{2,1,0:T(8,128)S(1)} all-gather(f32[1,144,128]{2,1,0:T(8,128)S(1)} %shard_map.88), channel_id=4, replica_groups=mesh['outer'=16,'ring'=12,'narrow'=4] {'narrow'}, dimensions={0}, use_global_device_ids=true | all-gather | bytes 368640 | tf_op jit(solution)/shard_map/all_gather | solution.py:811
  99.1 0.8 shard_map.89
  100.0 5.6 %collective-permute-start.12 = (f32[1,32,128]{2,1,0:T(8,128)S(1)}, f32[1,32,128]{2,1,0:T(8,128)S(1)}, u32[]{:S(2)}, u32[]{:S(2)}) collective-permute-start(f32[1,32,128]{2,1,0:T(8,128)S(1)} %get-tuple-element.104), channel_id=1, source_target_pairs={{0,764},{4,8},{8,4},{12,16},{16,12},{20,24},{24,20},{28,32},{32,28... | collective-permute-start | bytes 49160 | tf_op jit(solution)/shard_map/ppermute | solution.py:783
  105.5 1.9 %collective-permute-start.13 = (f32[1,32,128]{2,1,0:T(8,128)S(1)}, f32[1,32,128]{2,1,0:T(8,128)S(1)}, u32[]{:S(2)}, u32[]{:S(2)}) collective-permute-start(f32[1,32,128]{2,1,0:T(8,128)S(1)} %get-tuple-element.105), channel_id=1, source_target_pairs={{0,4},{4,0},{8,12},{12,8},{16,20},{20,16},{24,28},{28,24},{32,36},... | collective-permute-start | bytes 49160 | tf_op jit(solution)/shard_map/ppermute | solution.py:790
  107.5 0.5 shard_map.90.kv_in
  107.9 2.2 %collective-permute-done.12.h0 = f32[1,32,128]{2,1,0:T(8,128)S(1)} collective-permute-done((f32[1,32,128]{2,1,0:T(8,128)S(1)}, f32[1,32,128]{2,1,0:T(8,128)S(1)}, u32[]{:S(2)}, u32[]{:S(2)}) %collective-permute-start.12) | collective-permute-done | bytes 16416 | tf_op jit(solution)/shard_map/ppermute | solution.py:783
  110.2 0.1 collective-permute-done.13.h1
  110.3 1.1 shard_map.91
  111.4 6.2 %all-to-all-start = ((f32[64,1,128]{2,1,0:T(1,128)}), f32[64,1,128]{2,1,0:T(1,128)S(1)}, u32[]{:S(2)}, u32[]{:S(2)}) async-start(f32[64,1,128]{2,1,0:T(1,128)} %bitcast.5), calls=%async_computation | async-start | bytes 65536 | tf_op jit(solution)/shard_map/all_to_all | solution.py:896
  117.6 0.4 shard_map.92
  118.1 8.3 %collective-permute-start.14 = (f32[1,32,128]{2,1,0:T(8,128)S(1)}, f32[1,32,128]{2,1,0:T(8,128)S(1)}, u32[]{:S(2)}, u32[]{:S(2)}) collective-permute-start(f32[1,32,128]{2,1,0:T(8,128)S(1)} %get-tuple-element.115), channel_id=1, source_target_pairs={{0,764},{4,8},{8,4},{12,16},{16,12},{20,24},{24,20},{28,32},{32,28... | collective-permute-start | bytes 49160 | tf_op jit(solution)/shard_map/ppermute | solution.py:783
  126.4 0.1 copy.11.order_ref
  126.5 0.4 shard_map.93.spread_ref
  127.0 0.6 all_to_all.15
  127.6 3.5 %all-to-all-start.1 = ((f32[12,1,128]{2,1,0:T(1,128)}), f32[12,1,128]{2,1,0:T(1,128)S(1)}, u32[]{:S(2)}, u32[]{:S(2)}) async-start(f32[12,1,128]{2,1,0:T(1,128)} %all_to_all.15), calls=%async_computation.1 | async-start | bytes 12288 | tf_op jit(solution)/shard_map/all_to_all | solution.py:908
  131.1 3.3 %all-gather.3 = f32[2,32,128]{2,1,0:T(8,128)S(1)} all-gather(f32[1,32,128]{2,1,0:T(8,128)S(1)} %get-tuple-element.116), channel_id=5, replica_groups={{0,4},{8,12},{16,20},{24,28},{32,36},{40,44},{1,5},{9,13},{17,21},{25,2..., dimensions={0}, use_global_device_ids=true | all-gather | bytes 49152 | tf_op jit(solution)/shard_map/all_gather | solution.py:909
  134.5 6.8 %all-gather.4 = f32[4,16,128]{2,1,0:T(8,128)S(1)} all-gather(f32[1,16,128]{2,1,0:T(8,128)S(1)} %shard_map.94), channel_id=6, replica_groups=mesh['outer'=16,'ring'=12,'narrow'=4] {'narrow'}, dimensions={0}, use_global_device_ids=true | all-gather | bytes 40960 | tf_op jit(solution)/shard_map/all_gather | solution.py:913
  141.3 0.4 shard_map.95.late_ref
  141.7 0.8 shard_map.96
  (22 shorter events, 0.4 us)
Async XLA Ops:
  3.3 27.4 %collective-permute-start = (f32[2,32,128]{2,1,0:T(8,128)S(1)}, f32[2,32,128]{2,1,0:T(8,128)S(1)}, u32[]{:S(2)}, u32[]{:S(2)}) collective-permute-start(f32[2,32,128]{2,1,0:T(8,128)S(1)} %get-tuple-element.62), channel_id=1, source_target_pairs={{0,764},{4,8},{8,4},{12,16},{16,12},{20,24},{24,20},{28,32},{32,28... | collective-permute-start | bytes 98312 | tf_op jit(solution)/shard_map/ppermute | solution.py:783
  23.8 6.9 %collective-permute-start.1 = (f32[2,32,128]{2,1,0:T(8,128)S(1)}, f32[2,32,128]{2,1,0:T(8,128)S(1)}, u32[]{:S(2)}, u32[]{:S(2)}) collective-permute-start(f32[2,32,128]{2,1,0:T(8,128)S(1)} %get-tuple-element.63), channel_id=1, source_target_pairs={{0,4},{4,0},{8,12},{12,8},{16,20},{20,16},{24,28},{28,24},{32,36},... | collective-permute-start | bytes 98312 | tf_op jit(solution)/shard_map/ppermute | solution.py:790
  25.7 12.5 %collective-permute-start.2 = (f32[6,4,16,128]{3,2,1,0:T(8,128)S(1)}, f32[6,4,16,128]{3,2,1,0:T(8,128)S(1)}, u32[]{:S(2)}, u32[]{:S(2)}) collective-permute-start(f32[6,4,16,128]{3,2,1,0:T(8,128)S(1)} %get-tuple-element.65), channel_id=1, source_target_pairs={{0,1},{1,2},{2,3},{3,0},{4,5},{5,6},{6,7},{7,4},{8,9},{9,10},{10,1... | collective-permute-start | bytes 589832 | tf_op jit(solution)/shard_map/ppermute | solution.py:816
  28.8 9.4 %collective-permute-start.3 = (f32[6,4,16,128]{3,2,1,0:T(8,128)S(1)}, f32[6,4,16,128]{3,2,1,0:T(8,128)S(1)}, u32[]{:S(2)}, u32[]{:S(2)}) collective-permute-start(f32[6,4,16,128]{3,2,1,0:T(8,128)S(1)} %get-tuple-element.66), channel_id=1, source_target_pairs={{0,3},{1,0},{2,1},{3,2},{4,7},{5,4},{6,5},{7,6},{8,11},{9,8},{10,9... | collective-permute-start | bytes 589832 | tf_op jit(solution)/shard_map/ppermute | solution.py:817
  30.7 7.5 %copy-start.1 = (bf16[384,256]{1,0:T(8,128)(2,1)S(1)}, bf16[384,256]{1,0:T(8,128)(2,1)}, u32[]{:S(2)}) copy-start(bf16[384,256]{1,0:T(8,128)(2,1)} %constant.8.clone.grad_ref) | copy-start | bytes 589828
  30.8 7.4 %copy-start = (bf16[256,256]{1,0:T(8,128)(2,1)S(1)}, bf16[256,256]{1,0:T(8,128)(2,1)}, u32[]{:S(2)}) copy-start(bf16[256,256]{1,0:T(8,128)(2,1)} %constant.9.clone.diver_ref) | copy-start | bytes 393220
  39.1 10.2 %collective-permute-start.4 = (f32[1,32,128]{2,1,0:T(8,128)S(1)}, f32[1,32,128]{2,1,0:T(8,128)S(1)}, u32[]{:S(2)}, u32[]{:S(2)}) collective-permute-start(f32[1,32,128]{2,1,0:T(8,128)S(1)} %get-tuple-element.70), channel_id=1, source_target_pairs={{0,764},{4,8},{8,4},{12,16},{16,12},{20,24},{24,20},{28,32},{32,28... | collective-permute-start | bytes 49160 | tf_op jit(solution)/shard_map/ppermute | solution.py:783
  42.6 6.6 %collective-permute-start.5 = (f32[1,32,128]{2,1,0:T(8,128)S(1)}, f32[1,32,128]{2,1,0:T(8,128)S(1)}, u32[]{:S(2)}, u32[]{:S(2)}) collective-permute-start(f32[1,32,128]{2,1,0:T(8,128)S(1)} %get-tuple-element.71), channel_id=1, source_target_pairs={{0,4},{4,0},{8,12},{12,8},{16,20},{20,16},{24,28},{28,24},{32,36},... | collective-permute-start | bytes 49160 | tf_op jit(solution)/shard_map/ppermute | solution.py:790
  49.9 10.2 %collective-permute-start.6 = (f32[1,32,128]{2,1,0:T(8,128)S(1)}, f32[1,32,128]{2,1,0:T(8,128)S(1)}, u32[]{:S(2)}, u32[]{:S(2)}) collective-permute-start(f32[1,32,128]{2,1,0:T(8,128)S(1)} %get-tuple-element.79), channel_id=1, source_target_pairs={{0,764},{4,8},{8,4},{12,16},{16,12},{20,24},{24,20},{28,32},{32,28... | collective-permute-start | bytes 49160 | tf_op jit(solution)/shard_map/ppermute | solution.py:783
  55.1 4.9 %collective-permute-start.7 = (f32[1,32,128]{2,1,0:T(8,128)S(1)}, f32[1,32,128]{2,1,0:T(8,128)S(1)}, u32[]{:S(2)}, u32[]{:S(2)}) collective-permute-start(f32[1,32,128]{2,1,0:T(8,128)S(1)} %get-tuple-element.80), channel_id=1, source_target_pairs={{0,4},{4,0},{8,12},{12,8},{16,20},{20,16},{24,28},{28,24},{32,36},... | collective-permute-start | bytes 49160 | tf_op jit(solution)/shard_map/ppermute | solution.py:790
  69.3 10.2 %collective-permute-start.8 = (f32[1,32,128]{2,1,0:T(8,128)S(1)}, f32[1,32,128]{2,1,0:T(8,128)S(1)}, u32[]{:S(2)}, u32[]{:S(2)}) collective-permute-start(f32[1,32,128]{2,1,0:T(8,128)S(1)} %get-tuple-element.90), channel_id=1, source_target_pairs={{0,764},{4,8},{8,4},{12,16},{16,12},{20,24},{24,20},{28,32},{32,28... | collective-permute-start | bytes 49160 | tf_op jit(solution)/shard_map/ppermute | solution.py:783
  75.3 4.8 %collective-permute-start.9 = (f32[1,32,128]{2,1,0:T(8,128)S(1)}, f32[1,32,128]{2,1,0:T(8,128)S(1)}, u32[]{:S(2)}, u32[]{:S(2)}) collective-permute-start(f32[1,32,128]{2,1,0:T(8,128)S(1)} %get-tuple-element.91), channel_id=1, source_target_pairs={{0,4},{4,0},{8,12},{12,8},{16,20},{20,16},{24,28},{28,24},{32,36},... | collective-permute-start | bytes 49160 | tf_op jit(solution)/shard_map/ppermute | solution.py:790
  80.7 10.3 %collective-permute-start.10 = (f32[1,32,128]{2,1,0:T(8,128)S(1)}, f32[1,32,128]{2,1,0:T(8,128)S(1)}, u32[]{:S(2)}, u32[]{:S(2)}) collective-permute-start(f32[1,32,128]{2,1,0:T(8,128)S(1)} %get-tuple-element.96), channel_id=1, source_target_pairs={{0,764},{4,8},{8,4},{12,16},{16,12},{20,24},{24,20},{28,32},{32,28... | collective-permute-start | bytes 49160 | tf_op jit(solution)/shard_map/ppermute | solution.py:783
  86.1 4.9 %collective-permute-start.11 = (f32[1,32,128]{2,1,0:T(8,128)S(1)}, f32[1,32,128]{2,1,0:T(8,128)S(1)}, u32[]{:S(2)}, u32[]{:S(2)}) collective-permute-start(f32[1,32,128]{2,1,0:T(8,128)S(1)} %get-tuple-element.97), channel_id=1, source_target_pairs={{0,4},{4,0},{8,12},{12,8},{16,20},{20,16},{24,28},{28,24},{32,36},... | collective-permute-start | bytes 49160 | tf_op jit(solution)/shard_map/ppermute | solution.py:790
  100.0 10.2 %collective-permute-start.12 = (f32[1,32,128]{2,1,0:T(8,128)S(1)}, f32[1,32,128]{2,1,0:T(8,128)S(1)}, u32[]{:S(2)}, u32[]{:S(2)}) collective-permute-start(f32[1,32,128]{2,1,0:T(8,128)S(1)} %get-tuple-element.104), channel_id=1, source_target_pairs={{0,764},{4,8},{8,4},{12,16},{16,12},{20,24},{24,20},{28,32},{32,28... | collective-permute-start | bytes 49160 | tf_op jit(solution)/shard_map/ppermute | solution.py:783
  105.5 4.8 %collective-permute-start.13 = (f32[1,32,128]{2,1,0:T(8,128)S(1)}, f32[1,32,128]{2,1,0:T(8,128)S(1)}, u32[]{:S(2)}, u32[]{:S(2)}) collective-permute-start(f32[1,32,128]{2,1,0:T(8,128)S(1)} %get-tuple-element.105), channel_id=1, source_target_pairs={{0,4},{4,0},{8,12},{12,8},{16,20},{20,16},{24,28},{28,24},{32,36},... | collective-permute-start | bytes 49160 | tf_op jit(solution)/shard_map/ppermute | solution.py:790
  111.4 15.5 %all-to-all-start = ((f32[64,1,128]{2,1,0:T(1,128)}), f32[64,1,128]{2,1,0:T(1,128)S(1)}, u32[]{:S(2)}, u32[]{:S(2)}) async-start(f32[64,1,128]{2,1,0:T(1,128)} %bitcast.5), calls=%async_computation | async-start | bytes 65536 | tf_op jit(solution)/shard_map/all_to_all | solution.py:896
  118.1 8.3 %copy-start.2 = (s32[1,1,64]{2,1,0:T(1,128)S(1)}, s32[1,1,64]{2,1,0:T(1,128)}, u32[]{:S(2)}) copy-start(s32[1,1,64]{2,1,0:T(1,128)} %param.8) | copy-start | bytes 772
  118.1 16.3 %collective-permute-start.14 = (f32[1,32,128]{2,1,0:T(8,128)S(1)}, f32[1,32,128]{2,1,0:T(8,128)S(1)}, u32[]{:S(2)}, u32[]{:S(2)}) collective-permute-start(f32[1,32,128]{2,1,0:T(8,128)S(1)} %get-tuple-element.115), channel_id=1, source_target_pairs={{0,764},{4,8},{8,4},{12,16},{16,12},{20,24},{24,20},{28,32},{32,28... | collective-permute-start | bytes 49160 | tf_op jit(solution)/shard_map/ppermute | solution.py:783
  127.6 14.1 %all-to-all-start.1 = ((f32[12,1,128]{2,1,0:T(1,128)}), f32[12,1,128]{2,1,0:T(1,128)S(1)}, u32[]{:S(2)}, u32[]{:S(2)}) async-start(f32[12,1,128]{2,1,0:T(1,128)} %all_to_all.15), calls=%async_computation.1 | async-start | bytes 12288 | tf_op jit(solution)/shard_map/all_to_all | solution.py:908

commit v9 on v8

--- a/solution.py
+++ b/solution.py
@@ -715,19 +715,24 @@
         out_ref[f] = dot(pick, high) + (dot(pick, middle) + dot(pick, rest))
 
 
-def spread_early_kernel(
-    order_ref, first_ref, second_ref, residual_ref, image_ref, out_ref, spread_ref
-):
-    refs = (first_ref, second_ref, residual_ref, image_ref)
+def spread_early_kernel(order_ref, first_ref, residual_ref, image_ref, out_ref, spread_ref):
+    refs = (first_ref, residual_ref, image_ref)
     spread_fields(order_ref, [lambda i, ref=ref: ref[i] for ref in refs], out_ref, spread_ref)
 
 
-def spread_late_kernel(kv_in, h0, h1, h2, order_ref, out_ref, spread_ref):
-    spread_fields(order_ref, [completed(kv_in, (h0, h1, h2))], out_ref, spread_ref)
+def spread_late_kernel(kv_in, h0, h1, h2, second_ref, order_ref, out_ref, spread_ref):
+    fields = [lambda i: second_ref[i], completed(kv_in, (h0, h1, h2))]
+    spread_fields(order_ref, fields, out_ref, spread_ref)
+
+
+def half_sum_kernel(rows_ref, out_ref):
+    out_ref[...] = jnp.broadcast_to(
+        jnp.sum(rows_ref[...], axis=0, keepdims=True), out_ref.shape
+    )
 
 
 def last_kernel(sums_ref, spread_ref, late_ref, solution_ref, residual_ref):
-    sums = jnp.sum(sums_ref[...], axis=0, keepdims=True)
+    sums = jnp.sum(sums_ref[...], axis=0)
     lane = lane_iota(1)
 
     def total(d):
@@ -742,9 +747,9 @@
     alpha1 = rz1 / energy
     first_scale = alpha0 + alpha1 * share
     second_scale = alpha1 * alpha0
-    solution_ref[...] = first_scale * spread_ref[0] - second_scale * spread_ref[1]
+    solution_ref[...] = first_scale * spread_ref[0] - second_scale * late_ref[0]
     residual_ref[...] = (
-        spread_ref[2] - first_scale * spread_ref[3] + second_scale * late_ref[0]
+        spread_ref[1] - first_scale * spread_ref[2] + second_scale * late_ref[1]
     )
 
 
@@ -885,6 +890,11 @@
     )
     (kv,) = call(rest_kernel, [FIELD], [], *parts, diver)
     halo = swap_wide(far, near)
+    order = element_order.reshape(64, 1)
+    (spread,) = call(
+        spread_early_kernel, [(3, 64, 512)], [(64, 512)], order, first, residual, image
+    )
+    kv, spread = lax.optimization_barrier((kv, spread))
     sums_shape = (lax.axis_size(REST), LANES)
     second, *parts, sums = call(
         sixth_kernel,
@@ -893,17 +903,13 @@
         kv, *halo, image, inverse, start, residual, early, metric, grad,
         out_spaces=[pltpu.VMEM] * 3 + [pltpu.HBM],
     )
-    sums = lax.all_to_all(sums, REST, 0, 0)
+    sums = lax.all_to_all(sums[:, None], REST, 0, 0)
     kv, far, near, pack = call(
         rest_faces_kernel, [FIELD] + faces() + packs(), [], *parts, diver
     )
-    order = element_order.reshape(64, 1)
-    (spread,) = call(
-        spread_early_kernel, [(4, 64, 512)], [(64, 512)], order, first, second, residual, image
-    )
     far = swap_far(far)
     ring = lax.axis_size("ring")
-    sums = jnp.broadcast_to(jnp.sum(sums, axis=0, keepdims=True), (ring, LANES))
+    (sums,) = call(half_sum_kernel, [(ring, 1, LANES)], [], sums)
     near, sums = lax.optimization_barrier((near, sums))
     sums = lax.all_to_all(sums, "ring", 0, 0)
     near = lax.all_gather(
@@ -911,7 +917,7 @@
     )
     (pack,) = call(pack_kernel, [pack.shape], [], pack, far, near)
     halo = far, near, lax.all_gather(pack, "narrow")
-    (late,) = call(spread_late_kernel, [(1, 64, 512)], [(64, 512)], kv, *halo, order)
+    (late,) = call(spread_late_kernel, [(2, 64, 512)], [(64, 512)], kv, *halo, second, order)
     return tuple(call(last_kernel, [(64, 512), (64, 512)], [], sums, spread, late))
 
 

time: 143 us -> 143 us (level)
    pallas_call x20 -> x21, Pallas kernels: 12.2 us -> 12.8 us  [call(): pl.pallas_call(kernel, out_shape=[jax.ShapeDtypeStruct(s, F32) for s in o...]
  transfers between devices with their start and end apart: 17 -> 17, of which waited for: 7 -> 8; matrix products, arithmetic and copies ran while one was open for 0% -> 0% of each run, Pallas kernels for 3% -> 3%
where the time goes in v9:
time: 143 us
  starting transfers between devices  80.8 us (57%)
  blocking collectives  33.8 us (24%)
  waiting for transfers between devices  14.2 us (10%)
  Pallas kernels  12.8 us (9%)
    ppermute x7, starting transfers between devices, swap_far(): lax.ppermute(far, WIDE, [(w, (w + 1 if w % 2 else w - 1) % count) for w i...  54.5 us
    all_gather x2, blocking collectives, swap_edged(): return (far, near, lax.all_gather(pack, 'narrow'))  16.3 us
    pallas_call x21, Pallas kernels, call(): pl.pallas_call(kernel, out_shape=[jax.ShapeDtypeStruct(s, F32) for s in o...  12.8 us
    ppermute x7, waiting for transfers between devices, swap_far(): lax.ppermute(far, WIDE, [(w, (w + 1 if w % 2 else w - 1) % count) for w i...  12.7 us
    ppermute x6, starting transfers between devices, swap_wide(): lax.ppermute(near, WIDE, [(w, w ^ 1) for w in range(count)])  11.6 us
    all_gather x1, blocking collectives, swap_all(): return (far, near, lax.all_gather(pack, 'narrow'))  7.34 us
    all_gather x1, blocking collectives, local(): halo = (far, near, lax.all_gather(pack, 'narrow'))  6.82 us
    all_to_all x1, starting transfers between devices, local(): sums = lax.all_to_all(sums[:, None], REST, 0, 0)  6.22 us
  transfers between devices with their start and end apart: 17, of which 8 were waited for; matrix products, arithmetic and copies ran while one was open for 0% of the time, Pallas kernels for 3%

profile of v9, /device:TPU:1, one launch (start us, length us, event | category | flops | bytes accessed | tf_op | source)
XLA Modules:
  0.0 142.6 jit_solution(93265962398512003)
XLA Ops:
  0.6 2.6 %shard_map.77 = (f32[7,8,32,128]{3,2,1,0:T(8,128)S(1)}, f32[8,32,128]{2,1,0:T(8,128)S(1)}, f32[8,32,128]{2,1,0:T(8,128)S(1)}, f32[2,32,128]{2,1,0:T(8,128)S(1)},...) custom-call(s32[1,64]{1,0:T(1,128)} %bitcast.14, ...), custom_call_target="tpu_custom_call" | custom-call | tf_op jit(solution)/shard_map/pallas_call | solution.py:762
  3.3 20.5 %collective-permute-start = (f32[2,32,128]{2,1,0:T(8,128)S(1)}, f32[2,32,128]{2,1,0:T(8,128)S(1)}, u32[]{:S(2)}, u32[]{:S(2)}) collective-permute-start(f32[2,32,128]{2,1,0:T(8,128)S(1)} %get-tuple-element.64), channel_id=1, source_target_pairs={{0,764},{4,8},{8,4},{12,16},{16,12},{20,24},{24,20},{28,32},{32,28... | collective-permute-start | bytes 98312 | tf_op jit(solution)/shard_map/ppermute | solution.py:788
  23.8 1.9 %collective-permute-start.1 = (f32[2,32,128]{2,1,0:T(8,128)S(1)}, f32[2,32,128]{2,1,0:T(8,128)S(1)}, u32[]{:S(2)}, u32[]{:S(2)}) collective-permute-start(f32[2,32,128]{2,1,0:T(8,128)S(1)} %get-tuple-element.65), channel_id=1, source_target_pairs={{0,4},{4,0},{8,12},{12,8},{16,20},{20,16},{24,28},{28,24},{32,36},... | collective-permute-start | bytes 98312 | tf_op jit(solution)/shard_map/ppermute | solution.py:795
  25.7 3.1 %collective-permute-start.2 = (f32[6,4,16,128]{3,2,1,0:T(8,128)S(1)}, f32[6,4,16,128]{3,2,1,0:T(8,128)S(1)}, u32[]{:S(2)}, u32[]{:S(2)}) collective-permute-start(f32[6,4,16,128]{3,2,1,0:T(8,128)S(1)} %get-tuple-element.67), channel_id=1, source_target_pairs={{0,1},{1,2},{2,3},{3,0},{4,5},{5,6},{6,7},{7,4},{8,9},{9,10},{10,1... | collective-permute-start | bytes 589832 | tf_op jit(solution)/shard_map/ppermute | solution.py:821
  28.8 1.9 %collective-permute-start.3 = (f32[6,4,16,128]{3,2,1,0:T(8,128)S(1)}, f32[6,4,16,128]{3,2,1,0:T(8,128)S(1)}, u32[]{:S(2)}, u32[]{:S(2)}) collective-permute-start(f32[6,4,16,128]{3,2,1,0:T(8,128)S(1)} %get-tuple-element.68), channel_id=1, source_target_pairs={{0,3},{1,0},{2,1},{3,2},{4,7},{5,4},{6,5},{7,6},{8,11},{9,8},{10,9... | collective-permute-start | bytes 589832 | tf_op jit(solution)/shard_map/ppermute | solution.py:822
  30.8 7.3 %all-gather = f32[8,48,128]{2,1,0:T(8,128)S(1)} all-gather(f32[2,48,128]{2,1,0:T(8,128)S(1)} %shard_map.78), channel_id=2, replica_groups=mesh['outer'=16,'ring'=12,'narrow'=4] {'narrow'}, dimensions={0}, use_global_device_ids=true | all-gather | bytes 245760 | tf_op jit(solution)/shard_map/all_gather | solution.py:801
  38.2 0.8 shard_map.79
  39.1 3.6 %collective-permute-start.4 = (f32[1,32,128]{2,1,0:T(8,128)S(1)}, f32[1,32,128]{2,1,0:T(8,128)S(1)}, u32[]{:S(2)}, u32[]{:S(2)}) collective-permute-start(f32[1,32,128]{2,1,0:T(8,128)S(1)} %get-tuple-element.72), channel_id=1, source_target_pairs={{0,764},{4,8},{8,4},{12,16},{16,12},{20,24},{24,20},{28,32},{32,28... | collective-permute-start | bytes 49160 | tf_op jit(solution)/shard_map/ppermute | solution.py:788
  42.6 2.0 %collective-permute-start.5 = (f32[1,32,128]{2,1,0:T(8,128)S(1)}, f32[1,32,128]{2,1,0:T(8,128)S(1)}, u32[]{:S(2)}, u32[]{:S(2)}) collective-permute-start(f32[1,32,128]{2,1,0:T(8,128)S(1)} %get-tuple-element.73), channel_id=1, source_target_pairs={{0,4},{4,0},{8,12},{12,8},{16,20},{20,16},{24,28},{28,24},{32,36},... | collective-permute-start | bytes 49160 | tf_op jit(solution)/shard_map/ppermute | solution.py:795
  44.6 0.5 shard_map.80.kv_in
  45.1 4.2 %collective-permute-done.4.h0 = f32[1,32,128]{2,1,0:T(8,128)S(1)} collective-permute-done((f32[1,32,128]{2,1,0:T(8,128)S(1)}, f32[1,32,128]{2,1,0:T(8,128)S(1)}, u32[]{:S(2)}, u32[]{:S(2)}) %collective-permute-start.4) | collective-permute-done | bytes 16416 | tf_op jit(solution)/shard_map/ppermute | solution.py:788
  49.3 0.6 shard_map.81
  49.9 5.3 %collective-permute-start.6 = (f32[1,32,128]{2,1,0:T(8,128)S(1)}, f32[1,32,128]{2,1,0:T(8,128)S(1)}, u32[]{:S(2)}, u32[]{:S(2)}) collective-permute-start(f32[1,32,128]{2,1,0:T(8,128)S(1)} %get-tuple-element.81), channel_id=1, source_target_pairs={{0,764},{4,8},{8,4},{12,16},{16,12},{20,24},{24,20},{28,32},{32,28... | collective-permute-start | bytes 49160 | tf_op jit(solution)/shard_map/ppermute | solution.py:788
  55.1 1.9 %collective-permute-start.7 = (f32[1,32,128]{2,1,0:T(8,128)S(1)}, f32[1,32,128]{2,1,0:T(8,128)S(1)}, u32[]{:S(2)}, u32[]{:S(2)}) collective-permute-start(f32[1,32,128]{2,1,0:T(8,128)S(1)} %get-tuple-element.82), channel_id=1, source_target_pairs={{0,4},{4,0},{8,12},{12,8},{16,20},{20,16},{24,28},{28,24},{32,36},... | collective-permute-start | bytes 49160 | tf_op jit(solution)/shard_map/ppermute | solution.py:795
  57.1 0.4 shard_map.82
  57.5 2.5 %collective-permute-done.6.far_ref.h0 = f32[1,32,128]{2,1,0:T(8,128)S(1)} collective-permute-done((f32[1,32,128]{2,1,0:T(8,128)S(1)}, f32[1,32,128]{2,1,0:T(8,128)S(1)}, u32[]{:S(2)}, u32[]{:S(2)}) %collective-permute-start.6) | collective-permute-done | bytes 16416 | tf_op jit(solution)/shard_map/ppermute | solution.py:788
  60.2 8.3 %all-gather.1 = f32[4,144,128]{2,1,0:T(8,128)S(1)} all-gather(f32[1,144,128]{2,1,0:T(8,128)S(1)} %shard_map.83), channel_id=3, replica_groups=mesh['outer'=16,'ring'=12,'narrow'=4] {'narrow'}, dimensions={0}, use_global_device_ids=true | all-gather | bytes 368640 | tf_op jit(solution)/shard_map/all_gather | solution.py:816
  68.4 0.8 shard_map.84
  69.3 6.0 %collective-permute-start.8 = (f32[1,32,128]{2,1,0:T(8,128)S(1)}, f32[1,32,128]{2,1,0:T(8,128)S(1)}, u32[]{:S(2)}, u32[]{:S(2)}) collective-permute-start(f32[1,32,128]{2,1,0:T(8,128)S(1)} %get-tuple-element.92), channel_id=1, source_target_pairs={{0,764},{4,8},{8,4},{12,16},{16,12},{20,24},{24,20},{28,32},{32,28... | collective-permute-start | bytes 49160 | tf_op jit(solution)/shard_map/ppermute | solution.py:788
  75.3 1.9 %collective-permute-start.9 = (f32[1,32,128]{2,1,0:T(8,128)S(1)}, f32[1,32,128]{2,1,0:T(8,128)S(1)}, u32[]{:S(2)}, u32[]{:S(2)}) collective-permute-start(f32[1,32,128]{2,1,0:T(8,128)S(1)} %get-tuple-element.93), channel_id=1, source_target_pairs={{0,4},{4,0},{8,12},{12,8},{16,20},{20,16},{24,28},{28,24},{32,36},... | collective-permute-start | bytes 49160 | tf_op jit(solution)/shard_map/ppermute | solution.py:795
  77.2 0.5 shard_map.85
  77.7 1.8 %collective-permute-done.8.h0 = f32[1,32,128]{2,1,0:T(8,128)S(1)} collective-permute-done((f32[1,32,128]{2,1,0:T(8,128)S(1)}, f32[1,32,128]{2,1,0:T(8,128)S(1)}, u32[]{:S(2)}, u32[]{:S(2)}) %collective-permute-start.8) | collective-permute-done | bytes 16416 | tf_op jit(solution)/shard_map/ppermute | solution.py:788
  79.5 0.6 collective-permute-done.9.h1
  80.1 0.6 shard_map.86
  80.7 5.4 %collective-permute-start.10 = (f32[1,32,128]{2,1,0:T(8,128)S(1)}, f32[1,32,128]{2,1,0:T(8,128)S(1)}, u32[]{:S(2)}, u32[]{:S(2)}) collective-permute-start(f32[1,32,128]{2,1,0:T(8,128)S(1)} %get-tuple-element.98), channel_id=1, source_target_pairs={{0,764},{4,8},{8,4},{12,16},{16,12},{20,24},{24,20},{28,32},{32,28... | collective-permute-start | bytes 49160 | tf_op jit(solution)/shard_map/ppermute | solution.py:788
  86.1 1.9 %collective-permute-start.11 = (f32[1,32,128]{2,1,0:T(8,128)S(1)}, f32[1,32,128]{2,1,0:T(8,128)S(1)}, u32[]{:S(2)}, u32[]{:S(2)}) collective-permute-start(f32[1,32,128]{2,1,0:T(8,128)S(1)} %get-tuple-element.99), channel_id=1, source_target_pairs={{0,4},{4,0},{8,12},{12,8},{16,20},{20,16},{24,28},{28,24},{32,36},... | collective-permute-start | bytes 49160 | tf_op jit(solution)/shard_map/ppermute | solution.py:795
  88.0 0.4 shard_map.87
  88.5 2.5 %collective-permute-done.10.far_ref.h0 = f32[1,32,128]{2,1,0:T(8,128)S(1)} collective-permute-done((f32[1,32,128]{2,1,0:T(8,128)S(1)}, f32[1,32,128]{2,1,0:T(8,128)S(1)}, u32[]{:S(2)}, u32[]{:S(2)}) %collective-permute-start.10) | collective-permute-done | bytes 16416 | tf_op jit(solution)/shard_map/ppermute | solution.py:788
  91.1 8.0 %all-gather.2 = f32[4,144,128]{2,1,0:T(8,128)S(1)} all-gather(f32[1,144,128]{2,1,0:T(8,128)S(1)} %shard_map.88), channel_id=4, replica_groups=mesh['outer'=16,'ring'=12,'narrow'=4] {'narrow'}, dimensions={0}, use_global_device_ids=true | all-gather | bytes 368640 | tf_op jit(solution)/shard_map/all_gather | solution.py:816
  99.1 0.8 shard_map.89
  100.0 5.6 %collective-permute-start.12 = (f32[1,32,128]{2,1,0:T(8,128)S(1)}, f32[1,32,128]{2,1,0:T(8,128)S(1)}, u32[]{:S(2)}, u32[]{:S(2)}) collective-permute-start(f32[1,32,128]{2,1,0:T(8,128)S(1)} %get-tuple-element.107), channel_id=1, source_target_pairs={{0,764},{4,8},{8,4},{12,16},{16,12},{20,24},{24,20},{28,32},{32,28... | collective-permute-start | bytes 49160 | tf_op jit(solution)/shard_map/ppermute | solution.py:788
  105.5 1.9 %collective-permute-start.13 = (f32[1,32,128]{2,1,0:T(8,128)S(1)}, f32[1,32,128]{2,1,0:T(8,128)S(1)}, u32[]{:S(2)}, u32[]{:S(2)}) collective-permute-start(f32[1,32,128]{2,1,0:T(8,128)S(1)} %get-tuple-element.108), channel_id=1, source_target_pairs={{0,4},{4,0},{8,12},{12,8},{16,20},{20,16},{24,28},{28,24},{32,36},... | collective-permute-start | bytes 49160 | tf_op jit(solution)/shard_map/ppermute | solution.py:795
  107.5 0.1 copy.10.order_ref
  107.6 0.4 shard_map.91.spread_ref
  108.0 0.5 shard_map.90.kv_in
  108.4 1.7 %collective-permute-done.12.h0 = f32[1,32,128]{2,1,0:T(8,128)S(1)} collective-permute-done((f32[1,32,128]{2,1,0:T(8,128)S(1)}, f32[1,32,128]{2,1,0:T(8,128)S(1)}, u32[]{:S(2)}, u32[]{:S(2)}) %collective-permute-start.12) | collective-permute-done | bytes 16416 | tf_op jit(solution)/shard_map/ppermute | solution.py:788
  110.2 0.2 collective-permute-done.13.h1
  110.3 1.1 shard_map.92
  111.4 6.2 %all-to-all-start = ((f32[64,1,128]{2,1,0:T(1,128)}), f32[64,1,128]{2,1,0:T(1,128)S(1)}, u32[]{:S(2)}, u32[]{:S(2)}) async-start(f32[64,1,128]{2,1,0:T(1,128)} %bitcast.5), calls=%async_computation | async-start | bytes 65536 | tf_op jit(solution)/shard_map/all_to_all | solution.py:906
  117.6 0.4 shard_map.93
  118.1 8.2 %collective-permute-start.14 = (f32[1,32,128]{2,1,0:T(8,128)S(1)}, f32[1,32,128]{2,1,0:T(8,128)S(1)}, u32[]{:S(2)}, u32[]{:S(2)}) collective-permute-start(f32[1,32,128]{2,1,0:T(8,128)S(1)} %get-tuple-element.118), channel_id=1, source_target_pairs={{0,764},{4,8},{8,4},{12,16},{16,12},{20,24},{24,20},{28,32},{32,28... | collective-permute-start | bytes 49160 | tf_op jit(solution)/shard_map/ppermute | solution.py:788
  126.3 0.7 all-to-all-done.rows_ref
  126.9 0.7 shard_map.94
  127.6 3.5 %all-to-all-start.1 = ((f32[12,1,128]{2,1,0:T(1,128)}), f32[12,1,128]{2,1,0:T(1,128)S(1)}, u32[]{:S(2)}, u32[]{:S(2)}) async-start(f32[12,1,128]{2,1,0:T(1,128)} %shard_map.94), calls=%async_computation.1 | async-start | bytes 12288 | tf_op jit(solution)/shard_map/all_to_all | solution.py:914
  131.1 3.3 %all-gather.3 = f32[2,32,128]{2,1,0:T(8,128)S(1)} all-gather(f32[1,32,128]{2,1,0:T(8,128)S(1)} %get-tuple-element.119), channel_id=5, replica_groups={{0,4},{8,12},{16,20},{24,28},{32,36},{40,44},{1,5},{9,13},{17,21},{25,2..., dimensions={0}, use_global_device_ids=true | all-gather | bytes 49152 | tf_op jit(solution)/shard_map/all_gather | solution.py:915
  134.4 6.8 %all-gather.4 = f32[4,16,128]{2,1,0:T(8,128)S(1)} all-gather(f32[1,16,128]{2,1,0:T(8,128)S(1)} %shard_map.95), channel_id=6, replica_groups=mesh['outer'=16,'ring'=12,'narrow'=4] {'narrow'}, dimensions={0}, use_global_device_ids=true | all-gather | bytes 40960 | tf_op jit(solution)/shard_map/all_gather | solution.py:919
  141.3 0.4 shard_map.96.late_ref
  141.7 0.8 shard_map.97
  (19 shorter events, 0.4 us)
Async XLA Ops:
  3.3 27.4 %collective-permute-start = (f32[2,32,128]{2,1,0:T(8,128)S(1)}, f32[2,32,128]{2,1,0:T(8,128)S(1)}, u32[]{:S(2)}, u32[]{:S(2)}) collective-permute-start(f32[2,32,128]{2,1,0:T(8,128)S(1)} %get-tuple-element.64), channel_id=1, source_target_pairs={{0,764},{4,8},{8,4},{12,16},{16,12},{20,24},{24,20},{28,32},{32,28... | collective-permute-start | bytes 98312 | tf_op jit(solution)/shard_map/ppermute | solution.py:788
  23.8 6.9 %collective-permute-start.1 = (f32[2,32,128]{2,1,0:T(8,128)S(1)}, f32[2,32,128]{2,1,0:T(8,128)S(1)}, u32[]{:S(2)}, u32[]{:S(2)}) collective-permute-start(f32[2,32,128]{2,1,0:T(8,128)S(1)} %get-tuple-element.65), channel_id=1, source_target_pairs={{0,4},{4,0},{8,12},{12,8},{16,20},{20,16},{24,28},{28,24},{32,36},... | collective-permute-start | bytes 98312 | tf_op jit(solution)/shard_map/ppermute | solution.py:795
  25.7 12.5 %collective-permute-start.2 = (f32[6,4,16,128]{3,2,1,0:T(8,128)S(1)}, f32[6,4,16,128]{3,2,1,0:T(8,128)S(1)}, u32[]{:S(2)}, u32[]{:S(2)}) collective-permute-start(f32[6,4,16,128]{3,2,1,0:T(8,128)S(1)} %get-tuple-element.67), channel_id=1, source_target_pairs={{0,1},{1,2},{2,3},{3,0},{4,5},{5,6},{6,7},{7,4},{8,9},{9,10},{10,1... | collective-permute-start | bytes 589832 | tf_op jit(solution)/shard_map/ppermute | solution.py:821
  28.8 9.4 %collective-permute-start.3 = (f32[6,4,16,128]{3,2,1,0:T(8,128)S(1)}, f32[6,4,16,128]{3,2,1,0:T(8,128)S(1)}, u32[]{:S(2)}, u32[]{:S(2)}) collective-permute-start(f32[6,4,16,128]{3,2,1,0:T(8,128)S(1)} %get-tuple-element.68), channel_id=1, source_target_pairs={{0,3},{1,0},{2,1},{3,2},{4,7},{5,4},{6,5},{7,6},{8,11},{9,8},{10,9... | collective-permute-start | bytes 589832 | tf_op jit(solution)/shard_map/ppermute | solution.py:822
  30.7 7.5 %copy-start.1 = (bf16[384,256]{1,0:T(8,128)(2,1)S(1)}, bf16[384,256]{1,0:T(8,128)(2,1)}, u32[]{:S(2)}) copy-start(bf16[384,256]{1,0:T(8,128)(2,1)} %constant.6.clone.grad_ref) | copy-start | bytes 589828
  30.8 7.4 %copy-start = (bf16[256,256]{1,0:T(8,128)(2,1)S(1)}, bf16[256,256]{1,0:T(8,128)(2,1)}, u32[]{:S(2)}) copy-start(bf16[256,256]{1,0:T(8,128)(2,1)} %constant.7.clone.diver_ref) | copy-start | bytes 393220
  39.1 10.2 %collective-permute-start.4 = (f32[1,32,128]{2,1,0:T(8,128)S(1)}, f32[1,32,128]{2,1,0:T(8,128)S(1)}, u32[]{:S(2)}, u32[]{:S(2)}) collective-permute-start(f32[1,32,128]{2,1,0:T(8,128)S(1)} %get-tuple-element.72), channel_id=1, source_target_pairs={{0,764},{4,8},{8,4},{12,16},{16,12},{20,24},{24,20},{28,32},{32,28... | collective-permute-start | bytes 49160 | tf_op jit(solution)/shard_map/ppermute | solution.py:788
  42.6 6.6 %collective-permute-start.5 = (f32[1,32,128]{2,1,0:T(8,128)S(1)}, f32[1,32,128]{2,1,0:T(8,128)S(1)}, u32[]{:S(2)}, u32[]{:S(2)}) collective-permute-start(f32[1,32,128]{2,1,0:T(8,128)S(1)} %get-tuple-element.73), channel_id=1, source_target_pairs={{0,4},{4,0},{8,12},{12,8},{16,20},{20,16},{24,28},{28,24},{32,36},... | collective-permute-start | bytes 49160 | tf_op jit(solution)/shard_map/ppermute | solution.py:795
  49.9 10.2 %collective-permute-start.6 = (f32[1,32,128]{2,1,0:T(8,128)S(1)}, f32[1,32,128]{2,1,0:T(8,128)S(1)}, u32[]{:S(2)}, u32[]{:S(2)}) collective-permute-start(f32[1,32,128]{2,1,0:T(8,128)S(1)} %get-tuple-element.81), channel_id=1, source_target_pairs={{0,764},{4,8},{8,4},{12,16},{16,12},{20,24},{24,20},{28,32},{32,28... | collective-permute-start | bytes 49160 | tf_op jit(solution)/shard_map/ppermute | solution.py:788
  55.1 4.9 %collective-permute-start.7 = (f32[1,32,128]{2,1,0:T(8,128)S(1)}, f32[1,32,128]{2,1,0:T(8,128)S(1)}, u32[]{:S(2)}, u32[]{:S(2)}) collective-permute-start(f32[1,32,128]{2,1,0:T(8,128)S(1)} %get-tuple-element.82), channel_id=1, source_target_pairs={{0,4},{4,0},{8,12},{12,8},{16,20},{20,16},{24,28},{28,24},{32,36},... | collective-permute-start | bytes 49160 | tf_op jit(solution)/shard_map/ppermute | solution.py:795
  69.3 10.2 %collective-permute-start.8 = (f32[1,32,128]{2,1,0:T(8,128)S(1)}, f32[1,32,128]{2,1,0:T(8,128)S(1)}, u32[]{:S(2)}, u32[]{:S(2)}) collective-permute-start(f32[1,32,128]{2,1,0:T(8,128)S(1)} %get-tuple-element.92), channel_id=1, source_target_pairs={{0,764},{4,8},{8,4},{12,16},{16,12},{20,24},{24,20},{28,32},{32,28... | collective-permute-start | bytes 49160 | tf_op jit(solution)/shard_map/ppermute | solution.py:788
  75.3 4.8 %collective-permute-start.9 = (f32[1,32,128]{2,1,0:T(8,128)S(1)}, f32[1,32,128]{2,1,0:T(8,128)S(1)}, u32[]{:S(2)}, u32[]{:S(2)}) collective-permute-start(f32[1,32,128]{2,1,0:T(8,128)S(1)} %get-tuple-element.93), channel_id=1, source_target_pairs={{0,4},{4,0},{8,12},{12,8},{16,20},{20,16},{24,28},{28,24},{32,36},... | collective-permute-start | bytes 49160 | tf_op jit(solution)/shard_map/ppermute | solution.py:795
  80.7 10.3 %collective-permute-start.10 = (f32[1,32,128]{2,1,0:T(8,128)S(1)}, f32[1,32,128]{2,1,0:T(8,128)S(1)}, u32[]{:S(2)}, u32[]{:S(2)}) collective-permute-start(f32[1,32,128]{2,1,0:T(8,128)S(1)} %get-tuple-element.98), channel_id=1, source_target_pairs={{0,764},{4,8},{8,4},{12,16},{16,12},{20,24},{24,20},{28,32},{32,28... | collective-permute-start | bytes 49160 | tf_op jit(solution)/shard_map/ppermute | solution.py:788
  86.1 4.9 %collective-permute-start.11 = (f32[1,32,128]{2,1,0:T(8,128)S(1)}, f32[1,32,128]{2,1,0:T(8,128)S(1)}, u32[]{:S(2)}, u32[]{:S(2)}) collective-permute-start(f32[1,32,128]{2,1,0:T(8,128)S(1)} %get-tuple-element.99), channel_id=1, source_target_pairs={{0,4},{4,0},{8,12},{12,8},{16,20},{20,16},{24,28},{28,24},{32,36},... | collective-permute-start | bytes 49160 | tf_op jit(solution)/shard_map/ppermute | solution.py:795
  100.0 10.2 %collective-permute-start.12 = (f32[1,32,128]{2,1,0:T(8,128)S(1)}, f32[1,32,128]{2,1,0:T(8,128)S(1)}, u32[]{:S(2)}, u32[]{:S(2)}) collective-permute-start(f32[1,32,128]{2,1,0:T(8,128)S(1)} %get-tuple-element.107), channel_id=1, source_target_pairs={{0,764},{4,8},{8,4},{12,16},{16,12},{20,24},{24,20},{28,32},{32,28... | collective-permute-start | bytes 49160 | tf_op jit(solution)/shard_map/ppermute | solution.py:788
  105.5 1.9 %copy-start.2 = (s32[1,1,64]{2,1,0:T(1,128)S(1)}, s32[1,1,64]{2,1,0:T(1,128)}, u32[]{:S(2)}) copy-start(s32[1,1,64]{2,1,0:T(1,128)} %param.8) | copy-start | bytes 772
  105.5 4.8 %collective-permute-start.13 = (f32[1,32,128]{2,1,0:T(8,128)S(1)}, f32[1,32,128]{2,1,0:T(8,128)S(1)}, u32[]{:S(2)}, u32[]{:S(2)}) collective-permute-start(f32[1,32,128]{2,1,0:T(8,128)S(1)} %get-tuple-element.108), channel_id=1, source_target_pairs={{0,4},{4,0},{8,12},{12,8},{16,20},{20,16},{24,28},{28,24},{32,36},... | collective-permute-start | bytes 49160 | tf_op jit(solution)/shard_map/ppermute | solution.py:795
  111.4 15.5 %all-to-all-start = ((f32[64,1,128]{2,1,0:T(1,128)}), f32[64,1,128]{2,1,0:T(1,128)S(1)}, u32[]{:S(2)}, u32[]{:S(2)}) async-start(f32[64,1,128]{2,1,0:T(1,128)} %bitcast.5), calls=%async_computation | async-start | bytes 65536 | tf_op jit(solution)/shard_map/all_to_all | solution.py:906
  118.1 16.3 %collective-permute-start.14 = (f32[1,32,128]{2,1,0:T(8,128)S(1)}, f32[1,32,128]{2,1,0:T(8,128)S(1)}, u32[]{:S(2)}, u32[]{:S(2)}) collective-permute-start(f32[1,32,128]{2,1,0:T(8,128)S(1)} %get-tuple-element.118), channel_id=1, source_target_pairs={{0,764},{4,8},{8,4},{12,16},{16,12},{20,24},{24,20},{28,32},{32,28... | collective-permute-start | bytes 49160 | tf_op jit(solution)/shard_map/ppermute | solution.py:788
  127.6 14.1 %all-to-all-start.1 = ((f32[12,1,128]{2,1,0:T(1,128)}), f32[12,1,128]{2,1,0:T(1,128)S(1)}, u32[]{:S(2)}, u32[]{:S(2)}) async-start(f32[12,1,128]{2,1,0:T(1,128)} %shard_map.94), calls=%async_computation.1 | async-start | bytes 12288 | tf_op jit(solution)/shard_map/all_to_all | solution.py:914

commit v10 on v9

--- a/solution.py
+++ b/solution.py
@@ -82,7 +82,7 @@
 GRAD_PARTS = split_const(GRAD)
 GRAD_HL = np.concatenate([GRAD_PARTS[0], GRAD_PARTS[0], GRAD_PARTS[1]], axis=0)
 DIVER_HL = np.concatenate(split_const(DIVER), axis=1)
-ABS_HL = np.stack(split_const(np.abs(DIVER)))
+ABS_HL = np.concatenate(split_const(np.abs(DIVER)), axis=1)
 
 
 def split(value):
@@ -94,11 +94,6 @@
     return lax.dot_general(
         left, right, (((1,), (0,)), ((), ())), preferred_element_type=jnp.float32
     )
-
-
-def dot_split(value, matrix_ref):
-    high, low = split(value)
-    return dot(high, matrix_ref[0]) + (dot(low, matrix_ref[0]) + dot(high, matrix_ref[1]))
 
 
 def dot_grad(value, grad_ref):
@@ -414,13 +409,16 @@
     ]
 
 
-def store_faces(flux_ref, part_ref, diver_ref, far_ref, near_ref):
-    first, last = (
-        own_assembly(u) for u in whole_planes(flux_ref, part_ref, diver_ref, (0, NODES - 1))
-    )
+def store_faces(first, last, far_ref, near_ref, field=0):
+    first, last = own_assembly(first), own_assembly(last)
     even = is_even()
-    near_ref[0] = jnp.where(even, last, first)
-    far_ref[0] = jnp.where(even, first, last)
+    near_ref[field] = jnp.where(even, last, first)
+    far_ref[field] = jnp.where(even, first, last)
+
+
+def store_flux_faces(flux_ref, part_ref, diver_ref, far_ref, near_ref, field=0):
+    planes = whole_planes(flux_ref, part_ref, diver_ref, (0, NODES - 1))
+    store_faces(*planes, far_ref, near_ref, field)
 
 
 def rest_kernel(flux_ref, part_ref, diver_ref, kv_ref):
@@ -482,8 +480,8 @@
 
 def place_kernel(
     order_hbm, load_hbm, geom_hbm, abs_hbm,
-    metric_ref, load_kv, bound_kv, far_ref, near_ref, pack_ref, lo_ref, hi_ref,
-    flux_ref, work_ref, order_ref, load_ref, geom_ref, abs_ref, sems,
+    metric_ref, placed_ref, flux_ref, part_ref, far_ref, near_ref,
+    order_ref, load_ref, geom_ref, abs_ref, sems,
 ):
     copies = [
         pltpu.make_async_copy(source, target, sems.at[c])
@@ -512,14 +510,10 @@
     middle = (load - high.astype(jnp.float32) - rest.astype(jnp.float32)).astype(jnp.bfloat16)
 
     def store_load(i, value):
-        work_ref[i] = value
+        placed_ref[i] = value
 
     spread(dot(pick, high) + (dot(pick, rest) + dot(pick, middle)), store_load)
-    even = is_even()
-    store_assembled(
-        load_kv, far_ref, near_ref, even, lambda i: work_ref[i], 0, pack_ref
-    )
-    store_edges(lo_ref, hi_ref, 3, 3, [edge(load_kv[i]) for i in range(NODES)])
+    store_faces(placed_ref[0], placed_ref[NODES - 1], far_ref, near_ref, 0)
 
     copies[2].wait()
     for c in range(7):
@@ -528,12 +522,6 @@
             metric_ref[c, i] = value
 
         spread(dot(pick, geom_ref[c]), store_metric)
-    for slot, c in enumerate(WHOLE):
-        store_edges(lo_ref, hi_ref, slot, slot, [edge(metric_ref[c, i]) for i in range(NODES)])
-    for slot, c in enumerate(LINES):
-        lines = line_pack(lambda i, c=c: metric_ref[c, i])
-        lo_ref[5, slot] = lines
-        hi_ref[5, slot] = lines
 
     lane = lane_iota(8)
     q_a = jnp.zeros((8, LANES), jnp.float32)
@@ -553,14 +541,27 @@
             flux_ref[1, at] = g[4] * q_z + g[5] * q_a + g[2] * q_r
         part_z = along_nodes_plain(h_z, ABS_DERIV.T)
         for i in range(NODES):
-            work_ref[i, rows] = part_z[i] + jnp.abs(metric_ref[6, i, rows])
-    flux = jnp.concatenate([flux_ref[0], flux_ref[1]], axis=1)
+            part_ref[i, rows] = part_z[i] + jnp.abs(metric_ref[6, i, rows])
     copies[3].wait()
-    work_ref[...] += dot_split(flux, abs_ref).reshape(FIELD)
-    store_assembled(
-        bound_kv, far_ref, near_ref, even, lambda i: work_ref[i], 1, pack_ref
-    )
-    store_edges(lo_ref, hi_ref, 4, 4, [edge(bound_kv[i]) for i in range(NODES)])
+    store_flux_faces(flux_ref, part_ref, abs_ref, far_ref, near_ref, 1)
+
+
+def rest_place_kernel(
+    metric_ref, placed_ref, flux_ref, part_ref, abs_ref, load_kv, bound_kv, pack_ref, lo_ref, hi_ref
+):
+    planes = whole_planes(flux_ref, part_ref, abs_ref, range(NODES))
+    for i in range(NODES):
+        load_kv[i] = own_assembly(placed_ref[i])
+        bound_kv[i] = own_assembly(planes[i])
+    for field, kv in enumerate((load_kv, bound_kv)):
+        pack_ref[field] = line_pack(lambda i, kv=kv: kv[i])
+        store_edges(lo_ref, hi_ref, 3 + field, 3 + field, [edge(kv[i]) for i in range(NODES)])
+    for slot, c in enumerate(WHOLE):
+        store_edges(lo_ref, hi_ref, slot, slot, [edge(metric_ref[c, i]) for i in range(NODES)])
+    for slot, c in enumerate(LINES):
+        lines = line_pack(lambda i, c=c: metric_ref[c, i])
+        lo_ref[5, slot] = lines
+        hi_ref[5, slot] = lines
 
 
 def first_kernel(
@@ -591,7 +592,7 @@
         for i, value in enumerate(ghost_lines(left_ref[5, slot], right_ref[5, slot])):
             ghost_metric[c, i] = value
     apply_flux(v_ref, metric_ref, ghost_metric, grad_ref, flux_ref, part_ref)
-    store_faces(flux_ref, part_ref, diver_ref, far_ref, near_ref)
+    store_flux_faces(flux_ref, part_ref, diver_ref, far_ref, near_ref)
 
 
 def second_kernel(
@@ -608,7 +609,7 @@
         v_ref[i] = result
         start_ref[i] = result + (RHO2 * RHO1) * update + STEP2 * inverse * source
     apply_flux(v_ref, metric_ref, None, grad_ref, flux_ref, part_ref)
-    store_faces(flux_ref, part_ref, diver_ref, far_ref, near_ref)
+    store_flux_faces(flux_ref, part_ref, diver_ref, far_ref, near_ref)
 
 
 def third_kernel(
@@ -628,7 +629,7 @@
     for i in range(NODES):
         v_ref[i, ROWS:] = start[i] - STEP2 * ghost_inverse[i] * sums(i)
     apply_flux(v_ref, metric_ref, ghost_metric, grad_ref, flux_ref, part_ref)
-    store_faces(flux_ref, part_ref, diver_ref, far_ref, near_ref)
+    store_flux_faces(flux_ref, part_ref, diver_ref, far_ref, near_ref)
     sums_ref[...] = sum_row([rz * plane])
 
 
@@ -644,7 +645,7 @@
         update_ref[i] = update
         start_ref[i] = (1.0 + RHO1 * RHO0 + STEP1 * CENTER) * update
     apply_flux(update_ref, metric_ref, None, grad_ref, flux_ref, part_ref)
-    store_faces(flux_ref, part_ref, diver_ref, far_ref, near_ref)
+    store_flux_faces(flux_ref, part_ref, diver_ref, far_ref, near_ref)
 
 
 def fifth_kernel(
@@ -665,7 +666,7 @@
     for i in range(NODES):
         v_ref[i, ROWS:] = start[i] - STEP1 * ghost_inverse[i] * sums(i)
     apply_flux(v_ref, metric_ref, ghost_metric, grad_ref, flux_ref, part_ref)
-    store_faces(flux_ref, part_ref, diver_ref, far_ref, near_ref)
+    store_flux_faces(flux_ref, part_ref, diver_ref, far_ref, near_ref)
 
 
 def sixth_kernel(
@@ -826,20 +827,29 @@
 def local(load, geom, element_order):
     grad = jnp.asarray(GRAD_HL)
     diver = jnp.asarray(DIVER_HL)
-    metric, load_kv, bound_kv, *face, lo, hi = call(
+    absolute = jnp.asarray(ABS_HL)
+    metric, *parts, far, near = call(
         place_kernel,
-        [(7,) + FIELD, FIELD, FIELD] + faces(2) + packs(2) + [edges(6)] * 2,
+        [(7,) + FIELD, FIELD, FLUX, FIELD] + faces(2),
         [
-            FLUX, FIELD,
             pltpu.VMEM((1, 64), jnp.int32), pltpu.VMEM(load.shape, load.dtype),
             pltpu.VMEM(geom.shape, geom.dtype), pltpu.VMEM(ABS_HL.shape, jnp.bfloat16),
             pltpu.SemaphoreType.DMA((4,)),
         ],
-        *(pltpu.with_memory_space_constraint(x, pltpu.HBM) for x in (element_order.reshape(1, 64), load, geom, jnp.asarray(ABS_HL))),
+        *(
+            pltpu.with_memory_space_constraint(x, pltpu.HBM)
+            for x in (element_order.reshape(1, 64), load, geom, absolute)
+        ),
         space=pltpu.HBM,
     )
+    load_kv, bound_kv, pack, lo, hi = call(
+        rest_place_kernel,
+        [FIELD, FIELD] + packs(2) + [edges(6)] * 2,
+        [],
+        metric, *parts, absolute,
+    )
     sides = swap_edges(lo, hi)
-    halo = swap_all(*face, GROWS)
+    halo = swap_all(far, near, pack, GROWS)
     residual, inverse, update, ghost_inverse, ghost_metric, *parts, far, near = call(
         first_kernel,
         [FIELD, FIELD, FIELD, GHOST, (7,) + GHOST, BIG_FLUX, BIG] + faces(),

time: 143 us -> 144 us (level)
    pallas_call x21 -> x22, Pallas kernels: 12.8 us -> 13.3 us  [call(): pl.pallas_call(kernel, out_shape=[jax.ShapeDtypeStruct(s, F32) for s in o...]
  transfers between devices with their start and end apart: 17 -> 17, of which waited for: 8 -> 8; matrix products, arithmetic and copies ran while one was open for 0% -> 0% of each run, Pallas kernels for 3% -> 4%
where the time goes in v10:
time: 144 us; the launch traced here: 143 us
  starting transfers between devices  80.8 us (56%)
  blocking collectives  33.8 us (23%)
  waiting for transfers between devices  14.2 us (10%)
  Pallas kernels  13.3 us (9%)
    ppermute x7, starting transfers between devices, swap_far(): lax.ppermute(far, WIDE, [(w, (w + 1 if w % 2 else w - 1) % count) for w i...  54.3 us
    all_gather x2, blocking collectives, swap_edged(): return (far, near, lax.all_gather(pack, 'narrow'))  16.3 us
    pallas_call x22, Pallas kernels, call(): pl.pallas_call(kernel, out_shape=[jax.ShapeDtypeStruct(s, F32) for s in o...  13.3 us
    ppermute x7, waiting for transfers between devices, swap_far(): lax.ppermute(far, WIDE, [(w, (w + 1 if w % 2 else w - 1) % count) for w i...  12.7 us
    ppermute x6, starting transfers between devices, swap_wide(): lax.ppermute(near, WIDE, [(w, w ^ 1) for w in range(count)])  11.8 us
    all_gather x1, blocking collectives, swap_all(): return (far, near, lax.all_gather(pack, 'narrow'))  7.34 us
    all_gather x1, blocking collectives, local(): halo = (far, near, lax.all_gather(pack, 'narrow'))  6.82 us
    all_to_all x1, starting transfers between devices, local(): sums = lax.all_to_all(sums[:, None], REST, 0, 0)  6.22 us
  transfers between devices with their start and end apart: 17, of which 8 were waited for; matrix products, arithmetic and copies ran while one was open for 0% of the time, Pallas kernels for 4%

profile of v10, /device:TPU:1, one launch (start us, length us, event | category | flops | bytes accessed | tf_op | source)
XLA Modules:
  0.0 143.1 jit_solution(10109921474112814334)
XLA Ops:
  0.6 2.2 %shard_map.77 = (f32[7,8,32,128]{3,2,1,0:T(8,128)S(1)}, f32[8,32,128]{2,1,0:T(8,128)S(1)}, f32[2,256,128]{2,1,0:T(8,128)S(1)}, f32[8,32,128]{2,1,0:T(8,128)S(1)}...) custom-call(s32[1,64]{1,0:T(1,128)} %bitcast.14, f32[64,512]{1,0:T(8,128)} %load_hbm.1, ...), custom_call_target="tpu_custom_call" | custom-call | tf_op jit(solution)/shard_map/pallas_call | solution.py:763
  2.9 20.5 %collective-permute-start = (f32[2,32,128]{2,1,0:T(8,128)S(1)}, f32[2,32,128]{2,1,0:T(8,128)S(1)}, u32[]{:S(2)}, u32[]{:S(2)}) collective-permute-start(f32[2,32,128]{2,1,0:T(8,128)S(1)} %get-tuple-element.71), channel_id=1, source_target_pairs={{0,764},{4,8},{8,4},{12,16},{16,12},{20,24},{24,20},{28,32},{32,28... | collective-permute-start | bytes 98312 | tf_op jit(solution)/shard_map/ppermute | solution.py:789
  23.4 1.9 %collective-permute-start.1 = (f32[2,32,128]{2,1,0:T(8,128)S(1)}, f32[2,32,128]{2,1,0:T(8,128)S(1)}, u32[]{:S(2)}, u32[]{:S(2)}) collective-permute-start(f32[2,32,128]{2,1,0:T(8,128)S(1)} %get-tuple-element.72), channel_id=1, source_target_pairs={{0,4},{4,0},{8,12},{12,8},{16,20},{20,16},{24,28},{28,24},{32,36},... | collective-permute-start | bytes 98312 | tf_op jit(solution)/shard_map/ppermute | solution.py:796
  25.3 0.9 shard_map.78
  26.2 3.1 %collective-permute-start.2 = (f32[6,4,16,128]{3,2,1,0:T(8,128)S(1)}, f32[6,4,16,128]{3,2,1,0:T(8,128)S(1)}, u32[]{:S(2)}, u32[]{:S(2)}) collective-permute-start(f32[6,4,16,128]{3,2,1,0:T(8,128)S(1)} %get-tuple-element.74), channel_id=1, source_target_pairs={{0,1},{1,2},{2,3},{3,0},{4,5},{5,6},{6,7},{7,4},{8,9},{9,10},{10,1... | collective-permute-start | bytes 589832 | tf_op jit(solution)/shard_map/ppermute | solution.py:822
  29.3 1.9 %collective-permute-start.3 = (f32[6,4,16,128]{3,2,1,0:T(8,128)S(1)}, f32[6,4,16,128]{3,2,1,0:T(8,128)S(1)}, u32[]{:S(2)}, u32[]{:S(2)}) collective-permute-start(f32[6,4,16,128]{3,2,1,0:T(8,128)S(1)} %get-tuple-element.75), channel_id=1, source_target_pairs={{0,3},{1,0},{2,1},{3,2},{4,7},{5,4},{6,5},{7,6},{8,11},{9,8},{10,9... | collective-permute-start | bytes 589832 | tf_op jit(solution)/shard_map/ppermute | solution.py:823
  31.4 7.3 %all-gather = f32[8,48,128]{2,1,0:T(8,128)S(1)} all-gather(f32[2,48,128]{2,1,0:T(8,128)S(1)} %shard_map.79), channel_id=2, replica_groups=mesh['outer'=16,'ring'=12,'narrow'=4] {'narrow'}, dimensions={0}, use_global_device_ids=true | all-gather | bytes 245760 | tf_op jit(solution)/shard_map/all_gather | solution.py:802
  38.7 0.8 shard_map.80
  39.6 3.3 %collective-permute-start.4 = (f32[1,32,128]{2,1,0:T(8,128)S(1)}, f32[1,32,128]{2,1,0:T(8,128)S(1)}, u32[]{:S(2)}, u32[]{:S(2)}) collective-permute-start(f32[1,32,128]{2,1,0:T(8,128)S(1)} %get-tuple-element.78), channel_id=1, source_target_pairs={{0,764},{4,8},{8,4},{12,16},{16,12},{20,24},{24,20},{28,32},{32,28... | collective-permute-start | bytes 49160 | tf_op jit(solution)/shard_map/ppermute | solution.py:789
  42.9 2.2 %collective-permute-start.5 = (f32[1,32,128]{2,1,0:T(8,128)S(1)}, f32[1,32,128]{2,1,0:T(8,128)S(1)}, u32[]{:S(2)}, u32[]{:S(2)}) collective-permute-start(f32[1,32,128]{2,1,0:T(8,128)S(1)} %get-tuple-element.79), channel_id=1, source_target_pairs={{0,4},{4,0},{8,12},{12,8},{16,20},{20,16},{24,28},{28,24},{32,36},... | collective-permute-start | bytes 49160 | tf_op jit(solution)/shard_map/ppermute | solution.py:796
  45.1 0.5 shard_map.81.kv_in
  45.6 4.2 %collective-permute-done.4.h0 = f32[1,32,128]{2,1,0:T(8,128)S(1)} collective-permute-done((f32[1,32,128]{2,1,0:T(8,128)S(1)}, f32[1,32,128]{2,1,0:T(8,128)S(1)}, u32[]{:S(2)}, u32[]{:S(2)}) %collective-permute-start.4) | collective-permute-done | bytes 16416 | tf_op jit(solution)/shard_map/ppermute | solution.py:789
  49.8 0.6 shard_map.82
  50.4 5.3 %collective-permute-start.6 = (f32[1,32,128]{2,1,0:T(8,128)S(1)}, f32[1,32,128]{2,1,0:T(8,128)S(1)}, u32[]{:S(2)}, u32[]{:S(2)}) collective-permute-start(f32[1,32,128]{2,1,0:T(8,128)S(1)} %get-tuple-element.87), channel_id=1, source_target_pairs={{0,764},{4,8},{8,4},{12,16},{16,12},{20,24},{24,20},{28,32},{32,28... | collective-permute-start | bytes 49160 | tf_op jit(solution)/shard_map/ppermute | solution.py:789
  55.7 1.9 %collective-permute-start.7 = (f32[1,32,128]{2,1,0:T(8,128)S(1)}, f32[1,32,128]{2,1,0:T(8,128)S(1)}, u32[]{:S(2)}, u32[]{:S(2)}) collective-permute-start(f32[1,32,128]{2,1,0:T(8,128)S(1)} %get-tuple-element.88), channel_id=1, source_target_pairs={{0,4},{4,0},{8,12},{12,8},{16,20},{20,16},{24,28},{28,24},{32,36},... | collective-permute-start | bytes 49160 | tf_op jit(solution)/shard_map/ppermute | solution.py:796
  57.6 0.4 shard_map.83
  58.0 2.5 %collective-permute-done.6.far_ref.h0 = f32[1,32,128]{2,1,0:T(8,128)S(1)} collective-permute-done((f32[1,32,128]{2,1,0:T(8,128)S(1)}, f32[1,32,128]{2,1,0:T(8,128)S(1)}, u32[]{:S(2)}, u32[]{:S(2)}) %collective-permute-start.6) | collective-permute-done | bytes 16416 | tf_op jit(solution)/shard_map/ppermute | solution.py:789
  60.7 8.3 %all-gather.1 = f32[4,144,128]{2,1,0:T(8,128)S(1)} all-gather(f32[1,144,128]{2,1,0:T(8,128)S(1)} %shard_map.84), channel_id=3, replica_groups=mesh['outer'=16,'ring'=12,'narrow'=4] {'narrow'}, dimensions={0}, use_global_device_ids=true | all-gather | bytes 368640 | tf_op jit(solution)/shard_map/all_gather | solution.py:817
  69.0 0.8 shard_map.85
  69.8 6.0 %collective-permute-start.8 = (f32[1,32,128]{2,1,0:T(8,128)S(1)}, f32[1,32,128]{2,1,0:T(8,128)S(1)}, u32[]{:S(2)}, u32[]{:S(2)}) collective-permute-start(f32[1,32,128]{2,1,0:T(8,128)S(1)} %get-tuple-element.98), channel_id=1, source_target_pairs={{0,764},{4,8},{8,4},{12,16},{16,12},{20,24},{24,20},{28,32},{32,28... | collective-permute-start | bytes 49160 | tf_op jit(solution)/shard_map/ppermute | solution.py:789
  75.8 1.9 %collective-permute-start.9 = (f32[1,32,128]{2,1,0:T(8,128)S(1)}, f32[1,32,128]{2,1,0:T(8,128)S(1)}, u32[]{:S(2)}, u32[]{:S(2)}) collective-permute-start(f32[1,32,128]{2,1,0:T(8,128)S(1)} %get-tuple-element.99), channel_id=1, source_target_pairs={{0,4},{4,0},{8,12},{12,8},{16,20},{20,16},{24,28},{28,24},{32,36},... | collective-permute-start | bytes 49160 | tf_op jit(solution)/shard_map/ppermute | solution.py:796
  77.8 0.5 shard_map.86
  78.2 1.8 %collective-permute-done.8.h0 = f32[1,32,128]{2,1,0:T(8,128)S(1)} collective-permute-done((f32[1,32,128]{2,1,0:T(8,128)S(1)}, f32[1,32,128]{2,1,0:T(8,128)S(1)}, u32[]{:S(2)}, u32[]{:S(2)}) %collective-permute-start.8) | collective-permute-done | bytes 16416 | tf_op jit(solution)/shard_map/ppermute | solution.py:789
  80.0 0.6 collective-permute-done.9.h1
  80.6 0.6 shard_map.87
  81.2 5.4 %collective-permute-start.10 = (f32[1,32,128]{2,1,0:T(8,128)S(1)}, f32[1,32,128]{2,1,0:T(8,128)S(1)}, u32[]{:S(2)}, u32[]{:S(2)}) collective-permute-start(f32[1,32,128]{2,1,0:T(8,128)S(1)} %get-tuple-element.104), channel_id=1, source_target_pairs={{0,764},{4,8},{8,4},{12,16},{16,12},{20,24},{24,20},{28,32},{32,28... | collective-permute-start | bytes 49160 | tf_op jit(solution)/shard_map/ppermute | solution.py:789
  86.6 1.9 %collective-permute-start.11 = (f32[1,32,128]{2,1,0:T(8,128)S(1)}, f32[1,32,128]{2,1,0:T(8,128)S(1)}, u32[]{:S(2)}, u32[]{:S(2)}) collective-permute-start(f32[1,32,128]{2,1,0:T(8,128)S(1)} %get-tuple-element.105), channel_id=1, source_target_pairs={{0,4},{4,0},{8,12},{12,8},{16,20},{20,16},{24,28},{28,24},{32,36},... | collective-permute-start | bytes 49160 | tf_op jit(solution)/shard_map/ppermute | solution.py:796
  88.6 0.4 shard_map.88
  89.0 2.5 %collective-permute-done.10.far_ref.h0 = f32[1,32,128]{2,1,0:T(8,128)S(1)} collective-permute-done((f32[1,32,128]{2,1,0:T(8,128)S(1)}, f32[1,32,128]{2,1,0:T(8,128)S(1)}, u32[]{:S(2)}, u32[]{:S(2)}) %collective-permute-start.10) | collective-permute-done | bytes 16416 | tf_op jit(solution)/shard_map/ppermute | solution.py:789
  91.6 8.0 %all-gather.2 = f32[4,144,128]{2,1,0:T(8,128)S(1)} all-gather(f32[1,144,128]{2,1,0:T(8,128)S(1)} %shard_map.89), channel_id=4, replica_groups=mesh['outer'=16,'ring'=12,'narrow'=4] {'narrow'}, dimensions={0}, use_global_device_ids=true | all-gather | bytes 368640 | tf_op jit(solution)/shard_map/all_gather | solution.py:817
  99.6 0.8 shard_map.90
  100.5 5.6 %collective-permute-start.12 = (f32[1,32,128]{2,1,0:T(8,128)S(1)}, f32[1,32,128]{2,1,0:T(8,128)S(1)}, u32[]{:S(2)}, u32[]{:S(2)}) collective-permute-start(f32[1,32,128]{2,1,0:T(8,128)S(1)} %get-tuple-element.113), channel_id=1, source_target_pairs={{0,764},{4,8},{8,4},{12,16},{16,12},{20,24},{24,20},{28,32},{32,28... | collective-permute-start | bytes 49160 | tf_op jit(solution)/shard_map/ppermute | solution.py:789
  106.1 1.9 %collective-permute-start.13 = (f32[1,32,128]{2,1,0:T(8,128)S(1)}, f32[1,32,128]{2,1,0:T(8,128)S(1)}, u32[]{:S(2)}, u32[]{:S(2)}) collective-permute-start(f32[1,32,128]{2,1,0:T(8,128)S(1)} %get-tuple-element.114), channel_id=1, source_target_pairs={{0,4},{4,0},{8,12},{12,8},{16,20},{20,16},{24,28},{28,24},{32,36},... | collective-permute-start | bytes 49160 | tf_op jit(solution)/shard_map/ppermute | solution.py:796
  108.1 0.4 shard_map.92.spread_ref
  108.5 0.5 shard_map.91.kv_in
  109.0 1.7 %collective-permute-done.12.h0 = f32[1,32,128]{2,1,0:T(8,128)S(1)} collective-permute-done((f32[1,32,128]{2,1,0:T(8,128)S(1)}, f32[1,32,128]{2,1,0:T(8,128)S(1)}, u32[]{:S(2)}, u32[]{:S(2)}) %collective-permute-start.12) | collective-permute-done | bytes 16416 | tf_op jit(solution)/shard_map/ppermute | solution.py:789
  110.7 0.2 collective-permute-done.13.h1
  110.8 1.1 shard_map.93
  111.9 6.2 %all-to-all-start = ((f32[64,1,128]{2,1,0:T(1,128)}), f32[64,1,128]{2,1,0:T(1,128)S(1)}, u32[]{:S(2)}, u32[]{:S(2)}) async-start(f32[64,1,128]{2,1,0:T(1,128)} %bitcast.5), calls=%async_computation | async-start | bytes 65536 | tf_op jit(solution)/shard_map/all_to_all | solution.py:916
  118.2 0.4 shard_map.94
  118.6 8.2 %collective-permute-start.14 = (f32[1,32,128]{2,1,0:T(8,128)S(1)}, f32[1,32,128]{2,1,0:T(8,128)S(1)}, u32[]{:S(2)}, u32[]{:S(2)}) collective-permute-start(f32[1,32,128]{2,1,0:T(8,128)S(1)} %get-tuple-element.124), channel_id=1, source_target_pairs={{0,764},{4,8},{8,4},{12,16},{16,12},{20,24},{24,20},{28,32},{32,28... | collective-permute-start | bytes 49160 | tf_op jit(solution)/shard_map/ppermute | solution.py:789
  126.8 0.7 all-to-all-done.rows_ref
  127.5 0.7 shard_map.95
  128.1 3.5 %all-to-all-start.1 = ((f32[12,1,128]{2,1,0:T(1,128)}), f32[12,1,128]{2,1,0:T(1,128)S(1)}, u32[]{:S(2)}, u32[]{:S(2)}) async-start(f32[12,1,128]{2,1,0:T(1,128)} %shard_map.95), calls=%async_computation.1 | async-start | bytes 12288 | tf_op jit(solution)/shard_map/all_to_all | solution.py:924
  131.6 3.3 %all-gather.3 = f32[2,32,128]{2,1,0:T(8,128)S(1)} all-gather(f32[1,32,128]{2,1,0:T(8,128)S(1)} %get-tuple-element.125), channel_id=5, replica_groups={{0,4},{8,12},{16,20},{24,28},{32,36},{40,44},{1,5},{9,13},{17,21},{25,2..., dimensions={0}, use_global_device_ids=true | all-gather | bytes 49152 | tf_op jit(solution)/shard_map/all_gather | solution.py:925
  134.9 6.8 %all-gather.4 = f32[4,16,128]{2,1,0:T(8,128)S(1)} all-gather(f32[1,16,128]{2,1,0:T(8,128)S(1)} %shard_map.96), channel_id=6, replica_groups=mesh['outer'=16,'ring'=12,'narrow'=4] {'narrow'}, dimensions={0}, use_global_device_ids=true | all-gather | bytes 40960 | tf_op jit(solution)/shard_map/all_gather | solution.py:929
  141.8 0.4 shard_map.97.late_ref
  142.2 0.8 shard_map.98
  (22 shorter events, 0.5 us)
Async XLA Ops:
  0.6 24.7 %copy-start.2 = (bf16[256,256]{1,0:T(8,128)(2,1)S(1)}, bf16[256,256]{1,0:T(8,128)(2,1)}, u32[]{:S(2)}) copy-start(bf16[256,256]{1,0:T(8,128)(2,1)} %constant.8.clone.abs_hbm.abs_ref) | copy-start | bytes 393220
  2.9 28.3 %collective-permute-start = (f32[2,32,128]{2,1,0:T(8,128)S(1)}, f32[2,32,128]{2,1,0:T(8,128)S(1)}, u32[]{:S(2)}, u32[]{:S(2)}) collective-permute-start(f32[2,32,128]{2,1,0:T(8,128)S(1)} %get-tuple-element.71), channel_id=1, source_target_pairs={{0,764},{4,8},{8,4},{12,16},{16,12},{20,24},{24,20},{28,32},{32,28... | collective-permute-start | bytes 98312 | tf_op jit(solution)/shard_map/ppermute | solution.py:789
  23.4 7.8 %collective-permute-start.1 = (f32[2,32,128]{2,1,0:T(8,128)S(1)}, f32[2,32,128]{2,1,0:T(8,128)S(1)}, u32[]{:S(2)}, u32[]{:S(2)}) collective-permute-start(f32[2,32,128]{2,1,0:T(8,128)S(1)} %get-tuple-element.72), channel_id=1, source_target_pairs={{0,4},{4,0},{8,12},{12,8},{16,20},{20,16},{24,28},{28,24},{32,36},... | collective-permute-start | bytes 98312 | tf_op jit(solution)/shard_map/ppermute | solution.py:796
  26.2 12.5 %collective-permute-start.2 = (f32[6,4,16,128]{3,2,1,0:T(8,128)S(1)}, f32[6,4,16,128]{3,2,1,0:T(8,128)S(1)}, u32[]{:S(2)}, u32[]{:S(2)}) collective-permute-start(f32[6,4,16,128]{3,2,1,0:T(8,128)S(1)} %get-tuple-element.74), channel_id=1, source_target_pairs={{0,1},{1,2},{2,3},{3,0},{4,5},{5,6},{6,7},{7,4},{8,9},{9,10},{10,1... | collective-permute-start | bytes 589832 | tf_op jit(solution)/shard_map/ppermute | solution.py:822
  29.3 9.4 %collective-permute-start.3 = (f32[6,4,16,128]{3,2,1,0:T(8,128)S(1)}, f32[6,4,16,128]{3,2,1,0:T(8,128)S(1)}, u32[]{:S(2)}, u32[]{:S(2)}) collective-permute-start(f32[6,4,16,128]{3,2,1,0:T(8,128)S(1)} %get-tuple-element.75), channel_id=1, source_target_pairs={{0,3},{1,0},{2,1},{3,2},{4,7},{5,4},{6,5},{7,6},{8,11},{9,8},{10,9... | collective-permute-start | bytes 589832 | tf_op jit(solution)/shard_map/ppermute | solution.py:823
  31.2 7.5 %copy-start.1 = (bf16[384,256]{1,0:T(8,128)(2,1)S(1)}, bf16[384,256]{1,0:T(8,128)(2,1)}, u32[]{:S(2)}) copy-start(bf16[384,256]{1,0:T(8,128)(2,1)} %constant.6.clone.grad_ref) | copy-start | bytes 589828
  31.4 7.4 %copy-start = (bf16[256,256]{1,0:T(8,128)(2,1)S(1)}, bf16[256,256]{1,0:T(8,128)(2,1)}, u32[]{:S(2)}) copy-start(bf16[256,256]{1,0:T(8,128)(2,1)} %constant.7.clone.diver_ref) | copy-start | bytes 393220
  39.6 10.2 %collective-permute-start.4 = (f32[1,32,128]{2,1,0:T(8,128)S(1)}, f32[1,32,128]{2,1,0:T(8,128)S(1)}, u32[]{:S(2)}, u32[]{:S(2)}) collective-permute-start(f32[1,32,128]{2,1,0:T(8,128)S(1)} %get-tuple-element.78), channel_id=1, source_target_pairs={{0,764},{4,8},{8,4},{12,16},{16,12},{20,24},{24,20},{28,32},{32,28... | collective-permute-start | bytes 49160 | tf_op jit(solution)/shard_map/ppermute | solution.py:789
  42.9 6.9 %collective-permute-start.5 = (f32[1,32,128]{2,1,0:T(8,128)S(1)}, f32[1,32,128]{2,1,0:T(8,128)S(1)}, u32[]{:S(2)}, u32[]{:S(2)}) collective-permute-start(f32[1,32,128]{2,1,0:T(8,128)S(1)} %get-tuple-element.79), channel_id=1, source_target_pairs={{0,4},{4,0},{8,12},{12,8},{16,20},{20,16},{24,28},{28,24},{32,36},... | collective-permute-start | bytes 49160 | tf_op jit(solution)/shard_map/ppermute | solution.py:796
  50.4 10.2 %collective-permute-start.6 = (f32[1,32,128]{2,1,0:T(8,128)S(1)}, f32[1,32,128]{2,1,0:T(8,128)S(1)}, u32[]{:S(2)}, u32[]{:S(2)}) collective-permute-start(f32[1,32,128]{2,1,0:T(8,128)S(1)} %get-tuple-element.87), channel_id=1, source_target_pairs={{0,764},{4,8},{8,4},{12,16},{16,12},{20,24},{24,20},{28,32},{32,28... | collective-permute-start | bytes 49160 | tf_op jit(solution)/shard_map/ppermute | solution.py:789
  55.7 4.9 %collective-permute-start.7 = (f32[1,32,128]{2,1,0:T(8,128)S(1)}, f32[1,32,128]{2,1,0:T(8,128)S(1)}, u32[]{:S(2)}, u32[]{:S(2)}) collective-permute-start(f32[1,32,128]{2,1,0:T(8,128)S(1)} %get-tuple-element.88), channel_id=1, source_target_pairs={{0,4},{4,0},{8,12},{12,8},{16,20},{20,16},{24,28},{28,24},{32,36},... | collective-permute-start | bytes 49160 | tf_op jit(solution)/shard_map/ppermute | solution.py:796
  69.8 10.2 %collective-permute-start.8 = (f32[1,32,128]{2,1,0:T(8,128)S(1)}, f32[1,32,128]{2,1,0:T(8,128)S(1)}, u32[]{:S(2)}, u32[]{:S(2)}) collective-permute-start(f32[1,32,128]{2,1,0:T(8,128)S(1)} %get-tuple-element.98), channel_id=1, source_target_pairs={{0,764},{4,8},{8,4},{12,16},{16,12},{20,24},{24,20},{28,32},{32,28... | collective-permute-start | bytes 49160 | tf_op jit(solution)/shard_map/ppermute | solution.py:789
  75.8 4.8 %collective-permute-start.9 = (f32[1,32,128]{2,1,0:T(8,128)S(1)}, f32[1,32,128]{2,1,0:T(8,128)S(1)}, u32[]{:S(2)}, u32[]{:S(2)}) collective-permute-start(f32[1,32,128]{2,1,0:T(8,128)S(1)} %get-tuple-element.99), channel_id=1, source_target_pairs={{0,4},{4,0},{8,12},{12,8},{16,20},{20,16},{24,28},{28,24},{32,36},... | collective-permute-start | bytes 49160 | tf_op jit(solution)/shard_map/ppermute | solution.py:796
  81.2 10.3 %collective-permute-start.10 = (f32[1,32,128]{2,1,0:T(8,128)S(1)}, f32[1,32,128]{2,1,0:T(8,128)S(1)}, u32[]{:S(2)}, u32[]{:S(2)}) collective-permute-start(f32[1,32,128]{2,1,0:T(8,128)S(1)} %get-tuple-element.104), channel_id=1, source_target_pairs={{0,764},{4,8},{8,4},{12,16},{16,12},{20,24},{24,20},{28,32},{32,28... | collective-permute-start | bytes 49160 | tf_op jit(solution)/shard_map/ppermute | solution.py:789
  86.6 4.9 %collective-permute-start.11 = (f32[1,32,128]{2,1,0:T(8,128)S(1)}, f32[1,32,128]{2,1,0:T(8,128)S(1)}, u32[]{:S(2)}, u32[]{:S(2)}) collective-permute-start(f32[1,32,128]{2,1,0:T(8,128)S(1)} %get-tuple-element.105), channel_id=1, source_target_pairs={{0,4},{4,0},{8,12},{12,8},{16,20},{20,16},{24,28},{28,24},{32,36},... | collective-permute-start | bytes 49160 | tf_op jit(solution)/shard_map/ppermute | solution.py:796
  100.5 10.2 %collective-permute-start.12 = (f32[1,32,128]{2,1,0:T(8,128)S(1)}, f32[1,32,128]{2,1,0:T(8,128)S(1)}, u32[]{:S(2)}, u32[]{:S(2)}) collective-permute-start(f32[1,32,128]{2,1,0:T(8,128)S(1)} %get-tuple-element.113), channel_id=1, source_target_pairs={{0,764},{4,8},{8,4},{12,16},{16,12},{20,24},{24,20},{28,32},{32,28... | collective-permute-start | bytes 49160 | tf_op jit(solution)/shard_map/ppermute | solution.py:789
  106.1 1.9 %copy-start.3 = (s32[1,1,64]{2,1,0:T(1,128)S(1)}, s32[1,1,64]{2,1,0:T(1,128)}, u32[]{:S(2)}) copy-start(s32[1,1,64]{2,1,0:T(1,128)} %param.8) | copy-start | bytes 772
  106.1 4.8 %collective-permute-start.13 = (f32[1,32,128]{2,1,0:T(8,128)S(1)}, f32[1,32,128]{2,1,0:T(8,128)S(1)}, u32[]{:S(2)}, u32[]{:S(2)}) collective-permute-start(f32[1,32,128]{2,1,0:T(8,128)S(1)} %get-tuple-element.114), channel_id=1, source_target_pairs={{0,4},{4,0},{8,12},{12,8},{16,20},{20,16},{24,28},{28,24},{32,36},... | collective-permute-start | bytes 49160 | tf_op jit(solution)/shard_map/ppermute | solution.py:796
  111.9 15.5 %all-to-all-start = ((f32[64,1,128]{2,1,0:T(1,128)}), f32[64,1,128]{2,1,0:T(1,128)S(1)}, u32[]{:S(2)}, u32[]{:S(2)}) async-start(f32[64,1,128]{2,1,0:T(1,128)} %bitcast.5), calls=%async_computation | async-start | bytes 65536 | tf_op jit(solution)/shard_map/all_to_all | solution.py:916
  118.6 16.3 %collective-permute-start.14 = (f32[1,32,128]{2,1,0:T(8,128)S(1)}, f32[1,32,128]{2,1,0:T(8,128)S(1)}, u32[]{:S(2)}, u32[]{:S(2)}) collective-permute-start(f32[1,32,128]{2,1,0:T(8,128)S(1)} %get-tuple-element.124), channel_id=1, source_target_pairs={{0,764},{4,8},{8,4},{12,16},{16,12},{20,24},{24,20},{28,32},{32,28... | collective-permute-start | bytes 49160 | tf_op jit(solution)/shard_map/ppermute | solution.py:789
  128.1 14.1 %all-to-all-start.1 = ((f32[12,1,128]{2,1,0:T(1,128)}), f32[12,1,128]{2,1,0:T(1,128)S(1)}, u32[]{:S(2)}, u32[]{:S(2)}) async-start(f32[12,1,128]{2,1,0:T(1,128)} %shard_map.95), calls=%async_computation.1 | async-start | bytes 12288 | tf_op jit(solution)/shard_map/all_to_all | solution.py:924

commit v11 on v9

--- a/solution.py
+++ b/solution.py
@@ -895,7 +895,7 @@
         spread_early_kernel, [(3, 64, 512)], [(64, 512)], order, first, residual, image
     )
     kv, spread = lax.optimization_barrier((kv, spread))
-    sums_shape = (lax.axis_size(REST), LANES)
+    sums_shape = (lax.axis_size("ring"), LANES)
     second, *parts, sums = call(
         sixth_kernel,
         [FIELD, FLUX, FIELD, sums_shape],
@@ -903,15 +903,15 @@
         kv, *halo, image, inverse, start, residual, early, metric, grad,
         out_spaces=[pltpu.VMEM] * 3 + [pltpu.HBM],
     )
-    sums = lax.all_to_all(sums[:, None], REST, 0, 0)
+    sums = lax.all_to_all(sums[:, None], "ring", 0, 0)
     kv, far, near, pack = call(
         rest_faces_kernel, [FIELD] + faces() + packs(), [], *parts, diver
     )
     far = swap_far(far)
     ring = lax.axis_size("ring")
-    (sums,) = call(half_sum_kernel, [(ring, 1, LANES)], [], sums)
+    (sums,) = call(half_sum_kernel, [(lax.axis_size(REST), 1, LANES)], [], sums)
     near, sums = lax.optimization_barrier((near, sums))
-    sums = lax.all_to_all(sums, "ring", 0, 0)
+    sums = lax.all_to_all(sums, REST, 0, 0)
     near = lax.all_gather(
         near, "ring", axis_index_groups=[[v, v + 1] for v in range(0, ring, 2)]
     )

time: 143 us -> 152 us (1.063)
  waiting for transfers between devices: 14.2 us -> 21.8 us
    all_to_all x2, waiting for transfers between devices: 0.68 us -> 8.3 us  [the longest x1 8.3 us: local(): sums = lax.all_to_all(sums[:, None], 'ring', 0, 0)]
  transfers between devices with their start and end apart: 17 -> 17, of which waited for: 8 -> 8; matrix products, arithmetic and copies ran while one was open for 0% -> 0% of each run, Pallas kernels for 3% -> 2%
where the time goes in v11:
time: 152 us; the launch traced here: 151 us
  starting transfers between devices  81.6 us (54%)
  blocking collectives  33.7 us (22%)
  waiting for transfers between devices  21.8 us (14%)
  Pallas kernels  12.2 us (8%)
    ppermute x7, starting transfers between devices, swap_far(): lax.ppermute(far, WIDE, [(w, (w + 1 if w % 2 else w - 1) % count) for w i...  54.2 us
    all_gather x2, blocking collectives, swap_edged(): return (far, near, lax.all_gather(pack, 'narrow'))  16.3 us
    ppermute x7, waiting for transfers between devices, swap_far(): lax.ppermute(far, WIDE, [(w, (w + 1 if w % 2 else w - 1) % count) for w i...  12.7 us
    pallas_call x21, Pallas kernels, call(): pl.pallas_call(kernel, out_shape=[jax.ShapeDtypeStruct(s, F32) for s in o...  12.2 us
    ppermute x6, starting transfers between devices, swap_wide(): lax.ppermute(near, WIDE, [(w, w ^ 1) for w in range(count)])  11.6 us
    all_to_all x1, waiting for transfers between devices, local(): sums = lax.all_to_all(sums[:, None], 'ring', 0, 0)  8.3 us
    all_to_all x1, starting transfers between devices, local(): sums = lax.all_to_all(sums, REST, 0, 0)  7.35 us
    all_gather x1, blocking collectives, swap_all(): return (far, near, lax.all_gather(pack, 'narrow'))  7.34 us
  transfers between devices with their start and end apart: 17, of which 8 were waited for; matrix products, arithmetic and copies ran while one was open for 0% of the time, Pallas kernels for 2%

profile of v11, /device:TPU:1, one launch (start us, length us, event | category | flops | bytes accessed | tf_op | source)
XLA Modules:
  0.0 150.9 jit_solution(17856424344040215697)
XLA Ops:
  0.6 2.6 %shard_map.77 = (f32[7,8,32,128]{3,2,1,0:T(8,128)S(1)}, f32[8,32,128]{2,1,0:T(8,128)S(1)}, f32[8,32,128]{2,1,0:T(8,128)S(1)}, f32[2,32,128]{2,1,0:T(8,128)S(1)},...) custom-call(s32[1,64]{1,0:T(1,128)} %bitcast.13, ...), custom_call_target="tpu_custom_call" | custom-call | tf_op jit(solution)/shard_map/pallas_call | solution.py:762
  3.3 20.5 %collective-permute-start = (f32[2,32,128]{2,1,0:T(8,128)S(1)}, f32[2,32,128]{2,1,0:T(8,128)S(1)}, u32[]{:S(2)}, u32[]{:S(2)}) collective-permute-start(f32[2,32,128]{2,1,0:T(8,128)S(1)} %get-tuple-element.64), channel_id=1, source_target_pairs={{0,764},{4,8},{8,4},{12,16},{16,12},{20,24},{24,20},{28,32},{32,28... | collective-permute-start | bytes 98312 | tf_op jit(solution)/shard_map/ppermute | solution.py:788
  23.8 1.9 %collective-permute-start.1 = (f32[2,32,128]{2,1,0:T(8,128)S(1)}, f32[2,32,128]{2,1,0:T(8,128)S(1)}, u32[]{:S(2)}, u32[]{:S(2)}) collective-permute-start(f32[2,32,128]{2,1,0:T(8,128)S(1)} %get-tuple-element.65), channel_id=1, source_target_pairs={{0,4},{4,0},{8,12},{12,8},{16,20},{20,16},{24,28},{28,24},{32,36},... | collective-permute-start | bytes 98312 | tf_op jit(solution)/shard_map/ppermute | solution.py:795
  25.7 3.1 %collective-permute-start.2 = (f32[6,4,16,128]{3,2,1,0:T(8,128)S(1)}, f32[6,4,16,128]{3,2,1,0:T(8,128)S(1)}, u32[]{:S(2)}, u32[]{:S(2)}) collective-permute-start(f32[6,4,16,128]{3,2,1,0:T(8,128)S(1)} %get-tuple-element.67), channel_id=1, source_target_pairs={{0,1},{1,2},{2,3},{3,0},{4,5},{5,6},{6,7},{7,4},{8,9},{9,10},{10,1... | collective-permute-start | bytes 589832 | tf_op jit(solution)/shard_map/ppermute | solution.py:821
  28.8 1.9 %collective-permute-start.3 = (f32[6,4,16,128]{3,2,1,0:T(8,128)S(1)}, f32[6,4,16,128]{3,2,1,0:T(8,128)S(1)}, u32[]{:S(2)}, u32[]{:S(2)}) collective-permute-start(f32[6,4,16,128]{3,2,1,0:T(8,128)S(1)} %get-tuple-element.68), channel_id=1, source_target_pairs={{0,3},{1,0},{2,1},{3,2},{4,7},{5,4},{6,5},{7,6},{8,11},{9,8},{10,9... | collective-permute-start | bytes 589832 | tf_op jit(solution)/shard_map/ppermute | solution.py:822
  30.8 7.3 %all-gather = f32[8,48,128]{2,1,0:T(8,128)S(1)} all-gather(f32[2,48,128]{2,1,0:T(8,128)S(1)} %shard_map.78), channel_id=2, replica_groups=mesh['outer'=16,'ring'=12,'narrow'=4] {'narrow'}, dimensions={0}, use_global_device_ids=true | all-gather | bytes 245760 | tf_op jit(solution)/shard_map/all_gather | solution.py:801
  38.2 0.8 shard_map.79
  39.1 3.6 %collective-permute-start.4 = (f32[1,32,128]{2,1,0:T(8,128)S(1)}, f32[1,32,128]{2,1,0:T(8,128)S(1)}, u32[]{:S(2)}, u32[]{:S(2)}) collective-permute-start(f32[1,32,128]{2,1,0:T(8,128)S(1)} %get-tuple-element.72), channel_id=1, source_target_pairs={{0,764},{4,8},{8,4},{12,16},{16,12},{20,24},{24,20},{28,32},{32,28... | collective-permute-start | bytes 49160 | tf_op jit(solution)/shard_map/ppermute | solution.py:788
  42.6 2.0 %collective-permute-start.5 = (f32[1,32,128]{2,1,0:T(8,128)S(1)}, f32[1,32,128]{2,1,0:T(8,128)S(1)}, u32[]{:S(2)}, u32[]{:S(2)}) collective-permute-start(f32[1,32,128]{2,1,0:T(8,128)S(1)} %get-tuple-element.73), channel_id=1, source_target_pairs={{0,4},{4,0},{8,12},{12,8},{16,20},{20,16},{24,28},{28,24},{32,36},... | collective-permute-start | bytes 49160 | tf_op jit(solution)/shard_map/ppermute | solution.py:795
  44.6 0.5 shard_map.80.kv_in
  45.1 4.2 %collective-permute-done.4.h0 = f32[1,32,128]{2,1,0:T(8,128)S(1)} collective-permute-done((f32[1,32,128]{2,1,0:T(8,128)S(1)}, f32[1,32,128]{2,1,0:T(8,128)S(1)}, u32[]{:S(2)}, u32[]{:S(2)}) %collective-permute-start.4) | collective-permute-done | bytes 16416 | tf_op jit(solution)/shard_map/ppermute | solution.py:788
  49.3 0.6 shard_map.81
  49.9 5.3 %collective-permute-start.6 = (f32[1,32,128]{2,1,0:T(8,128)S(1)}, f32[1,32,128]{2,1,0:T(8,128)S(1)}, u32[]{:S(2)}, u32[]{:S(2)}) collective-permute-start(f32[1,32,128]{2,1,0:T(8,128)S(1)} %get-tuple-element.81), channel_id=1, source_target_pairs={{0,764},{4,8},{8,4},{12,16},{16,12},{20,24},{24,20},{28,32},{32,28... | collective-permute-start | bytes 49160 | tf_op jit(solution)/shard_map/ppermute | solution.py:788
  55.2 1.9 %collective-permute-start.7 = (f32[1,32,128]{2,1,0:T(8,128)S(1)}, f32[1,32,128]{2,1,0:T(8,128)S(1)}, u32[]{:S(2)}, u32[]{:S(2)}) collective-permute-start(f32[1,32,128]{2,1,0:T(8,128)S(1)} %get-tuple-element.82), channel_id=1, source_target_pairs={{0,4},{4,0},{8,12},{12,8},{16,20},{20,16},{24,28},{28,24},{32,36},... | collective-permute-start | bytes 49160 | tf_op jit(solution)/shard_map/ppermute | solution.py:795
  57.1 0.4 shard_map.82
  57.5 2.5 %collective-permute-done.6.far_ref.h0 = f32[1,32,128]{2,1,0:T(8,128)S(1)} collective-permute-done((f32[1,32,128]{2,1,0:T(8,128)S(1)}, f32[1,32,128]{2,1,0:T(8,128)S(1)}, u32[]{:S(2)}, u32[]{:S(2)}) %collective-permute-start.6) | collective-permute-done | bytes 16416 | tf_op jit(solution)/shard_map/ppermute | solution.py:788
  60.2 8.3 %all-gather.1 = f32[4,144,128]{2,1,0:T(8,128)S(1)} all-gather(f32[1,144,128]{2,1,0:T(8,128)S(1)} %shard_map.83), channel_id=3, replica_groups=mesh['outer'=16,'ring'=12,'narrow'=4] {'narrow'}, dimensions={0}, use_global_device_ids=true | all-gather | bytes 368640 | tf_op jit(solution)/shard_map/all_gather | solution.py:816
  68.4 0.8 shard_map.84
  69.3 6.0 %collective-permute-start.8 = (f32[1,32,128]{2,1,0:T(8,128)S(1)}, f32[1,32,128]{2,1,0:T(8,128)S(1)}, u32[]{:S(2)}, u32[]{:S(2)}) collective-permute-start(f32[1,32,128]{2,1,0:T(8,128)S(1)} %get-tuple-element.92), channel_id=1, source_target_pairs={{0,764},{4,8},{8,4},{12,16},{16,12},{20,24},{24,20},{28,32},{32,28... | collective-permute-start | bytes 49160 | tf_op jit(solution)/shard_map/ppermute | solution.py:788
  75.3 1.9 %collective-permute-start.9 = (f32[1,32,128]{2,1,0:T(8,128)S(1)}, f32[1,32,128]{2,1,0:T(8,128)S(1)}, u32[]{:S(2)}, u32[]{:S(2)}) collective-permute-start(f32[1,32,128]{2,1,0:T(8,128)S(1)} %get-tuple-element.93), channel_id=1, source_target_pairs={{0,4},{4,0},{8,12},{12,8},{16,20},{20,16},{24,28},{28,24},{32,36},... | collective-permute-start | bytes 49160 | tf_op jit(solution)/shard_map/ppermute | solution.py:795
  77.3 0.5 shard_map.85
  77.7 1.7 %collective-permute-done.8.h0 = f32[1,32,128]{2,1,0:T(8,128)S(1)} collective-permute-done((f32[1,32,128]{2,1,0:T(8,128)S(1)}, f32[1,32,128]{2,1,0:T(8,128)S(1)}, u32[]{:S(2)}, u32[]{:S(2)}) %collective-permute-start.8) | collective-permute-done | bytes 16416 | tf_op jit(solution)/shard_map/ppermute | solution.py:788
  79.5 0.6 collective-permute-done.9.h1
  80.1 0.6 shard_map.86
  80.7 5.4 %collective-permute-start.10 = (f32[1,32,128]{2,1,0:T(8,128)S(1)}, f32[1,32,128]{2,1,0:T(8,128)S(1)}, u32[]{:S(2)}, u32[]{:S(2)}) collective-permute-start(f32[1,32,128]{2,1,0:T(8,128)S(1)} %get-tuple-element.98), channel_id=1, source_target_pairs={{0,764},{4,8},{8,4},{12,16},{16,12},{20,24},{24,20},{28,32},{32,28... | collective-permute-start | bytes 49160 | tf_op jit(solution)/shard_map/ppermute | solution.py:788
  86.1 1.9 %collective-permute-start.11 = (f32[1,32,128]{2,1,0:T(8,128)S(1)}, f32[1,32,128]{2,1,0:T(8,128)S(1)}, u32[]{:S(2)}, u32[]{:S(2)}) collective-permute-start(f32[1,32,128]{2,1,0:T(8,128)S(1)} %get-tuple-element.99), channel_id=1, source_target_pairs={{0,4},{4,0},{8,12},{12,8},{16,20},{20,16},{24,28},{28,24},{32,36},... | collective-permute-start | bytes 49160 | tf_op jit(solution)/shard_map/ppermute | solution.py:795
  88.1 0.4 shard_map.87
  88.5 2.5 %collective-permute-done.10.far_ref.h0 = f32[1,32,128]{2,1,0:T(8,128)S(1)} collective-permute-done((f32[1,32,128]{2,1,0:T(8,128)S(1)}, f32[1,32,128]{2,1,0:T(8,128)S(1)}, u32[]{:S(2)}, u32[]{:S(2)}) %collective-permute-start.10) | collective-permute-done | bytes 16416 | tf_op jit(solution)/shard_map/ppermute | solution.py:788
  91.1 8.0 %all-gather.2 = f32[4,144,128]{2,1,0:T(8,128)S(1)} all-gather(f32[1,144,128]{2,1,0:T(8,128)S(1)} %shard_map.88), channel_id=4, replica_groups=mesh['outer'=16,'ring'=12,'narrow'=4] {'narrow'}, dimensions={0}, use_global_device_ids=true | all-gather | bytes 368640 | tf_op jit(solution)/shard_map/all_gather | solution.py:816
  99.1 0.8 shard_map.89
  100.0 5.6 %collective-permute-start.12 = (f32[1,32,128]{2,1,0:T(8,128)S(1)}, f32[1,32,128]{2,1,0:T(8,128)S(1)}, u32[]{:S(2)}, u32[]{:S(2)}) collective-permute-start(f32[1,32,128]{2,1,0:T(8,128)S(1)} %get-tuple-element.107), channel_id=1, source_target_pairs={{0,764},{4,8},{8,4},{12,16},{16,12},{20,24},{24,20},{28,32},{32,28... | collective-permute-start | bytes 49160 | tf_op jit(solution)/shard_map/ppermute | solution.py:788
  105.6 1.9 %collective-permute-start.13 = (f32[1,32,128]{2,1,0:T(8,128)S(1)}, f32[1,32,128]{2,1,0:T(8,128)S(1)}, u32[]{:S(2)}, u32[]{:S(2)}) collective-permute-start(f32[1,32,128]{2,1,0:T(8,128)S(1)} %get-tuple-element.108), channel_id=1, source_target_pairs={{0,4},{4,0},{8,12},{12,8},{16,20},{20,16},{24,28},{28,24},{32,36},... | collective-permute-start | bytes 49160 | tf_op jit(solution)/shard_map/ppermute | solution.py:795
  107.6 0.4 shard_map.91.spread_ref
  108.0 0.5 shard_map.90.kv_in
  108.5 1.7 %collective-permute-done.12.h0 = f32[1,32,128]{2,1,0:T(8,128)S(1)} collective-permute-done((f32[1,32,128]{2,1,0:T(8,128)S(1)}, f32[1,32,128]{2,1,0:T(8,128)S(1)}, u32[]{:S(2)}, u32[]{:S(2)}) %collective-permute-start.12) | collective-permute-done | bytes 16416 | tf_op jit(solution)/shard_map/ppermute | solution.py:788
  110.2 0.2 collective-permute-done.13.h1
  110.3 0.5 shard_map.92
  110.8 0.6 broadcast_in_dim.3
  111.4 3.5 %all-to-all-start = ((f32[12,1,128]{2,1,0:T(1,128)}), f32[12,1,128]{2,1,0:T(1,128)S(1)}, u32[]{:S(2)}, u32[]{:S(2)}) async-start(f32[12,1,128]{2,1,0:T(1,128)} %broadcast_in_dim.3), calls=%async_computation | async-start | bytes 12288 | tf_op jit(solution)/shard_map/all_to_all | solution.py:906
  114.9 0.4 shard_map.93
  115.3 8.3 %all-to-all-done.rows_ref = f32[12,1,128]{2,1,0:T(1,128)S(1)} async-done(((f32[12,1,128]{2,1,0:T(1,128)}), f32[12,1,128]{2,1,0:T(1,128)S(1)}, u32[]{:S(2)}, u32[]{:S(2)}) %all-to-all-start) | async-done | bytes 6176 | tf_op jit(solution)/shard_map/all_to_all | solution.py:906
  123.6 0.6 shard_map.94
  124.3 7.4 %all-to-all-start.1 = ((f32[64,1,128]{2,1,0:T(1,128)}), f32[64,1,128]{2,1,0:T(1,128)S(1)}, u32[]{:S(2)}, u32[]{:S(2)}) async-start(f32[64,1,128]{2,1,0:T(1,128)} %shard_map.94), calls=%async_computation.1 | async-start | bytes 65536 | tf_op jit(solution)/shard_map/all_to_all | solution.py:914
  131.6 7.8 %collective-permute-start.14 = (f32[1,32,128]{2,1,0:T(8,128)S(1)}, f32[1,32,128]{2,1,0:T(8,128)S(1)}, u32[]{:S(2)}, u32[]{:S(2)}) collective-permute-start(f32[1,32,128]{2,1,0:T(8,128)S(1)} %get-tuple-element.118), channel_id=1, source_target_pairs={{0,764},{4,8},{8,4},{12,16},{16,12},{20,24},{24,20},{28,32},{32,28... | collective-permute-start | bytes 49160 | tf_op jit(solution)/shard_map/ppermute | solution.py:788
  139.4 3.6 %all-gather.3 = f32[2,32,128]{2,1,0:T(8,128)S(1)} all-gather(f32[1,32,128]{2,1,0:T(8,128)S(1)} %get-tuple-element.119), channel_id=5, replica_groups={{0,4},{8,12},{16,20},{24,28},{32,36},{40,44},{1,5},{9,13},{17,21},{25,2..., dimensions={0}, use_global_device_ids=true | all-gather | bytes 49152 | tf_op jit(solution)/shard_map/all_gather | solution.py:915
  143.1 6.5 %all-gather.4 = f32[4,16,128]{2,1,0:T(8,128)S(1)} all-gather(f32[1,16,128]{2,1,0:T(8,128)S(1)} %shard_map.95), channel_id=6, replica_groups=mesh['outer'=16,'ring'=12,'narrow'=4] {'narrow'}, dimensions={0}, use_global_device_ids=true | all-gather | bytes 40960 | tf_op jit(solution)/shard_map/all_gather | solution.py:919
  149.6 0.4 shard_map.96.late_ref
  150.0 0.9 shard_map.97
  (20 shorter events, 0.5 us)
Async XLA Ops:
  3.3 27.4 %collective-permute-start = (f32[2,32,128]{2,1,0:T(8,128)S(1)}, f32[2,32,128]{2,1,0:T(8,128)S(1)}, u32[]{:S(2)}, u32[]{:S(2)}) collective-permute-start(f32[2,32,128]{2,1,0:T(8,128)S(1)} %get-tuple-element.64), channel_id=1, source_target_pairs={{0,764},{4,8},{8,4},{12,16},{16,12},{20,24},{24,20},{28,32},{32,28... | collective-permute-start | bytes 98312 | tf_op jit(solution)/shard_map/ppermute | solution.py:788
  23.8 6.9 %collective-permute-start.1 = (f32[2,32,128]{2,1,0:T(8,128)S(1)}, f32[2,32,128]{2,1,0:T(8,128)S(1)}, u32[]{:S(2)}, u32[]{:S(2)}) collective-permute-start(f32[2,32,128]{2,1,0:T(8,128)S(1)} %get-tuple-element.65), channel_id=1, source_target_pairs={{0,4},{4,0},{8,12},{12,8},{16,20},{20,16},{24,28},{28,24},{32,36},... | collective-permute-start | bytes 98312 | tf_op jit(solution)/shard_map/ppermute | solution.py:795
  25.7 12.5 %collective-permute-start.2 = (f32[6,4,16,128]{3,2,1,0:T(8,128)S(1)}, f32[6,4,16,128]{3,2,1,0:T(8,128)S(1)}, u32[]{:S(2)}, u32[]{:S(2)}) collective-permute-start(f32[6,4,16,128]{3,2,1,0:T(8,128)S(1)} %get-tuple-element.67), channel_id=1, source_target_pairs={{0,1},{1,2},{2,3},{3,0},{4,5},{5,6},{6,7},{7,4},{8,9},{9,10},{10,1... | collective-permute-start | bytes 589832 | tf_op jit(solution)/shard_map/ppermute | solution.py:821
  28.8 9.4 %collective-permute-start.3 = (f32[6,4,16,128]{3,2,1,0:T(8,128)S(1)}, f32[6,4,16,128]{3,2,1,0:T(8,128)S(1)}, u32[]{:S(2)}, u32[]{:S(2)}) collective-permute-start(f32[6,4,16,128]{3,2,1,0:T(8,128)S(1)} %get-tuple-element.68), channel_id=1, source_target_pairs={{0,3},{1,0},{2,1},{3,2},{4,7},{5,4},{6,5},{7,6},{8,11},{9,8},{10,9... | collective-permute-start | bytes 589832 | tf_op jit(solution)/shard_map/ppermute | solution.py:822
  30.7 7.5 %copy-start.1 = (bf16[384,256]{1,0:T(8,128)(2,1)S(1)}, bf16[384,256]{1,0:T(8,128)(2,1)}, u32[]{:S(2)}) copy-start(bf16[384,256]{1,0:T(8,128)(2,1)} %constant.6.clone.grad_ref) | copy-start | bytes 589828
  30.8 7.4 %copy-start = (bf16[256,256]{1,0:T(8,128)(2,1)S(1)}, bf16[256,256]{1,0:T(8,128)(2,1)}, u32[]{:S(2)}) copy-start(bf16[256,256]{1,0:T(8,128)(2,1)} %constant.7.clone.diver_ref) | copy-start | bytes 393220
  39.1 10.2 %collective-permute-start.4 = (f32[1,32,128]{2,1,0:T(8,128)S(1)}, f32[1,32,128]{2,1,0:T(8,128)S(1)}, u32[]{:S(2)}, u32[]{:S(2)}) collective-permute-start(f32[1,32,128]{2,1,0:T(8,128)S(1)} %get-tuple-element.72), channel_id=1, source_target_pairs={{0,764},{4,8},{8,4},{12,16},{16,12},{20,24},{24,20},{28,32},{32,28... | collective-permute-start | bytes 49160 | tf_op jit(solution)/shard_map/ppermute | solution.py:788
  42.6 6.6 %collective-permute-start.5 = (f32[1,32,128]{2,1,0:T(8,128)S(1)}, f32[1,32,128]{2,1,0:T(8,128)S(1)}, u32[]{:S(2)}, u32[]{:S(2)}) collective-permute-start(f32[1,32,128]{2,1,0:T(8,128)S(1)} %get-tuple-element.73), channel_id=1, source_target_pairs={{0,4},{4,0},{8,12},{12,8},{16,20},{20,16},{24,28},{28,24},{32,36},... | collective-permute-start | bytes 49160 | tf_op jit(solution)/shard_map/ppermute | solution.py:795
  49.9 10.2 %collective-permute-start.6 = (f32[1,32,128]{2,1,0:T(8,128)S(1)}, f32[1,32,128]{2,1,0:T(8,128)S(1)}, u32[]{:S(2)}, u32[]{:S(2)}) collective-permute-start(f32[1,32,128]{2,1,0:T(8,128)S(1)} %get-tuple-element.81), channel_id=1, source_target_pairs={{0,764},{4,8},{8,4},{12,16},{16,12},{20,24},{24,20},{28,32},{32,28... | collective-permute-start | bytes 49160 | tf_op jit(solution)/shard_map/ppermute | solution.py:788
  55.2 4.9 %collective-permute-start.7 = (f32[1,32,128]{2,1,0:T(8,128)S(1)}, f32[1,32,128]{2,1,0:T(8,128)S(1)}, u32[]{:S(2)}, u32[]{:S(2)}) collective-permute-start(f32[1,32,128]{2,1,0:T(8,128)S(1)} %get-tuple-element.82), channel_id=1, source_target_pairs={{0,4},{4,0},{8,12},{12,8},{16,20},{20,16},{24,28},{28,24},{32,36},... | collective-permute-start | bytes 49160 | tf_op jit(solution)/shard_map/ppermute | solution.py:795
  69.3 10.2 %collective-permute-start.8 = (f32[1,32,128]{2,1,0:T(8,128)S(1)}, f32[1,32,128]{2,1,0:T(8,128)S(1)}, u32[]{:S(2)}, u32[]{:S(2)}) collective-permute-start(f32[1,32,128]{2,1,0:T(8,128)S(1)} %get-tuple-element.92), channel_id=1, source_target_pairs={{0,764},{4,8},{8,4},{12,16},{16,12},{20,24},{24,20},{28,32},{32,28... | collective-permute-start | bytes 49160 | tf_op jit(solution)/shard_map/ppermute | solution.py:788
  75.3 4.8 %collective-permute-start.9 = (f32[1,32,128]{2,1,0:T(8,128)S(1)}, f32[1,32,128]{2,1,0:T(8,128)S(1)}, u32[]{:S(2)}, u32[]{:S(2)}) collective-permute-start(f32[1,32,128]{2,1,0:T(8,128)S(1)} %get-tuple-element.93), channel_id=1, source_target_pairs={{0,4},{4,0},{8,12},{12,8},{16,20},{20,16},{24,28},{28,24},{32,36},... | collective-permute-start | bytes 49160 | tf_op jit(solution)/shard_map/ppermute | solution.py:795
  80.7 10.3 %collective-permute-start.10 = (f32[1,32,128]{2,1,0:T(8,128)S(1)}, f32[1,32,128]{2,1,0:T(8,128)S(1)}, u32[]{:S(2)}, u32[]{:S(2)}) collective-permute-start(f32[1,32,128]{2,1,0:T(8,128)S(1)} %get-tuple-element.98), channel_id=1, source_target_pairs={{0,764},{4,8},{8,4},{12,16},{16,12},{20,24},{24,20},{28,32},{32,28... | collective-permute-start | bytes 49160 | tf_op jit(solution)/shard_map/ppermute | solution.py:788
  86.1 4.9 %collective-permute-start.11 = (f32[1,32,128]{2,1,0:T(8,128)S(1)}, f32[1,32,128]{2,1,0:T(8,128)S(1)}, u32[]{:S(2)}, u32[]{:S(2)}) collective-permute-start(f32[1,32,128]{2,1,0:T(8,128)S(1)} %get-tuple-element.99), channel_id=1, source_target_pairs={{0,4},{4,0},{8,12},{12,8},{16,20},{20,16},{24,28},{28,24},{32,36},... | collective-permute-start | bytes 49160 | tf_op jit(solution)/shard_map/ppermute | solution.py:795
  100.0 10.2 %collective-permute-start.12 = (f32[1,32,128]{2,1,0:T(8,128)S(1)}, f32[1,32,128]{2,1,0:T(8,128)S(1)}, u32[]{:S(2)}, u32[]{:S(2)}) collective-permute-start(f32[1,32,128]{2,1,0:T(8,128)S(1)} %get-tuple-element.107), channel_id=1, source_target_pairs={{0,764},{4,8},{8,4},{12,16},{16,12},{20,24},{24,20},{28,32},{32,28... | collective-permute-start | bytes 49160 | tf_op jit(solution)/shard_map/ppermute | solution.py:788
  105.5 1.9 %copy-start.2 = (s32[1,1,64]{2,1,0:T(1,128)S(1)}, s32[1,1,64]{2,1,0:T(1,128)}, u32[]{:S(2)}) copy-start(s32[1,1,64]{2,1,0:T(1,128)} %param.8) | copy-start | bytes 772
  105.6 4.8 %collective-permute-start.13 = (f32[1,32,128]{2,1,0:T(8,128)S(1)}, f32[1,32,128]{2,1,0:T(8,128)S(1)}, u32[]{:S(2)}, u32[]{:S(2)}) collective-permute-start(f32[1,32,128]{2,1,0:T(8,128)S(1)} %get-tuple-element.108), channel_id=1, source_target_pairs={{0,4},{4,0},{8,12},{12,8},{16,20},{20,16},{24,28},{28,24},{32,36},... | collective-permute-start | bytes 49160 | tf_op jit(solution)/shard_map/ppermute | solution.py:795
  111.4 12.2 %all-to-all-start = ((f32[12,1,128]{2,1,0:T(1,128)}), f32[12,1,128]{2,1,0:T(1,128)S(1)}, u32[]{:S(2)}, u32[]{:S(2)}) async-start(f32[12,1,128]{2,1,0:T(1,128)} %broadcast_in_dim.3), calls=%async_computation | async-start | bytes 12288 | tf_op jit(solution)/shard_map/all_to_all | solution.py:906
  124.3 25.7 %all-to-all-start.1 = ((f32[64,1,128]{2,1,0:T(1,128)}), f32[64,1,128]{2,1,0:T(1,128)S(1)}, u32[]{:S(2)}, u32[]{:S(2)}) async-start(f32[64,1,128]{2,1,0:T(1,128)} %shard_map.94), calls=%async_computation.1 | async-start | bytes 65536 | tf_op jit(solution)/shard_map/all_to_all | solution.py:914
  131.6 11.3 %collective-permute-start.14 = (f32[1,32,128]{2,1,0:T(8,128)S(1)}, f32[1,32,128]{2,1,0:T(8,128)S(1)}, u32[]{:S(2)}, u32[]{:S(2)}) collective-permute-start(f32[1,32,128]{2,1,0:T(8,128)S(1)} %get-tuple-element.118), channel_id=1, source_target_pairs={{0,764},{4,8},{8,4},{12,16},{16,12},{20,24},{24,20},{28,32},{32,28... | collective-permute-start | bytes 49160 | tf_op jit(solution)/shard_map/ppermute | solution.py:788
